TPU v7x, 32 devices: a whole 2x2x4 slice. The times are simulated.
32 devices in a mesh: dp: 16 (over z, y, core), tensor: 2 (over x).
Axes of the slice: x: 2, y: 2, z: 4, core: 2. Of those that a mesh axis runs over, the one named last changes fastest.
Arguments:
- tokens: bfloat16 [16384, 1024], P(('dp', 'tensor')), may hold values from -6 to 6
- cond: bfloat16 [16, 128], P('dp'), may hold values from -6 to 6
- doc_lengths: int32 [16, 4], P('dp'), may hold values from 1 to 512, 1024 in all within a row
- w_ada: bfloat16 [128, 6144], replicated, may hold values from -0.25 to 0.25
- b_ada: float32 [6144], replicated, may hold values from -3 to 3
- gain_one: float32 [1024], replicated, may hold values from 0.5 to 1.5
- w_qkv: bfloat16 [3, 1024, 1024], P(None, None, 'tensor'), may hold values from -0.1875 to 0.1875
- w_out: bfloat16 [1024, 1024], P('tensor'), may hold values from -1.5 to 1.5
- gain_two: float32 [1024], replicated, may hold values from 0.5 to 1.5
- w_up: bfloat16 [1024, 4096], P(None, 'tensor'), may hold values from -0.1875 to 0.1875
- b_up: float32 [4096], P('tensor'), may hold values from -3 to 3
- w_down: bfloat16 [4096, 1024], P('tensor'), may hold values from -0.09375 to 0.09375
- b_down: float32 [1024], replicated, may hold values from -3 to 3
- cotangent: bfloat16 [16384, 1024], P(('dp', 'tensor')), may hold values from -6 to 6
Outputs:
- output: bfloat16 [16384, 1024], P(('dp', 'tensor'))
- grad_tokens: bfloat16 [16384, 1024], P(('dp', 'tensor'))
- grad_cond: float32 [16, 128], P('dp')
- grad_w_ada: float32 [128, 6144], replicated
- grad_b_ada: float32 [6144], replicated
- grad_gain_one: float32 [1024], replicated
- grad_w_qkv: float32 [3, 1024, 1024], P(None, None, 'tensor')
- grad_w_out: float32 [1024, 1024], P('tensor')
- grad_gain_two: float32 [1024], replicated
- grad_w_up: float32 [1024, 4096], P(None, 'tensor')
- grad_b_up: float32 [4096], P('tensor')
- grad_w_down: float32 [4096, 1024], P('tensor')
- grad_b_down: float32 [1024], replicated
Inputs may be any that keep to these rules, and one draw needn't show every extreme that they name: `doc_lengths`: each row sums to 1024, and its longest document has exactly half of 1024 tokens.
All inputs are finite; a program needn't handle non-finite values.
Results may differ from a plain program's by a relative error of at most 0.013.
The roundings to bfloat16 on the way count: a program that leaves them out, or rounds other values in their place, can miss the bound.
Values may be sent and summed in bfloat16 or wider, within the bound.
A program may use at most 192 MiB of HBM per device.

v0:
```python
import math

import jax
import jax.numpy as jnp
from jax import lax
from jax.sharding import PartitionSpec as P

HEAD = 64
BLOCK_MAX = 512


norm_eps = 1e-05
rope_base = 10000.0
masked_score = -1e30


def layer_norm(values, gain):
    center = values - jnp.mean(values, axis=-1, keepdims=True)
    spread = jnp.mean(center * center, axis=-1, keepdims=True)
    return center * lax.rsqrt(spread + norm_eps) * gain


def modulate(values, gain, shift, scale):
    return layer_norm(values, gain) * (1.0 + scale) + shift


def rotate(values, cosine, sine):
    half_size = values.shape[-1] // 2
    turned = jnp.concatenate([-values[..., half_size:], values[..., :half_size]], axis=-1)
    return values * cosine + turned * sine


def documents(lengths, length_all):
    doc_ends = jnp.cumsum(lengths)
    starts = doc_ends - lengths
    places = jnp.arange(length_all, dtype=jnp.int32)
    inside = ((places[:, None] >= starts[None, :]) & (places[:, None] < doc_ends[None, :])).astype(
        jnp.int32
    )
    numbers = jnp.arange(lengths.shape[0], dtype=jnp.int32)
    segment = jnp.sum(inside * numbers[None, :], axis=1)
    doc_first = jnp.sum(inside * starts[None, :], axis=1)
    doc_last = jnp.sum(inside * doc_ends[None, :], axis=1)
    return (segment, doc_first, doc_last)


def rope_tables(offsets, head_size):
    exponent = jnp.arange(head_size // 2, dtype=jnp.float32) * (2.0 / head_size)
    frequency = jnp.power(jnp.float32(rope_base), -exponent)
    angles = offsets.astype(jnp.float32)[:, None] * frequency[None, :]
    angles = jnp.concatenate([angles, angles], axis=-1)
    return (jnp.cos(angles)[:, None, :], jnp.sin(angles)[:, None, :])


def attend_forward(queries, keys_all, values_all, segment, low_block, high_block, block_rows):
    local_heads = queries.shape[1]
    score_scale = 1.0 / math.sqrt(queries.shape[2])

    def one_block(block_index):
        row_start = block_index * block_rows
        query_block = lax.dynamic_slice_in_dim(queries, row_start, block_rows, 0)
        query_docs = lax.dynamic_slice_in_dim(segment, row_start, block_rows, 0)

        def scores_at(key_index):
            key_start = key_index * block_rows
            key_block = lax.dynamic_slice_in_dim(keys_all, key_start, block_rows, 0)
            key_docs = lax.dynamic_slice_in_dim(segment, key_start, block_rows, 0)
            same_doc = (query_docs[:, None] == key_docs[None, :])[None]
            raw_scores = (
                jnp.einsum(
                    "qhd,khd->hqk", query_block, key_block, preferred_element_type=jnp.float32
                )
                * score_scale
            )
            return (same_doc, jnp.where(same_doc, raw_scores, masked_score))

        def stat_step(key_index, stats_now):
            row_top, row_total = stats_now
            same_doc, scores = scores_at(key_index)
            new_top = jnp.maximum(row_top, jnp.max(scores, axis=-1))
            exp_terms = jnp.where(same_doc, jnp.exp(scores - new_top[..., None]), 0.0)
            return (new_top, row_total * jnp.exp(row_top - new_top) + jnp.sum(exp_terms, axis=-1))

        start_top = jnp.full((local_heads, block_rows), masked_score, jnp.float32)
        start_total = jnp.zeros((local_heads, block_rows), jnp.float32)
        row_top, row_total = lax.fori_loop(
            low_block[block_index], high_block[block_index], stat_step, (start_top, start_total)
        )

        def out_step(key_index, summed):
            same_doc, scores = scores_at(key_index)
            weights = jnp.where(
                same_doc, jnp.exp(scores - row_top[..., None]) / row_total[..., None], 0.0
            ).astype(jnp.bfloat16)
            value_block = lax.dynamic_slice_in_dim(
                values_all, key_index * block_rows, block_rows, 0
            )
            return summed + jnp.einsum(
                "hqk,khd->qhd", weights, value_block, preferred_element_type=jnp.float32
            )

        mixed_block = lax.fori_loop(
            low_block[block_index],
            high_block[block_index],
            out_step,
            jnp.zeros(query_block.shape, jnp.float32),
        )
        return (mixed_block, row_top, row_total)

    return lax.map(one_block, jnp.arange(queries.shape[0] // block_rows, dtype=jnp.int32))


def attend_backward(
    queries,
    keys_all,
    values_all,
    segment,
    low_block,
    high_block,
    block_rows,
    row_tops,
    row_totals,
    grad_mixed,
):
    local_heads = queries.shape[1]
    score_scale = 1.0 / math.sqrt(queries.shape[2])

    def one_block(grads_kv, block_index):
        row_start = block_index * block_rows
        query_block = lax.dynamic_slice_in_dim(queries, row_start, block_rows, 0)
        query_docs = lax.dynamic_slice_in_dim(segment, row_start, block_rows, 0)
        grad_block = lax.dynamic_slice_in_dim(grad_mixed, row_start, block_rows, 0)
        row_top = row_tops[block_index]
        row_total = row_totals[block_index]

        def probs_at(key_index):
            key_start = key_index * block_rows
            key_block = lax.dynamic_slice_in_dim(keys_all, key_start, block_rows, 0)
            value_block = lax.dynamic_slice_in_dim(values_all, key_start, block_rows, 0)
            key_docs = lax.dynamic_slice_in_dim(segment, key_start, block_rows, 0)
            same_doc = (query_docs[:, None] == key_docs[None, :])[None]
            raw_scores = (
                jnp.einsum(
                    "qhd,khd->hqk", query_block, key_block, preferred_element_type=jnp.float32
                )
                * score_scale
            )
            probs = jnp.where(
                same_doc, jnp.exp(raw_scores - row_top[..., None]) / row_total[..., None], 0.0
            )
            grad_probs = jnp.einsum(
                "qhd,khd->hqk", grad_block, value_block, preferred_element_type=jnp.float32
            )
            return (probs, grad_probs, key_block)

        def delta_step(key_index, row_delta):
            probs, grad_probs, key_block = probs_at(key_index)
            return row_delta + jnp.sum(probs * grad_probs, axis=-1)

        row_delta = lax.fori_loop(
            low_block[block_index],
            high_block[block_index],
            delta_step,
            jnp.zeros((local_heads, block_rows), jnp.float32),
        )

        def grad_step(key_index, running):
            grad_query, grad_keys, grad_values = running
            probs, grad_probs, key_block = probs_at(key_index)
            grad_scores = (probs * (grad_probs - row_delta[..., None])).astype(jnp.bfloat16)
            key_start = key_index * block_rows
            grad_query = (
                grad_query
                + jnp.einsum(
                    "hqk,khd->qhd", grad_scores, key_block, preferred_element_type=jnp.float32
                )
                * score_scale
            )
            key_part = (
                jnp.einsum(
                    "hqk,qhd->khd", grad_scores, query_block, preferred_element_type=jnp.float32
                )
                * score_scale
            )
            value_part = jnp.einsum(
                "hqk,qhd->khd",
                probs.astype(jnp.bfloat16),
                grad_block,
                preferred_element_type=jnp.float32,
            )
            grad_keys = lax.dynamic_update_slice_in_dim(
                grad_keys,
                lax.dynamic_slice_in_dim(grad_keys, key_start, block_rows, 0) + key_part,
                key_start,
                0,
            )
            grad_values = lax.dynamic_update_slice_in_dim(
                grad_values,
                lax.dynamic_slice_in_dim(grad_values, key_start, block_rows, 0) + value_part,
                key_start,
                0,
            )
            return (grad_query, grad_keys, grad_values)

        start_query = jnp.zeros(query_block.shape, jnp.float32)
        grad_query, grad_keys, grad_values = lax.fori_loop(
            low_block[block_index],
            high_block[block_index],
            grad_step,
            (start_query, grads_kv[0], grads_kv[1]),
        )
        return ((grad_keys, grad_values), grad_query)

    start_kv = (jnp.zeros(keys_all.shape, jnp.float32), jnp.zeros(values_all.shape, jnp.float32))
    block_numbers = jnp.arange(queries.shape[0] // block_rows, dtype=jnp.int32)
    (grad_keys, grad_values), grad_queries = lax.scan(one_block, start_kv, block_numbers)
    return (grad_queries.reshape(queries.shape), grad_keys, grad_values)


def body(
    tokens,
    cond,
    doc_lengths,
    w_ada,
    b_ada,
    gain_one,
    w_qkv,
    w_out,
    gain_two,
    w_up,
    b_up,
    w_down,
    b_down,
    cotangent,
):
    tensor_size = lax.axis_size("tensor")
    local_rows = tokens.shape[0]
    seq_rows = local_rows * tensor_size
    block_rows = min(BLOCK_MAX, seq_rows)
    local_width = w_qkv.shape[2]
    local_heads = local_width // HEAD
    segment, doc_first, doc_last = documents(doc_lengths[0], seq_rows)
    cosine, sine = rope_tables(jnp.arange(seq_rows, dtype=jnp.int32) - doc_first, HEAD)
    block_count = seq_rows // block_rows
    low_block = doc_first.reshape(block_count, block_rows)[:, 0] // block_rows
    high_block = (doc_last.reshape(block_count, block_rows)[:, -1] + block_rows - 1) // block_rows
    modulation = jnp.dot(cond, w_ada, preferred_element_type=jnp.float32)[0] + b_ada
    shift_a, scale_a, gate_a, shift_m, scale_m, gate_m = jnp.split(modulation, 6)
    x_rows = tokens.astype(jnp.float32)

    def forward_pass():
        act_one = modulate(x_rows, gain_one, shift_a, scale_a).astype(jnp.bfloat16)
        rows_one = lax.all_gather(act_one, "tensor", axis=0, tiled=True)
        projected_qkv = jnp.einsum(
            "sd,tde->tse", rows_one, w_qkv, preferred_element_type=jnp.float32
        )
        projected_qkv = projected_qkv.reshape(3, seq_rows, local_heads, HEAD)
        query_rows = rotate(projected_qkv[0], cosine, sine).astype(jnp.bfloat16)
        key_rows = rotate(projected_qkv[1], cosine, sine).astype(jnp.bfloat16)
        value_rows = projected_qkv[2].astype(jnp.bfloat16)
        mixed_blocks, row_tops, row_totals = attend_forward(
            query_rows, key_rows, value_rows, segment, low_block, high_block, block_rows
        )
        mixed_heads = mixed_blocks.reshape(seq_rows, local_width).astype(jnp.bfloat16)
        projected = lax.psum_scatter(
            jnp.dot(mixed_heads, w_out, preferred_element_type=jnp.float32),
            "tensor",
            scatter_dimension=0,
            tiled=True,
        )
        middle = x_rows + gate_a * projected
        act_two = modulate(middle, gain_two, shift_m, scale_m).astype(jnp.bfloat16)
        rows_two = lax.all_gather(act_two, "tensor", axis=0, tiled=True)
        pre_act = jnp.dot(rows_two, w_up, preferred_element_type=jnp.float32) + b_up
        hidden = jax.nn.gelu(pre_act, approximate=True).astype(jnp.bfloat16)
        branch = (
            lax.psum_scatter(
                jnp.dot(hidden, w_down, preferred_element_type=jnp.float32),
                "tensor",
                scatter_dimension=0,
                tiled=True,
            )
            + b_down
        )
        return {
            "rows_one": rows_one,
            "query_rows": query_rows,
            "key_rows": key_rows,
            "value_rows": value_rows,
            "row_tops": row_tops,
            "row_totals": row_totals,
            "mixed_heads": mixed_heads,
            "projected": projected,
            "middle": middle,
            "rows_two": rows_two,
            "pre_act": pre_act,
            "hidden": hidden,
            "branch": branch,
            "output": middle + gate_m * branch,
        }

    first_pass = forward_pass()
    output = first_pass["output"].astype(jnp.bfloat16)
    forward_state = forward_pass()
    grad_out = cotangent.astype(jnp.float32)
    grad_branch = (grad_out * gate_m).astype(jnp.bfloat16)
    grad_gate_m = jnp.sum(grad_out * forward_state["branch"], axis=0)
    grad_b_down = jnp.sum(grad_branch.astype(jnp.float32), axis=0)
    full_branch = lax.all_gather(grad_branch, "tensor", axis=0, tiled=True)
    grad_w_down = jnp.einsum(
        "sf,sd->fd", forward_state["hidden"], full_branch, preferred_element_type=jnp.float32
    )
    grad_hidden = jnp.einsum("sd,fd->sf", full_branch, w_down, preferred_element_type=jnp.float32)
    gelu_value, gelu_back = jax.vjp(
        lambda values: jax.nn.gelu(values, approximate=True), forward_state["pre_act"]
    )
    grad_pre = gelu_back(grad_hidden)[0].astype(jnp.bfloat16)
    grad_b_up = jnp.sum(grad_pre.astype(jnp.float32), axis=0)
    grad_w_up = jnp.einsum(
        "sd,sf->df", forward_state["rows_two"], grad_pre, preferred_element_type=jnp.float32
    )
    grad_act_two = lax.psum_scatter(
        jnp.einsum("sf,df->sd", grad_pre, w_up, preferred_element_type=jnp.float32),
        "tensor",
        scatter_dimension=0,
        tiled=True,
    )
    second_value, second_back = jax.vjp(
        modulate, forward_state["middle"], gain_two, shift_m, scale_m
    )
    grad_middle, grad_gain_two, grad_shift_m, grad_scale_m = second_back(grad_act_two)
    grad_middle = grad_middle + grad_out
    grad_proj = (grad_middle * gate_a).astype(jnp.bfloat16)
    grad_gate_a = jnp.sum(grad_middle * forward_state["projected"], axis=0)
    full_proj = lax.all_gather(grad_proj, "tensor", axis=0, tiled=True)
    grad_w_out = jnp.einsum(
        "se,sd->ed", forward_state["mixed_heads"], full_proj, preferred_element_type=jnp.float32
    )
    grad_mixed = jnp.einsum(
        "sd,ed->se", full_proj, w_out, preferred_element_type=jnp.float32
    ).astype(jnp.bfloat16)
    grad_mixed = grad_mixed.reshape(seq_rows, local_heads, HEAD)
    grad_query, grad_key, grad_value = attend_backward(
        forward_state["query_rows"],
        forward_state["key_rows"],
        forward_state["value_rows"],
        segment,
        low_block,
        high_block,
        block_rows,
        forward_state["row_tops"],
        forward_state["row_totals"],
        grad_mixed,
    )
    rope_value, rope_back = jax.vjp(
        lambda values: rotate(values, cosine, sine),
        jnp.zeros((seq_rows, local_heads, HEAD), jnp.float32),
    )
    grad_qkv = (
        jnp.stack([rope_back(grad_query)[0], rope_back(grad_key)[0], grad_value])
        .reshape(3, seq_rows, local_width)
        .astype(jnp.bfloat16)
    )
    grad_w_qkv = jnp.einsum(
        "sd,tse->tde", forward_state["rows_one"], grad_qkv, preferred_element_type=jnp.float32
    )
    grad_act_one = lax.psum_scatter(
        jnp.einsum("tse,tde->sd", grad_qkv, w_qkv, preferred_element_type=jnp.float32),
        "tensor",
        scatter_dimension=0,
        tiled=True,
    )
    first_value, first_back = jax.vjp(modulate, x_rows, gain_one, shift_a, scale_a)
    grad_x, grad_gain_one, grad_shift_a, grad_scale_a = first_back(grad_act_one)
    grad_x = grad_x + grad_middle
    grad_mod_part = jnp.concatenate(
        [grad_shift_a, grad_scale_a, grad_gate_a, grad_shift_m, grad_scale_m, grad_gate_m]
    )
    grad_mod, grad_gain_one, grad_gain_two, grad_b_down = lax.psum(
        (grad_mod_part, grad_gain_one, grad_gain_two, grad_b_down), "tensor"
    )
    grad_cond = jnp.dot(w_ada.astype(jnp.float32), grad_mod, precision=lax.Precision.HIGHEST)[
        None, :
    ]
    grad_w_ada = cond.astype(jnp.float32)[0][:, None] * grad_mod[None, :]
    grad_b_ada = grad_mod
    (
        grad_w_ada,
        grad_b_ada,
        grad_gain_one,
        grad_w_qkv,
        grad_w_out,
        grad_gain_two,
        grad_w_up,
        grad_b_up,
        grad_w_down,
        grad_b_down,
    ) = lax.psum(
        (
            grad_w_ada,
            grad_b_ada,
            grad_gain_one,
            grad_w_qkv,
            grad_w_out,
            grad_gain_two,
            grad_w_up,
            grad_b_up,
            grad_w_down,
            grad_b_down,
        ),
        "dp",
    )
    return (
        output,
        grad_x.astype(jnp.bfloat16),
        grad_cond,
        grad_w_ada,
        grad_b_ada,
        grad_gain_one,
        grad_w_qkv,
        grad_w_out,
        grad_gain_two,
        grad_w_up,
        grad_b_up,
        grad_w_down,
        grad_b_down,
    )


def solution(mesh):
    placed = (
        P(("dp", "tensor"), None),
        P("dp", None),
        P("dp", None),
        P(),
        P(),
        P(),
        P(None, None, "tensor"),
        P("tensor", None),
        P(),
        P(None, "tensor"),
        P("tensor"),
        P("tensor", None),
        P(),
        P(("dp", "tensor"), None),
    )
    return jax.shard_map(
        body,
        mesh=mesh,
        in_specs=placed,
        out_specs=(
            P(("dp", "tensor"), None),
            P(("dp", "tensor"), None),
            P("dp", None),
            P(),
            P(),
            P(),
            P(None, None, "tensor"),
            P("tensor", None),
            P(),
            P(None, "tensor"),
            P("tensor"),
            P("tensor", None),
            P(),
        ),
        check_vma=False,
    )
```

profile of v0, /device:TPU:0, one launch (start us, length us, event | category | flops | bytes accessed | tf_op | source)
XLA Modules:
  0.0 1404.8 jit_solution(15902784697805481889)
XLA Ops:
  16.4 33.5 %all-gather.6.cloned.1.call-done = bf16[1024,1024]{1,0:T(8,128)(2,1)} async-done(((bf16[512,1024]{1,0:T(8,128)(2,1)}), bf16[1024,1024]{1,0:T(8,128)(2,1)}) %all-gather.6.cloned.1.call-update) | async-done | bytes 2097168 | tf_op jit(solution)/shard_map/all_gather | solution.py:253
  49.9 5.2 convolution_bitcast_fusion.1
  61.3 54.9 %while.111 = (s32[]{:T(128)}, bf16[2,512,8,64]{1,3,2,0:T(8,128)(2,1)}, f32[2,8,512]{2,1,0:T(8,128)S(1)}, f32[2,8,512]{2,1,0:T(8,128)S(1)}, s32[2]{0:T(128)S(1)},...) while((s32[]{:T(128)}, ...), condition=%wide.region_25.26_spmd, body=%wide.region_18.25_spmd.sunk | while | flops 835461120 | bytes 27367852 | solution.py:110
  68.7 6.4 while.117
  76.2 10.7 while.118
  78.5 5.9 fusion.258
  95.9 6.4 while.117
  103.4 10.7 while.118
  105.7 5.9 fusion.258
  119.9 3.3 fusion.150
  123.3 84.6 %reduce-scatter.11.cloned.1.call-done = f32[512,1024]{1,0:T(8,128)} async-done(((f32[1024,1024]{1,0:T(8,128)}), f32[512,1024]{1,0:T(8,128)}) %reduce-scatter.11.cloned.1.call-update) | async-done | bytes 2097168 | tf_op jit(solution)/shard_map/reduce_scatter | solution.py:265
  216.3 29.9 %all-gather.12.cloned.1.call-done = bf16[1024,1024]{1,0:T(8,128)(2,1)} async-done(((bf16[512,1024]{1,0:T(8,128)(2,1)}), bf16[1024,1024]{1,0:T(8,128)(2,1)}) %all-gather.12.cloned.1.call-update) | async-done | bytes 2097168 | tf_op jit(solution)/shard_map/all_gather | solution.py:273
  246.2 10.9 fusion.151
  257.0 24.3 %all-gather.10.cloned.1.call-done = bf16[1024,1024]{1,0:T(8,128)(2,1)} async-done(((bf16[512,1024]{1,0:T(8,128)(2,1)}), bf16[1024,1024]{1,0:T(8,128)(2,1)}) %all-gather.10.cloned.1.call-update) | async-done | bytes 2097168 | tf_op jit(solution)/shard_map/all_gather | solution.py:309
  281.4 15.5 %convert_reduce_fusion = (f32[2048]{0:T(1024)}, bf16[1024,2048]{1,0:T(8,128)(2,1)S(1)}, bf16[1024,2048]{1,0:T(8,128)(2,1)}) fusion(f32[1024,2048]{1,0:T(8,128)} %fusion.151, f32[2048]{0:T(1024)S(1)} %copy-done.73, bf16[1024,1024]{1,0:T(8,128)(2,1)} %all-gather.10.cloned.1.call-done, bf16[2048,1024]{1,0:T(8,128)(2,1)} %param.43), kind=kOutput, calls=%fused_computation.109 | convolution fusion | flops 4347394048 | bytes 23085056 | tf_op jit(solution)/shard_map/sd,fd->sf/dot_general | solution.py:313
  298.8 6.1 fusion.152
  305.2 54.2 %reduce-scatter.13.cloned.1.call-done = f32[512,1024]{1,0:T(8,128)} async-done(((f32[1024,1024]{1,0:T(8,128)}), f32[512,1024]{1,0:T(8,128)}) %reduce-scatter.13.cloned.1.call-update) | async-done | bytes 2097168 | tf_op jit(solution)/shard_map/reduce_scatter | solution.py:322
  359.4 4.0 multiply_reduce_fusion
  368.1 55.8 %while.108 = (s32[]{:T(128)}, bf16[2,512,8,64]{1,3,2,0:T(8,128)(2,1)}, s32[2]{0:T(128)S(1)}, s32[2]{0:T(128)S(1)}, s32[2]{0:T(128)S(1)}, /*index=5*/s32[1024]{0:...) while((s32[]{:T(128)}, ...), condition=%wide.region_13.14_spmd, body=%wide.region_6.13_spmd.sunk | while | flops 835461120 | bytes 27302296 | solution.py:110
  375.3 6.6 while.115
  382.9 11.0 while.116
  385.3 5.9 fusion.265
  403.2 6.5 while.115
  410.8 11.0 while.116
  413.2 5.9 fusion.265
  426.5 3.3 fusion.149
  430.4 4.1 convolution_convert_fusion
  437.6 115.3 %while.114 = (s32[]{:T(128)}, f32[1024,8,64]{0,2,1:T(8,128)}, f32[1024,8,64]{0,2,1:T(8,128)}, f32[2,512,8,64]{1,0,3,2:T(2,128)}, s32[2]{0:T(128)S(1)}, /*index=5...) while((s32[]{:T(128)}, f32[1024,8,64]{0,2,1:T(8,128)}, ...), condition=%wide.region_38.39_spmd, body=%wide.region_32.38_spmd.sunk | while | flops 1910243328 | bytes 119264984 | solution.py:216
  445.9 7.4 while.119
  449.5 3.1 fusion.237
  454.4 18.0 %while.120 = (s32[]{:T(128)}, f32[512,8,64]{0,2,1:T(8,128)}, f32[1024,8,64]{0,2,1:T(8,128)}, f32[1024,8,64]{0,2,1:T(8,128)}, s32[]{:T(128)}, /*index=5*/bf16[102...) while((s32[]{:T(128)}, f32[512,8,64]{0,2,1:T(8,128)}, ...), condition=%wide.region_37.37_spmd, body=%wide.region_36.36_spmd.sunk | while | flops 1360527360 | bytes 86041032 | solution.py:206
  456.6 3.8 bitcast_select_fusion.7
  466.0 3.9 fusion.251
  472.4 3.4 copy.128
  475.8 19.6 %dynamic_update_slice.38 = f32[2,512,8,64]{1,0,3,2:T(2,128)} dynamic-update-slice(f32[2,512,8,64]{1,0,3,2:T(2,128)} %get-tuple-element.2031, f32[1,512,8,64]{1,0,3,2:T(1,128)} %copy.128, s32[]{:T(128)} %get-tuple-element.2028, s32[]{:T(128)} %constant.196.clone.1..sunk.6, s32[]{:T(128)} %constant.196.clone.1..sunk.6, s32[]{:T(128)} %constant.196.clone.1..sunk.6) | dynamic-update-slice | bytes 2097156 | tf_op jit(solution)/shard_map/while/body/jit(dynamic_update_index_in_dim)/dynamic_update_slice | solution.py:110
  503.8 7.4 while.119
  507.4 3.1 fusion.237
  512.2 17.7 %while.120 = (s32[]{:T(128)}, f32[512,8,64]{0,2,1:T(8,128)}, f32[1024,8,64]{0,2,1:T(8,128)}, f32[1024,8,64]{0,2,1:T(8,128)}, s32[]{:T(128)}, /*index=5*/bf16[102...) while((s32[]{:T(128)}, f32[512,8,64]{0,2,1:T(8,128)}, ...), condition=%wide.region_37.37_spmd, body=%wide.region_36.36_spmd.sunk | while | flops 1360527360 | bytes 86041032 | solution.py:206
  514.5 3.9 bitcast_select_fusion.7
  523.9 3.6 fusion.251
  530.0 3.4 copy.128
  533.4 19.6 %dynamic_update_slice.38 = f32[2,512,8,64]{1,0,3,2:T(2,128)} dynamic-update-slice(f32[2,512,8,64]{1,0,3,2:T(2,128)} %get-tuple-element.2031, f32[1,512,8,64]{1,0,3,2:T(1,128)} %copy.128, s32[]{:T(128)} %get-tuple-element.2028, s32[]{:T(128)} %constant.196.clone.1..sunk.6, s32[]{:T(128)} %constant.196.clone.1..sunk.6, s32[]{:T(128)} %constant.196.clone.1..sunk.6) | dynamic-update-slice | bytes 2097156 | tf_op jit(solution)/shard_map/while/body/jit(dynamic_update_index_in_dim)/dynamic_update_slice | solution.py:110
  553.0 4.3 reshape.410
  574.8 6.8 convolution_bitcast_fusion.2
  581.8 131.3 %reduce-scatter.15.cloned.1.call-done = f32[512,1024]{1,0:T(8,128)} async-done(((f32[1024,1024]{1,0:T(8,128)}), f32[512,1024]{1,0:T(8,128)}) %reduce-scatter.15.cloned.1.call-update) | async-done | bytes 2097168 | tf_op jit(solution)/shard_map/reduce_scatter | solution.py:367
  713.1 3.6 fusion.115
  721.2 10.0 fusion.153
  731.4 23.0 %all-gather.8.cloned.1.call-done = bf16[1024,1024]{1,0:T(8,128)(2,1)} async-done(((bf16[512,1024]{1,0:T(8,128)(2,1)}), bf16[1024,1024]{1,0:T(8,128)(2,1)}) %all-gather.8.cloned.1.call-update) | async-done | bytes 2097168 | tf_op jit(solution)/shard_map/all_gather | solution.py:273
  754.4 15.3 %fusion.98 = f32[1024,1024]{1,0:T(8,128)} fusion(bf16[2048,1024]{1,0:T(8,128)(2,1)} %param.43, f32[2048]{0:T(1024)S(1)} %copy-done.74, bf16[1024,1024]{1,0:T(8,128)(2,1)} %all-gather.8.cloned.1.call-done, bf16[1024,2048]{1,0:T(8,128)(2,1)} %param.41), kind=kOutput, calls=%fused_computation.111 | convolution fusion | flops 8610906112 | bytes 14688256 | tf_op jit(solution)/shard_map/dot_general | solution.py:278
  770.4 11.2 fusion.156
  781.6 6.8 fusion.157
  791.8 5.4 convolution_bitcast_fusion
  797.2 13.6 reduce-scatter.17.cloned.1.call-done
  810.9 56.7 %reduce-scatter.9.cloned.1.call-done = f32[512,1024]{1,0:T(8,128)} async-done(((f32[1024,1024]{1,0:T(8,128)}), f32[512,1024]{1,0:T(8,128)}) %reduce-scatter.9.cloned.1.call-update) | async-done | bytes 2097168 | tf_op jit(solution)/shard_map/reduce_scatter | solution.py:277
  867.6 7.5 fusion.113
  875.2 7.3 all-reduce.6
  885.2 63.5 %all-reduce.4 = (f32[6144]{0:T(1024)}, f32[1024]{0:T(1024)}, f32[1024]{0:T(1024)}, f32[2048]{0:T(1024)}, f32[1024]{0:T(1024)}) all-reduce(f32[6144]{0:T(1024)S(1)} %get-tuple-element.867, f32[1024]{0:T(1024)S(1)} %get-tuple-element.868, f32[1024]{0:T(1024)S(1)} %get-tuple-element.869, ...), channel_id=1, replica_groups=mesh['dp'=16,'tensor'=2] {'dp'}, use_global_device_ids=true, to_apply=%region_51.52 | all-reduce | flops 11264 | bytes 90112 | tf_op jit(solution)/shard_map/psum | solution.py:398
  948.7 3.3 fusion.154
  951.9 422.8 %all-reduce.9.cloned.1.call-done = (f32[128,6144]{1,0:T(8,128)}, f32[3,1024,512]{1,2,0:T(8,128)}, f32[512,1024]{1,0:T(8,128)}, f32[1024,2048]{1,0:T(8,128)}, f32[2048,1024]{1,0:T(8,128)}) async-done(((f32[128,6144]{1,0:T(8,128)}, f32[3,1024,512]{1,2,0:T(8,128)}, f32[512,1024]{1,0:T(8,128)}, f32[1024,2048]{1,0:T(8,128)}, f32[2048,1024]{1,0:T(8,128)}), (f32[128,6144]{1,0:T(8,128)}, f32[3,1024,512]{1,2,0:T(8,128)}, ...) | async-done | bytes 28311568 | tf_op jit(solution)/shard_map/psum | solution.py:398
  1374.7 6.6 copy.91
  1381.3 4.0 copy.227
  1385.3 3.6 copy.228
  1388.9 4.3 copy.229
  1394.1 3.4 copy.230
  (402 shorter events, 149.5 us)
Async XLA Ops:
  7.2 42.7 %copy-start = (bf16[3,1024,512]{2,1,0:T(8,128)(2,1)S(1)}, bf16[3,1024,512]{2,1,0:T(8,128)(2,1)}, u32[]{:S(2)}) copy-start(bf16[3,1024,512]{2,1,0:T(8,128)(2,1)} %param.38) | copy-start | bytes 9437188
  7.2 5.2 copy-start.46
  7.2 42.6 %all-gather.6.cloned.1.call-start = ((), (), s32[]{:S(2)}) async-start(), calls=%async_computation.6 | async-start | bytes 3145728 | tf_op jit(solution)/shard_map/all_gather | solution.py:253
  7.3 3.3 copy-start.12
  13.9 194.0 %reduce-scatter.11.cloned.1.call-start = ((), (), s32[]{:S(2)}) async-start(), calls=%async_computation.11 | async-start | bytes 6291456 | tf_op jit(solution)/shard_map/reduce_scatter | solution.py:265
  16.3 41.2 %copy-start.27 = (f32[1024,64]{0,1:T(8,128)}, f32[1024,64]{0,1:T(8,128)S(1)}, u32[]{:S(2)}) copy-start(f32[1024,64]{0,1:T(8,128)S(1)} %get-tuple-element.909) | copy-start | bytes 786436
  116.2 3.7 copy-start.25
  123.2 84.7 %copy-start.36 = (f32[1024]{0:T(1024)S(1)}, f32[1024]{0:T(1024)}, u32[]{:S(2)}) copy-start(f32[1024]{0:T(1024)} %get-tuple-element.915) | copy-start | bytes 12292
  123.2 122.9 %all-gather.12.cloned.1.call-start = ((), (), s32[]{:S(2)}) async-start(), calls=%async_computation.12 | async-start | bytes 3145728 | tf_op jit(solution)/shard_map/all_gather | solution.py:273
  212.9 68.5 %all-gather.10.cloned.1.call-start = ((), (), s32[]{:S(2)}) async-start(), calls=%async_computation.10 | async-start | bytes 3145728 | tf_op jit(solution)/shard_map/all_gather | solution.py:309
  216.1 65.3 %copy-start.73 = (f32[2048]{0:T(1024)S(1)}, f32[2048]{0:T(1024)}, u32[]{:S(2)}) copy-start(f32[2048]{0:T(1024)} %param.42) | copy-start | bytes 24580
  216.1 143.3 %reduce-scatter.13.cloned.1.call-start = ((), (), s32[]{:S(2)}) async-start(), calls=%async_computation.13 | async-start | bytes 6291456 | tf_op jit(solution)/shard_map/reduce_scatter | solution.py:322
  281.4 17.5 %copy-start.69 = (bf16[1024,2048]{1,0:T(8,128)(2,1)S(1)}, bf16[1024,2048]{1,0:T(8,128)(2,1)}, u32[]{:S(2)}) copy-start(bf16[1024,2048]{1,0:T(8,128)(2,1)} %param.41) | copy-start | bytes 12582916
  304.9 125.4 %all-gather.14.cloned.1.call-start = ((), (), s32[]{:S(2)}) async-start(), calls=%async_computation.14 | async-start | bytes 3145728 | tf_op jit(solution)/shard_map/all_gather | solution.py:335
  359.4 4.1 copy-start.15
  359.4 4.1 copy-start.21
  366.9 214.8 %reduce-scatter.7.cloned.1.call-start = ((), (), s32[]{:S(2)}) async-start(), calls=%async_computation.7 | async-start | bytes 6291456 | tf_op jit(solution)/shard_map/reduce_scatter | solution.py:265
  429.9 283.2 %reduce-scatter.15.cloned.1.call-start = ((), (), s32[]{:S(2)}) async-start(), calls=%async_computation.15 | async-start | bytes 6291456 | tf_op jit(solution)/shard_map/reduce_scatter | solution.py:367
  437.6 8.3 copy-start.65
  437.6 8.3 copy-start.67
  437.7 8.3 copy-start.76
  456.6 3.9 copy-start.4
  456.6 3.9 copy-start.11
  472.4 23.1 %copy-start.66 = (s32[2]{0:T(128)S(1)}, s32[2]{0:T(128)}, u32[]{:S(2)}) copy-start(s32[2]{0:T(128)} %copy-done.65) | copy-start | bytes 28 | tf_op jit(solution)/shard_map/while
  472.4 23.1 %copy-start.68 = (s32[2]{0:T(128)S(1)}, s32[2]{0:T(128)}, u32[]{:S(2)}) copy-start(s32[2]{0:T(128)} %copy-done.67) | copy-start | bytes 28 | tf_op jit(solution)/shard_map/while
  472.4 23.0 %copy-start.77 = (s32[2]{0:T(128)S(1)}, s32[2]{0:T(128)}, u32[]{:S(2)}) copy-start(s32[2]{0:T(128)} %copy-done.76) | copy-start | bytes 28 | tf_op jit(solution)/shard_map/while
  495.5 8.3 copy-start.65
  495.5 8.3 copy-start.67
  495.5 8.3 copy-start.76
  514.4 3.9 copy-start.4
  514.4 3.9 copy-start.11
  529.9 23.0 %copy-start.66 = (s32[2]{0:T(128)S(1)}, s32[2]{0:T(128)}, u32[]{:S(2)}) copy-start(s32[2]{0:T(128)} %copy-done.65) | copy-start | bytes 28 | tf_op jit(solution)/shard_map/while
  530.0 23.0 %copy-start.68 = (s32[2]{0:T(128)S(1)}, s32[2]{0:T(128)}, u32[]{:S(2)}) copy-start(s32[2]{0:T(128)} %copy-done.67) | copy-start | bytes 28 | tf_op jit(solution)/shard_map/while
  530.0 23.0 %copy-start.77 = (s32[2]{0:T(128)S(1)}, s32[2]{0:T(128)}, u32[]{:S(2)}) copy-start(s32[2]{0:T(128)} %copy-done.76) | copy-start | bytes 28 | tf_op jit(solution)/shard_map/while
  553.0 4.3 copy-start.28
  581.7 131.4 %copy-start.37 = (f32[1024]{0:T(1024)S(1)}, f32[1024]{0:T(1024)}, u32[]{:S(2)}) copy-start(f32[1024]{0:T(1024)} %get-tuple-element.915) | copy-start | bytes 12292
  581.7 131.4 %copy-start.39 = (f32[1024]{0:T(1024)S(1)}, f32[1024]{0:T(1024)}, u32[]{:S(2)}) copy-start(f32[1024]{0:T(1024)} %copy-done.38) | copy-start | bytes 12292
  581.7 131.4 %copy-start.43 = (f32[512]{0:T(512)S(1)}, f32[512]{0:T(512)}, u32[]{:S(2)}) copy-start(f32[512]{0:T(512)} %copy-done.42) | copy-start | bytes 6148
  581.7 131.4 %copy-start.47 = (f32[1024]{0:T(1024)S(1)}, f32[1024]{0:T(1024)}, u32[]{:S(2)}) copy-start(f32[1024]{0:T(1024)} %param.37) | copy-start | bytes 12292
  581.7 135.0 %copy-start.57 = (f32[512]{0:T(512)S(1)}, f32[512]{0:T(512)}, u32[]{:S(2)}) copy-start(f32[512]{0:T(512)} %copy-done.56) | copy-start | bytes 6148
  581.7 135.0 %copy-start.53 = (f32[512]{0:T(512)S(1)}, f32[512]{0:T(512)}, u32[]{:S(2)}) copy-start(f32[512]{0:T(512)} %copy-done.52) | copy-start | bytes 6148
  581.7 172.7 %all-gather.8.cloned.1.call-start = ((), (), s32[]{:S(2)}) async-start(), calls=%async_computation.8 | async-start | bytes 3145728 | tf_op jit(solution)/shard_map/all_gather | solution.py:273
  713.1 3.7 copy-start.13
  713.1 3.7 copy-start.16
  713.1 4.1 copy-start.18
  721.1 89.8 %reduce-scatter.17.cloned.1.call-start = ((), (), s32[]{:S(2)}) async-start(), calls=%async_computation.16 | async-start | bytes 6291456 | tf_op jit(solution)/shard_map/reduce_scatter | solution.py:277
  731.1 23.3 %copy-start.74 = (f32[2048]{0:T(1024)S(1)}, f32[2048]{0:T(1024)}, u32[]{:S(2)}) copy-start(f32[2048]{0:T(1024)} %param.42) | copy-start | bytes 24580
  731.2 136.4 %reduce-scatter.9.cloned.1.call-start = ((), (), s32[]{:S(2)}) async-start(), calls=%async_computation.9 | async-start | bytes 6291456 | tf_op jit(solution)/shard_map/reduce_scatter | solution.py:277
  769.7 605.0 %all-reduce.9.cloned.1.call-start = ((), (), s32[]{:S(2)}) async-start(), calls=%async_computation.17 | async-start | bytes 56623104 | tf_op jit(solution)/shard_map/psum | solution.py:398
  770.4 11.2 copy-start.71
  770.4 11.2 copy-start.79
  781.6 6.8 copy-start.24
  781.6 6.8 copy-start.72
  788.4 3.4 copy-start.70
  791.8 75.8 %copy-start.49 = (f32[1024]{0:T(1024)S(1)}, f32[1024]{0:T(1024)}, u32[]{:S(2)}) copy-start(f32[1024]{0:T(1024)} %get-tuple-element.910) | copy-start | bytes 12292
  791.8 75.8 %copy-start.55 = (f32[512]{0:T(512)S(1)}, f32[512]{0:T(512)}, u32[]{:S(2)}) copy-start(f32[512]{0:T(512)} %copy-done.54) | copy-start | bytes 6148
  791.8 75.8 %copy-start.63 = (f32[1024]{0:T(1024)S(1)}, f32[1024]{0:T(1024)}, u32[]{:S(2)}) copy-start(f32[1024]{0:T(1024)} %param.44) | copy-start | bytes 12292
  797.2 77.9 %copy-start.61 = (f32[1024]{0:T(1024)S(1)}, f32[1024]{0:T(1024)}, u32[]{:S(2)}) copy-start(f32[1024]{0:T(1024)} %get-tuple-element.657) | copy-start | bytes 12292
  797.2 77.9 %copy-start.60 = (f32[1024]{0:T(1024)S(1)}, f32[1024]{0:T(1024)}, u32[]{:S(2)}) copy-start(f32[1024]{0:T(1024)} %get-tuple-element.653) | copy-start | bytes 12292
  797.2 77.9 %copy-start.58 = (f32[1024]{0:T(1024)S(1)}, f32[1024]{0:T(1024)}, u32[]{:S(2)}) copy-start(f32[1024]{0:T(1024)} %get-tuple-element.873) | copy-start | bytes 12292
  797.2 77.9 %copy-start.59 = (f32[1024]{0:T(1024)S(1)}, f32[1024]{0:T(1024)}, u32[]{:S(2)}) copy-start(f32[1024]{0:T(1024)} %get-tuple-element.651) | copy-start | bytes 12292
  1381.3 7.6 copy-start.22
  1385.3 7.9 slice-start
  1388.9 5.2 slice-start.1
  (46 other events, 80.8 us)
Sparse Core Ops, SparseCore 0:
  14.0 35.8 all-gather.5
  123.3 84.4 reduce-scatter.10
  213.0 33.1 all-gather.11
  248.2 33.1 all-gather.9
  305.0 54.3 reduce-scatter.12
  367.1 33.1 all-gather.13
  430.0 85.1 reduce-scatter.6
  581.8 131.2 reduce-scatter.14
  721.2 33.1 all-gather.7
  756.5 54.2 reduce-scatter.16
  813.3 54.3 reduce-scatter.8
  884.6 490.0 all-reduce.8
where the time goes:
time: 1420 us; the launch traced here: 1400 us
  waiting for transfers between devices  874 us (62%)
  matrix products  180 us (13%)
  local copies, waits for them, and re-layouts  148 us (10%)
  blocking collectives  70.8 us (5%)
  other arithmetic  58.6 us (4%)
  loops' own time  55.6 us (4%)
  between operations  15.4 us (1%)
    psum x1, waiting for transfers between devices, body(): lax.psum((grad_w_ada, grad_b_ada, grad_gain_one, grad_w_qkv, grad_w_out,...  423 us
    reduce_scatter x1, waiting for transfers between devices, body(): lax.psum_scatter(jnp.einsum('tse,tde->sd', grad_qkv, w_qkv, preferred_ele...  131 us
    reduce_scatter x2, waiting for transfers between devices, forward_pass(): lax.psum_scatter(jnp.dot(mixed_heads, w_out, preferred_element_type=jnp.f...  84.6 us
    reduce_scatter x2, waiting for transfers between devices, forward_pass(): lax.psum_scatter(jnp.dot(hidden, w_down, preferred_element_type=jnp.float...  70.4 us
    psum x1, blocking collectives, body(): lax.psum((grad_w_ada, grad_b_ada, grad_gain_one, grad_w_qkv, grad_w_out,...  63.5 us
    dynamic_update_slice x10, local copies, waits for them, and re-layouts, attend_forward(): lax.map(one_block, jnp.arange(queries.shape[0] // block_rows, dtype=jnp.i...  54.4 us
    reduce_scatter x1, waiting for transfers between devices, body(): lax.psum_scatter(jnp.einsum('sf,df->sd', grad_pre, w_up, preferred_elemen...  54.2 us
    all_gather x2, waiting for transfers between devices, forward_pass(): rows_two = lax.all_gather(act_two, 'tensor', axis=0, tiled=True)  52.8 us
  transfers between devices with their start and end apart: 12, of which 10 were waited for; matrix products, arithmetic and copies ran while one was open for 17% of the time, Pallas kernels for 0%

commit v1 on v0

v1 whole, which is shorter than its diff:
```python
import functools

import jax
import jax.numpy as jnp
from jax import lax
from jax.experimental import pallas as pl
from jax.experimental.pallas import tpu as pltpu
from jax.sharding import PartitionSpec as P

HEAD = 64
PAIR = 2 * HEAD
BLOCK = 256
ROWS = 512

norm_eps = 1e-05
rope_base = 10000.0
masked_score = -1e30
f32, bf16 = jnp.float32, jnp.bfloat16


def layer_norm(values, gain):
    center = values - jnp.mean(values, axis=-1, keepdims=True)
    spread = jnp.mean(center * center, axis=-1, keepdims=True)
    return center * lax.rsqrt(spread + norm_eps) * gain


def modulate(values, gain, shift, scale):
    return layer_norm(values, gain) * (1.0 + scale) + shift


def documents(lengths, places):
    numbers = jnp.arange(lengths.shape[0], dtype=jnp.int32)
    earlier = (numbers[None, :] < numbers[:, None]).astype(jnp.int32)
    starts = jnp.sum(earlier * lengths[None, :], axis=1)
    ends = starts + lengths
    inside = ((places[:, None] >= starts[None, :]) & (places[:, None] < ends[None, :])).astype(
        jnp.int32
    )
    segment = jnp.sum(inside * numbers[None, :], axis=1)
    doc_first = jnp.sum(inside * starts[None, :], axis=1)
    return segment, doc_first


def rope_tables(offsets):
    exponent = jnp.arange(HEAD // 2, dtype=f32) * (2.0 / HEAD)
    frequency = jnp.power(jnp.float32(rope_base), -exponent)
    angles = offsets.astype(f32)[:, None] * frequency[None, :]
    cosine, sine = jnp.cos(angles), jnp.sin(angles)
    repeat = PAIR // (HEAD // 2)
    return jnp.concatenate([cosine] * repeat, axis=-1), jnp.concatenate([sine] * repeat, axis=-1)


def turned(values):
    lane = lax.broadcasted_iota(jnp.int32, values.shape, 1)
    half = HEAD // 2
    from_right = pltpu.roll(values, PAIR - half, axis=1)
    from_left = pltpu.roll(values, half, axis=1)
    return jnp.where(lane % HEAD < half, -from_right, from_left)


def mm(a, b, da, db):
    return lax.dot_general(a, b, (((da,), (db,)), ((), ())), preferred_element_type=f32)


def qkv_kernel(x_ref, w_ref, cos_ref, sin_ref, o_ref):
    which = pl.program_id(1)
    y = mm(x_ref[...], w_ref[...], 1, 0)

    @pl.when(which < 2)
    def _():
        factor = jnp.where(which == 0, HEAD**-0.5, 1.0)
        for p in range(y.shape[1] // PAIR):
            u = y[:, p * PAIR : (p + 1) * PAIR]
            r = u * cos_ref[...] + turned(u) * sin_ref[...]
            o_ref[:, p * PAIR : (p + 1) * PAIR] = (r.astype(bf16) * factor.astype(bf16)).astype(bf16)

    @pl.when(which == 2)
    def _():
        o_ref[...] = y.astype(bf16)


def project_qkv(rows, w_qkv, cosine, sine):
    count, depth = rows.shape
    width = w_qkv.shape[2]
    return pl.pallas_call(
        qkv_kernel,
        grid=(count // ROWS, 3),
        in_specs=[
            pl.BlockSpec((ROWS, depth), lambda r, t: (r, 0)),
            pl.BlockSpec((None, depth, width), lambda r, t: (t, 0, 0)),
            pl.BlockSpec((ROWS, PAIR), lambda r, t: (r, 0)),
            pl.BlockSpec((ROWS, PAIR), lambda r, t: (r, 0)),
        ],
        out_specs=pl.BlockSpec((None, ROWS, width), lambda r, t: (t, r, 0)),
        out_shape=jax.ShapeDtypeStruct((3, count, width), bf16),
        compiler_params=pltpu.CompilerParams(vmem_limit_bytes=32 << 20),
        cost_estimate=pl.CostEstimate(
            flops=6 * count * depth * width, bytes_accessed=8 * count * width, transcendentals=0
        ),
        name="qkv",
    )(rows, w_qkv, cosine, sine)


def head_lanes(block, h):
    lane = lax.broadcasted_iota(jnp.int32, block.shape, 1)
    return jnp.where(lane // HEAD == h, block, jnp.zeros_like(block))


def transposed(block):
    return block.astype(f32).T


def forward_kernel(flag_ref, q_ref, k_ref, v_ref, segr_ref, segc_ref, o_ref, lse_ref, vt, m, l, acc):
    blocks = q_ref.shape[0] // BLOCK
    for b in range(blocks):
        vt[b] = transposed(v_ref[b * BLOCK : (b + 1) * BLOCK, :]).astype(bf16)

    @pl.loop(0, blocks)
    def _(qi):
        rows = pl.ds(pl.multiple_of(qi * BLOCK, BLOCK), BLOCK)
        q = q_ref[rows, :]
        m[...] = jnp.full(m.shape, masked_score, f32)
        l[...] = jnp.zeros(l.shape, f32)
        acc[...] = jnp.zeros(acc.shape, f32)

        @pl.loop(0, blocks)
        def _(ki):
            @pl.when(flag_ref[qi * blocks + ki] > 0)
            def _():
                cols = pl.ds(pl.multiple_of(ki * BLOCK, BLOCK), BLOCK)
                k = k_ref[cols, :]
                docs = segc_ref[cols, :]
                same = jnp.concatenate([docs] * (BLOCK // 128), axis=1) == segr_ref[qi]
                for h in range(2):
                    lo, hi = h * HEAD, (h + 1) * HEAD
                    s = jnp.where(same, mm(k, head_lanes(q, h), 1, 1), masked_score)
                    top = jnp.maximum(m[h], jnp.max(s, axis=0, keepdims=True))
                    p = jnp.exp(s - top)
                    shrink = jnp.exp(m[h] - top)
                    m[h] = top
                    l[h] = l[h] * shrink + jnp.sum(p, axis=0, keepdims=True)
                    acc[lo:hi, :] = acc[lo:hi, :] * shrink + mm(vt[ki, lo:hi, :], p.astype(bf16), 1, 0)

        for h in range(2):
            lo, hi = h * HEAD, (h + 1) * HEAD
            lse_ref[h, qi] = m[h] + jnp.log(l[h])
            acc[lo:hi, :] = acc[lo:hi, :] / l[h]
        o_ref[rows, :] = acc[...].T.astype(bf16)


def backward_kernel(
    flag_ref, q_ref, k_ref, v_ref, g_ref, o_ref, lse_ref, segr_ref, segc_ref, cos_ref, sin_ref,
    out_ref, kt, dk, dv, dq,
):
    blocks = q_ref.shape[0] // BLOCK
    for b in range(blocks):
        kt[b] = transposed(k_ref[b * BLOCK : (b + 1) * BLOCK, :]).astype(bf16)
    dk[...] = jnp.zeros(dk.shape, f32)
    dv[...] = jnp.zeros(dv.shape, f32)

    def turn_back(u, rows):
        return (u * cos_ref[rows, :] - turned(u) * sin_ref[rows, :]).astype(bf16)

    @pl.loop(0, blocks)
    def _(qi):
        rows = pl.ds(pl.multiple_of(qi * BLOCK, BLOCK), BLOCK)
        q, g = q_ref[rows, :], g_ref[rows, :]
        both = (g.astype(f32) * o_ref[rows, :].astype(f32)).T
        dq[...] = jnp.zeros(dq.shape, f32)

        @pl.loop(0, blocks)
        def _(ki):
            @pl.when(flag_ref[qi * blocks + ki] > 0)
            def _():
                cols = pl.ds(pl.multiple_of(ki * BLOCK, BLOCK), BLOCK)
                k, v = k_ref[cols, :], v_ref[cols, :]
                docs = segc_ref[cols, :]
                same = jnp.concatenate([docs] * (BLOCK // 128), axis=1) == segr_ref[qi]
                dk_sum, dv_sum = dk[cols, :], dv[cols, :]
                for h in range(2):
                    lo, hi = h * HEAD, (h + 1) * HEAD
                    delta = jnp.sum(both[lo:hi, :], axis=0, keepdims=True)
                    qh, gh = head_lanes(q, h), head_lanes(g, h)
                    s = jnp.where(same, mm(k, qh, 1, 1), masked_score)
                    p = jnp.exp(s - lse_ref[h, qi])
                    ds = (p * (mm(v, gh, 1, 1) - delta)).astype(bf16)
                    dv_sum = dv_sum + mm(p.astype(bf16), gh, 1, 0)
                    dk_sum = dk_sum + mm(ds, qh, 1, 0)
                    dq[lo:hi, :] = dq[lo:hi, :] + mm(kt[ki, lo:hi, :], ds, 1, 0)
                dk[cols, :] = dk_sum
                dv[cols, :] = dv_sum

        out_ref[0, rows, :] = turn_back(dq[...].T * (HEAD**-0.5), rows)

    @pl.loop(0, blocks)
    def _(b):
        rows = pl.ds(pl.multiple_of(b * BLOCK, BLOCK), BLOCK)
        out_ref[1, rows, :] = turn_back(dk[rows, :], rows)
        out_ref[2, rows, :] = dv[rows, :].astype(bf16)


def pieces_of(qkv, length):
    return [pl.BlockSpec((None, length, PAIR), functools.partial(lambda t, p, *_: (t, 0, p), t)) for t in range(3)]


def attend_forward(flags, qkv, seg_rows, seg_cols):
    _, length, width = qkv.shape
    blocks, pairs = length // BLOCK, width // PAIR
    return pl.pallas_call(
        forward_kernel,
        grid_spec=pltpu.PrefetchScalarGridSpec(
            num_scalar_prefetch=1,
            grid=(pairs,),
            in_specs=[
                *pieces_of(qkv, length),
                pl.BlockSpec((blocks, 1, BLOCK), lambda p, *_: (0, 0, 0)),
                pl.BlockSpec((length, 128), lambda p, *_: (0, 0)),
            ],
            out_specs=[
                pl.BlockSpec((length, PAIR), lambda p, *_: (0, p)),
                pl.BlockSpec((2, blocks, 1, BLOCK), lambda p, *_: (p, 0, 0, 0)),
            ],
            scratch_shapes=[
                pltpu.VMEM((blocks, PAIR, BLOCK), bf16),
                pltpu.VMEM((2, 1, BLOCK), f32),
                pltpu.VMEM((2, 1, BLOCK), f32),
                pltpu.VMEM((PAIR, BLOCK), f32),
            ],
        ),
        out_shape=[
            jax.ShapeDtypeStruct((length, width), bf16),
            jax.ShapeDtypeStruct((2 * pairs, blocks, 1, BLOCK), f32),
        ],
        compiler_params=pltpu.CompilerParams(vmem_limit_bytes=48 << 20),
        cost_estimate=pl.CostEstimate(
            flops=4 * length * length * width, bytes_accessed=8 * length * width, transcendentals=length * length * width // HEAD
        ),
        name="attend",
    )(flags, qkv, qkv, qkv, seg_rows, seg_cols)


def attend_backward(flags, qkv, grad, mixed, lse, seg_rows, seg_cols, cosine, sine):
    _, length, width = qkv.shape
    blocks, pairs = length // BLOCK, width // PAIR
    whole = pl.BlockSpec((length, PAIR), lambda p, *_: (0, p))
    table = pl.BlockSpec((length, PAIR), lambda p, *_: (0, 0))
    return pl.pallas_call(
        backward_kernel,
        grid_spec=pltpu.PrefetchScalarGridSpec(
            num_scalar_prefetch=1,
            grid=(pairs,),
            in_specs=[
                *pieces_of(qkv, length),
                whole,
                whole,
                pl.BlockSpec((2, blocks, 1, BLOCK), lambda p, *_: (p, 0, 0, 0)),
                pl.BlockSpec((blocks, 1, BLOCK), lambda p, *_: (0, 0, 0)),
                table,
                table,
                table,
            ],
            out_specs=pl.BlockSpec((3, length, PAIR), lambda p, *_: (0, 0, p)),
            scratch_shapes=[
                pltpu.VMEM((blocks, PAIR, BLOCK), bf16),
                pltpu.VMEM((length, PAIR), f32),
                pltpu.VMEM((length, PAIR), f32),
                pltpu.VMEM((PAIR, BLOCK), f32),
            ],
        ),
        out_shape=jax.ShapeDtypeStruct((3, length, width), bf16),
        compiler_params=pltpu.CompilerParams(vmem_limit_bytes=56 << 20),
        cost_estimate=pl.CostEstimate(
            flops=10 * length * length * width, bytes_accessed=16 * length * width, transcendentals=length * length * width // HEAD
        ),
        name="attend_back",
    )(flags, qkv, qkv, qkv, grad, mixed, lse, seg_rows, seg_cols, cosine, sine)


def body(
    tokens, cond, doc_lengths, w_ada, b_ada, gain_one, w_qkv, w_out, gain_two, w_up, b_up, w_down, b_down, cotangent
):
    tensor_size, dp_size = lax.axis_size("tensor"), lax.axis_size("dp")
    pair = tensor_size == 2
    cube = dp_size & (dp_size - 1) == 0
    own = tokens.shape[0]
    length = own * tensor_size
    me, place = lax.axis_index("tensor"), lax.axis_index("dp")

    def other(values):
        return lax.ppermute(values, "tensor", [(0, 1), (1, 0)])

    def all_rows(values):
        if pair:
            return jnp.concatenate([values, other(values)], axis=0)
        return lax.all_gather(values, "tensor", axis=0, tiled=True)

    def own_sum(values):
        if pair:
            return values[:own] + other(values[own:].astype(bf16)).astype(f32)
        return lax.psum_scatter(values, "tensor", scatter_dimension=0, tiled=True)

    def bit_of(b):
        return (place >> b) & 1

    def across(values, b):
        return lax.ppermute(values, "dp", [(d, d ^ (1 << b)) for d in range(dp_size)])

    def sum_over_dp(part):
        bits = dp_size.bit_length() - 1
        if not cube or part.shape[0] % (16 << bits):
            return lax.psum(part, "dp")
        for b in range(bits):
            half = part.shape[0] // 2
            low, high = part[:half], part[half:]
            first = bit_of(b) == 0
            send = jnp.where(first, high, low).astype(bf16)
            part = jnp.where(first, low, high) + across(send, b).astype(f32)
        part = part.astype(bf16)
        for b in reversed(range(bits)):
            got = across(part, b)
            first = bit_of(b) == 0
            part = jnp.concatenate([jnp.where(first, part, got), jnp.where(first, got, part)], axis=0)
        return part.astype(f32)

    places = jnp.arange(length, dtype=jnp.int32)
    if pair:
        places = (places + me * own) % length
    segment, doc_first = documents(doc_lengths[0], places)
    cosine, sine = rope_tables(places - doc_first)
    blocks = length // BLOCK
    in_blocks = segment.reshape(blocks, BLOCK)
    least, most = jnp.min(in_blocks, axis=1), jnp.max(in_blocks, axis=1)
    meets = (least[:, None] <= most[None, :]) & (least[None, :] <= most[:, None])
    flags = meets.astype(jnp.int32).reshape(-1)
    seg_rows = in_blocks[:, None, :]
    seg_cols = jnp.broadcast_to(segment[:, None], (length, 128))

    modulation = jnp.dot(cond, w_ada, preferred_element_type=f32)[0] + b_ada
    shift_a, scale_a, gate_a, shift_m, scale_m, gate_m = jnp.split(modulation, 6)
    x_rows = tokens.astype(f32)
    grad_out = cotangent.astype(f32)

    act_one = modulate(x_rows, gain_one, shift_a, scale_a).astype(bf16)
    rows_one = all_rows(act_one)
    grad_branch = (grad_out * gate_m).astype(bf16)
    full_branch = all_rows(grad_branch)
    qkv = project_qkv(rows_one, w_qkv, cosine, sine)
    mixed, lse = attend_forward(flags, qkv, seg_rows, seg_cols)
    projected = own_sum(jnp.dot(mixed, w_out, preferred_element_type=f32))
    middle = x_rows + gate_a * projected
    rows_two = all_rows(modulate(middle, gain_two, shift_m, scale_m).astype(bf16))
    pre_act = jnp.dot(rows_two, w_up, preferred_element_type=f32) + b_up
    hidden = jax.nn.gelu(pre_act, approximate=True).astype(bf16)

    grad_hidden = jnp.einsum("sd,fd->sf", full_branch, w_down, preferred_element_type=f32)
    _, gelu_back = jax.vjp(lambda values: jax.nn.gelu(values, approximate=True), pre_act)
    grad_pre = gelu_back(grad_hidden)[0].astype(bf16)
    grad_act_two = own_sum(jnp.einsum("sf,df->sd", grad_pre, w_up, preferred_element_type=f32))
    grad_w_down = sum_over_dp(jnp.einsum("sf,sd->fd", hidden, full_branch, preferred_element_type=f32))
    grad_w_up = sum_over_dp(jnp.einsum("sd,sf->df", rows_two, grad_pre, preferred_element_type=f32))

    branch = own_sum(jnp.dot(hidden, w_down, preferred_element_type=f32)) + b_down
    output = (middle + gate_m * branch).astype(bf16)
    grad_gate_m = jnp.sum(grad_out * branch, axis=0)
    grad_b_down = jnp.sum(grad_branch.astype(f32), axis=0)
    grad_b_up = jnp.sum(grad_pre.astype(f32), axis=0)

    _, second_back = jax.vjp(modulate, middle, gain_two, shift_m, scale_m)
    grad_middle, grad_gain_two, grad_shift_m, grad_scale_m = second_back(grad_act_two)
    grad_middle = grad_middle + grad_out
    full_proj = all_rows((grad_middle * gate_a).astype(bf16))
    grad_gate_a = jnp.sum(grad_middle * projected, axis=0)
    grad_mixed = jnp.einsum("sd,ed->se", full_proj, w_out, preferred_element_type=f32).astype(bf16)
    grad_w_out = sum_over_dp(jnp.einsum("se,sd->ed", mixed, full_proj, preferred_element_type=f32))
    grad_qkv = attend_backward(flags, qkv, grad_mixed, mixed, lse, seg_rows, seg_cols, cosine, sine)
    grad_act_one = own_sum(jnp.einsum("tse,tde->sd", grad_qkv, w_qkv, preferred_element_type=f32))
    grad_w_qkv = jnp.einsum("sd,tse->tde", rows_one, grad_qkv, preferred_element_type=f32)
    grad_w_qkv = sum_over_dp(grad_w_qkv.reshape(-1, grad_w_qkv.shape[2])).reshape(grad_w_qkv.shape)

    _, first_back = jax.vjp(modulate, x_rows, gain_one, shift_a, scale_a)
    grad_x, grad_gain_one, grad_shift_a, grad_scale_a = first_back(grad_act_one)
    grad_x = (grad_x + grad_middle).astype(bf16)

    small = jnp.concatenate(
        [
            grad_shift_a, grad_scale_a, grad_gate_a, grad_shift_m, grad_scale_m, grad_gate_m,
            grad_gain_one, grad_gain_two, grad_b_down,
        ]
    )
    small = lax.psum(small, "tensor")
    mod_size = modulation.shape[0]
    grad_mod = small[:mod_size]
    grad_cond = jnp.dot(w_ada.astype(f32), grad_mod, precision=lax.Precision.HIGHEST)[None, :]
    everyone = lax.all_gather(
        jnp.concatenate([small, grad_b_up, cond[0].astype(f32)])[None, :], "dp", axis=0, tiled=True
    )
    conds = everyone[:, -cond.shape[1] :]
    mods = everyone[:, :mod_size]
    grad_w_ada = jnp.einsum("nc,nm->cm", conds, mods, precision=lax.Precision.HIGHEST, preferred_element_type=f32)
    sums = jnp.sum(everyone, axis=0)
    width = tokens.shape[1]
    grad_b_ada = sums[:mod_size]
    grad_gain_one, grad_gain_two, grad_b_down = jnp.split(sums[mod_size : mod_size + 3 * width], 3)
    grad_b_up = sums[mod_size + 3 * width : -cond.shape[1]]
    return (
        output, grad_x, grad_cond, grad_w_ada, grad_b_ada, grad_gain_one, grad_w_qkv, grad_w_out, grad_gain_two,
        grad_w_up, grad_b_up, grad_w_down, grad_b_down,
    )


def solution(mesh):
    placed = (
        P(("dp", "tensor"), None), P("dp", None), P("dp", None), P(), P(), P(), P(None, None, "tensor"),
        P("tensor", None), P(), P(None, "tensor"), P("tensor"), P("tensor", None), P(), P(("dp", "tensor"), None),
    )
    return jax.shard_map(
        body,
        mesh=mesh,
        in_specs=placed,
        out_specs=(
            P(("dp", "tensor"), None), P(("dp", "tensor"), None), P("dp", None), P(), P(), P(),
            P(None, None, "tensor"), P("tensor", None), P(), P(None, "tensor"), P("tensor"), P("tensor", None), P(),
        ),
        check_vma=False,
    )
```

time: 1420 us -> 544 us (0.38)
  waiting for transfers between devices: 874 us -> 216 us
  local copies, waits for them, and re-layouts: 148 us -> 20.9 us
  matrix products: 180 us -> 78.4 us
  Pallas kernels: 0 us -> 87.1 us
  loops' own time: 55.6 us -> 0 us
  blocking collectives: 70.8 us -> 28.4 us
  starting transfers between devices: 1.75 us -> 29.1 us
    psum x1 -> x0, waiting for transfers between devices: 423 us -> none  [body(): lax.psum((grad_w_ada, grad_b_ada, grad_gain_one, grad_w_qkv, grad_w_out,...]
    reduce_scatter x6 -> x0, waiting for transfers between devices: 340 us -> none  [the longest x1 131 us: body(): lax.psum_scatter(jnp.einsum('tse,tde->sd', grad_qkv, w_qkv, preferred_ele...]
    ppermute x0 -> x40, waiting for transfers between devices: none -> 216 us  [the longest x8 108 us: other(): return lax.ppermute(values, 'tensor', [(0, 1), (1, 0)])]
    all_gather x5 -> x0, waiting for transfers between devices: 111 us -> none  [the longest x2 52.8 us: forward_pass(): rows_two = lax.all_gather(act_two, 'tensor', axis=0, tiled=True)]
    dot_general x38 -> x14, matrix products: 180 us -> 78.4 us  [the longest x1 14 us: body(): jnp.einsum('sd,fd->sf', full_branch, w_down, preferred_element_type=f32)]
    pallas_call x0 -> x3, Pallas kernels: none -> 87.1 us  [the longest x1 42.4 us: attend_backward(): pl.pallas_call(backward_kernel, grid_spec=pltpu.PrefetchScalarGridSpec(nu...]
    psum x2 -> x1, blocking collectives: 70.8 us -> 8.6 us  [body(): small = lax.psum(small, 'tensor')]
    another operation x15 -> x0, loops' own time: 55.6 us -> none  [the longest x4 18.4 us: one_block(): lax.fori_loop(low_block[block_index], high_block[block_index], out_step,...]
  transfers between devices with their start and end apart: 12 -> 40, of which waited for: 10 -> 22; matrix products, arithmetic and copies ran while one was open for 17% -> 26% of each run, Pallas kernels for 0% -> 8%
where the time goes in v1:
time: 544 us; the launch traced here: 535 us
  waiting for transfers between devices  216 us (40%)
  Pallas kernels  87.1 us (16%)
  matrix products  78.4 us (14%)
  other arithmetic  71.9 us (13%)
  starting transfers between devices  29.1 us (5%)
  blocking collectives  28.4 us (5%)
  local copies, waits for them, and re-layouts  20.9 us (4%)
    ppermute x8, waiting for transfers between devices, other(): return lax.ppermute(values, 'tensor', [(0, 1), (1, 0)])  108 us
    ppermute x32, waiting for transfers between devices, across(): return lax.ppermute(values, 'dp', [(d, d ^ 1 << b) for d in range(dp_size)])  108 us
    pallas_call x1, Pallas kernels, attend_backward(): pl.pallas_call(backward_kernel, grid_spec=pltpu.PrefetchScalarGridSpec(nu...  42.4 us
    pallas_call x1, Pallas kernels, attend_forward(): pl.pallas_call(forward_kernel, grid_spec=pltpu.PrefetchScalarGridSpec(num...  37.9 us
    all_gather x1, blocking collectives, body(): lax.all_gather(jnp.concatenate([small, grad_b_up, cond[0].astype(f32)])[N...  19.8 us
    add x12, other arithmetic, sum_over_dp(): part = jnp.where(first, low, high) + across(send, b).astype(f32)  18.9 us
    ppermute x32, starting transfers between devices, across(): return lax.ppermute(values, 'dp', [(d, d ^ 1 << b) for d in range(dp_size)])  17 us
    convert_element_type x4, other arithmetic, sum_over_dp(): return part.astype(f32)  14 us
  transfers between devices with their start and end apart: 40, of which 22 were waited for; matrix products, arithmetic and copies ran while one was open for 26% of the time, Pallas kernels for 8%

profile of v1, /device:TPU:0, one launch (start us, length us, event | category | flops | bytes accessed | tf_op | source)
XLA Modules:
  0.0 534.6 jit_solution(12700013223873321776)
XLA Ops:
  0.7 1.6 convert_reduce_fusion.1
  2.3 1.6 fusion.19
  4.9 3.0 collective-permute-start
  8.5 1.9 multiply_sine_fusion
  11.3 19.8 %collective-permute-done = bf16[512,1024]{1,0:T(8,128)(2,1)} collective-permute-done((bf16[512,1024]{1,0:T(8,128)(2,1)S(1)}, bf16[512,1024]{1,0:T(8,128)(2,1)}, u32[]{:S(2)}, u32[]{:S(2)}) %collective-permute-start) | collective-permute-done | bytes 1048608 | tf_op jit(solution)/shard_map/ppermute | solution.py:290
  32.6 6.9 %qkv.1.q_ref.k_ref.v_ref = bf16[3,1024,512]{2,1,0:T(8,128)(2,1)S(1)} custom-call(bf16[1024,1024]{1,0:T(8,128)(2,1)S(1)} %pad_maximum_fusion.1.x_ref, bf16[3,1024,512]{2,1,0:T(8,128)(2,1)S(1)} %copy-done.6, f32[1024,128]{1,0:T(8,128)S(1)} %get-tuple-element.86.cos_ref, f32[1024,128]{1,0:T(8,128)S(1)} %get-tuple-element.87.sin_ref), custom_call_target="tpu_custom_call" | custom-call | flops 3221225472 | bytes 4194304 | tf_op jit(solution)/shard_map/qkv/pallas_call | solution.py:85
  39.7 37.9 %attend.1 = (bf16[1024,512]{1,0:T(8,128)(2,1)S(1)}, f32[8,4,1,256]{3,2,1,0:T(1,128)S(1)}) custom-call(s32[16]{0:T(128)S(1)} %reshape.164.flag_ref, bf16[3,1024,512]{2,1,0:T(8,128)(2,1)S(1)} %qkv.1.q_ref.k_ref.v_ref, bf16[3,1024,512]{2,1,0:T(8,128)(2,1)S(1)} %qkv.1.q_ref.k_ref.v_ref, bf16[3,1024,512]{2,1,0:T(8,128)(2,1)S(1)} %qkv.1.q_ref.k_ref.v_ref, ...), custom_call_target="tpu_custom_call" | custom-call | flops 2147483648 | bytes 4194304 | tf_op jit(solution)/shard_map/attend/pallas_call | solution.py:209
  79.1 1.8 collective-permute-start.1
  81.0 22.6 %collective-permute-done.1 = bf16[512,1024]{1,0:T(8,128)(2,1)S(1)} collective-permute-done((bf16[512,1024]{1,0:T(8,128)(2,1)S(1)}, bf16[512,1024]{1,0:T(8,128)(2,1)S(1)}, u32[]{:S(2)}, u32[]{:S(2)}) %collective-permute-start.1) | collective-permute-done | bytes 1048608 | tf_op jit(solution)/shard_map/ppermute | solution.py:290
  110.0 23.1 %collective-permute-done.2 = bf16[512,1024]{1,0:T(8,128)(2,1)} collective-permute-done((bf16[512,1024]{1,0:T(8,128)(2,1)}, bf16[512,1024]{1,0:T(8,128)(2,1)}, u32[]{:S(2)}, u32[]{:S(2)}) %collective-permute-start.2) | collective-permute-done | bytes 1048608 | tf_op jit(solution)/shard_map/ppermute | solution.py:290
  133.1 7.1 %fusion.29 = f32[1024,2048]{1,0:T(8,128)S(1)} fusion(bf16[1024,2048]{1,0:T(8,128)(2,1)} %param.23, bf16[512,1024]{1,0:T(8,128)(2,1)} %collective-permute-done.2, bf16[512,1024]{1,0:T(8,128)(2,1)} %add_convert_fusion.2), kind=kOutput, calls=%fused_computation.90 | convolution fusion | flops 4299161600 | bytes 14680064 | tf_op jit(solution)/shard_map/dot_general | solution.py:352
  140.2 12.7 %collective-permute-done.4 = bf16[512,1024]{1,0:T(8,128)(2,1)} collective-permute-done((bf16[512,1024]{1,0:T(8,128)(2,1)}, bf16[512,1024]{1,0:T(8,128)(2,1)}, u32[]{:S(2)}, u32[]{:S(2)}) %collective-permute-start.4) | collective-permute-done | bytes 1048608 | tf_op jit(solution)/shard_map/ppermute | solution.py:290
  152.9 8.1 %fusion.26 = f32[2048,1024]{1,0:T(8,128)S(1)} fusion(bf16[512,1024]{1,0:T(8,128)(2,1)} %collective-permute-done.4, bf16[512,1024]{1,0:T(8,128)(2,1)} %get-tuple-element.32, f32[1024,2048]{1,0:T(8,128)S(1)} %fusion.29, f32[2048]{0:T(1024)S(1)} %copy-done.50), kind=kOutput, calls=%fused_computation.87 | convolution fusion | flops 4320133120 | bytes 18882560 | tf_op jit(solution)/shard_map/sf,sd->fd/dot_general | solution.py:359
  161.0 1.7 select_convert_fusion
  163.9 14.0 %convert_reduce_fusion = (f32[2048]{0:T(1024)S(1)}, bf16[1024,2048]{1,0:T(8,128)(2,1)}) fusion(f32[1024,2048]{1,0:T(8,128)} %copy-done.53, f32[2048]{0:T(1024)S(1)} %copy-done.50, bf16[2048,1024]{1,0:T(8,128)(2,1)S(1)} %copy-done.46, bf16[512,1024]{1,0:T(8,128)(2,1)} %collective-permute-done.4, bf16[512,1024]{1,0:T(8,128)(2,1)} %get-tuple-element.32), kind=kOutput, calls=%fused_computation.9 | convolution fusion | flops 4347394048 | bytes 18890752 | tf_op jit(solution)/shard_map/sd,fd->sf/dot_general | solution.py:355
  177.9 6.8 %fusion.58 = f32[1024,1024]{1,0:T(8,128)S(1)} fusion(bf16[1024,2048]{1,0:T(8,128)(2,1)} %get-tuple-element.85, bf16[1024,2048]{1,0:T(8,128)(2,1)S(1)} %copy-done.45), kind=kOutput, calls=%fused_computation.212 | convolution fusion | flops 4294967296 | bytes 12582912 | tf_op jit(solution)/shard_map/sf,df->sd/dot_general | solution.py:358
  186.1 7.0 %fusion.28 = f32[1024,2048]{1,0:T(8,128)S(1)} fusion(bf16[1024,2048]{1,0:T(8,128)(2,1)} %get-tuple-element.85, bf16[512,1024]{1,0:T(8,128)(2,1)} %collective-permute-done.2, bf16[512,1024]{1,0:T(8,128)(2,1)} %add_convert_fusion.2), kind=kOutput, calls=%fused_computation.89 | convolution fusion | flops 4299161600 | bytes 14680064 | tf_op jit(solution)/shard_map/sd,sf->df/dot_general | solution.py:360
  193.1 1.7 select_convert_fusion.1
  194.8 14.3 %collective-permute-done.5 = bf16[512,1024]{1,0:T(8,128)(2,1)S(1)} collective-permute-done((bf16[512,1024]{1,0:T(8,128)(2,1)S(1)}, bf16[512,1024]{1,0:T(8,128)(2,1)S(1)}, u32[]{:S(2)}, u32[]{:S(2)}) %collective-permute-start.5) | collective-permute-done | bytes 1048608 | tf_op jit(solution)/shard_map/ppermute | solution.py:290
  214.5 8.2 %fusion.50 = f32[1024,1024]{1,0:T(8,128)S(1)} fusion(bf16[2048,1024]{1,0:T(8,128)(2,1)S(1)} %copy-done.47, f32[1024,2048]{1,0:T(8,128)} %copy-done.53, f32[2048]{0:T(1024)S(1)} %copy-done.50), kind=kOutput, calls=%fused_computation.205 | convolution fusion | flops 4315938816 | bytes 16785408 | tf_op jit(solution)/shard_map/dot_general | solution.py:362
  225.1 3.2 convert_add_fusion
  229.5 9.3 %collective-permute-done.6 = bf16[512,1024]{1,0:T(8,128)(2,1)} collective-permute-done((bf16[512,1024]{1,0:T(8,128)(2,1)S(1)}, bf16[512,1024]{1,0:T(8,128)(2,1)}, u32[]{:S(2)}, u32[]{:S(2)}) %collective-permute-start.6) | collective-permute-done | bytes 1048608 | tf_op jit(solution)/shard_map/ppermute | solution.py:290
  238.7 2.5 fusion.25
  241.4 3.1 convert_add_fusion.1
  244.9 1.7 copy-done.49
  246.6 3.5 convolution_convert_fusion.g_ref
  250.1 42.4 %attend_back.1 = bf16[3,1024,512]{2,1,0:T(8,128)(2,1)} custom-call(s32[16]{0:T(128)} %copy-done.5, bf16[3,1024,512]{2,1,0:T(8,128)(2,1)} %copy-done.9, bf16[3,1024,512]{2,1,0:T(8,128)(2,1)} %copy-done.9, bf16[3,1024,512]{2,1,0:T(8,128)(2,1)} %copy-done.9, bf16[1024,512]{1,0:T(8,128)(2,1)} %convolution_convert_fusion.g_ref, bf16[1024,512]{1,0:T(8,128)(2,1)} %copy-done.8, ...), custom_call_target="tpu_custom_call" | custom-call | flops 5368709120 | bytes 8388608 | tf_op jit(solution)/shard_map/attend_back/pallas_call | solution.py:247
  294.3 7.1 %convolution_bitcast_fusion.1 = f32[1024,1024]{1,0:T(8,128)} fusion(bf16[3,1024,512]{2,1,0:T(8,128)(2,1)} %attend_back.1, bf16[3,1024,512]{2,1,0:T(8,128)(2,1)S(1)} %copy-done.7), kind=kOutput, calls=%fused_computation.37 | convolution fusion | flops 3221225472 | bytes 10485760 | tf_op jit(solution)/shard_map/tse,tde->sd/dot_general | solution.py:376
  303.0 6.6 %convolution_bitcast_fusion = f32[3,1024,512]{1,2,0:T(8,128)} fusion(bf16[3,1024,512]{2,1,0:T(8,128)(2,1)S(1)} %copy-done.52, bf16[512,1024]{1,0:T(8,128)(2,1)} %collective-permute-done, bf16[512,1024]{1,0:T(8,128)(2,1)S(1)} %copy-done.34), kind=kOutput, calls=%fused_computation.32 | convolution fusion | flops 3225419776 | bytes 11534336 | tf_op jit(solution)/shard_map/sd,tse->tde/dot_general | solution.py:377
  309.6 6.6 %copy.33 = f32[3,1024,512]{2,1,0:T(8,128)} copy(f32[3,1024,512]{1,2,0:T(8,128)} %convolution_bitcast_fusion) | data formatting | bytes 12582912 | tf_op jit(solution)/shard_map/sd,tse->tde/transpose | solution.py:377
  316.2 1.7 slice.329
  317.9 1.7 collective-permute-start.7
  319.8 4.4 select_convert_fusion.2
  324.2 1.6 collective-permute-done.19
  327.2 2.1 convert_add_fusion.5
  330.3 1.9 collective-permute-done.20
  332.2 2.1 collective-permute-start.21
  334.3 2.0 convert_add_fusion.6
  336.4 6.7 %collective-permute-done.7 = bf16[512,1024]{1,0:T(8,128)(2,1)S(1)} collective-permute-done((bf16[512,1024]{1,0:T(8,128)(2,1)S(1)}, bf16[512,1024]{1,0:T(8,128)(2,1)S(1)}, u32[]{:S(2)}, u32[]{:S(2)}) %collective-permute-start.7) | collective-permute-done | bytes 1048608 | tf_op jit(solution)/shard_map/ppermute | solution.py:290
  348.2 4.1 fusion.22
  352.4 8.6 %psum.7 = f32[9216]{0:T(1024)S(1)} all-reduce(f32[9216]{0:T(1024)S(1)} %constant_dynamic-update-slice_fusion), channel_id=1, replica_groups=mesh['dp'=16,'tensor'=2] {'tensor'}, use_global_device_ids=true, to_apply=%region_22.23 | all-reduce | flops 9216 | bytes 73728 | tf_op jit(solution)/shard_map/psum | solution.py:390
  361.1 19.8 %all-gather.1 = f32[16,1,11392]{2,1,0:T(1,128)S(1)} all-gather(f32[1,1,11392]{2,1,0:T(1,128)S(1)} %reshape.167), channel_id=2, replica_groups=mesh['dp'=16,'tensor'=2] {'dp'}, dimensions={0}, use_global_device_ids=true | all-gather | bytes 774656 | tf_op jit(solution)/shard_map/all_gather | solution.py:394
  380.9 1.8 fusion.59
  383.3 1.7 collective-permute-start.22
  385.0 1.9 convert_add_fusion.8
  388.4 3.0 collective-permute-start.27
  391.4 4.2 convert_add_fusion.2
  396.3 9.3 %collective-permute-done.35 = bf16[128,1024]{1,0:T(8,128)(2,1)S(1)} collective-permute-done((bf16[128,1024]{1,0:T(8,128)(2,1)S(1)}, bf16[128,1024]{1,0:T(8,128)(2,1)S(1)}, u32[]{:S(2)}, u32[]{:S(2)}) %collective-permute-start.35) | collective-permute-done | bytes 262176 | tf_op jit(solution)/shard_map/ppermute | solution.py:306
  405.8 11.1 %collective-permute-done.27 = bf16[64,2048]{1,0:T(8,128)(2,1)S(1)} collective-permute-done((bf16[64,2048]{1,0:T(8,128)(2,1)S(1)}, bf16[64,2048]{1,0:T(8,128)(2,1)S(1)}, u32[]{:S(2)}, u32[]{:S(2)}) %collective-permute-start.27) | collective-permute-done | bytes 262176 | tf_op jit(solution)/shard_map/ppermute | solution.py:306
  417.1 11.1 %collective-permute-done.36 = bf16[128,1024]{1,0:T(8,128)(2,1)S(1)} collective-permute-done((bf16[128,1024]{1,0:T(8,128)(2,1)S(1)}, bf16[128,1024]{1,0:T(8,128)(2,1)S(1)}, u32[]{:S(2)}, u32[]{:S(2)}) %collective-permute-start.36) | collective-permute-done | bytes 262176 | tf_op jit(solution)/shard_map/ppermute | solution.py:306
  428.6 5.2 collective-permute-done.28
  434.5 2.1 collective-permute-start.10
  436.6 8.4 %collective-permute-done.37 = bf16[256,1024]{1,0:T(8,128)(2,1)S(1)} collective-permute-done((bf16[256,1024]{1,0:T(8,128)(2,1)S(1)}, bf16[256,1024]{1,0:T(8,128)(2,1)S(1)}, u32[]{:S(2)}, u32[]{:S(2)}) %collective-permute-start.37) | collective-permute-done | bytes 524320 | tf_op jit(solution)/shard_map/ppermute | solution.py:306
  446.1 10.2 %collective-permute-done.29 = bf16[128,2048]{1,0:T(8,128)(2,1)S(1)} collective-permute-done((bf16[128,2048]{1,0:T(8,128)(2,1)S(1)}, bf16[128,2048]{1,0:T(8,128)(2,1)S(1)}, u32[]{:S(2)}, u32[]{:S(2)}) %collective-permute-start.29) | collective-permute-done | bytes 524320 | tf_op jit(solution)/shard_map/ppermute | solution.py:306
  456.5 8.1 %collective-permute-done.10 = bf16[384,512]{1,0:T(8,128)(2,1)S(1)} collective-permute-done((bf16[384,512]{1,0:T(8,128)(2,1)S(1)}, bf16[384,512]{1,0:T(8,128)(2,1)S(1)}, u32[]{:S(2)}, u32[]{:S(2)}) %collective-permute-start.10) | collective-permute-done | bytes 393248 | tf_op jit(solution)/shard_map/ppermute | solution.py:306
  466.1 10.6 %collective-permute-done.11 = bf16[192,512]{1,0:T(8,128)(2,1)S(1)} collective-permute-done((bf16[192,512]{1,0:T(8,128)(2,1)S(1)}, bf16[192,512]{1,0:T(8,128)(2,1)S(1)}, u32[]{:S(2)}, u32[]{:S(2)}) %collective-permute-start.11) | collective-permute-done | bytes 196640 | tf_op jit(solution)/shard_map/ppermute | solution.py:306
  477.1 10.6 %collective-permute-done.12 = bf16[192,512]{1,0:T(8,128)(2,1)S(1)} collective-permute-done((bf16[192,512]{1,0:T(8,128)(2,1)S(1)}, bf16[192,512]{1,0:T(8,128)(2,1)S(1)}, u32[]{:S(2)}, u32[]{:S(2)}) %collective-permute-start.12) | collective-permute-done | bytes 196640 | tf_op jit(solution)/shard_map/ppermute | solution.py:306
  488.8 4.1 collective-permute-done.30
  493.7 5.2 collective-permute-done.13
  501.5 4.3 fusion.30
  507.7 10.2 %collective-permute-done.14 = bf16[768,512]{1,0:T(8,128)(2,1)S(1)} collective-permute-done((bf16[768,512]{1,0:T(8,128)(2,1)S(1)}, bf16[768,512]{1,0:T(8,128)(2,1)S(1)}, u32[]{:S(2)}, u32[]{:S(2)}) %collective-permute-start.14) | collective-permute-done | bytes 786464 | tf_op jit(solution)/shard_map/ppermute | solution.py:306
  521.0 4.3 maximum_convert_fusion
  525.3 4.5 maximum_convert_fusion.1
  530.5 3.6 convert.18
  (268 shorter events, 52.3 us)
Async XLA Ops:
  4.9 27.7 %copy-start.33 = (bf16[512,1024]{1,0:T(8,128)(2,1)}, bf16[512,1024]{1,0:T(8,128)(2,1)S(1)}, u32[]{:S(2)}) copy-start(bf16[512,1024]{1,0:T(8,128)(2,1)S(1)} %fusion.16) | copy-start | bytes 3145732
  4.9 26.3 %collective-permute-start = (bf16[512,1024]{1,0:T(8,128)(2,1)S(1)}, bf16[512,1024]{1,0:T(8,128)(2,1)}, u32[]{:S(2)}, u32[]{:S(2)}) collective-permute-start(bf16[512,1024]{1,0:T(8,128)(2,1)S(1)} %fusion.16), channel_id=1, source_target_pairs={{0,1},{1,0},{2,3},{3,2},{4,5},{5,4},{6,7},{7,6},{8,9},{9,8},{10,11... | collective-permute-start | bytes 3145736 | tf_op jit(solution)/shard_map/ppermute | solution.py:290
  8.1 31.6 %copy-start.4 = (s32[1024]{0:T(1024)}, s32[1024]{0:T(1024)S(1)}, u32[]{:S(2)}) copy-start(s32[1024]{0:T(1024)S(1)} %get-tuple-element.28) | copy-start | bytes 12292
  8.5 31.2 %copy-start.5 = (s32[16]{0:T(128)}, s32[16]{0:T(128)S(1)}, u32[]{:S(2)}) copy-start(s32[16]{0:T(128)S(1)} %reshape.164.flag_ref) | copy-start | bytes 196
  11.3 21.3 %copy-start.2 = (f32[1024,128]{1,0:T(8,128)}, f32[1024,128]{1,0:T(8,128)S(1)}, u32[]{:S(2)}) copy-start(f32[1024,128]{1,0:T(8,128)S(1)} %get-tuple-element.86.cos_ref) | copy-start | bytes 1572868
  11.3 21.3 %copy-start.3 = (f32[1024,128]{1,0:T(8,128)}, f32[1024,128]{1,0:T(8,128)S(1)}, u32[]{:S(2)}) copy-start(f32[1024,128]{1,0:T(8,128)S(1)} %get-tuple-element.87.sin_ref) | copy-start | bytes 1572868
  11.3 21.3 %copy-start.6 = (bf16[3,1024,512]{2,1,0:T(8,128)(2,1)S(1)}, bf16[3,1024,512]{2,1,0:T(8,128)(2,1)}, u32[]{:S(2)}) copy-start(bf16[3,1024,512]{2,1,0:T(8,128)(2,1)} %w_ref.1) | copy-start | bytes 9437188
  39.5 38.2 %copy-start.9 = (bf16[3,1024,512]{2,1,0:T(8,128)(2,1)}, bf16[3,1024,512]{2,1,0:T(8,128)(2,1)S(1)}, u32[]{:S(2)}) copy-start(bf16[3,1024,512]{2,1,0:T(8,128)(2,1)S(1)} %qkv.1.q_ref.k_ref.v_ref) | copy-start | bytes 9437188
  39.7 37.9 %copy-start.1 = (s32[1024,128]{1,0:T(8,128)}, s32[1024,128]{1,0:T(8,128)S(1)}, u32[]{:S(2)}) copy-start(s32[1024,128]{1,0:T(8,128)S(1)} %broadcast_in_dim.14.segc_ref) | copy-start | bytes 1572868
  39.7 38.0 %copy-start.48 = (bf16[512,1024]{1,0:T(8,128)(2,1)S(1)}, bf16[512,1024]{1,0:T(8,128)(2,1)}, u32[]{:S(2)}) copy-start(bf16[512,1024]{1,0:T(8,128)(2,1)} %param.21) | copy-start | bytes 3145732
  77.7 161.1 %copy-start.8 = (bf16[1024,512]{1,0:T(8,128)(2,1)}, bf16[1024,512]{1,0:T(8,128)(2,1)S(1)}, u32[]{:S(2)}) copy-start(bf16[1024,512]{1,0:T(8,128)(2,1)S(1)} %get-tuple-element.15.o_ref) | copy-start | bytes 3145732
  79.0 25.1 %copy-start.29 = (f32[1024,1024]{1,0:T(8,128)}, f32[1024,1024]{1,0:T(8,128)S(1)}, u32[]{:S(2)}) copy-start(f32[1024,1024]{1,0:T(8,128)S(1)} %fusion.57) | copy-start | bytes 12582916
  79.0 24.6 %copy-start.15 = (bf16[512,1024]{1,0:T(8,128)(2,1)S(1)}, bf16[512,1024]{1,0:T(8,128)(2,1)}, u32[]{:S(2)}) copy-start(bf16[512,1024]{1,0:T(8,128)(2,1)} %param.14) | copy-start | bytes 3145732
  79.1 24.4 %collective-permute-start.1 = (bf16[512,1024]{1,0:T(8,128)(2,1)S(1)}, bf16[512,1024]{1,0:T(8,128)(2,1)S(1)}, u32[]{:S(2)}, u32[]{:S(2)}) collective-permute-start(bf16[512,1024]{1,0:T(8,128)(2,1)S(1)} %slice.332), channel_id=1, source_target_pairs={{0,1},{1,0},{2,3},{3,2},{4,5},{5,4},{6,7},{7,6},{8,9},{9,8},{10,11... | collective-permute-start | bytes 3145736 | tf_op jit(solution)/shard_map/ppermute | solution.py:290
  106.7 26.4 %collective-permute-start.2 = (bf16[512,1024]{1,0:T(8,128)(2,1)}, bf16[512,1024]{1,0:T(8,128)(2,1)}, u32[]{:S(2)}, u32[]{:S(2)}) collective-permute-start(bf16[512,1024]{1,0:T(8,128)(2,1)} %add_convert_fusion.2), channel_id=1, source_target_pairs={{0,1},{1,0},{2,3},{3,2},{4,5},{5,4},{6,7},{7,6},{8,9},{9,8},{10,11... | collective-permute-start | bytes 3145736 | tf_op jit(solution)/shard_map/ppermute | solution.py:290
  109.4 43.5 %collective-permute-start.4 = (bf16[512,1024]{1,0:T(8,128)(2,1)}, bf16[512,1024]{1,0:T(8,128)(2,1)}, u32[]{:S(2)}, u32[]{:S(2)}) collective-permute-start(bf16[512,1024]{1,0:T(8,128)(2,1)} %get-tuple-element.32), channel_id=1, source_target_pairs={{0,1},{1,0},{2,3},{3,2},{4,5},{5,4},{6,7},{7,6},{8,9},{9,8},{10,11... | collective-permute-start | bytes 3145736 | tf_op jit(solution)/shard_map/ppermute | solution.py:290
  110.0 42.9 %copy-start.50 = (f32[2048]{0:T(1024)S(1)}, f32[2048]{0:T(1024)}, u32[]{:S(2)}) copy-start(f32[2048]{0:T(1024)} %param.24) | copy-start | bytes 24580
  140.2 20.8 %copy-start.53 = (f32[1024,2048]{1,0:T(8,128)}, f32[1024,2048]{1,0:T(8,128)S(1)}, u32[]{:S(2)}) copy-start(f32[1024,2048]{1,0:T(8,128)S(1)} %fusion.29) | copy-start | bytes 25165828
  162.7 15.2 %copy-start.45 = (bf16[1024,2048]{1,0:T(8,128)(2,1)S(1)}, bf16[1024,2048]{1,0:T(8,128)(2,1)}, u32[]{:S(2)}) copy-start(bf16[1024,2048]{1,0:T(8,128)(2,1)} %param.23) | copy-start | bytes 12582916
  162.7 62.4 %collective-permute-start.32 = (bf16[1024,1024]{1,0:T(8,128)(2,1)}, bf16[1024,1024]{1,0:T(8,128)(2,1)}, u32[]{:S(2)}, u32[]{:S(2)}) collective-permute-start(bf16[1024,1024]{1,0:T(8,128)(2,1)} %select_convert_fusion), channel_id=1, source_target_pairs={{0,2},{2,0},{4,6},{6,4},{8,10},{10,8},{12,14},{14,12},{16,18},{18,... | collective-permute-start | bytes 6291464 | tf_op jit(solution)/shard_map/ppermute | solution.py:306
  184.8 24.2 %collective-permute-start.5 = (bf16[512,1024]{1,0:T(8,128)(2,1)S(1)}, bf16[512,1024]{1,0:T(8,128)(2,1)S(1)}, u32[]{:S(2)}, u32[]{:S(2)}) collective-permute-start(bf16[512,1024]{1,0:T(8,128)(2,1)S(1)} %slice.330), channel_id=1, source_target_pairs={{0,1},{1,0},{2,3},{3,2},{4,5},{5,4},{6,7},{7,6},{8,9},{9,8},{10,11... | collective-permute-start | bytes 3145736 | tf_op jit(solution)/shard_map/ppermute | solution.py:290
  193.1 16.0 %copy-start.12 = (f32[512,1024]{1,0:T(8,128)S(1)}, f32[512,1024]{1,0:T(8,128)}, u32[]{:S(2)}) copy-start(f32[512,1024]{1,0:T(8,128)} %copy-done.11) | copy-start | bytes 6291460
  194.8 46.7 %collective-permute-start.24 = (bf16[512,2048]{1,0:T(8,128)(2,1)}, bf16[512,2048]{1,0:T(8,128)(2,1)}, u32[]{:S(2)}, u32[]{:S(2)}) collective-permute-start(bf16[512,2048]{1,0:T(8,128)(2,1)} %select_convert_fusion.1), channel_id=1, source_target_pairs={{0,2},{2,0},{4,6},{6,4},{8,10},{10,8},{12,14},{14,12},{16,18},{18,... | collective-permute-start | bytes 6291464 | tf_op jit(solution)/shard_map/ppermute | solution.py:306
  212.5 10.1 %copy-start.38 = (bf16[512,1024]{1,0:T(8,128)(2,1)}, bf16[512,1024]{1,0:T(8,128)(2,1)S(1)}, u32[]{:S(2)}) copy-start(bf16[512,1024]{1,0:T(8,128)(2,1)S(1)} %multiply_convert_fusion.1) | copy-start | bytes 3145732
  212.5 26.2 %collective-permute-start.6 = (bf16[512,1024]{1,0:T(8,128)(2,1)S(1)}, bf16[512,1024]{1,0:T(8,128)(2,1)}, u32[]{:S(2)}, u32[]{:S(2)}) collective-permute-start(bf16[512,1024]{1,0:T(8,128)(2,1)S(1)} %multiply_convert_fusion.1), channel_id=1, source_target_pairs={{0,1},{1,0},{2,3},{3,2},{4,5},{5,4},{6,7},{7,6},{8,9},{9,8},{10,11... | collective-permute-start | bytes 3145736 | tf_op jit(solution)/shard_map/ppermute | solution.py:290
  223.9 122.6 %collective-permute-start.3 = (bf16[512,1024]{1,0:T(8,128)(2,1)}, bf16[512,1024]{1,0:T(8,128)(2,1)}, u32[]{:S(2)}, u32[]{:S(2)}) collective-permute-start(bf16[512,1024]{1,0:T(8,128)(2,1)} %slice.331), channel_id=1, source_target_pairs={{0,1},{1,0},{2,3},{3,2},{4,5},{5,4},{6,7},{7,6},{8,9},{9,8},{10,11... | collective-permute-start | bytes 3145736 | tf_op jit(solution)/shard_map/ppermute | solution.py:290
  228.3 12.9 %copy-start.19 = (f32[1024,1024]{1,0:T(8,128)}, f32[1024,1024]{1,0:T(8,128)S(1)}, u32[]{:S(2)}) copy-start(f32[1024,1024]{1,0:T(8,128)S(1)} %convert_add_fusion) | copy-start | bytes 12582916
  228.3 10.4 %copy-start.39 = (bf16[512,1024]{1,0:T(8,128)(2,1)S(1)}, bf16[512,1024]{1,0:T(8,128)(2,1)}, u32[]{:S(2)}) copy-start(bf16[512,1024]{1,0:T(8,128)(2,1)} %copy-done.38) | copy-start | bytes 3145732
  229.5 96.4 %collective-permute-start.33 = (bf16[512,1024]{1,0:T(8,128)(2,1)}, bf16[512,1024]{1,0:T(8,128)(2,1)}, u32[]{:S(2)}, u32[]{:S(2)}) collective-permute-start(bf16[512,1024]{1,0:T(8,128)(2,1)} %select_convert_fusion.3), channel_id=1, source_target_pairs={{0,4},{2,6},{4,0},{6,2},{8,12},{10,14},{12,8},{14,10},{16,20},{18,... | collective-permute-start | bytes 3145736 | tf_op jit(solution)/shard_map/ppermute | solution.py:306
  241.3 51.1 %collective-permute-start.16 = (bf16[256,1024]{1,0:T(8,128)(2,1)S(1)}, bf16[256,1024]{1,0:T(8,128)(2,1)S(1)}, u32[]{:S(2)}, u32[]{:S(2)}) collective-permute-start(bf16[256,1024]{1,0:T(8,128)(2,1)S(1)} %select_convert_fusion.8), channel_id=1, source_target_pairs={{0,2},{2,0},{4,6},{6,4},{8,10},{10,8},{12,14},{14,12},{16,18},{18,... | collective-permute-start | bytes 1572872 | tf_op jit(solution)/shard_map/ppermute | solution.py:306
  244.8 87.4 %collective-permute-start.25 = (bf16[256,2048]{1,0:T(8,128)(2,1)S(1)}, bf16[256,2048]{1,0:T(8,128)(2,1)}, u32[]{:S(2)}, u32[]{:S(2)}) collective-permute-start(bf16[256,2048]{1,0:T(8,128)(2,1)S(1)} %select_convert_fusion.4), channel_id=1, source_target_pairs={{0,4},{2,6},{4,0},{6,2},{8,12},{10,14},{12,8},{14,10},{16,20},{18,... | collective-permute-start | bytes 3145736 | tf_op jit(solution)/shard_map/ppermute | solution.py:306
  292.8 8.8 %collective-permute-start.17 = (bf16[128,1024]{1,0:T(8,128)(2,1)S(1)}, bf16[128,1024]{1,0:T(8,128)(2,1)S(1)}, u32[]{:S(2)}, u32[]{:S(2)}) collective-permute-start(bf16[128,1024]{1,0:T(8,128)(2,1)S(1)} %select_convert_fusion.12), channel_id=1, source_target_pairs={{0,4},{2,6},{4,0},{6,2},{8,12},{10,14},{12,8},{14,10},{16,20},{18,... | collective-permute-start | bytes 786440 | tf_op jit(solution)/shard_map/ppermute | solution.py:306
  294.3 8.7 %copy-start.52 = (bf16[3,1024,512]{2,1,0:T(8,128)(2,1)S(1)}, bf16[3,1024,512]{2,1,0:T(8,128)(2,1)}, u32[]{:S(2)}) copy-start(bf16[3,1024,512]{2,1,0:T(8,128)(2,1)} %attend_back.1) | copy-start | bytes 9437188
  301.7 17.9 %collective-permute-start.18 = (bf16[64,1024]{1,0:T(8,128)(2,1)S(1)}, bf16[64,1024]{1,0:T(8,128)(2,1)S(1)}, u32[]{:S(2)}, u32[]{:S(2)}) collective-permute-start(bf16[64,1024]{1,0:T(8,128)(2,1)S(1)} %select_convert_fusion.14), channel_id=1, source_target_pairs={{0,8},{2,10},{4,12},{6,14},{8,0},{10,2},{12,4},{14,6},{16,24},{18,... | collective-permute-start | bytes 393224 | tf_op jit(solution)/shard_map/ppermute | solution.py:306
  317.9 25.2 %collective-permute-start.7 = (bf16[512,1024]{1,0:T(8,128)(2,1)S(1)}, bf16[512,1024]{1,0:T(8,128)(2,1)S(1)}, u32[]{:S(2)}, u32[]{:S(2)}) collective-permute-start(bf16[512,1024]{1,0:T(8,128)(2,1)S(1)} %slice.329), channel_id=1, source_target_pairs={{0,1},{1,0},{2,3},{3,2},{4,5},{5,4},{6,7},{7,6},{8,9},{9,8},{10,11... | collective-permute-start | bytes 3145736 | tf_op jit(solution)/shard_map/ppermute | solution.py:290
  319.7 6.2 %collective-permute-start.19 = (bf16[32,1024]{1,0:T(8,128)(2,1)S(1)}, bf16[32,1024]{1,0:T(8,128)(2,1)S(1)}, u32[]{:S(2)}, u32[]{:S(2)}) collective-permute-start(bf16[32,1024]{1,0:T(8,128)(2,1)S(1)} %select_convert_fusion.15), channel_id=1, source_target_pairs={{0,16},{2,18},{4,20},{6,22},{8,24},{10,26},{12,28},{14,30},{16,0},... | collective-permute-start | bytes 196616 | tf_op jit(solution)/shard_map/ppermute | solution.py:306
  325.9 65.5 %collective-permute-start.8 = (bf16[1536,512]{1,0:T(8,128)(2,1)}, bf16[1536,512]{1,0:T(8,128)(2,1)}, u32[]{:S(2)}, u32[]{:S(2)}) collective-permute-start(bf16[1536,512]{1,0:T(8,128)(2,1)} %select_convert_fusion.2), channel_id=1, source_target_pairs={{0,2},{2,0},{4,6},{6,4},{8,10},{10,8},{12,14},{14,12},{16,18},{18,... | collective-permute-start | bytes 4718600 | tf_op jit(solution)/shard_map/ppermute | solution.py:306
  325.9 6.3 %collective-permute-start.20 = (bf16[32,1024]{1,0:T(8,128)(2,1)S(1)}, bf16[32,1024]{1,0:T(8,128)(2,1)S(1)}, u32[]{:S(2)}, u32[]{:S(2)}) collective-permute-start(bf16[32,1024]{1,0:T(8,128)(2,1)S(1)} %add_convert_fusion.6), channel_id=1, source_target_pairs={{0,16},{2,18},{4,20},{6,22},{8,24},{10,26},{12,28},{14,30},{16,0},... | collective-permute-start | bytes 196616 | tf_op jit(solution)/shard_map/ppermute | solution.py:306
  329.4 15.0 %copy-start.37 = (f32[1024,1024]{1,0:T(8,128)S(1)}, f32[1024,1024]{1,0:T(8,128)}, u32[]{:S(2)}) copy-start(f32[1024,1024]{1,0:T(8,128)} %convolution_bitcast_fusion.1) | copy-start | bytes 12582916
  332.2 52.8 %collective-permute-start.34 = (bf16[256,1024]{1,0:T(8,128)(2,1)}, bf16[256,1024]{1,0:T(8,128)(2,1)}, u32[]{:S(2)}, u32[]{:S(2)}) collective-permute-start(bf16[256,1024]{1,0:T(8,128)(2,1)} %select_convert_fusion.6), channel_id=1, source_target_pairs={{0,8},{2,10},{4,12},{6,14},{8,0},{10,2},{12,4},{14,6},{16,24},{18,... | collective-permute-start | bytes 1572872 | tf_op jit(solution)/shard_map/ppermute | solution.py:306
  332.2 51.0 %collective-permute-start.21 = (bf16[64,1024]{1,0:T(8,128)(2,1)S(1)}, bf16[64,1024]{1,0:T(8,128)(2,1)S(1)}, u32[]{:S(2)}, u32[]{:S(2)}) collective-permute-start(bf16[64,1024]{1,0:T(8,128)(2,1)S(1)} %pad_maximum_fusion.26), channel_id=1, source_target_pairs={{0,8},{2,10},{4,12},{6,14},{8,0},{10,2},{12,4},{14,6},{16,24},{18,... | collective-permute-start | bytes 393224 | tf_op jit(solution)/shard_map/ppermute | solution.py:306
  334.3 12.2 %copy-start.32 = (bf16[512,1024]{1,0:T(8,128)(2,1)S(1)}, bf16[512,1024]{1,0:T(8,128)(2,1)}, u32[]{:S(2)}) copy-start(bf16[512,1024]{1,0:T(8,128)(2,1)} %copy-done.31) | copy-start | bytes 3145732
  334.3 12.2 %copy-start.36 = (f32[1024,1024]{1,0:T(8,128)S(1)}, f32[1024,1024]{1,0:T(8,128)}, u32[]{:S(2)}) copy-start(f32[1024,1024]{1,0:T(8,128)} %copy-done.35) | copy-start | bytes 12582916
  336.3 8.1 %copy-start.16 = (bf16[512,1024]{1,0:T(8,128)(2,1)S(1)}, bf16[512,1024]{1,0:T(8,128)(2,1)}, u32[]{:S(2)}) copy-start(bf16[512,1024]{1,0:T(8,128)(2,1)} %param.14) | copy-start | bytes 3145732
  343.2 43.9 %collective-permute-start.26 = (bf16[128,2048]{1,0:T(8,128)(2,1)S(1)}, bf16[128,2048]{1,0:T(8,128)(2,1)}, u32[]{:S(2)}, u32[]{:S(2)}) collective-permute-start(bf16[128,2048]{1,0:T(8,128)(2,1)S(1)} %select_convert_fusion.7), channel_id=1, source_target_pairs={{0,8},{2,10},{4,12},{6,14},{8,0},{10,2},{12,4},{14,6},{16,24},{18,... | collective-permute-start | bytes 1572872 | tf_op jit(solution)/shard_map/ppermute | solution.py:306
  383.3 93.5 %collective-permute-start.22 = (bf16[128,1024]{1,0:T(8,128)(2,1)S(1)}, bf16[128,1024]{1,0:T(8,128)(2,1)S(1)}, u32[]{:S(2)}, u32[]{:S(2)}) collective-permute-start(bf16[128,1024]{1,0:T(8,128)(2,1)S(1)} %pad_maximum_fusion.25), channel_id=1, source_target_pairs={{0,4},{2,6},{4,0},{6,2},{8,12},{10,14},{12,8},{14,10},{16,20},{18,... | collective-permute-start | bytes 786440 | tf_op jit(solution)/shard_map/ppermute | solution.py:306
  387.0 18.7 %collective-permute-start.35 = (bf16[128,1024]{1,0:T(8,128)(2,1)S(1)}, bf16[128,1024]{1,0:T(8,128)(2,1)S(1)}, u32[]{:S(2)}, u32[]{:S(2)}) collective-permute-start(bf16[128,1024]{1,0:T(8,128)(2,1)S(1)} %select_convert_fusion.10), channel_id=1, source_target_pairs={{0,16},{2,18},{4,20},{6,22},{8,24},{10,26},{12,28},{14,30},{16,0},... | collective-permute-start | bytes 786440 | tf_op jit(solution)/shard_map/ppermute | solution.py:306
  388.4 28.5 %collective-permute-start.27 = (bf16[64,2048]{1,0:T(8,128)(2,1)S(1)}, bf16[64,2048]{1,0:T(8,128)(2,1)S(1)}, u32[]{:S(2)}, u32[]{:S(2)}) collective-permute-start(bf16[64,2048]{1,0:T(8,128)(2,1)S(1)} %select_convert_fusion.11), channel_id=1, source_target_pairs={{0,16},{2,18},{4,20},{6,22},{8,24},{10,26},{12,28},{14,30},{16,0},... | collective-permute-start | bytes 786440 | tf_op jit(solution)/shard_map/ppermute | solution.py:306
  395.7 38.2 %collective-permute-start.9 = (bf16[768,512]{1,0:T(8,128)(2,1)S(1)}, bf16[768,512]{1,0:T(8,128)(2,1)S(1)}, u32[]{:S(2)}, u32[]{:S(2)}) collective-permute-start(bf16[768,512]{1,0:T(8,128)(2,1)S(1)} %select_convert_fusion.5), channel_id=1, source_target_pairs={{0,4},{2,6},{4,0},{6,2},{8,12},{10,14},{12,8},{14,10},{16,20},{18,... | collective-permute-start | bytes 2359304 | tf_op jit(solution)/shard_map/ppermute | solution.py:306
  405.8 22.4 %collective-permute-start.36 = (bf16[128,1024]{1,0:T(8,128)(2,1)S(1)}, bf16[128,1024]{1,0:T(8,128)(2,1)S(1)}, u32[]{:S(2)}, u32[]{:S(2)}) collective-permute-start(bf16[128,1024]{1,0:T(8,128)(2,1)S(1)} %add_convert_fusion.3), channel_id=1, source_target_pairs={{0,16},{2,18},{4,20},{6,22},{8,24},{10,26},{12,28},{14,30},{16,0},... | collective-permute-start | bytes 786440 | tf_op jit(solution)/shard_map/ppermute | solution.py:306
  417.0 16.8 %collective-permute-start.28 = (bf16[64,2048]{1,0:T(8,128)(2,1)S(1)}, bf16[64,2048]{1,0:T(8,128)(2,1)S(1)}, u32[]{:S(2)}, u32[]{:S(2)}) collective-permute-start(bf16[64,2048]{1,0:T(8,128)(2,1)S(1)} %add_convert_fusion.4), channel_id=1, source_target_pairs={{0,16},{2,18},{4,20},{6,22},{8,24},{10,26},{12,28},{14,30},{16,0},... | collective-permute-start | bytes 786440 | tf_op jit(solution)/shard_map/ppermute | solution.py:306
  428.3 16.8 %collective-permute-start.37 = (bf16[256,1024]{1,0:T(8,128)(2,1)S(1)}, bf16[256,1024]{1,0:T(8,128)(2,1)S(1)}, u32[]{:S(2)}, u32[]{:S(2)}) collective-permute-start(bf16[256,1024]{1,0:T(8,128)(2,1)S(1)} %pad_maximum_fusion.23), channel_id=1, source_target_pairs={{0,8},{2,10},{4,12},{6,14},{8,0},{10,2},{12,4},{14,6},{16,24},{18,... | collective-permute-start | bytes 1572872 | tf_op jit(solution)/shard_map/ppermute | solution.py:306
  433.9 22.4 %collective-permute-start.29 = (bf16[128,2048]{1,0:T(8,128)(2,1)S(1)}, bf16[128,2048]{1,0:T(8,128)(2,1)S(1)}, u32[]{:S(2)}, u32[]{:S(2)}) collective-permute-start(bf16[128,2048]{1,0:T(8,128)(2,1)S(1)} %pad_maximum_fusion.22), channel_id=1, source_target_pairs={{0,8},{2,10},{4,12},{6,14},{8,0},{10,2},{12,4},{14,6},{16,24},{18,... | collective-permute-start | bytes 1572872 | tf_op jit(solution)/shard_map/ppermute | solution.py:306
  434.5 30.1 %collective-permute-start.10 = (bf16[384,512]{1,0:T(8,128)(2,1)S(1)}, bf16[384,512]{1,0:T(8,128)(2,1)S(1)}, u32[]{:S(2)}, u32[]{:S(2)}) collective-permute-start(bf16[384,512]{1,0:T(8,128)(2,1)S(1)} %select_convert_fusion.9), channel_id=1, source_target_pairs={{0,8},{2,10},{4,12},{6,14},{8,0},{10,2},{12,4},{14,6},{16,24},{18,... | collective-permute-start | bytes 1179656 | tf_op jit(solution)/shard_map/ppermute | solution.py:306
  445.3 42.6 %collective-permute-start.38 = (bf16[512,1024]{1,0:T(8,128)(2,1)S(1)}, bf16[512,1024]{1,0:T(8,128)(2,1)S(1)}, u32[]{:S(2)}, u32[]{:S(2)}) collective-permute-start(bf16[512,1024]{1,0:T(8,128)(2,1)S(1)} %pad_maximum_fusion.17), channel_id=1, source_target_pairs={{0,4},{2,6},{4,0},{6,2},{8,12},{10,14},{12,8},{14,10},{16,20},{18,... | collective-permute-start | bytes 3145736 | tf_op jit(solution)/shard_map/ppermute | solution.py:306
  464.8 11.8 %collective-permute-start.11 = (bf16[192,512]{1,0:T(8,128)(2,1)S(1)}, bf16[192,512]{1,0:T(8,128)(2,1)S(1)}, u32[]{:S(2)}, u32[]{:S(2)}) collective-permute-start(bf16[192,512]{1,0:T(8,128)(2,1)S(1)} %select_convert_fusion.13), channel_id=1, source_target_pairs={{0,16},{2,18},{4,20},{6,22},{8,24},{10,26},{12,28},{14,30},{16,0},... | collective-permute-start | bytes 589832 | tf_op jit(solution)/shard_map/ppermute | solution.py:306
  465.6 27.3 %collective-permute-start.30 = (bf16[256,2048]{1,0:T(8,128)(2,1)S(1)}, bf16[256,2048]{1,0:T(8,128)(2,1)S(1)}, u32[]{:S(2)}, u32[]{:S(2)}) collective-permute-start(bf16[256,2048]{1,0:T(8,128)(2,1)S(1)} %pad_maximum_fusion.16), channel_id=1, source_target_pairs={{0,4},{2,6},{4,0},{6,2},{8,12},{10,14},{12,8},{14,10},{16,20},{18,... | collective-permute-start | bytes 3145736 | tf_op jit(solution)/shard_map/ppermute | solution.py:306
  476.8 11.0 %collective-permute-start.12 = (bf16[192,512]{1,0:T(8,128)(2,1)S(1)}, bf16[192,512]{1,0:T(8,128)(2,1)S(1)}, u32[]{:S(2)}, u32[]{:S(2)}) collective-permute-start(bf16[192,512]{1,0:T(8,128)(2,1)S(1)} %add_convert_fusion.5), channel_id=1, source_target_pairs={{0,16},{2,18},{4,20},{6,22},{8,24},{10,26},{12,28},{14,30},{16,0},... | collective-permute-start | bytes 589832 | tf_op jit(solution)/shard_map/ppermute | solution.py:306
  477.0 28.8 %collective-permute-start.23 = (bf16[256,1024]{1,0:T(8,128)(2,1)S(1)}, bf16[256,1024]{1,0:T(8,128)(2,1)S(1)}, u32[]{:S(2)}, u32[]{:S(2)}) collective-permute-start(bf16[256,1024]{1,0:T(8,128)(2,1)S(1)} %pad_maximum_fusion.21), channel_id=1, source_target_pairs={{0,2},{2,0},{4,6},{6,4},{8,10},{10,8},{12,14},{14,12},{16,18},{18,... | collective-permute-start | bytes 1572872 | tf_op jit(solution)/shard_map/ppermute | solution.py:306
  487.8 11.1 %collective-permute-start.13 = (bf16[384,512]{1,0:T(8,128)(2,1)S(1)}, bf16[384,512]{1,0:T(8,128)(2,1)S(1)}, u32[]{:S(2)}, u32[]{:S(2)}) collective-permute-start(bf16[384,512]{1,0:T(8,128)(2,1)S(1)} %pad_maximum_fusion.24), channel_id=1, source_target_pairs={{0,8},{2,10},{4,12},{6,14},{8,0},{10,2},{12,4},{14,6},{16,24},{18,... | collective-permute-start | bytes 1179656 | tf_op jit(solution)/shard_map/ppermute | solution.py:306
  488.7 29.6 %collective-permute-start.39 = (bf16[1024,1024]{1,0:T(8,128)(2,1)S(1)}, bf16[1024,1024]{1,0:T(8,128)(2,1)S(1)}, u32[]{:S(2)}, u32[]{:S(2)}) collective-permute-start(bf16[1024,1024]{1,0:T(8,128)(2,1)S(1)} %pad_maximum_fusion.6), channel_id=1, source_target_pairs={{0,2},{2,0},{4,6},{6,4},{8,10},{10,8},{12,14},{14,12},{16,18},{18,... | collective-permute-start | bytes 6291464 | tf_op jit(solution)/shard_map/ppermute | solution.py:306
  493.6 26.2 %collective-permute-start.31 = (bf16[512,2048]{1,0:T(8,128)(2,1)S(1)}, bf16[512,2048]{1,0:T(8,128)(2,1)S(1)}, u32[]{:S(2)}, u32[]{:S(2)}) collective-permute-start(bf16[512,2048]{1,0:T(8,128)(2,1)S(1)} %pad_maximum_fusion.5), channel_id=1, source_target_pairs={{0,2},{2,0},{4,6},{6,4},{8,10},{10,8},{12,14},{14,12},{16,18},{18,... | collective-permute-start | bytes 6291464 | tf_op jit(solution)/shard_map/ppermute | solution.py:306
  499.2 18.7 %collective-permute-start.14 = (bf16[768,512]{1,0:T(8,128)(2,1)S(1)}, bf16[768,512]{1,0:T(8,128)(2,1)S(1)}, u32[]{:S(2)}, u32[]{:S(2)}) collective-permute-start(bf16[768,512]{1,0:T(8,128)(2,1)S(1)} %pad_maximum_fusion.18), channel_id=1, source_target_pairs={{0,4},{2,6},{4,0},{6,2},{8,12},{10,14},{12,8},{14,10},{16,20},{18,... | collective-permute-start | bytes 2359304 | tf_op jit(solution)/shard_map/ppermute | solution.py:306
  518.2 11.5 %collective-permute-start.15 = (bf16[1536,512]{1,0:T(8,128)(2,1)S(1)}, bf16[1536,512]{1,0:T(8,128)(2,1)S(1)}, u32[]{:S(2)}, u32[]{:S(2)}) collective-permute-start(bf16[1536,512]{1,0:T(8,128)(2,1)S(1)} %pad_maximum_fusion.7), channel_id=1, source_target_pairs={{0,2},{2,0},{4,6},{6,4},{8,10},{10,8},{12,14},{14,12},{16,18},{18,... | collective-permute-start | bytes 4718600 | tf_op jit(solution)/shard_map/ppermute | solution.py:306
  (30 other events, 98.0 us)

commit v2 on v1

--- a/solution.py
+++ b/solution.py
@@ -276,55 +276,624 @@
     )(flags, qkv, qkv, qkv, grad, mixed, lse, seg_rows, seg_cols, cosine, sine)
 
 
-def body(
+def qkv_pair_kernel(own_ref, got_ref, w_ref, cos_ref, sin_ref, *refs):
+    o_ref, rows_ref = refs[-2:]
+    which = pl.program_id(0)
+    half = own_ref.shape[0]
+
+    @pl.when(which == 0)
+    def _():
+        rows_ref[:half, :] = own_ref[...]
+        rows_ref[half:, :] = got_ref[...]
+
+    y = mm(rows_ref[...], w_ref[...], 1, 0)
+
+    @pl.when(which < 2)
+    def _():
+        factor = jnp.where(which == 0, HEAD**-0.5, 1.0)
+        for p in range(y.shape[1] // PAIR):
+            u = y[:, p * PAIR : (p + 1) * PAIR]
+            r = u * cos_ref[...] + turned(u) * sin_ref[...]
+            o_ref[:, p * PAIR : (p + 1) * PAIR] = (r.astype(bf16) * factor.astype(bf16)).astype(bf16)
+
+    @pl.when(which == 2)
+    def _():
+        o_ref[...] = y.astype(bf16)
+
+
+def project_pair(j, own, got, w_qkv, cosine, sine, before, length):
+    half, depth = own.shape
+    width = w_qkv.shape[2]
+    chunk = 2 * half
+    table = pl.BlockSpec((chunk, PAIR), lambda t: (j, 0))
+    return pl.pallas_call(
+        qkv_pair_kernel,
+        grid=(3,),
+        in_specs=[
+            pl.BlockSpec((half, depth), lambda t: (0, 0)),
+            pl.BlockSpec((half, depth), lambda t: (0, 0)),
+            pl.BlockSpec((None, depth, width), lambda t: (t, 0, 0)),
+            table,
+            table,
+            *[pl.BlockSpec(memory_space=pl.ANY) for _ in before],
+        ],
+        out_specs=[
+            pl.BlockSpec((None, chunk, width), lambda t: (t, j, 0)),
+            pl.BlockSpec((chunk, depth), lambda t: (j, 0)),
+        ],
+        out_shape=[
+            jax.ShapeDtypeStruct((3, length, width), bf16),
+            jax.ShapeDtypeStruct((length, depth), bf16),
+        ],
+        input_output_aliases={5 + i: i for i in range(len(before))},
+        compiler_params=pltpu.CompilerParams(vmem_limit_bytes=32 << 20),
+        cost_estimate=pl.CostEstimate(
+            flops=6 * chunk * depth * width, bytes_accessed=8 * depth * width, transcendentals=0
+        ),
+        name="qkv",
+    )(own, got, w_qkv, cosine, sine, *before)
+
+
+def forward_chunk_kernel(q_ref, k_ref, v_ref, segr_ref, segc_ref, o_ref, lse_ref, vt):
+    length, count = k_ref.shape[0], q_ref.shape[0]
+    for b in range(0, length, BLOCK):
+        vt[:, b : b + BLOCK] = transposed(v_ref[b : b + BLOCK, :]).astype(bf16)
+    q = q_ref[...]
+    outs = []
+    for h in range(2):
+        qh = head_lanes(q, h)
+        scores = []
+        for b in range(0, length, BLOCK):
+            same = jnp.concatenate([segc_ref[b : b + BLOCK, :]] * (count // 128), axis=1) == segr_ref[...]
+            scores.append(jnp.where(same, mm(k_ref[b : b + BLOCK, :], qh, 1, 1), masked_score))
+        top = functools.reduce(jnp.maximum, [jnp.max(s, axis=0, keepdims=True) for s in scores])
+        total, summed = 0.0, 0.0
+        for i, s in enumerate(scores):
+            p = jnp.exp(s - top)
+            total = total + jnp.sum(p, axis=0, keepdims=True)
+            summed = summed + mm(vt[h * HEAD : (h + 1) * HEAD, i * BLOCK : (i + 1) * BLOCK], p.astype(bf16), 1, 0)
+        lse_ref[h] = top + jnp.log(total)
+        outs.append(summed / total)
+    o_ref[...] = jnp.concatenate(outs, axis=0).T.astype(bf16)
+
+
+def pair_pieces(j, length, chunk):
+    return [
+        pl.BlockSpec((None, chunk, PAIR), lambda p: (0, j, p)),
+        pl.BlockSpec((None, length, PAIR), lambda p: (1, 0, p)),
+        pl.BlockSpec((None, length, PAIR), lambda p: (2, 0, p)),
+    ]
+
+
+def attend_forward_pair(j, chunk, qkv, seg_rows, seg_cols):
+    _, length, width = qkv.shape
+    pairs = width // PAIR
+    return pl.pallas_call(
+        forward_chunk_kernel,
+        grid=(pairs,),
+        in_specs=[
+            *pair_pieces(j, length, chunk),
+            pl.BlockSpec((1, chunk), lambda p: (0, j)),
+            pl.BlockSpec((length, 128), lambda p: (0, 0)),
+        ],
+        out_specs=[
+            pl.BlockSpec((chunk, PAIR), lambda p: (0, p)),
+            pl.BlockSpec((2, 1, chunk), lambda p: (p, 0, 0)),
+        ],
+        out_shape=[
+            jax.ShapeDtypeStruct((chunk, width), bf16),
+            jax.ShapeDtypeStruct((2 * pairs, 1, chunk), f32),
+        ],
+        scratch_shapes=[pltpu.VMEM((PAIR, length), bf16)],
+        compiler_params=pltpu.CompilerParams(vmem_limit_bytes=48 << 20),
+        cost_estimate=pl.CostEstimate(
+            flops=16 * chunk * length * width,
+            bytes_accessed=8 * length * width,
+            transcendentals=chunk * length * width // HEAD,
+        ),
+        name="attend",
+    )(qkv, qkv, qkv, seg_rows, seg_cols)
+
+
+def backward_chunk_kernel(
+    last, q_ref, k_ref, v_ref, g_ref, o_ref, lse_ref, segr_ref, segc_ref, cos_ref, sin_ref, cos_all, sin_all, *refs
+):
+    if last:
+        dk_in, dv_in, _, dq_ref, dk_ref, dv_ref, kt, dk, dv = refs
+        dk[...] = dk_in[...]
+        dv[...] = dv_in[...]
+    else:
+        dq_ref, dk, dv, kt = refs
+        dk[...] = jnp.zeros(dk.shape, f32)
+        dv[...] = jnp.zeros(dv.shape, f32)
+    length, count = k_ref.shape[0], q_ref.shape[0]
+    for b in range(0, length, BLOCK):
+        kt[:, b : b + BLOCK] = transposed(k_ref[b : b + BLOCK, :]).astype(bf16)
+    q, g = q_ref[...], g_ref[...]
+    both = (g.astype(f32) * o_ref[...].astype(f32)).T
+    qh = [head_lanes(q, h) for h in range(2)]
+    gh = [head_lanes(g, h) for h in range(2)]
+    delta = [jnp.sum(both[h * HEAD : (h + 1) * HEAD, :], axis=0, keepdims=True) for h in range(2)]
+    q_two, g_two = jnp.concatenate(qh, axis=0), jnp.concatenate(gh, axis=0)
+    dq = [0.0, 0.0]
+    for b in range(0, length, BLOCK):
+        cols = slice(b, b + BLOCK)
+        k, v = k_ref[cols, :], v_ref[cols, :]
+        same = jnp.concatenate([segc_ref[cols, :]] * (count // 128), axis=1) == segr_ref[...]
+        ps, ds = [], []
+        for h in range(2):
+            s = jnp.where(same, mm(k, qh[h], 1, 1), masked_score)
+            p = jnp.exp(s - lse_ref[h])
+            d = (p * (mm(v, gh[h], 1, 1) - delta[h])).astype(bf16)
+            ps.append(p.astype(bf16))
+            ds.append(d)
+            dq[h] = dq[h] + mm(kt[h * HEAD : (h + 1) * HEAD, cols], d, 1, 0)
+        dv[cols, :] += mm(jnp.concatenate(ps, axis=1), g_two, 1, 0)
+        dk[cols, :] += mm(jnp.concatenate(ds, axis=1), q_two, 1, 0)
+
+    def turn_back(u, cosine, sine):
+        return (u * cosine - turned(u) * sine).astype(bf16)
+
+    dq_ref[...] = turn_back(jnp.concatenate(dq, axis=0).T * (HEAD**-0.5), cos_ref[...], sin_ref[...])
+    if last:
+        for b in range(0, length, BLOCK):
+            rows = slice(b, b + BLOCK)
+            dk_ref[rows, :] = turn_back(dk[rows, :], cos_all[rows, :], sin_all[rows, :])
+            dv_ref[rows, :] = dv[rows, :].astype(bf16)
+
+
+def attend_backward_pair(j, chunk, qkv, grad, mixed, lse, seg_rows, seg_cols, cosine, sine, before):
+    _, length, width = qkv.shape
+    pairs = width // PAIR
+    last = bool(before)
+    whole = pl.BlockSpec((length, PAIR), lambda p: (0, p))
+    part = pl.BlockSpec((chunk, PAIR), lambda p: (0, p))
+    table = pl.BlockSpec((chunk, PAIR), lambda p: (j, 0))
+    table_all = pl.BlockSpec((length, PAIR), lambda p: (0, 0))
+    dq_before = before[:1]
+    return pl.pallas_call(
+        functools.partial(backward_chunk_kernel, last),
+        grid=(pairs,),
+        in_specs=[
+            *pair_pieces(j, length, chunk),
+            part,
+            part,
+            pl.BlockSpec((2, 1, chunk), lambda p: (p, 0, 0)),
+            pl.BlockSpec((1, chunk), lambda p: (0, j)),
+            table_all,
+            table,
+            table,
+            table_all,
+            table_all,
+            *([whole, whole, pl.BlockSpec(memory_space=pl.ANY)] if last else []),
+        ],
+        out_specs=[pl.BlockSpec((chunk, PAIR), lambda p: (j, p)), whole, whole],
+        out_shape=[
+            jax.ShapeDtypeStruct((length, width), bf16),
+            jax.ShapeDtypeStruct((length, width), bf16 if last else f32),
+            jax.ShapeDtypeStruct((length, width), bf16 if last else f32),
+        ],
+        scratch_shapes=[
+            pltpu.VMEM((PAIR, length), bf16),
+            *([pltpu.VMEM((length, PAIR), f32)] * 2 if last else []),
+        ],
+        input_output_aliases={14: 0} if last else {},
+        compiler_params=pltpu.CompilerParams(vmem_limit_bytes=56 << 20),
+        cost_estimate=pl.CostEstimate(
+            flops=40 * chunk * length * width,
+            bytes_accessed=16 * length * width,
+            transcendentals=chunk * length * width // HEAD,
+        ),
+        name="attend_back",
+    )(
+        qkv, qkv, qkv, grad, mixed, lse, seg_rows, seg_cols, cosine, sine, cosine, sine,
+        *((*before[1:], *dq_before) if last else ()),
+    )
+
+
+def mlp_kernel(own_ref, got_ref, b_own_ref, b_got_ref, up_ref, bias_ref, down_ref, *refs):
+    rows_ref, hidden_ref, pre_ref, own_grad, got_grad, own_branch, got_branch, bias_grad, grads, branch = refs[-10:]
+    tile, tiles = pl.program_id(0), pl.num_programs(0)
+    half = own_ref.shape[0]
+
+    @pl.when(tile == 0)
+    def _():
+        rows_ref[:half, :] = own_ref[...]
+        rows_ref[half:, :] = got_ref[...]
+
+    up, down = up_ref[...], down_ref[...]
+    cubic, root = 0.044715, (2.0 / jnp.pi) ** 0.5
+    for part in range(2):
+        rows = slice(part * half, (part + 1) * half)
+        back = (b_own_ref, b_got_ref)[part]
+        u = mm((own_ref, got_ref)[part][...], up, 1, 0) + bias_ref[...]
+        square = u * u
+        t = jnp.tanh(root * u * (1.0 + cubic * square))
+        hidden = (0.5 * u * (1.0 + t)).astype(bf16)
+        slope = 0.5 * (1.0 + t) + 0.5 * u * (1.0 - t * t) * (root * (1.0 + 3.0 * cubic * square))
+        grad = mm(back[...], down, 1, 1) * slope
+        grad_low = grad.astype(bf16)
+        hidden_ref[rows, :] = hidden
+        pre_ref[rows, :] = grad_low
+        total = jnp.sum(grad_low.astype(f32), axis=0, keepdims=True)
+        more, more_branch = mm(grad_low, up, 1, 1), mm(hidden, down, 1, 0)
+
+        @pl.when(tile == 0)
+        def _():
+            grads[rows, :] = more
+            branch[rows, :] = more_branch
+
+        @pl.when(tile > 0)
+        def _():
+            grads[rows, :] += more
+            branch[rows, :] += more_branch
+
+        if part == 0:
+            bias_grad[...] = total
+        else:
+            bias_grad[...] += total
+
+    @pl.when(tile == tiles - 1)
+    def _():
+        own_grad[...] = grads[:half, :]
+        got_grad[...] = grads[half:, :].astype(bf16)
+        own_branch[...] = branch[:half, :]
+        got_branch[...] = branch[half:, :].astype(bf16)
+
+
+def mlp_pair(j, own, got, back_own, back_got, w_up, b_up, w_down, before, length):
+    half, depth = own.shape
+    width = w_up.shape[1]
+    chunk, tile = 2 * half, 512
+    small = pl.BlockSpec((half, depth), lambda t: (0, 0))
+    wide = pl.BlockSpec((chunk, tile), lambda t: (j, t))
+    return pl.pallas_call(
+        mlp_kernel,
+        grid=(width // tile,),
+        in_specs=[
+            small, small, small, small,
+            pl.BlockSpec((depth, tile), lambda t: (0, t)),
+            pl.BlockSpec((1, tile), lambda t: (0, t)),
+            pl.BlockSpec((tile, depth), lambda t: (t, 0)),
+            *[pl.BlockSpec(memory_space=pl.ANY) for _ in before],
+        ],
+        out_specs=[
+            pl.BlockSpec((chunk, depth), lambda t: (j, 0)), wide, wide,
+            small, small, small, small,
+            pl.BlockSpec((1, tile), lambda t: (0, t)),
+        ],
+        out_shape=[
+            jax.ShapeDtypeStruct((length, depth), bf16),
+            jax.ShapeDtypeStruct((length, width), bf16),
+            jax.ShapeDtypeStruct((length, width), bf16),
+            jax.ShapeDtypeStruct((half, depth), f32),
+            jax.ShapeDtypeStruct((half, depth), bf16),
+            jax.ShapeDtypeStruct((half, depth), f32),
+            jax.ShapeDtypeStruct((half, depth), bf16),
+            jax.ShapeDtypeStruct((1, width), f32),
+        ],
+        scratch_shapes=[pltpu.VMEM((chunk, depth), f32), pltpu.VMEM((chunk, depth), f32)],
+        input_output_aliases={7 + i: i for i in range(len(before))},
+        compiler_params=pltpu.CompilerParams(vmem_limit_bytes=56 << 20),
+        cost_estimate=pl.CostEstimate(
+            flops=12 * chunk * depth * width, bytes_accessed=12 * depth * width, transcendentals=chunk * width
+        ),
+        name="mlp",
+    )(own, got, back_own, back_got, w_up, b_up[None, :], w_down, *before)
+
+
+def qkv_back_kernel(q_ref, k_ref, v_ref, w_ref, o_ref):
+    total = mm(q_ref[...], w_ref[0], 1, 1) + mm(k_ref[...], w_ref[1], 1, 1) + mm(v_ref[...], w_ref[2], 1, 1)
+    o_ref[...] = total.astype(o_ref.dtype)
+
+
+def project_back_pair(part, half, dq, dk, dv, w_qkv, kind):
+    length, width = dq.shape
+    depth = w_qkv.shape[1]
+    block = pl.BlockSpec((half, width), lambda c: (2 * c + part, 0))
+    return pl.pallas_call(
+        qkv_back_kernel,
+        grid=(length // (2 * half),),
+        in_specs=[block, block, block, pl.BlockSpec((3, depth, width), lambda c: (0, 0, 0))],
+        out_specs=pl.BlockSpec((half, depth), lambda c: (c, 0)),
+        out_shape=jax.ShapeDtypeStruct((length // 2, depth), kind),
+        compiler_params=pltpu.CompilerParams(vmem_limit_bytes=32 << 20),
+        cost_estimate=pl.CostEstimate(
+            flops=3 * length * depth * width, bytes_accessed=6 * depth * width, transcendentals=0
+        ),
+        name="qkv_back",
+    )(dq, dk, dv, w_qkv)
+
+
+MESH = pl.DeviceIdType.MESH
+ADD_ROWS = 32
+
+
+def add_low(out, out_at, a, a_at, b, rows):
+    @pl.loop(0, rows // ADD_ROWS)
+    def _(i):
+        at = pl.multiple_of(i * ADD_ROWS, ADD_ROWS)
+        total = a[pl.ds(pl.multiple_of(a_at + at, ADD_ROWS), ADD_ROWS), :].astype(f32)
+        total = total + b[pl.ds(at, ADD_ROWS), :].astype(f32)
+        out[pl.ds(pl.multiple_of(out_at + at, ADD_ROWS), ADD_ROWS), :] = total.astype(bf16)
+
+
+class Unit:
+    def __init__(self, part, out, row, rows, held, got, send, recv, local, place):
+        self.part, self.out, self.row, self.rows = part, out, row, rows
+        self.held, self.got, self.send, self.recv, self.local = held, got, send, recv, local
+        self.bit = [(place // (1 << b)) % 2 for b in range(4)]
+        self.partner = [place + (1 - 2 * self.bit[b]) * (1 << b) for b in range(4)]
+        self.base = [row]
+        for b in range(4):
+            self.base.append(self.base[-1] + self.bit[b] * (rows >> (b + 1)))
+
+    def remote(self, src, dst, stage, b):
+        return pltpu.make_async_remote_copy(
+            src_ref=src,
+            dst_ref=dst,
+            send_sem=self.send.at[stage],
+            recv_sem=self.recv.at[stage],
+            device_id={"dp": self.partner[b]},
+            device_id_type=MESH,
+        )
+
+    def at(self, start, rows):
+        return pl.ds(pl.multiple_of(start, ADD_ROWS), rows)
+
+    def halving(self, b):
+        half = self.rows >> (b + 1)
+        if b == 0:
+            src = self.part.at[self.at(self.row + (1 - self.bit[0]) * half, half)]
+        else:
+            src = self.held[b - 1].at[self.at((1 - self.bit[b]) * half, half)]
+        return self.remote(src, self.got[b], b, b)
+
+    def keep(self):
+        half = self.rows // 2
+        return pltpu.make_async_copy(
+            self.part.at[self.at(self.row + self.bit[0] * half, half)], self.held[0], self.local.at[0]
+        )
+
+    def own(self):
+        return pltpu.make_async_copy(
+            self.held[3], self.out.at[self.at(self.base[4], self.rows >> 4)], self.local.at[1]
+        )
+
+    def gathering(self, b):
+        size = self.rows >> (b + 1)
+        spot = self.out.at[self.at(self.base[b + 1], size)]
+        return self.remote(self.held[3] if b == 3 else spot, spot, 7 - b, b)
+
+    def step(self, k):
+        if k == 0:
+            self.halving(0).start()
+            self.keep().start()
+        elif k == 1:
+            self.halving(0).wait()
+            self.keep().wait()
+            add_low(self.held[0], 0, self.held[0], 0, self.got[0], self.rows // 2)
+            self.halving(1).start()
+        elif k < 5:
+            b = k - 1
+            self.halving(b).wait()
+            half = self.rows >> (b + 1)
+            add_low(self.held[b], 0, self.held[b - 1], self.bit[b] * half, self.got[b], half)
+            if b < 3:
+                self.halving(b + 1).start()
+            else:
+                self.own().start()
+                self.gathering(3).start()
+        elif k == 5:
+            self.own().wait()
+            self.gathering(3).wait()
+            self.gathering(2).start()
+        elif k < 8:
+            self.gathering(8 - k).wait()
+            self.gathering(7 - k).start()
+        else:
+            self.gathering(0).wait()
+
+
+STEPS = 9
+
+
+def greet(targets):
+    barrier = pltpu.get_barrier_semaphore()
+    for target in targets:
+        pl.semaphore_signal(barrier, inc=1, device_id=target, device_id_type=MESH)
+    pl.semaphore_wait(barrier, len(targets))
+
+
+def reduce_kernel(cuts, arrays, *refs):
+    parts, outs, scratch = refs[:arrays], refs[arrays : 2 * arrays], refs[2 * arrays :]
+    place = lax.axis_index("dp")
+    units = []
+    for i, (which, row, rows) in enumerate(cuts):
+        mine = scratch[11 * i : 11 * (i + 1)]
+        units.append(Unit(parts[which], outs[which], row, rows, mine[:4], mine[4:8], *mine[8:], place))
+    greet([{"dp": partner} for partner in units[0].partner])
+    late = [0, 1, 3, 5, 7, 8, 9, 11, 13]
+    order = sorted((late[k] + 2 * i, k, i) for i in range(len(units)) for k in range(STEPS))
+    for _, k, i in order:
+        units[i].step(k)
+
+
+def unit_scratch(rows, columns):
+    return [
+        *[pltpu.VMEM((rows >> (b + 1), columns), bf16) for b in range(4)],
+        *[pltpu.VMEM((rows >> (b + 1), columns), bf16) for b in range(4)],
+        pltpu.SemaphoreType.DMA((8,)),
+        pltpu.SemaphoreType.DMA((8,)),
+        pltpu.SemaphoreType.DMA((2,)),
+    ]
+
+
+def reduce_over_dp(parts, cuts):
+    scratch = []
+    for which, _, rows in cuts:
+        scratch += unit_scratch(rows, parts[which].shape[1])
+    anywhere = pl.BlockSpec(memory_space=pl.ANY)
+    return pl.pallas_call(
+        functools.partial(reduce_kernel, cuts, len(parts)),
+        in_specs=[anywhere] * len(parts),
+        out_specs=[anywhere] * len(parts),
+        out_shape=[jax.ShapeDtypeStruct(p.shape, p.dtype) for p in parts],
+        scratch_shapes=scratch,
+        compiler_params=pltpu.CompilerParams(collective_id=1, has_side_effects=True, vmem_limit_bytes=40 << 20),
+        name="reduce",
+    )(*parts)
+
+
+def body_pair(
     tokens, cond, doc_lengths, w_ada, b_ada, gain_one, w_qkv, w_out, gain_two, w_up, b_up, w_down, b_down, cotangent
 ):
-    tensor_size, dp_size = lax.axis_size("tensor"), lax.axis_size("dp")
-    pair = tensor_size == 2
-    cube = dp_size & (dp_size - 1) == 0
+    dp_size = lax.axis_size("dp")
+    bits = dp_size.bit_length() - 1
+    own, width = tokens.shape
+    length = 2 * own
+    chunks = 2
+    half, chunk = own // chunks, length // chunks
+    me = lax.axis_index("tensor")
+
+    def swap(values):
+        return lax.ppermute(values, "tensor", [(0, 1), (1, 0)])
+
+    def across(values, b):
+        return lax.ppermute(values, "dp", [(d, d ^ (1 << b)) for d in range(dp_size)])
+
+    def gathered(row):
+        for b in reversed(range(bits)):
+            row = jnp.concatenate([row, across(row, b)], axis=0)
+        return row
+
+    step = jnp.arange(length, dtype=jnp.int32)
+    in_chunk = step % chunk
+    places = jnp.where(in_chunk < half, me, 1 - me) * own + (step // chunk) * half + in_chunk % half
+    segment, doc_first = documents(doc_lengths[0], places)
+    cosine, sine = rope_tables(places - doc_first)
+    seg_rows = segment[None, :]
+    seg_cols = jnp.broadcast_to(segment[:, None], (length, 128))
+
+    modulation = jnp.dot(cond, w_ada, preferred_element_type=f32)[0] + b_ada
+    shift_a, scale_a, gate_a, shift_m, scale_m, gate_m = jnp.split(modulation, 6)
+    cuts = [slice(c * half, (c + 1) * half) for c in range(chunks)]
+    x_rows = [tokens[cut].astype(f32) for cut in cuts]
+    grad_out = [cotangent[cut].astype(f32) for cut in cuts]
+    each = range(chunks)
+
+    act_one = [modulate(x_rows[c], gain_one, shift_a, scale_a).astype(bf16) for c in each]
+    got_one = [swap(act_one[c]) for c in each]
+    back = [(grad_out[c] * gate_m).astype(bf16) for c in each]
+    state = ()
+    for c in each:
+        state = project_pair(c, act_one[c], got_one[c], w_qkv, cosine, sine, state, length)
+    qkv, rows_one = state
+    got_back = [swap(back[c]) for c in each]
+    full_back = jnp.concatenate([piece for c in each for piece in (back[c], got_back[c])], axis=0)
+
+    mixed, lse, projected, middle, act_two, got_two = [], [], [], [], [], []
+    for c in each:
+        m, l = attend_forward_pair(c, chunk, qkv, seg_rows, seg_cols)
+        mixed.append(m)
+        lse.append(l)
+    sums = [swap(jnp.dot(mixed[c][half:], w_out, preferred_element_type=f32).astype(bf16)) for c in each]
+    for c in each:
+        projected.append(jnp.dot(mixed[c][:half], w_out, preferred_element_type=f32) + sums[c].astype(f32))
+        middle.append(x_rows[c] + gate_a * projected[c])
+        act_two.append(modulate(middle[c], gain_two, shift_m, scale_m).astype(bf16))
+        got_two.append(swap(act_two[c]))
+    state, pieces = (), []
+    for c in each:
+        out = mlp_pair(c, act_two[c], got_two[c], back[c], got_back[c], w_up, b_up, w_down, state, length)
+        state, rest = out[:3], out[3:]
+        pieces.append(rest)
+    rows_two, hidden, grad_pre = state
+    grad_b_up = sum(pieces[c][4] for c in each)[0]
+    grad_act_two = [pieces[c][0] + swap(pieces[c][1]).astype(f32) for c in each]
+    grad_w_down = mm(hidden, full_back, 0, 0).astype(bf16)
+    grad_w_up = mm(rows_two, grad_pre, 0, 0).astype(bf16)
+
+    vectors, grad_middle, full_proj, grad_mixed = [], [], [], []
+    for c in each:
+        _, second_back = jax.vjp(modulate, middle[c], gain_two, shift_m, scale_m)
+        grad, grad_gain_two, grad_shift_m, grad_scale_m = second_back(grad_act_two[c])
+        grad_middle.append(grad + grad_out[c])
+        vectors.append([grad_gain_two, grad_shift_m, grad_scale_m])
+        proj = (grad_middle[c] * gate_a).astype(bf16)
+        full_proj.append(jnp.concatenate([proj, swap(proj)], axis=0))
+        grad_mixed.append(mm(full_proj[c], w_out, 1, 1).astype(bf16))
+    grad_gain_two, grad_shift_m, grad_scale_m = [sum(parts) for parts in zip(*vectors)]
+    branch = [pieces[c][2] + swap(pieces[c][3]).astype(f32) + b_down for c in each]
+    output = jnp.concatenate([(middle[c] + gate_m * branch[c]).astype(bf16) for c in each], axis=0)
+    grad_gate_m = sum(jnp.sum(grad_out[c] * branch[c], axis=0) for c in each)
+    grad_b_down = sum(jnp.sum(back[c].astype(f32), axis=0) for c in each)
+    grad_gate_a = sum(jnp.sum(grad_middle[c] * projected[c], axis=0) for c in each)
+
+    grads = ()
+    for c in each:
+        grads = attend_backward_pair(
+            c, chunk, qkv, grad_mixed[c], mixed[c], lse[c], seg_rows, seg_cols, cosine, sine, grads
+        )
+    grad_w_out = sum(mm(mixed[c], full_proj[c], 0, 0) for c in each).astype(bf16)
+    for_other = swap(project_back_pair(1, half, *grads, w_qkv, bf16))
+    grad_act_one = project_back_pair(0, half, *grads, w_qkv, f32) + for_other.astype(f32)
+    grad_w_qkv = [mm(rows_one, grads[t], 0, 0).astype(bf16) for t in range(3)]
+    depth, wide = w_up.shape
+    cuts = (
+        (0, 0, wide // 2), (0, wide // 2, wide // 2), (1, 0, depth // 2), (1, depth // 2, depth // 2),
+        (2, 0, w_out.shape[0]), (3, 0, depth), (4, 0, depth), (5, 0, depth),
+    )
+    reduced = reduce_over_dp((grad_w_down, grad_w_up, grad_w_out, *grad_w_qkv), cuts)
+    grad_w_down, grad_w_up, grad_w_out, *grad_w_qkv = [r.astype(f32) for r in reduced]
+    grad_w_qkv = jnp.stack(grad_w_qkv)
+
+    x_all = tokens.astype(f32)
+    _, first_back = jax.vjp(modulate, x_all, gain_one, shift_a, scale_a)
+    grad_x, grad_gain_one, grad_shift_a, grad_scale_a = first_back(grad_act_one)
+    grad_x = (grad_x + jnp.concatenate(grad_middle, axis=0)).astype(bf16)
+
+    small = jnp.concatenate(
+        [
+            grad_shift_a, grad_scale_a, grad_gate_a, grad_shift_m, grad_scale_m, grad_gate_m,
+            grad_gain_one, grad_gain_two, grad_b_down,
+        ]
+    )[None, :]
+    small = small + swap(small)
+    mod_size = modulation.shape[0]
+    grad_mod = small[0, :mod_size]
+    grad_cond = jnp.dot(w_ada.astype(f32), grad_mod, precision=lax.Precision.HIGHEST)[None, :]
+    everyone = gathered(jnp.concatenate([small, grad_b_up[None, :], cond.astype(f32)], axis=1))
+    conds = everyone[:, -cond.shape[1] :]
+    mods = everyone[:, :mod_size]
+    grad_w_ada = jnp.einsum("nc,nm->cm", conds, mods, precision=lax.Precision.HIGHEST, preferred_element_type=f32)
+    sums = jnp.sum(everyone, axis=0)
+    grad_b_ada = sums[:mod_size]
+    grad_gain_one, grad_gain_two, grad_b_down = jnp.split(sums[mod_size : mod_size + 3 * width], 3)
+    grad_b_up = sums[mod_size + 3 * width : -cond.shape[1]]
+    return (
+        output, grad_x, grad_cond, grad_w_ada, grad_b_ada, grad_gain_one, grad_w_qkv, grad_w_out, grad_gain_two,
+        grad_w_up, grad_b_up, grad_w_down, grad_b_down,
+    )
+
+
+def body_any(
+    tokens, cond, doc_lengths, w_ada, b_ada, gain_one, w_qkv, w_out, gain_two, w_up, b_up, w_down, b_down, cotangent
+):
+    tensor_size = lax.axis_size("tensor")
     own = tokens.shape[0]
     length = own * tensor_size
-    me, place = lax.axis_index("tensor"), lax.axis_index("dp")
-
-    def other(values):
-        return lax.ppermute(values, "tensor", [(0, 1), (1, 0)])
 
     def all_rows(values):
-        if pair:
-            return jnp.concatenate([values, other(values)], axis=0)
         return lax.all_gather(values, "tensor", axis=0, tiled=True)
 
     def own_sum(values):
-        if pair:
-            return values[:own] + other(values[own:].astype(bf16)).astype(f32)
         return lax.psum_scatter(values, "tensor", scatter_dimension=0, tiled=True)
 
-    def bit_of(b):
-        return (place >> b) & 1
-
-    def across(values, b):
-        return lax.ppermute(values, "dp", [(d, d ^ (1 << b)) for d in range(dp_size)])
-
     def sum_over_dp(part):
-        bits = dp_size.bit_length() - 1
-        if not cube or part.shape[0] % (16 << bits):
-            return lax.psum(part, "dp")
-        for b in range(bits):
-            half = part.shape[0] // 2
-            low, high = part[:half], part[half:]
-            first = bit_of(b) == 0
-            send = jnp.where(first, high, low).astype(bf16)
-            part = jnp.where(first, low, high) + across(send, b).astype(f32)
-        part = part.astype(bf16)
-        for b in reversed(range(bits)):
-            got = across(part, b)
-            first = bit_of(b) == 0
-            part = jnp.concatenate([jnp.where(first, part, got), jnp.where(first, got, part)], axis=0)
-        return part.astype(f32)
+        return lax.psum(part, "dp")
 
     places = jnp.arange(length, dtype=jnp.int32)
-    if pair:
-        places = (places + me * own) % length
     segment, doc_first = documents(doc_lengths[0], places)
     cosine, sine = rope_tables(places - doc_first)
     blocks = length // BLOCK
@@ -409,12 +978,13 @@
 
 
 def solution(mesh):
+    swaps = mesh.shape["tensor"] == 2 and mesh.shape["dp"] == 16
     placed = (
         P(("dp", "tensor"), None), P("dp", None), P("dp", None), P(), P(), P(), P(None, None, "tensor"),
         P("tensor", None), P(), P(None, "tensor"), P("tensor"), P("tensor", None), P(), P(("dp", "tensor"), None),
     )
     return jax.shard_map(
-        body,
+        body_pair if swaps else body_any,
         mesh=mesh,
         in_specs=placed,
         out_specs=(

time: 544 us -> 482 us (0.89)
  Pallas kernels: 87.1 us -> 263 us
  waiting for transfers between devices: 216 us -> 109 us
  matrix products: 78.4 us -> 37.5 us
  other arithmetic: 71.9 us -> 37.2 us
  blocking collectives: 28.4 us -> 0 us
  starting transfers between devices: 29.1 us -> 18.4 us
  local copies, waits for them, and re-layouts: 20.9 us -> 10.2 us
    pallas_call x3 -> x11, Pallas kernels: 87.1 us -> 263 us  [the longest x1 158 us: reduce_over_dp(): pl.pallas_call(functools.partial(reduce_kernel, cuts, len(parts)), in_spe...]
    ppermute x32 -> x4, waiting for transfers between devices: 108 us -> 10.9 us  [across(): return lax.ppermute(values, 'dp', [(d, d ^ 1 << b) for d in range(dp_size)])]
    dot_general x14 -> x16, matrix products: 78.4 us -> 37.5 us  [the longest x9 28.1 us: mm(): lax.dot_general(a, b, (((da,), (db,)), ((), ())), preferred_element_type=...]
    all_gather x1 -> x0, blocking collectives: 19.8 us -> none  [body(): lax.all_gather(jnp.concatenate([small, grad_b_up, cond[0].astype(f32)])[N...]
    add x13 -> x4, other arithmetic: 18.9 us -> 0.06 us  [the longest x1 0.04 us: body_pair(): small = small + swap(small)]
    ppermute x32 -> x4, starting transfers between devices: 17 us -> 0.84 us  [across(): return lax.ppermute(values, 'dp', [(d, d ^ 1 << b) for d in range(dp_size)])]
    convert_element_type x29 -> x8, other arithmetic: 27.4 us -> 15.1 us  [the longest x3 12.7 us: body_pair(): r.astype(f32)]
    ppermute x8 -> x16, waiting for transfers between devices: 108 us -> 98 us  [swap(): return lax.ppermute(values, 'tensor', [(0, 1), (1, 0)])]
  transfers between devices with their start and end apart: 40 -> 20, of which waited for: 22 -> 15; matrix products, arithmetic and copies ran while one was open for 26% -> 11% of each run, Pallas kernels for 8% -> 42%
where the time goes in v2:
time: 482 us; the launch traced here: 477 us
  Pallas kernels  263 us (55%)
  waiting for transfers between devices  109 us (23%)
  matrix products  37.5 us (8%)
  other arithmetic  37.2 us (8%)
  starting transfers between devices  18.4 us (4%)
  local copies, waits for them, and re-layouts  10.2 us (2%)
    pallas_call x1, Pallas kernels, reduce_over_dp(): pl.pallas_call(functools.partial(reduce_kernel, cuts, len(parts)), in_spe...  158 us
    ppermute x16, waiting for transfers between devices, swap(): return lax.ppermute(values, 'tensor', [(0, 1), (1, 0)])  98 us
    pallas_call x2, Pallas kernels, mlp_pair(): pl.pallas_call(mlp_kernel, grid=(width // tile,), in_specs=[small, small,...  38.3 us
    pallas_call x2, Pallas kernels, attend_backward_pair(): pl.pallas_call(functools.partial(backward_chunk_kernel, last), grid=(pair...  35.9 us
    dot_general x9, matrix products, mm(): lax.dot_general(a, b, (((da,), (db,)), ((), ())), preferred_element_type=...  28.1 us
    pallas_call x2, Pallas kernels, attend_forward_pair(): pl.pallas_call(forward_chunk_kernel, grid=(pairs,), in_specs=[*pair_piece...  18.6 us
    ppermute x16, starting transfers between devices, swap(): return lax.ppermute(values, 'tensor', [(0, 1), (1, 0)])  17.5 us
    convert_element_type x3, other arithmetic, body_pair(): r.astype(f32)  12.7 us
  transfers between devices with their start and end apart: 20, of which 15 were waited for; matrix products, arithmetic and copies ran while one was open for 11% of the time, Pallas kernels for 42%

profile of v2, /device:TPU:0, one launch (start us, length us, event | category | flops | bytes accessed | tf_op | source)
XLA Modules:
  0.0 477.4 jit_solution(17807951668437332278)
XLA Ops:
  0.7 1.6 convert_reduce_fusion.2
  2.3 1.6 fusion.28
  4.8 3.0 collective-permute-start.1
  8.2 1.9 multiply_sine_fusion
  10.1 0.9 pad_maximum_fusion.7
  11.0 9.7 %collective-permute-done.1.got_ref = bf16[256,1024]{1,0:T(8,128)(2,1)} collective-permute-done((bf16[256,1024]{1,0:T(8,128)(2,1)S(1)}, bf16[256,1024]{1,0:T(8,128)(2,1)}, u32[]{:S(2)}, u32[]{:S(2)}) %collective-permute-start.1) | collective-permute-done | bytes 524320 | tf_op jit(solution)/shard_map/ppermute | solution.py:760
  20.7 4.7 qkv.2
  25.4 5.6 %collective-permute-done.got_ref = bf16[256,1024]{1,0:T(8,128)(2,1)S(1)} collective-permute-done((bf16[256,1024]{1,0:T(8,128)(2,1)S(1)}, bf16[256,1024]{1,0:T(8,128)(2,1)S(1)}, u32[]{:S(2)}, u32[]{:S(2)}) %collective-permute-start) | collective-permute-done | bytes 524320 | tf_op jit(solution)/shard_map/ppermute | solution.py:760
  31.0 3.5 qkv.3
  34.7 1.1 copy-done.10
  35.9 9.3 %attend.3 = (bf16[512,512]{1,0:T(8,128)(2,1)S(1)}, f32[8,1,512]{2,1,0:T(1,128)S(1)}) custom-call(bf16[3,1024,512]{2,1,0:T(8,128)(2,1)S(1)} %get-tuple-element.51.q_ref.k_ref.v_ref, bf16[3,1024,512]{2,1,0:T(8,128)(2,1)S(1)} %get-tuple-element.51.q_ref.k_ref.v_ref, bf16[3,1024,512]{2,1,0:T(8,128)(2,1)S(1)} %get-tuple-element.51.q_ref.k_ref.v_ref, ...), custom_call_target="tpu_custom_call" | custom-call | flops 4294967296 | bytes 4194304 | tf_op jit(solution)/shard_map/attend/pallas_call | solution.py:371
  45.2 9.3 %attend.2 = (bf16[512,512]{1,0:T(8,128)(2,1)S(1)}, f32[8,1,512]{2,1,0:T(1,128)S(1)}) custom-call(bf16[3,1024,512]{2,1,0:T(8,128)(2,1)S(1)} %get-tuple-element.51.q_ref.k_ref.v_ref, bf16[3,1024,512]{2,1,0:T(8,128)(2,1)S(1)} %get-tuple-element.51.q_ref.k_ref.v_ref, bf16[3,1024,512]{2,1,0:T(8,128)(2,1)S(1)} %get-tuple-element.51.q_ref.k_ref.v_ref, ...), custom_call_target="tpu_custom_call" | custom-call | flops 4294967296 | bytes 4194304 | tf_op jit(solution)/shard_map/attend/pallas_call | solution.py:371
  55.1 1.8 collective-permute-start.6
  57.7 1.1 convert_reduce_fusion.4
  58.8 1.7 collective-permute-start.4
  61.5 8.5 %collective-permute-done.6 = bf16[256,1024]{1,0:T(8,128)(2,1)S(1)} collective-permute-done((bf16[256,1024]{1,0:T(8,128)(2,1)S(1)}, bf16[256,1024]{1,0:T(8,128)(2,1)S(1)}, u32[]{:S(2)}, u32[]{:S(2)}) %collective-permute-start.6) | collective-permute-done | bytes 524320 | tf_op jit(solution)/shard_map/ppermute | solution.py:760
  70.0 11.2 %collective-permute-done.2 = bf16[256,1024]{1,0:T(8,128)(2,1)S(1)} collective-permute-done((bf16[256,1024]{1,0:T(8,128)(2,1)S(1)}, bf16[256,1024]{1,0:T(8,128)(2,1)S(1)}, u32[]{:S(2)}, u32[]{:S(2)}) %collective-permute-start.2) | collective-permute-done | bytes 524320 | tf_op jit(solution)/shard_map/ppermute | solution.py:760
  81.2 1.7 fusion.77
  84.1 1.8 collective-permute-start.3
  86.7 5.8 %collective-permute-done.4.b_got_ref = bf16[256,1024]{1,0:T(8,128)(2,1)} collective-permute-done((bf16[256,1024]{1,0:T(8,128)(2,1)S(1)}, bf16[256,1024]{1,0:T(8,128)(2,1)}, u32[]{:S(2)}, u32[]{:S(2)}) %collective-permute-start.4) | collective-permute-done | bytes 524320 | tf_op jit(solution)/shard_map/ppermute | solution.py:760
  92.6 22.4 %collective-permute-done.3.got_ref = bf16[256,1024]{1,0:T(8,128)(2,1)S(1)} collective-permute-done((bf16[256,1024]{1,0:T(8,128)(2,1)S(1)}, bf16[256,1024]{1,0:T(8,128)(2,1)S(1)}, u32[]{:S(2)}, u32[]{:S(2)}) %collective-permute-start.3) | collective-permute-done | bytes 524320 | tf_op jit(solution)/shard_map/ppermute | solution.py:760
  115.7 19.0 %mlp.2 = (bf16[1024,1024]{1,0:T(8,128)(2,1)}, bf16[1024,2048]{1,0:T(8,128)(2,1)}, bf16[1024,2048]{1,0:T(8,128)(2,1)}, f32[256,1024]{1,0:T(8,128)}, bf16[256,1024...) custom-call(bf16[256,1024]{1,0:T(8,128)(2,1)} %copy-done.48, ...), custom_call_target="tpu_custom_call" | custom-call | flops 12884901888 | bytes 25165824 | tf_op jit(solution)/shard_map/mlp/pallas_call | solution.py:550
  134.8 19.2 %mlp.3 = (bf16[1024,1024]{1,0:T(8,128)(2,1)}, bf16[1024,2048]{1,0:T(8,128)(2,1)}, bf16[1024,2048]{1,0:T(8,128)(2,1)}, f32[256,1024]{1,0:T(8,128)}, bf16[256,1024...) custom-call(bf16[256,1024]{1,0:T(8,128)(2,1)} %copy-done.47, ...), custom_call_target="tpu_custom_call", output_to_operand_aliasing={{0}: (7, {}), {1}: (8, {}), {2}: (9, {})} | custom-call | flops 12884901888 | bytes 25165824 | tf_op jit(solution)/shard_map/mlp/pallas_call | solution.py:550
  154.1 1.8 collective-permute-start.10
  156.2 1.8 collective-permute-start.9
  158.2 9.4 %convolution_convert_fusion.1.refs_0_ = bf16[2048,1024]{1,0:T(8,128)(2,1)} fusion(bf16[1024,2048]{1,0:T(8,128)(2,1)} %get-tuple-element.75, bf16[256,1024]{1,0:T(8,128)(2,1)} %collective-permute-done.8.b_got_ref, bf16[256,1024]{1,0:T(8,128)(2,1)} %get-tuple-element.132.b_own_ref, bf16[256,1024]{1,0:T(8,128)(2,1)} %collective-permute-done.4.b_got_ref, ...), kind=kOutput, calls=%fused_computation.1 | convolution fusion | flops 4305453056 | bytes 10485760 | tf_op jit(solution)/shard_map/dot_general | solution.py:62
  167.6 1.7 collective-permute-done.10
  169.2 11.2 %collective-permute-done.12 = bf16[256,1024]{1,0:T(8,128)(2,1)S(1)} collective-permute-done((bf16[256,1024]{1,0:T(8,128)(2,1)}, bf16[256,1024]{1,0:T(8,128)(2,1)S(1)}, u32[]{:S(2)}, u32[]{:S(2)}) %collective-permute-start.12) | collective-permute-done | bytes 524320 | tf_op jit(solution)/shard_map/ppermute | solution.py:760
  180.4 1.3 multiply_reduce_fusion.1
  182.3 9.4 %collective-permute-done.9 = bf16[256,1024]{1,0:T(8,128)(2,1)S(1)} collective-permute-done((bf16[256,1024]{1,0:T(8,128)(2,1)}, bf16[256,1024]{1,0:T(8,128)(2,1)S(1)}, u32[]{:S(2)}, u32[]{:S(2)}) %collective-permute-start.9) | collective-permute-done | bytes 524320 | tf_op jit(solution)/shard_map/ppermute | solution.py:760
  191.7 6.8 %collective-permute-done.5 = bf16[256,1024]{1,0:T(8,128)(2,1)S(1)} collective-permute-done((bf16[256,1024]{1,0:T(8,128)(2,1)}, bf16[256,1024]{1,0:T(8,128)(2,1)S(1)}, u32[]{:S(2)}, u32[]{:S(2)}) %collective-permute-start.5) | collective-permute-done | bytes 524320 | tf_op jit(solution)/shard_map/ppermute | solution.py:760
  198.6 1.1 fusion.36
  201.1 0.9 copy-done.26
  202.3 1.1 collective-permute-start.13
  204.2 6.3 %convolution_convert_fusion.refs_1_ = bf16[1024,2048]{1,0:T(8,128)(2,1)} fusion(bf16[1024,1024]{1,0:T(8,128)(2,1)S(1)} %copy-done.59, bf16[1024,2048]{1,0:T(8,128)(2,1)S(1)} %copy-done.58), kind=kOutput, calls=%fused_computation | convolution fusion | flops 4297064448 | bytes 10485760 | tf_op jit(solution)/shard_map/dot_general | solution.py:62
  210.5 1.1 collective-permute-start.11
  211.6 1.0 pad_maximum_fusion
  212.6 2.2 collective-permute-done.13
  215.7 1.5 convolution_convert_fusion.7.g_ref
  217.2 17.8 %attend_back.2 = (bf16[1024,512]{1,0:T(8,128)(2,1)}, f32[1024,512]{1,0:T(8,128)}, f32[1024,512]{1,0:T(8,128)}) custom-call(bf16[3,1024,512]{2,1,0:T(8,128)(2,1)} %copy-done.7, bf16[3,1024,512]{2,1,0:T(8,128)(2,1)} %copy-done.7, bf16[3,1024,512]{2,1,0:T(8,128)(2,1)} %copy-done.7, bf16[512,512]{1,0:T(8,128)(2,1)} %convolution_convert_fusion.7.g_ref, ...), custom_call_target="tpu_custom_call" | custom-call | flops 10737418240 | bytes 8388608 | tf_op jit(solution)/shard_map/attend_back/pallas_call | solution.py:454
  235.1 2.6 convolution_convert_fusion.8.g_ref
  237.7 18.1 %attend_back.3 = (bf16[1024,512]{1,0:T(8,128)(2,1)}, bf16[1024,512]{1,0:T(8,128)(2,1)}, bf16[1024,512]{1,0:T(8,128)(2,1)}) custom-call(bf16[3,1024,512]{2,1,0:T(8,128)(2,1)} %copy-done.7, bf16[3,1024,512]{2,1,0:T(8,128)(2,1)} %copy-done.7, bf16[3,1024,512]{2,1,0:T(8,128)(2,1)} %copy-done.7, ...), custom_call_target="tpu_custom_call", output_to_operand_aliasing={{0}: (14, {})} | custom-call | flops 10737418240 | bytes 8388608 | tf_op jit(solution)/shard_map/attend_back/pallas_call | solution.py:454
  255.8 3.3 convolution_convert_fusion.2.refs_5_
  259.1 1.3 convolution_convert_fusion.3.refs_4_
  260.7 2.0 qkv_back.3
  262.7 1.1 collective-permute-start.14
  263.8 1.8 fusion.37
  266.3 1.3 convolution_convert_fusion.4.refs_3_
  267.6 158.3 %reduce.8 = (bf16[2048,1024]{1,0:T(8,128)(2,1)S(1)}, bf16[1024,2048]{1,0:T(8,128)(2,1)}, bf16[512,1024]{1,0:T(8,128)(2,1)S(1)}, bf16[1024,512]{1,0:T(8,128)(2,1)...) custom-call(bf16[2048,1024]{1,0:T(8,128)(2,1)} %convolution_convert_fusion.1.refs_0_, ...), custom_call_target="tpu_custom_call" | custom-call | tf_op jit(solution)/shard_map/reduce/pallas_call | solution.py:737
  425.9 6.7 %convert_element_type.168 = f32[1024,2048]{1,0:T(8,128)} convert(bf16[1024,2048]{1,0:T(8,128)(2,1)} %get-tuple-element.83) | non-fusion elementwise | flops 2097152 | bytes 12582912 | tf_op jit(solution)/shard_map/convert_element_type | solution.py:848
  432.6 4.4 convert_element_type.169
  437.0 1.6 convert_element_type.167
  438.6 2.0 qkv_back.2
  440.6 3.2 maximum_convert_fusion
  443.8 2.5 fusion.8
  447.0 3.4 collective-permute-done.15
  450.6 2.3 fusion.74
  452.9 2.7 collective-permute-done.16
  455.7 4.5 collective-permute-done.17
  461.0 1.2 fusion.11
  462.2 3.7 collective-permute-done.18
  466.2 1.8 fusion.46
  470.4 2.5 concatenate.53
  472.9 4.3 fusion.38
  (196 shorter events, 15.9 us)
Async XLA Ops:
  0.6 3.3 copy-start
  0.7 3.6 copy-start.18
  0.7 3.3 copy-start.55
  0.7 3.6 copy-start.51
  0.7 3.6 copy-start.50
  3.9 4.1 copy-start.57
  4.8 15.9 %collective-permute-start.1 = (bf16[256,1024]{1,0:T(8,128)(2,1)S(1)}, bf16[256,1024]{1,0:T(8,128)(2,1)}, u32[]{:S(2)}, u32[]{:S(2)}) collective-permute-start(bf16[256,1024]{1,0:T(8,128)(2,1)S(1)} %get-tuple-element.129.own_ref), channel_id=1, source_target_pairs={{0,1},{1,0},{2,3},{3,2},{4,5},{5,4},{6,7},{7,6},{8,9},{9,8},{10,11... | collective-permute-start | bytes 1572872 | tf_op jit(solution)/shard_map/ppermute | solution.py:760
  7.8 23.2 %collective-permute-start = (bf16[256,1024]{1,0:T(8,128)(2,1)S(1)}, bf16[256,1024]{1,0:T(8,128)(2,1)S(1)}, u32[]{:S(2)}, u32[]{:S(2)}) collective-permute-start(bf16[256,1024]{1,0:T(8,128)(2,1)S(1)} %get-tuple-element.130.own_ref), channel_id=1, source_target_pairs={{0,1},{1,0},{2,3},{3,2},{4,5},{5,4},{6,7},{7,6},{8,9},{9,8},{10,11... | collective-permute-start | bytes 1572872 | tf_op jit(solution)/shard_map/ppermute | solution.py:760
  7.9 12.8 %copy-start.1 = (bf16[3,1024,512]{2,1,0:T(8,128)(2,1)S(1)}, bf16[3,1024,512]{2,1,0:T(8,128)(2,1)}, u32[]{:S(2)}) copy-start(bf16[3,1024,512]{2,1,0:T(8,128)(2,1)} %w_ref.7) | copy-start | bytes 9437188
  8.2 37.0 %copy-start.15 = (s32[1024]{0:T(1024)}, s32[1024]{0:T(1024)S(1)}, u32[]{:S(2)}) copy-start(s32[1024]{0:T(1024)S(1)} %get-tuple-element.107) | copy-start | bytes 12292
  11.0 20.0 %copy-start.12 = (f32[1024,128]{1,0:T(8,128)}, f32[1024,128]{1,0:T(8,128)S(1)}, u32[]{:S(2)}) copy-start(f32[1024,128]{1,0:T(8,128)S(1)} %get-tuple-element.157.cos_ref.cos_all) | copy-start | bytes 1572868
  11.0 20.0 %copy-start.13 = (f32[1024,128]{1,0:T(8,128)}, f32[1024,128]{1,0:T(8,128)S(1)}, u32[]{:S(2)}) copy-start(f32[1024,128]{1,0:T(8,128)S(1)} %get-tuple-element.158.sin_ref.sin_all) | copy-start | bytes 1572868
  34.5 10.6 %copy-start.7 = (bf16[3,1024,512]{2,1,0:T(8,128)(2,1)}, bf16[3,1024,512]{2,1,0:T(8,128)(2,1)S(1)}, u32[]{:S(2)}) copy-start(bf16[3,1024,512]{2,1,0:T(8,128)(2,1)S(1)} %get-tuple-element.51.q_ref.k_ref.v_ref) | copy-start | bytes 9437188
  35.9 9.3 %copy-start.14 = (s32[1024,128]{1,0:T(8,128)}, s32[1024,128]{1,0:T(8,128)S(1)}, u32[]{:S(2)}) copy-start(s32[1024,128]{1,0:T(8,128)S(1)} %broadcast_in_dim.33.segc_ref) | copy-start | bytes 1572868
  45.2 9.3 %copy-start.16 = (f32[8,1,512]{2,1,0:T(1,128)}, f32[8,1,512]{2,1,0:T(1,128)S(1)}, u32[]{:S(2)}) copy-start(f32[8,1,512]{2,1,0:T(1,128)S(1)} %get-tuple-element.63.lse_ref) | copy-start | bytes 49156
  45.2 15.8 %copy-start.5 = (bf16[512,512]{1,0:T(8,128)(2,1)}, bf16[512,512]{1,0:T(8,128)(2,1)S(1)}, u32[]{:S(2)}) copy-start(bf16[512,512]{1,0:T(8,128)(2,1)S(1)} %get-tuple-element.55.o_ref) | copy-start | bytes 1572868
  45.2 9.4 %copy-start.22 = (bf16[512,1024]{1,0:T(8,128)(2,1)S(1)}, bf16[512,1024]{1,0:T(8,128)(2,1)}, u32[]{:S(2)}) copy-start(bf16[512,1024]{1,0:T(8,128)(2,1)} %param.21) | copy-start | bytes 3145732
  54.6 4.2 copy-start.17
  54.6 26.7 %copy-start.8 = (bf16[512,512]{1,0:T(8,128)(2,1)}, bf16[512,512]{1,0:T(8,128)(2,1)S(1)}, u32[]{:S(2)}) copy-start(bf16[512,512]{1,0:T(8,128)(2,1)S(1)} %get-tuple-element.52.o_ref) | copy-start | bytes 1572868
  54.6 3.1 copy-start.30
  55.0 5.7 %copy-start.19 = (bf16[512,1024]{1,0:T(8,128)(2,1)S(1)}, bf16[512,1024]{1,0:T(8,128)(2,1)}, u32[]{:S(2)}) copy-start(bf16[512,1024]{1,0:T(8,128)(2,1)} %param.14) | copy-start | bytes 3145732
  55.1 14.9 %collective-permute-start.6 = (bf16[256,1024]{1,0:T(8,128)(2,1)S(1)}, bf16[256,1024]{1,0:T(8,128)(2,1)S(1)}, u32[]{:S(2)}, u32[]{:S(2)}) collective-permute-start(bf16[256,1024]{1,0:T(8,128)(2,1)S(1)} %convolution_convert_fusion.5), channel_id=1, source_target_pairs={{0,1},{1,0},{2,3},{3,2},{4,5},{5,4},{6,7},{7,6},{8,9},{9,8},{10,11... | collective-permute-start | bytes 1572872 | tf_op jit(solution)/shard_map/ppermute | solution.py:760
  57.3 23.9 %collective-permute-start.2 = (bf16[256,1024]{1,0:T(8,128)(2,1)S(1)}, bf16[256,1024]{1,0:T(8,128)(2,1)S(1)}, u32[]{:S(2)}, u32[]{:S(2)}) collective-permute-start(bf16[256,1024]{1,0:T(8,128)(2,1)S(1)} %convolution_convert_fusion.6), channel_id=1, source_target_pairs={{0,1},{1,0},{2,3},{3,2},{4,5},{5,4},{6,7},{7,6},{8,9},{9,8},{10,11... | collective-permute-start | bytes 1572872 | tf_op jit(solution)/shard_map/ppermute | solution.py:760
  58.8 24.1 %copy-start.45 = (bf16[256,1024]{1,0:T(8,128)(2,1)}, bf16[256,1024]{1,0:T(8,128)(2,1)S(1)}, u32[]{:S(2)}) copy-start(bf16[256,1024]{1,0:T(8,128)(2,1)S(1)} %get-tuple-element.112.b_own_ref) | copy-start | bytes 1572868
  58.8 33.8 %collective-permute-start.4 = (bf16[256,1024]{1,0:T(8,128)(2,1)S(1)}, bf16[256,1024]{1,0:T(8,128)(2,1)}, u32[]{:S(2)}, u32[]{:S(2)}) collective-permute-start(bf16[256,1024]{1,0:T(8,128)(2,1)S(1)} %get-tuple-element.112.b_own_ref), channel_id=1, source_target_pairs={{0,1},{1,0},{2,3},{3,2},{4,5},{5,4},{6,7},{7,6},{8,9},{9,8},{10,11... | collective-permute-start | bytes 1572872 | tf_op jit(solution)/shard_map/ppermute | solution.py:760
  60.5 74.3 %collective-permute-start.8 = (bf16[256,1024]{1,0:T(8,128)(2,1)}, bf16[256,1024]{1,0:T(8,128)(2,1)}, u32[]{:S(2)}, u32[]{:S(2)}) collective-permute-start(bf16[256,1024]{1,0:T(8,128)(2,1)} %get-tuple-element.132.b_own_ref), channel_id=1, source_target_pairs={{0,1},{1,0},{2,3},{3,2},{4,5},{5,4},{6,7},{7,6},{8,9},{9,8},{10,11... | collective-permute-start | bytes 1572872 | tf_op jit(solution)/shard_map/ppermute | solution.py:760
  61.4 21.4 %copy-start.28 = (f32[256,1024]{1,0:T(8,128)}, f32[256,1024]{1,0:T(8,128)S(1)}, u32[]{:S(2)}) copy-start(f32[256,1024]{1,0:T(8,128)S(1)} %fusion.41) | copy-start | bytes 3145732
  70.0 12.9 %copy-start.37 = (bf16[256,1024]{1,0:T(8,128)(2,1)}, bf16[256,1024]{1,0:T(8,128)(2,1)S(1)}, u32[]{:S(2)}) copy-start(bf16[256,1024]{1,0:T(8,128)(2,1)S(1)} %collective-permute-done.6) | copy-start | bytes 1572868
  84.1 31.6 %copy-start.48 = (bf16[256,1024]{1,0:T(8,128)(2,1)}, bf16[256,1024]{1,0:T(8,128)(2,1)S(1)}, u32[]{:S(2)}) copy-start(bf16[256,1024]{1,0:T(8,128)(2,1)S(1)} %get-tuple-element.148.own_ref) | copy-start | bytes 1572868
  84.1 50.6 %copy-start.47 = (bf16[256,1024]{1,0:T(8,128)(2,1)}, bf16[256,1024]{1,0:T(8,128)(2,1)S(1)}, u32[]{:S(2)}) copy-start(bf16[256,1024]{1,0:T(8,128)(2,1)S(1)} %get-tuple-element.149.own_ref) | copy-start | bytes 1572868
  84.1 30.8 %collective-permute-start.3 = (bf16[256,1024]{1,0:T(8,128)(2,1)S(1)}, bf16[256,1024]{1,0:T(8,128)(2,1)S(1)}, u32[]{:S(2)}, u32[]{:S(2)}) collective-permute-start(bf16[256,1024]{1,0:T(8,128)(2,1)S(1)} %get-tuple-element.148.own_ref), channel_id=1, source_target_pairs={{0,1},{1,0},{2,3},{3,2},{4,5},{5,4},{6,7},{7,6},{8,9},{9,8},{10,11... | collective-permute-start | bytes 1572872 | tf_op jit(solution)/shard_map/ppermute | solution.py:760
  86.4 48.4 %collective-permute-start.7 = (bf16[256,1024]{1,0:T(8,128)(2,1)S(1)}, bf16[256,1024]{1,0:T(8,128)(2,1)}, u32[]{:S(2)}, u32[]{:S(2)}) collective-permute-start(bf16[256,1024]{1,0:T(8,128)(2,1)S(1)} %get-tuple-element.149.own_ref), channel_id=1, source_target_pairs={{0,1},{1,0},{2,3},{3,2},{4,5},{5,4},{6,7},{7,6},{8,9},{9,8},{10,11... | collective-permute-start | bytes 1572872 | tf_op jit(solution)/shard_map/ppermute | solution.py:760
  134.8 23.4 %copy-start.46 = (bf16[256,1024]{1,0:T(8,128)(2,1)S(1)}, bf16[256,1024]{1,0:T(8,128)(2,1)}, u32[]{:S(2)}) copy-start(bf16[256,1024]{1,0:T(8,128)(2,1)} %copy-done.45) | copy-start | bytes 1572868
  154.1 15.1 %collective-permute-start.10 = (bf16[256,1024]{1,0:T(8,128)(2,1)}, bf16[256,1024]{1,0:T(8,128)(2,1)S(1)}, u32[]{:S(2)}, u32[]{:S(2)}) collective-permute-start(bf16[256,1024]{1,0:T(8,128)(2,1)} %get-tuple-element.62), channel_id=1, source_target_pairs={{0,1},{1,0},{2,3},{3,2},{4,5},{5,4},{6,7},{7,6},{8,9},{9,8},{10,11... | collective-permute-start | bytes 1572872 | tf_op jit(solution)/shard_map/ppermute | solution.py:760
  155.9 24.6 %collective-permute-start.12 = (bf16[256,1024]{1,0:T(8,128)(2,1)}, bf16[256,1024]{1,0:T(8,128)(2,1)S(1)}, u32[]{:S(2)}, u32[]{:S(2)}) collective-permute-start(bf16[256,1024]{1,0:T(8,128)(2,1)} %get-tuple-element.65), channel_id=1, source_target_pairs={{0,1},{1,0},{2,3},{3,2},{4,5},{5,4},{6,7},{7,6},{8,9},{9,8},{10,11... | collective-permute-start | bytes 1572872 | tf_op jit(solution)/shard_map/ppermute | solution.py:760
  156.2 35.5 %collective-permute-start.9 = (bf16[256,1024]{1,0:T(8,128)(2,1)}, bf16[256,1024]{1,0:T(8,128)(2,1)S(1)}, u32[]{:S(2)}, u32[]{:S(2)}) collective-permute-start(bf16[256,1024]{1,0:T(8,128)(2,1)} %get-tuple-element.60), channel_id=1, source_target_pairs={{0,1},{1,0},{2,3},{3,2},{4,5},{5,4},{6,7},{7,6},{8,9},{9,8},{10,11... | collective-permute-start | bytes 1572872 | tf_op jit(solution)/shard_map/ppermute | solution.py:760
  157.9 40.6 %collective-permute-start.5 = (bf16[256,1024]{1,0:T(8,128)(2,1)}, bf16[256,1024]{1,0:T(8,128)(2,1)S(1)}, u32[]{:S(2)}, u32[]{:S(2)}) collective-permute-start(bf16[256,1024]{1,0:T(8,128)(2,1)} %get-tuple-element.54), channel_id=1, source_target_pairs={{0,1},{1,0},{2,3},{3,2},{4,5},{5,4},{6,7},{7,6},{8,9},{9,8},{10,11... | collective-permute-start | bytes 1572872 | tf_op jit(solution)/shard_map/ppermute | solution.py:760
  158.2 22.3 %copy-start.21 = (f32[256,1024]{1,0:T(8,128)S(1)}, f32[256,1024]{1,0:T(8,128)}, u32[]{:S(2)}) copy-start(f32[256,1024]{1,0:T(8,128)} %copy-done.20) | copy-start | bytes 3145732
  158.2 22.3 %copy-start.33 = (f32[256,1024]{1,0:T(8,128)S(1)}, f32[256,1024]{1,0:T(8,128)}, u32[]{:S(2)}) copy-start(f32[256,1024]{1,0:T(8,128)} %get-tuple-element.64) | copy-start | bytes 3145732
  158.2 22.3 %copy-start.34 = (f32[256,1024]{1,0:T(8,128)S(1)}, f32[256,1024]{1,0:T(8,128)}, u32[]{:S(2)}) copy-start(f32[256,1024]{1,0:T(8,128)} %get-tuple-element.61) | copy-start | bytes 3145732
  181.7 16.8 %copy-start.31 = (bf16[512,1024]{1,0:T(8,128)(2,1)S(1)}, bf16[512,1024]{1,0:T(8,128)(2,1)}, u32[]{:S(2)}) copy-start(bf16[512,1024]{1,0:T(8,128)(2,1)} %param.27) | copy-start | bytes 3145732
  181.7 16.8 %copy-start.41 = (f32[256,1024]{1,0:T(8,128)S(1)}, f32[256,1024]{1,0:T(8,128)}, u32[]{:S(2)}) copy-start(f32[256,1024]{1,0:T(8,128)} %get-tuple-element.53) | copy-start | bytes 3145732
  181.7 16.8 %copy-start.42 = (f32[256,1024]{1,0:T(8,128)S(1)}, f32[256,1024]{1,0:T(8,128)}, u32[]{:S(2)}) copy-start(f32[256,1024]{1,0:T(8,128)} %get-tuple-element.59) | copy-start | bytes 3145732
  181.8 16.8 %copy-start.54 = (f32[1024]{0:T(1024)S(1)}, f32[1024]{0:T(1024)}, u32[]{:S(2)}) copy-start(f32[1024]{0:T(1024)} %param.26) | copy-start | bytes 12292
  200.4 3.1 copy-start.58
  201.1 3.1 copy-start.59
  202.3 32.8 %copy-start.35 = (bf16[256,1024]{1,0:T(8,128)(2,1)}, bf16[256,1024]{1,0:T(8,128)(2,1)S(1)}, u32[]{:S(2)}) copy-start(bf16[256,1024]{1,0:T(8,128)(2,1)S(1)} %get-tuple-element.153) | copy-start | bytes 1572868
  202.3 12.6 %collective-permute-start.13 = (bf16[256,1024]{1,0:T(8,128)(2,1)S(1)}, bf16[256,1024]{1,0:T(8,128)(2,1)S(1)}, u32[]{:S(2)}, u32[]{:S(2)}) collective-permute-start(bf16[256,1024]{1,0:T(8,128)(2,1)S(1)} %get-tuple-element.152), channel_id=1, source_target_pairs={{0,1},{1,0},{2,3},{3,2},{4,5},{5,4},{6,7},{7,6},{8,9},{9,8},{10,11... | collective-permute-start | bytes 1572872 | tf_op jit(solution)/shard_map/ppermute | solution.py:760
  204.2 6.3 %copy-start.52 = (f32[1,2048]{1,0:T(1,128)S(1)}, f32[1,2048]{1,0:T(1,128)}, u32[]{:S(2)}) copy-start(f32[1,2048]{1,0:T(1,128)} %get-tuple-element.73) | copy-start | bytes 24580
  204.2 6.3 %copy-start.53 = (f32[1,2048]{1,0:T(1,128)S(1)}, f32[1,2048]{1,0:T(1,128)}, u32[]{:S(2)}) copy-start(f32[1,2048]{1,0:T(1,128)} %get-tuple-element.74) | copy-start | bytes 24580
  210.4 5.3 %copy-start.23 = (bf16[512,1024]{1,0:T(8,128)(2,1)S(1)}, bf16[512,1024]{1,0:T(8,128)(2,1)}, u32[]{:S(2)}) copy-start(bf16[512,1024]{1,0:T(8,128)(2,1)} %param.21) | copy-start | bytes 3145732
  210.5 24.6 %collective-permute-start.11 = (bf16[256,1024]{1,0:T(8,128)(2,1)S(1)}, bf16[256,1024]{1,0:T(8,128)(2,1)}, u32[]{:S(2)}, u32[]{:S(2)}) collective-permute-start(bf16[256,1024]{1,0:T(8,128)(2,1)S(1)} %get-tuple-element.153), channel_id=1, source_target_pairs={{0,1},{1,0},{2,3},{3,2},{4,5},{5,4},{6,7},{7,6},{8,9},{9,8},{10,11... | collective-permute-start | bytes 1572872 | tf_op jit(solution)/shard_map/ppermute | solution.py:760
  255.8 3.3 copy-start.2
  255.8 3.3 copy-start.11
  260.7 3.2 copy-start.6
  260.7 3.2 copy-start.36
  262.7 181.1 %collective-permute-start.14 = (bf16[512,1024]{1,0:T(8,128)(2,1)S(1)}, bf16[512,1024]{1,0:T(8,128)(2,1)}, u32[]{:S(2)}, u32[]{:S(2)}) collective-permute-start(bf16[512,1024]{1,0:T(8,128)(2,1)S(1)} %qkv_back.3), channel_id=1, source_target_pairs={{0,1},{1,0},{2,3},{3,2},{4,5},{5,4},{6,7},{7,6},{8,9},{9,8},{10,11... | collective-permute-start | bytes 3145736 | tf_op jit(solution)/shard_map/ppermute | solution.py:760
  446.4 4.0 collective-permute-start.15
  450.5 10.5 %copy-start.25 = (f32[256,1024]{1,0:T(8,128)S(1)}, f32[256,1024]{1,0:T(8,128)}, u32[]{:S(2)}) copy-start(f32[256,1024]{1,0:T(8,128)} %copy-done.24) | copy-start | bytes 3145732
  450.5 10.5 %copy-start.27 = (f32[256,1024]{1,0:T(8,128)S(1)}, f32[256,1024]{1,0:T(8,128)}, u32[]{:S(2)}) copy-start(f32[256,1024]{1,0:T(8,128)} %copy-done.26) | copy-start | bytes 3145732
  450.5 5.0 %collective-permute-start.16 = (f32[1,11392]{1,0:T(1,128)S(1)}, f32[1,11392]{1,0:T(1,128)S(1)}, u32[]{:S(2)}, u32[]{:S(2)}) collective-permute-start(f32[1,11392]{1,0:T(1,128)S(1)} %pad_maximum_fusion.12), channel_id=1, source_target_pairs={{0,16},{2,18},{4,20},{6,22},{8,24},{10,26},{12,28},{14,30},{16,0},... | collective-permute-start | bytes 136712 | tf_op jit(solution)/shard_map/ppermute | solution.py:763
  455.7 4.6 collective-permute-start.17
  460.4 5.6 %collective-permute-start.18 = (f32[4,11392]{1,0:T(4,128)S(1)}, f32[4,11392]{1,0:T(4,128)S(1)}, u32[]{:S(2)}, u32[]{:S(2)}) collective-permute-start(f32[4,11392]{1,0:T(4,128)S(1)} %pad_maximum_fusion.10), channel_id=1, source_target_pairs={{0,4},{2,6},{4,0},{6,2},{8,12},{10,14},{12,8},{14,10},{16,20},{18,... | collective-permute-start | bytes 546824 | tf_op jit(solution)/shard_map/ppermute | solution.py:763
  466.1 2.3 collective-permute-start.19
  (16 other events, 24.7 us)

commit v3 on v2

--- a/solution.py
+++ b/solution.py
@@ -395,104 +395,8 @@
     )(qkv, qkv, qkv, seg_rows, seg_cols)
 
 
-def backward_chunk_kernel(
-    last, q_ref, k_ref, v_ref, g_ref, o_ref, lse_ref, segr_ref, segc_ref, cos_ref, sin_ref, cos_all, sin_all, *refs
-):
-    if last:
-        dk_in, dv_in, _, dq_ref, dk_ref, dv_ref, kt, dk, dv = refs
-        dk[...] = dk_in[...]
-        dv[...] = dv_in[...]
-    else:
-        dq_ref, dk, dv, kt = refs
-        dk[...] = jnp.zeros(dk.shape, f32)
-        dv[...] = jnp.zeros(dv.shape, f32)
-    length, count = k_ref.shape[0], q_ref.shape[0]
-    for b in range(0, length, BLOCK):
-        kt[:, b : b + BLOCK] = transposed(k_ref[b : b + BLOCK, :]).astype(bf16)
-    q, g = q_ref[...], g_ref[...]
-    both = (g.astype(f32) * o_ref[...].astype(f32)).T
-    qh = [head_lanes(q, h) for h in range(2)]
-    gh = [head_lanes(g, h) for h in range(2)]
-    delta = [jnp.sum(both[h * HEAD : (h + 1) * HEAD, :], axis=0, keepdims=True) for h in range(2)]
-    q_two, g_two = jnp.concatenate(qh, axis=0), jnp.concatenate(gh, axis=0)
-    dq = [0.0, 0.0]
-    for b in range(0, length, BLOCK):
-        cols = slice(b, b + BLOCK)
-        k, v = k_ref[cols, :], v_ref[cols, :]
-        same = jnp.concatenate([segc_ref[cols, :]] * (count // 128), axis=1) == segr_ref[...]
-        ps, ds = [], []
-        for h in range(2):
-            s = jnp.where(same, mm(k, qh[h], 1, 1), masked_score)
-            p = jnp.exp(s - lse_ref[h])
-            d = (p * (mm(v, gh[h], 1, 1) - delta[h])).astype(bf16)
-            ps.append(p.astype(bf16))
-            ds.append(d)
-            dq[h] = dq[h] + mm(kt[h * HEAD : (h + 1) * HEAD, cols], d, 1, 0)
-        dv[cols, :] += mm(jnp.concatenate(ps, axis=1), g_two, 1, 0)
-        dk[cols, :] += mm(jnp.concatenate(ds, axis=1), q_two, 1, 0)
-
-    def turn_back(u, cosine, sine):
-        return (u * cosine - turned(u) * sine).astype(bf16)
-
-    dq_ref[...] = turn_back(jnp.concatenate(dq, axis=0).T * (HEAD**-0.5), cos_ref[...], sin_ref[...])
-    if last:
-        for b in range(0, length, BLOCK):
-            rows = slice(b, b + BLOCK)
-            dk_ref[rows, :] = turn_back(dk[rows, :], cos_all[rows, :], sin_all[rows, :])
-            dv_ref[rows, :] = dv[rows, :].astype(bf16)
-
-
-def attend_backward_pair(j, chunk, qkv, grad, mixed, lse, seg_rows, seg_cols, cosine, sine, before):
-    _, length, width = qkv.shape
-    pairs = width // PAIR
-    last = bool(before)
-    whole = pl.BlockSpec((length, PAIR), lambda p: (0, p))
-    part = pl.BlockSpec((chunk, PAIR), lambda p: (0, p))
-    table = pl.BlockSpec((chunk, PAIR), lambda p: (j, 0))
-    table_all = pl.BlockSpec((length, PAIR), lambda p: (0, 0))
-    dq_before = before[:1]
-    return pl.pallas_call(
-        functools.partial(backward_chunk_kernel, last),
-        grid=(pairs,),
-        in_specs=[
-            *pair_pieces(j, length, chunk),
-            part,
-            part,
-            pl.BlockSpec((2, 1, chunk), lambda p: (p, 0, 0)),
-            pl.BlockSpec((1, chunk), lambda p: (0, j)),
-            table_all,
-            table,
-            table,
-            table_all,
-            table_all,
-            *([whole, whole, pl.BlockSpec(memory_space=pl.ANY)] if last else []),
-        ],
-        out_specs=[pl.BlockSpec((chunk, PAIR), lambda p: (j, p)), whole, whole],
-        out_shape=[
-            jax.ShapeDtypeStruct((length, width), bf16),
-            jax.ShapeDtypeStruct((length, width), bf16 if last else f32),
-            jax.ShapeDtypeStruct((length, width), bf16 if last else f32),
-        ],
-        scratch_shapes=[
-            pltpu.VMEM((PAIR, length), bf16),
-            *([pltpu.VMEM((length, PAIR), f32)] * 2 if last else []),
-        ],
-        input_output_aliases={14: 0} if last else {},
-        compiler_params=pltpu.CompilerParams(vmem_limit_bytes=56 << 20),
-        cost_estimate=pl.CostEstimate(
-            flops=40 * chunk * length * width,
-            bytes_accessed=16 * length * width,
-            transcendentals=chunk * length * width // HEAD,
-        ),
-        name="attend_back",
-    )(
-        qkv, qkv, qkv, grad, mixed, lse, seg_rows, seg_cols, cosine, sine, cosine, sine,
-        *((*before[1:], *dq_before) if last else ()),
-    )
-
-
 def mlp_kernel(own_ref, got_ref, b_own_ref, b_got_ref, up_ref, bias_ref, down_ref, *refs):
-    rows_ref, hidden_ref, pre_ref, own_grad, got_grad, own_branch, got_branch, bias_grad, grads, branch = refs[-10:]
+    rows_ref, hidden_ref, pre_ref, own_grad, got_grad, own_branch, got_branch, bias_grad, back, grads, branch = refs[-11:]
     tile, tiles = pl.program_id(0), pl.num_programs(0)
     half = own_ref.shape[0]
 
@@ -500,38 +404,31 @@
     def _():
         rows_ref[:half, :] = own_ref[...]
         rows_ref[half:, :] = got_ref[...]
-
-    up, down = up_ref[...], down_ref[...]
+        back[:half, :] = b_own_ref[...]
+        back[half:, :] = b_got_ref[...]
+
     cubic, root = 0.044715, (2.0 / jnp.pi) ** 0.5
-    for part in range(2):
-        rows = slice(part * half, (part + 1) * half)
-        back = (b_own_ref, b_got_ref)[part]
-        u = mm((own_ref, got_ref)[part][...], up, 1, 0) + bias_ref[...]
-        square = u * u
-        t = jnp.tanh(root * u * (1.0 + cubic * square))
-        hidden = (0.5 * u * (1.0 + t)).astype(bf16)
-        slope = 0.5 * (1.0 + t) + 0.5 * u * (1.0 - t * t) * (root * (1.0 + 3.0 * cubic * square))
-        grad = mm(back[...], down, 1, 1) * slope
-        grad_low = grad.astype(bf16)
-        hidden_ref[rows, :] = hidden
-        pre_ref[rows, :] = grad_low
-        total = jnp.sum(grad_low.astype(f32), axis=0, keepdims=True)
-        more, more_branch = mm(grad_low, up, 1, 1), mm(hidden, down, 1, 0)
-
-        @pl.when(tile == 0)
-        def _():
-            grads[rows, :] = more
-            branch[rows, :] = more_branch
-
-        @pl.when(tile > 0)
-        def _():
-            grads[rows, :] += more
-            branch[rows, :] += more_branch
-
-        if part == 0:
-            bias_grad[...] = total
-        else:
-            bias_grad[...] += total
+    u = mm(rows_ref[...], up_ref[...], 1, 0) + bias_ref[...]
+    square = u * u
+    t = jnp.tanh(u * (root + (root * cubic) * square))
+    rising = 0.5 * (1.0 + t)
+    hidden = (u * rising).astype(bf16)
+    slope = rising + (0.5 * u) * (1.0 - t * t) * (root + (3.0 * cubic * root) * square)
+    grad = (mm(back[...], down_ref[...], 1, 1) * slope).astype(bf16)
+    hidden_ref[...] = hidden
+    pre_ref[...] = grad
+    bias_grad[...] = jnp.sum(grad.astype(f32), axis=0, keepdims=True)
+    more, more_branch = mm(grad, up_ref[...], 1, 1), mm(hidden, down_ref[...], 1, 0)
+
+    @pl.when(tile == 0)
+    def _():
+        grads[...] = more
+        branch[...] = more_branch
+
+    @pl.when(tile > 0)
+    def _():
+        grads[...] += more
+        branch[...] += more_branch
 
     @pl.when(tile == tiles - 1)
     def _():
@@ -544,7 +441,7 @@
 def mlp_pair(j, own, got, back_own, back_got, w_up, b_up, w_down, before, length):
     half, depth = own.shape
     width = w_up.shape[1]
-    chunk, tile = 2 * half, 512
+    chunk, tile = 2 * half, min(width, 1024)
     small = pl.BlockSpec((half, depth), lambda t: (0, 0))
     wide = pl.BlockSpec((chunk, tile), lambda t: (j, t))
     return pl.pallas_call(
@@ -572,7 +469,11 @@
             jax.ShapeDtypeStruct((half, depth), bf16),
             jax.ShapeDtypeStruct((1, width), f32),
         ],
-        scratch_shapes=[pltpu.VMEM((chunk, depth), f32), pltpu.VMEM((chunk, depth), f32)],
+        scratch_shapes=[
+            pltpu.VMEM((chunk, depth), bf16),
+            pltpu.VMEM((chunk, depth), f32),
+            pltpu.VMEM((chunk, depth), f32),
+        ],
         input_output_aliases={7 + i: i for i in range(len(before))},
         compiler_params=pltpu.CompilerParams(vmem_limit_bytes=56 << 20),
         cost_estimate=pl.CostEstimate(
@@ -582,50 +483,28 @@
     )(own, got, back_own, back_got, w_up, b_up[None, :], w_down, *before)
 
 
-def qkv_back_kernel(q_ref, k_ref, v_ref, w_ref, o_ref):
-    total = mm(q_ref[...], w_ref[0], 1, 1) + mm(k_ref[...], w_ref[1], 1, 1) + mm(v_ref[...], w_ref[2], 1, 1)
-    o_ref[...] = total.astype(o_ref.dtype)
-
-
-def project_back_pair(part, half, dq, dk, dv, w_qkv, kind):
-    length, width = dq.shape
-    depth = w_qkv.shape[1]
-    block = pl.BlockSpec((half, width), lambda c: (2 * c + part, 0))
-    return pl.pallas_call(
-        qkv_back_kernel,
-        grid=(length // (2 * half),),
-        in_specs=[block, block, block, pl.BlockSpec((3, depth, width), lambda c: (0, 0, 0))],
-        out_specs=pl.BlockSpec((half, depth), lambda c: (c, 0)),
-        out_shape=jax.ShapeDtypeStruct((length // 2, depth), kind),
-        compiler_params=pltpu.CompilerParams(vmem_limit_bytes=32 << 20),
-        cost_estimate=pl.CostEstimate(
-            flops=3 * length * depth * width, bytes_accessed=6 * depth * width, transcendentals=0
-        ),
-        name="qkv_back",
-    )(dq, dk, dv, w_qkv)
-
-
 MESH = pl.DeviceIdType.MESH
 ADD_ROWS = 32
-
-
-def add_low(out, out_at, a, a_at, b, rows):
+STEPS = 9
+EDGES = 4
+
+
+def add_low(a, a_at, b, rows):
     @pl.loop(0, rows // ADD_ROWS)
     def _(i):
-        at = pl.multiple_of(i * ADD_ROWS, ADD_ROWS)
-        total = a[pl.ds(pl.multiple_of(a_at + at, ADD_ROWS), ADD_ROWS), :].astype(f32)
-        total = total + b[pl.ds(at, ADD_ROWS), :].astype(f32)
-        out[pl.ds(pl.multiple_of(out_at + at, ADD_ROWS), ADD_ROWS), :] = total.astype(bf16)
+        at = pl.ds(pl.multiple_of(i * ADD_ROWS, ADD_ROWS), ADD_ROWS)
+        kept = a[pl.ds(pl.multiple_of(a_at + i * ADD_ROWS, ADD_ROWS), ADD_ROWS), :].astype(f32)
+        b[at, :] = (kept + b[at, :].astype(f32)).astype(bf16)
 
 
 class Unit:
     def __init__(self, part, out, row, rows, held, got, send, recv, local, place):
         self.part, self.out, self.row, self.rows = part, out, row, rows
         self.held, self.got, self.send, self.recv, self.local = held, got, send, recv, local
-        self.bit = [(place // (1 << b)) % 2 for b in range(4)]
-        self.partner = [place + (1 - 2 * self.bit[b]) * (1 << b) for b in range(4)]
+        self.bit = [(place // (1 << b)) % 2 for b in range(EDGES)]
+        self.partner = [place + (1 - 2 * self.bit[b]) * (1 << b) for b in range(EDGES)]
         self.base = [row]
-        for b in range(4):
+        for b in range(EDGES):
             self.base.append(self.base[-1] + self.bit[b] * (rows >> (b + 1)))
 
     def remote(self, src, dst, stage, b):
@@ -644,41 +523,42 @@
     def halving(self, b):
         half = self.rows >> (b + 1)
         if b == 0:
-            src = self.part.at[self.at(self.row + (1 - self.bit[0]) * half, half)]
+            first = self.row if self.held is not None else 0
+            src = self.part.at[self.at(first + (1 - self.bit[0]) * half, half)]
         else:
-            src = self.held[b - 1].at[self.at((1 - self.bit[b]) * half, half)]
+            src = self.got[b - 1].at[self.at((1 - self.bit[b]) * half, half)]
         return self.remote(src, self.got[b], b, b)
 
     def keep(self):
         half = self.rows // 2
         return pltpu.make_async_copy(
-            self.part.at[self.at(self.row + self.bit[0] * half, half)], self.held[0], self.local.at[0]
+            self.part.at[self.at(self.row + self.bit[0] * half, half)], self.held, self.local.at[0]
         )
 
     def own(self):
         return pltpu.make_async_copy(
-            self.held[3], self.out.at[self.at(self.base[4], self.rows >> 4)], self.local.at[1]
+            self.got[3], self.out.at[self.at(self.base[4], self.rows >> 4)], self.local.at[1]
         )
 
     def gathering(self, b):
         size = self.rows >> (b + 1)
         spot = self.out.at[self.at(self.base[b + 1], size)]
-        return self.remote(self.held[3] if b == 3 else spot, spot, 7 - b, b)
+        return self.remote(self.got[3] if b == 3 else spot, spot, 7 - b, b)
 
     def step(self, k):
         if k == 0:
             self.halving(0).start()
-            self.keep().start()
-        elif k == 1:
-            self.halving(0).wait()
-            self.keep().wait()
-            add_low(self.held[0], 0, self.held[0], 0, self.got[0], self.rows // 2)
-            self.halving(1).start()
+            if self.held is not None:
+                self.keep().start()
         elif k < 5:
             b = k - 1
             self.halving(b).wait()
             half = self.rows >> (b + 1)
-            add_low(self.held[b], 0, self.held[b - 1], self.bit[b] * half, self.got[b], half)
+            if b == 0 and self.held is not None:
+                self.keep().wait()
+                add_low(self.held, 0, self.got[0], half)
+            else:
+                add_low(self.part if b == 0 else self.got[b - 1], self.bit[b] * half, self.got[b], half)
             if b < 3:
                 self.halving(b + 1).start()
             else:
@@ -695,7 +575,14 @@
             self.gathering(0).wait()
 
 
-STEPS = 9
+def unit_scratch(rows, columns, kept):
+    return [
+        pltpu.VMEM((rows // 2 if kept else rows, columns), bf16),
+        *[pltpu.VMEM((rows >> (b + 1), columns), bf16) for b in range(EDGES)],
+        pltpu.SemaphoreType.DMA((2 * EDGES,)),
+        pltpu.SemaphoreType.DMA((2 * EDGES,)),
+        pltpu.SemaphoreType.DMA((2,)),
+    ]
 
 
 def greet(targets):
@@ -705,44 +592,247 @@
     pl.semaphore_wait(barrier, len(targets))
 
 
-def reduce_kernel(cuts, arrays, *refs):
-    parts, outs, scratch = refs[:arrays], refs[arrays : 2 * arrays], refs[2 * arrays :]
-    place = lax.axis_index("dp")
+def tail_kernel(
+    down_part, up_part, qkv_hbm, mixed_hbm, rows_hbm, w_qkv_hbm, w_out_hbm,
+    own_grad, got_grad, middle, out_grad, rows_of, lse, segr, segc, cosine, sine,
+    down_sum, up_sum, out_sum, q_sum, k_sum, v_sum, mid_grad, one_grad, col_sums,
+    qkv, mixed, rows_one, w_qkv, w_out, proj, mix_grad, d_qkv, dk, dv, kt, from_x, send_one, got_one,
+    load, x_send, x_recv, *more,
+):
+    place, me = lax.axis_index("dp"), lax.axis_index("tensor")
+    length = rows_one.shape[0]
+    chunks, half, depth = got_grad.shape
+    chunk = 2 * half
+    width = mixed.shape[1]
+    pairs = width // PAIR
+    across = {"tensor": 1 - me}
+
+    wide, deep = up_part.shape[0], down_part.shape[0]
+    specs = [
+        (down_part, down_sum, 0, deep // 2), (down_part, down_sum, deep // 2, deep // 2),
+        (up_part, up_sum, 0, wide // 2), (up_part, up_sum, wide // 2, wide // 2),
+        (None, out_sum, 0, width), (None, v_sum, 0, depth), (None, k_sum, 0, depth), (None, q_sum, 0, depth),
+    ]
     units = []
-    for i, (which, row, rows) in enumerate(cuts):
-        mine = scratch[11 * i : 11 * (i + 1)]
-        units.append(Unit(parts[which], outs[which], row, rows, mine[:4], mine[4:8], *mine[8:], place))
-    greet([{"dp": partner} for partner in units[0].partner])
-    late = [0, 1, 3, 5, 7, 8, 9, 11, 13]
-    order = sorted((late[k] + 2 * i, k, i) for i in range(len(units)) for k in range(STEPS))
-    for _, k, i in order:
-        units[i].step(k)
-
-
-def unit_scratch(rows, columns):
-    return [
-        *[pltpu.VMEM((rows >> (b + 1), columns), bf16) for b in range(4)],
-        *[pltpu.VMEM((rows >> (b + 1), columns), bf16) for b in range(4)],
-        pltpu.SemaphoreType.DMA((8,)),
-        pltpu.SemaphoreType.DMA((8,)),
-        pltpu.SemaphoreType.DMA((2,)),
+    for i, (part, out, row, rows) in enumerate(specs):
+        own, *got, send, recv, local = more[8 * i : 8 * (i + 1)]
+        units.append(Unit(own if part is None else part, out, row, rows, None if part is None else own, got, send, recv, local, place))
+
+    def x_copy(src, dst, i):
+        return pltpu.make_async_remote_copy(
+            src_ref=src, dst_ref=dst, send_sem=x_send.at[i], recv_sem=x_recv.at[i],
+            device_id=across, device_id_type=MESH,
+        )
+
+    grads_in = [x_copy(got_grad.at[c], from_x.at[c], c) for c in range(chunks)]
+    projs = [x_copy(proj.at[c, :half], proj.at[c, half:], chunks + c) for c in range(chunks)]
+    ones = [x_copy(send_one.at[c], got_one.at[c], 2 * chunks + c) for c in range(chunks)]
+    loads = [
+        pltpu.make_async_copy(src, dst, load.at[i])
+        for i, (src, dst) in enumerate(
+            [(w_out_hbm, w_out), (mixed_hbm, mixed), (qkv_hbm, qkv), (rows_hbm, rows_one), (w_qkv_hbm, w_qkv)]
+        )
     ]
 
-
-def reduce_over_dp(parts, cuts):
-    scratch = []
-    for which, _, rows in cuts:
-        scratch += unit_scratch(rows, parts[which].shape[1])
-    anywhere = pl.BlockSpec(memory_space=pl.ANY)
+    late = [0, 5, 17, 24, 31, 38, 45, 65, 68]
+    turns = [(late[k] + (12 if k > 1 else 2) * i, k, i) for i in range(4) for k in range(STEPS)]
+    turns += [(t, k, 4) for k, t in enumerate([None, 47, 60, 66, 72, 78, 84, 104, 107]) if k]
+    for i in range(3):
+        turns += [(t + (6 if k > 1 else 3) * i, k, 5 + i) for k, t in enumerate([None, 88, 100, 106, 112, 118, 124, 134, 138]) if k]
+    turns = sorted(turns)
+    done = [0]
+
+    def until(time):
+        while done[0] < len(turns) and turns[done[0]][0] <= time:
+            _, k, i = turns[done[0]]
+            units[i].step(k)
+            done[0] += 1
+
+    greet([*[{"dp": partner} for partner in units[0].partner], across])
+    for c in range(chunks):
+        grads_in[c].start()
+    until(4)
+    for copy in loads:
+        copy.start()
+
+    gain, scale, gate = rows_of[0:1, :], rows_of[1:2, :], rows_of[2:3, :]
+    step_rows = 64
+
+    def norm_back(c):
+        grads_in[c].wait()
+
+        @pl.loop(0, half // step_rows)
+        def _(i):
+            at = pl.ds(pl.multiple_of(i * step_rows, step_rows), step_rows)
+            grad = own_grad[c, at, :] + from_x[c, at, :].astype(f32)
+            values = middle[c, at, :]
+            center = values - jnp.mean(values, axis=1, keepdims=True)
+            root = lax.rsqrt(jnp.mean(center * center, axis=1, keepdims=True) + norm_eps)
+            normal = center * root
+            inner = grad * (gain * (1.0 + scale))
+            back = root * (
+                inner - jnp.mean(inner, axis=1, keepdims=True) - normal * jnp.mean(inner * normal, axis=1, keepdims=True)
+            )
+            total = back + out_grad[c, at, :].astype(f32)
+            mid_grad[c, at, :] = total
+            proj[c, at, :] = (total * gate).astype(bf16)
+            shifted = jnp.sum(grad, axis=0, keepdims=True)
+            scaled = jnp.sum(grad * normal, axis=0, keepdims=True)
+            both = jnp.concatenate([shifted, scaled, jnp.zeros((6, depth), f32)], axis=0)
+            if c == 0:
+                fresh = jnp.where(i == 0, jnp.zeros_like(both), col_sums[...])
+                col_sums[...] = fresh + both
+            else:
+                col_sums[...] += both
+
+        projs[c].start()
+
+    norm_back(0)
+    until(20)
+    norm_back(1)
+    until(28)
+    loads[0].wait()
+    for c in range(chunks):
+        projs[c].wait()
+        mix_grad[c * chunk : (c + 1) * chunk, :] = mm(proj[c], w_out[...], 1, 1).astype(bf16)
+        until(32 + 10 * c)
+
+    loads[1].wait()
+    out_part = units[4].part
+    for r in range(0, width, 256):
+        out_part[r : r + 256, :] = (
+            mm(mixed[:chunk, r : r + 256], proj[0], 0, 0) + mm(mixed[chunk:, r : r + 256], proj[1], 0, 0)
+        ).astype(bf16)
+    units[4].step(0)
+    until(46)
+
+    loads[2].wait()
+
+    def turn_back(u, rows):
+        return (u * cosine[rows, :] - turned(u) * sine[rows, :]).astype(bf16)
+
+    def attend_back(p, c):
+        lanes = pl.ds(pl.multiple_of(p * PAIR, PAIR), PAIR)
+        rows = pl.ds(pl.multiple_of(c * chunk, chunk), chunk)
+        q, g = qkv[0, rows, lanes], mix_grad[rows, lanes]
+        both = (g.astype(f32) * mixed[rows, lanes].astype(f32)).T
+        qh = [head_lanes(q, h) for h in range(2)]
+        gh = [head_lanes(g, h) for h in range(2)]
+        delta = [jnp.sum(both[h * HEAD : (h + 1) * HEAD, :], axis=0, keepdims=True) for h in range(2)]
+        q_two, g_two = jnp.concatenate(qh, axis=0), jnp.concatenate(gh, axis=0)
+        docs = segr[:, rows]
+        dq = [0.0, 0.0]
+        for b in range(0, length, BLOCK):
+            cols = slice(b, b + BLOCK)
+            k, v = qkv[1, cols, lanes], qkv[2, cols, lanes]
+            turned_k = transposed(k).astype(bf16)
+            same = jnp.concatenate([segc[cols, :]] * (chunk // 128), axis=1) == docs
+            ps, ds = [], []
+            for h in range(2):
+                s = jnp.where(same, mm(k, qh[h], 1, 1), masked_score)
+                pr = jnp.exp(s - lse[c, 2 * p + h])
+                d = (pr * (mm(v, gh[h], 1, 1) - delta[h])).astype(bf16)
+                ps.append(pr.astype(bf16))
+                ds.append(d)
+                dq[h] = dq[h] + mm(turned_k[h * HEAD : (h + 1) * HEAD, :], d, 1, 0)
+            add_v = mm(jnp.concatenate(ps, axis=1), g_two, 1, 0)
+            add_k = mm(jnp.concatenate(ds, axis=1), q_two, 1, 0)
+            dv[cols, :] = jnp.where(c == 0, 0.0, dv[cols, :]) + add_v
+            dk[cols, :] = jnp.where(c == 0, 0.0, dk[cols, :]) + add_k
+        d_qkv[0, rows, lanes] = turn_back(jnp.concatenate(dq, axis=0).T * (HEAD**-0.5), rows)
+
+        @pl.when(c == chunks - 1)
+        def _():
+            @pl.loop(0, length // BLOCK)
+            def _(b):
+                at = pl.ds(pl.multiple_of(b * BLOCK, BLOCK), BLOCK)
+                d_qkv[1, at, lanes] = turn_back(dk[at, :], at)
+                d_qkv[2, at, lanes] = dv[at, :].astype(bf16)
+
+    @pl.loop(0, pairs * chunks)
+    def _(i):
+        attend_back(i // chunks, i % chunks)
+        for n in range(pairs * chunks):
+
+            @pl.when(i == n)
+            def _():
+                until(50 + 4.5 * n)
+
+    loads[4].wait()
+
+    def rows_back(start):
+        at = slice(start, start + half)
+        return (
+            mm(d_qkv[0, at, :], w_qkv[0], 1, 1) + mm(d_qkv[1, at, :], w_qkv[1], 1, 1) + mm(d_qkv[2, at, :], w_qkv[2], 1, 1)
+        )
+
+    for c in range(chunks):
+        send_one[c] = rows_back(c * chunk + half).astype(bf16)
+        ones[c].start()
+    until(83)
+    loads[3].wait()
+    for i in range(3):
+        part = units[5 + i].part
+
+        @pl.loop(0, depth // 256)
+        def _(r):
+            at = pl.ds(pl.multiple_of(r * 256, 256), 256)
+            part[at, :] = mm(rows_one[:, at], d_qkv[2 - i], 0, 0).astype(bf16)
+
+        units[5 + i].step(0)
+        until(87 + 3 * i)
+    for c in range(chunks):
+        one_grad[c] = rows_back(c * chunk)
+        until(97 + 3 * c)
+    for c in range(chunks):
+        ones[c].wait()
+        one_grad[c] = one_grad[c] + got_one[c].astype(f32)
+        until(108 + 3 * c)
+    until(1000)
+
+
+def tail(down_part, up_part, qkv, mixed, rows_one, w_qkv, w_out, own_grad, got_grad, middle, out_grad, rows_of, lse, segr, segc, cosine, sine):
+    _, length, width = qkv.shape
+    chunks, half, depth = got_grad.shape
+    anywhere, near = pl.BlockSpec(memory_space=pl.ANY), pl.BlockSpec(memory_space=pltpu.VMEM)
+    shaped = jax.ShapeDtypeStruct
+    (deep, _), (_, wide) = down_part.shape, up_part.shape
+    scratch = [
+        pltpu.VMEM(qkv.shape, bf16),
+        pltpu.VMEM(mixed.shape, bf16),
+        pltpu.VMEM(rows_one.shape, bf16),
+        pltpu.VMEM(w_qkv.shape, bf16),
+        pltpu.VMEM(w_out.shape, bf16),
+        pltpu.VMEM((chunks, 2 * half, depth), bf16),
+        pltpu.VMEM((length, width), bf16),
+        pltpu.VMEM((3, length, width), bf16),
+        pltpu.VMEM((length, PAIR), f32),
+        pltpu.VMEM((length, PAIR), f32),
+        pltpu.VMEM((8, 128), f32),
+        pltpu.VMEM(got_grad.shape, bf16),
+        pltpu.VMEM(got_grad.shape, bf16),
+        pltpu.VMEM(got_grad.shape, bf16),
+        pltpu.SemaphoreType.DMA((5,)),
+        pltpu.SemaphoreType.DMA((3 * chunks,)),
+        pltpu.SemaphoreType.DMA((3 * chunks,)),
+        *unit_scratch(deep // 2, depth, True) * 2,
+        *unit_scratch(depth // 2, wide, True) * 2,
+        *unit_scratch(width, depth, False),
+        *unit_scratch(depth, width, False) * 3,
+    ]
     return pl.pallas_call(
-        functools.partial(reduce_kernel, cuts, len(parts)),
-        in_specs=[anywhere] * len(parts),
-        out_specs=[anywhere] * len(parts),
-        out_shape=[jax.ShapeDtypeStruct(p.shape, p.dtype) for p in parts],
+        tail_kernel,
+        in_specs=[anywhere] * 7 + [near] * 10,
+        out_specs=[anywhere] * 6 + [near] * 3,
+        out_shape=[
+            shaped(down_part.shape, bf16), shaped(up_part.shape, bf16), shaped((width, depth), bf16),
+            *[shaped((depth, width), bf16)] * 3,
+            shaped(got_grad.shape, f32), shaped(got_grad.shape, f32), shaped((8, depth), f32),
+        ],
         scratch_shapes=scratch,
-        compiler_params=pltpu.CompilerParams(collective_id=1, has_side_effects=True, vmem_limit_bytes=40 << 20),
-        name="reduce",
-    )(*parts)
+        compiler_params=pltpu.CompilerParams(collective_id=1, has_side_effects=True, vmem_limit_bytes=61 << 20),
+        name="tail",
+    )(down_part, up_part, qkv, mixed, rows_one, w_qkv, w_out, own_grad, got_grad, middle, out_grad, rows_of, lse, segr, segc, cosine, sine)
 
 
 def body_pair(
@@ -810,48 +900,30 @@
         pieces.append(rest)
     rows_two, hidden, grad_pre = state
     grad_b_up = sum(pieces[c][4] for c in each)[0]
-    grad_act_two = [pieces[c][0] + swap(pieces[c][1]).astype(f32) for c in each]
     grad_w_down = mm(hidden, full_back, 0, 0).astype(bf16)
     grad_w_up = mm(rows_two, grad_pre, 0, 0).astype(bf16)
-
-    vectors, grad_middle, full_proj, grad_mixed = [], [], [], []
-    for c in each:
-        _, second_back = jax.vjp(modulate, middle[c], gain_two, shift_m, scale_m)
-        grad, grad_gain_two, grad_shift_m, grad_scale_m = second_back(grad_act_two[c])
-        grad_middle.append(grad + grad_out[c])
-        vectors.append([grad_gain_two, grad_shift_m, grad_scale_m])
-        proj = (grad_middle[c] * gate_a).astype(bf16)
-        full_proj.append(jnp.concatenate([proj, swap(proj)], axis=0))
-        grad_mixed.append(mm(full_proj[c], w_out, 1, 1).astype(bf16))
-    grad_gain_two, grad_shift_m, grad_scale_m = [sum(parts) for parts in zip(*vectors)]
     branch = [pieces[c][2] + swap(pieces[c][3]).astype(f32) + b_down for c in each]
     output = jnp.concatenate([(middle[c] + gate_m * branch[c]).astype(bf16) for c in each], axis=0)
     grad_gate_m = sum(jnp.sum(grad_out[c] * branch[c], axis=0) for c in each)
     grad_b_down = sum(jnp.sum(back[c].astype(f32), axis=0) for c in each)
-    grad_gate_a = sum(jnp.sum(grad_middle[c] * projected[c], axis=0) for c in each)
-
-    grads = ()
-    for c in each:
-        grads = attend_backward_pair(
-            c, chunk, qkv, grad_mixed[c], mixed[c], lse[c], seg_rows, seg_cols, cosine, sine, grads
-        )
-    grad_w_out = sum(mm(mixed[c], full_proj[c], 0, 0) for c in each).astype(bf16)
-    for_other = swap(project_back_pair(1, half, *grads, w_qkv, bf16))
-    grad_act_one = project_back_pair(0, half, *grads, w_qkv, f32) + for_other.astype(f32)
-    grad_w_qkv = [mm(rows_one, grads[t], 0, 0).astype(bf16) for t in range(3)]
-    depth, wide = w_up.shape
-    cuts = (
-        (0, 0, wide // 2), (0, wide // 2, wide // 2), (1, 0, depth // 2), (1, depth // 2, depth // 2),
-        (2, 0, w_out.shape[0]), (3, 0, depth), (4, 0, depth), (5, 0, depth),
+
+    in_chunks = (chunks, half, width)
+    *sums, grad_middle, grad_act_one, columns = tail(
+        grad_w_down, grad_w_up, qkv, jnp.concatenate(mixed, axis=0), rows_one, w_qkv, w_out,
+        jnp.stack([pieces[c][0] for c in each]), jnp.stack([pieces[c][1] for c in each]),
+        jnp.stack(middle), cotangent.reshape(in_chunks), jnp.stack([gain_two, scale_m, gate_a] + [gate_a] * 5),
+        jnp.stack(lse), seg_rows, seg_cols, cosine, sine,
     )
-    reduced = reduce_over_dp((grad_w_down, grad_w_up, grad_w_out, *grad_w_qkv), cuts)
-    grad_w_down, grad_w_up, grad_w_out, *grad_w_qkv = [r.astype(f32) for r in reduced]
-    grad_w_qkv = jnp.stack(grad_w_qkv)
+    grad_w_down, grad_w_up, grad_w_out, grad_q, grad_k, grad_v = [s.astype(f32) for s in sums]
+    grad_w_qkv = jnp.stack([grad_q, grad_k, grad_v])
+    grad_middle, grad_act_one = grad_middle.reshape(own, width), grad_act_one.reshape(own, width)
+    grad_shift_m, grad_scale_m, grad_gain_two = columns[0], columns[1] * gain_two, columns[1] * (1.0 + scale_m)
+    grad_gate_a = jnp.sum(grad_middle * jnp.concatenate(projected, axis=0), axis=0)
 
     x_all = tokens.astype(f32)
     _, first_back = jax.vjp(modulate, x_all, gain_one, shift_a, scale_a)
     grad_x, grad_gain_one, grad_shift_a, grad_scale_a = first_back(grad_act_one)
-    grad_x = (grad_x + jnp.concatenate(grad_middle, axis=0)).astype(bf16)
+    grad_x = (grad_x + grad_middle).astype(bf16)
 
     small = jnp.concatenate(
         [

time: 482 us -> 434 us (0.900)
  waiting for transfers between devices: 109 us -> 75.8 us
  matrix products: 37.5 us -> 27.2 us
  starting transfers between devices: 18.4 us -> 11.6 us
  other arithmetic: 37.2 us -> 43.8 us
  Pallas kernels: 263 us -> 258 us
    ppermute x16 -> x11, waiting for transfers between devices: 98 us -> 68.1 us  [swap(): return lax.ppermute(values, 'tensor', [(0, 1), (1, 0)])]
    dot_general x9 -> x2, matrix products: 28.1 us -> 17.1 us  [mm(): lax.dot_general(a, b, (((da,), (db,)), ((), ())), preferred_element_type=...]
    ppermute x16 -> x11, starting transfers between devices: 17.5 us -> 11.3 us  [swap(): return lax.ppermute(values, 'tensor', [(0, 1), (1, 0)])]
    pallas_call x2, Pallas kernels: 38.3 us -> 32.7 us  [mlp_pair(): pl.pallas_call(mlp_kernel, grid=(width // tile,), in_specs=[small, small,...]
    another operation x1 -> x5, other arithmetic: 3.19 us -> 8.32 us  [the longest x1 3.68 us: body_pair(): grad_w_qkv = jnp.stack([grad_q, grad_k, grad_v])]
    convert_element_type x5 -> x4, other arithmetic: 14.1 us -> 12.2 us  [the longest x3 10.4 us: body_pair(): s.astype(f32)]
    pallas_call x5 -> x1, Pallas kernels: 198 us -> 197 us  [tail(): pl.pallas_call(tail_kernel, in_specs=[anywhere] * 7 + [near] * 10, out_sp...]
  transfers between devices with their start and end apart: 20 -> 15, of which waited for: 15 -> 8; matrix products, arithmetic and copies ran while one was open for 11% -> 14% of each run, Pallas kernels for 42% -> 51%
where the time goes in v3:
time: 434 us; the launch traced here: 430 us
  Pallas kernels  258 us (59%)
  waiting for transfers between devices  75.8 us (17%)
  other arithmetic  43.8 us (10%)
  matrix products  27.2 us (6%)
  starting transfers between devices  11.6 us (3%)
  local copies, waits for them, and re-layouts  11.2 us (3%)
    pallas_call x1, Pallas kernels, tail(): pl.pallas_call(tail_kernel, in_specs=[anywhere] * 7 + [near] * 10, out_sp...  197 us
    ppermute x11, waiting for transfers between devices, swap(): return lax.ppermute(values, 'tensor', [(0, 1), (1, 0)])  68.1 us
    pallas_call x2, Pallas kernels, mlp_pair(): pl.pallas_call(mlp_kernel, grid=(width // tile,), in_specs=[small, small,...  32.7 us
    pallas_call x2, Pallas kernels, attend_forward_pair(): pl.pallas_call(forward_chunk_kernel, grid=(pairs,), in_specs=[*pair_piece...  18.8 us
    dot_general x2, matrix products, mm(): lax.dot_general(a, b, (((da,), (db,)), ((), ())), preferred_element_type=...  17.1 us
    ppermute x11, starting transfers between devices, swap(): return lax.ppermute(values, 'tensor', [(0, 1), (1, 0)])  11.3 us
    convert_element_type x3, other arithmetic, body_pair(): s.astype(f32)  10.4 us
    pallas_call x2, Pallas kernels, project_pair(): pl.pallas_call(qkv_pair_kernel, grid=(3,), in_specs=[pl.BlockSpec((half,...  10.1 us
  transfers between devices with their start and end apart: 15, of which 8 were waited for; matrix products, arithmetic and copies ran while one was open for 14% of the time, Pallas kernels for 51%

profile of v3, /device:TPU:0, one launch (start us, length us, event | category | flops | bytes accessed | tf_op | source)
XLA Modules:
  0.0 429.8 jit_solution(11601995140863107517)
XLA Ops:
  0.7 1.4 copy-done
  2.1 1.0 fusion.64
  3.0 0.7 add.197
  4.0 0.4 fusion.29
  4.5 1.5 fusion.33
  5.9 2.9 collective-permute-start
  9.2 1.9 multiply_sine_fusion
  11.1 0.9 pad_maximum_fusion.6
  12.0 20.3 %collective-permute-done.1.got_ref = bf16[256,1024]{1,0:T(8,128)(2,1)} collective-permute-done((bf16[256,1024]{1,0:T(8,128)(2,1)}, bf16[256,1024]{1,0:T(8,128)(2,1)}, u32[]{:S(2)}, u32[]{:S(2)}) %collective-permute-start.1) | collective-permute-done | bytes 524320 | tf_op jit(solution)/shard_map/ppermute | solution.py:850
  32.4 5.3 %qkv.2 = (bf16[3,1024,512]{2,1,0:T(8,128)(2,1)S(1)}, bf16[1024,1024]{1,0:T(8,128)(2,1)S(1)}) custom-call(bf16[256,1024]{1,0:T(8,128)(2,1)} %get-tuple-element.102.own_ref, bf16[256,1024]{1,0:T(8,128)(2,1)} %collective-permute-done.1.got_ref, bf16[3,1024,512]{2,1,0:T(8,128)(2,1)S(1)} %copy-done.1, f32[1024,128]{1,0:T(8,128)S(1)} %get-tuple-element.129.cos_ref.cosine, ...), custom_call_target="tpu_custom_call" | custom-call | flops 1610612736 | bytes 4194304 | tf_op jit(solution)/shard_map/qkv/pallas_call | solution.py:309
  37.7 4.8 %qkv.3 = (bf16[3,1024,512]{2,1,0:T(8,128)(2,1)S(1)}, bf16[1024,1024]{1,0:T(8,128)(2,1)S(1)}) custom-call(bf16[256,1024]{1,0:T(8,128)(2,1)} %get-tuple-element.103.own_ref, bf16[256,1024]{1,0:T(8,128)(2,1)} %collective-permute-done.got_ref, bf16[3,1024,512]{2,1,0:T(8,128)(2,1)S(1)} %copy-done.1, ...), custom_call_target="tpu_custom_call", output_to_operand_aliasing={{0}: (5, {}), {1}: (6, {})} | custom-call | flops 1610612736 | bytes 4194304 | tf_op jit(solution)/shard_map/qkv/pallas_call | solution.py:309
  42.5 1.3 copy-done.3
  44.1 9.4 %attend.3 = (bf16[512,512]{1,0:T(8,128)(2,1)S(1)}, f32[8,1,512]{2,1,0:T(1,128)S(1)}) custom-call(bf16[3,1024,512]{2,1,0:T(8,128)(2,1)S(1)} %get-tuple-element.48.q_ref.k_ref.v_ref.qkv_hbm, bf16[3,1024,512]{2,1,0:T(8,128)(2,1)S(1)} %get-tuple-element.48.q_ref.k_ref.v_ref.qkv_hbm, bf16[3,1024,512]{2,1,0:T(8,128)(2,1)S(1)} %get-tuple-element.48.q_ref.k_ref.v_ref.qkv_hbm, ...), custom_call_target="tpu_custom_call" | custom-call | flops 4294967296 | bytes 4194304 | tf_op jit(solution)/shard_map/attend/pallas_call | solution.py:371
  53.5 9.4 %attend.2 = (bf16[512,512]{1,0:T(8,128)(2,1)S(1)}, f32[8,1,512]{2,1,0:T(1,128)S(1)}) custom-call(bf16[3,1024,512]{2,1,0:T(8,128)(2,1)S(1)} %get-tuple-element.48.q_ref.k_ref.v_ref.qkv_hbm, bf16[3,1024,512]{2,1,0:T(8,128)(2,1)S(1)} %get-tuple-element.48.q_ref.k_ref.v_ref.qkv_hbm, bf16[3,1024,512]{2,1,0:T(8,128)(2,1)S(1)} %get-tuple-element.48.q_ref.k_ref.v_ref.qkv_hbm, ...), custom_call_target="tpu_custom_call" | custom-call | flops 4294967296 | bytes 4194304 | tf_op jit(solution)/shard_map/attend/pallas_call | solution.py:371
  63.0 0.5 convolution_convert_fusion.2
  63.4 1.8 collective-permute-start.6
  65.2 0.4 convolution_convert_fusion.3
  65.7 0.3 collective-permute-start.2
  66.0 1.1 convert_reduce_fusion.4
  67.1 1.7 collective-permute-start.8
  68.9 0.3 collective-permute-start.4
  69.3 9.0 %collective-permute-done.6 = bf16[256,1024]{1,0:T(8,128)(2,1)S(1)} collective-permute-done((bf16[256,1024]{1,0:T(8,128)(2,1)S(1)}, bf16[256,1024]{1,0:T(8,128)(2,1)S(1)}, u32[]{:S(2)}, u32[]{:S(2)}) %collective-permute-start.6) | collective-permute-done | bytes 524320 | tf_op jit(solution)/shard_map/ppermute | solution.py:850
  78.4 0.5 convert_add_fusion.2
  78.8 10.8 %collective-permute-done.2 = bf16[256,1024]{1,0:T(8,128)(2,1)S(1)} collective-permute-done((bf16[256,1024]{1,0:T(8,128)(2,1)S(1)}, bf16[256,1024]{1,0:T(8,128)(2,1)S(1)}, u32[]{:S(2)}, u32[]{:S(2)}) %collective-permute-start.2) | collective-permute-done | bytes 524320 | tf_op jit(solution)/shard_map/ppermute | solution.py:850
  89.6 1.6 fusion.70
  91.9 1.5 add_convert_fusion.3
  93.4 1.8 collective-permute-start.3
  95.2 0.7 stack.77.rows_of
  95.8 0.6 pad_maximum_fusion.12.lse
  96.5 1.1 pad_maximum_fusion.4.mixed_hbm
  97.8 1.5 pad_maximum_fusion.1.middle
  99.3 12.9 %collective-permute-done.4.b_got_ref = bf16[256,1024]{1,0:T(8,128)(2,1)} collective-permute-done((bf16[256,1024]{1,0:T(8,128)(2,1)S(1)}, bf16[256,1024]{1,0:T(8,128)(2,1)}, u32[]{:S(2)}, u32[]{:S(2)}) %collective-permute-start.4) | collective-permute-done | bytes 524320 | tf_op jit(solution)/shard_map/ppermute | solution.py:850
  112.2 11.2 %collective-permute-done.3.got_ref = bf16[256,1024]{1,0:T(8,128)(2,1)} collective-permute-done((bf16[256,1024]{1,0:T(8,128)(2,1)}, bf16[256,1024]{1,0:T(8,128)(2,1)}, u32[]{:S(2)}, u32[]{:S(2)}) %collective-permute-start.3) | collective-permute-done | bytes 524320 | tf_op jit(solution)/shard_map/ppermute | solution.py:850
  123.4 16.4 %mlp.2 = (bf16[1024,1024]{1,0:T(8,128)(2,1)}, bf16[1024,2048]{1,0:T(8,128)(2,1)}, bf16[1024,2048]{1,0:T(8,128)(2,1)}, f32[256,1024]{1,0:T(8,128)}, bf16[256,1024...) custom-call(bf16[256,1024]{1,0:T(8,128)(2,1)} %get-tuple-element.120.own_ref, ...), custom_call_target="tpu_custom_call" | custom-call | flops 12884901888 | bytes 25165824 | tf_op jit(solution)/shard_map/mlp/pallas_call | solution.py:447
  139.8 0.8 copy-done.45
  140.6 16.4 %mlp.3 = (bf16[1024,1024]{1,0:T(8,128)(2,1)}, bf16[1024,2048]{1,0:T(8,128)(2,1)}, bf16[1024,2048]{1,0:T(8,128)(2,1)}, f32[256,1024]{1,0:T(8,128)}, bf16[256,1024...) custom-call(bf16[256,1024]{1,0:T(8,128)(2,1)} %get-tuple-element.121, ...), custom_call_target="tpu_custom_call", output_to_operand_aliasing={{0}: (7, {}), {1}: (8, {}), {2}: (9, {})} | custom-call | flops 12884901888 | bytes 25165824 | tf_op jit(solution)/shard_map/mlp/pallas_call | solution.py:447
  157.0 1.8 collective-permute-start.9
  159.1 9.6 %convolution_convert_fusion.up_part = bf16[1024,2048]{1,0:T(8,128)(2,1)} fusion(bf16[1024,1024]{1,0:T(8,128)(2,1)} %get-tuple-element.59, bf16[1024,2048]{1,0:T(8,128)(2,1)} %get-tuple-element.60), kind=kOutput, calls=%fused_computation | convolution fusion | flops 4297064448 | bytes 10485760 | tf_op jit(solution)/shard_map/dot_general | solution.py:62
  168.7 1.5 pad_maximum_fusion.own_grad
  170.2 1.1 pad_maximum_fusion.5.got_grad
  171.2 1.1 copy-done.47
  172.5 7.5 %convolution_convert_fusion.1.down_part = bf16[2048,1024]{1,0:T(8,128)(2,1)} fusion(bf16[1024,2048]{1,0:T(8,128)(2,1)S(1)} %copy-done.47, bf16[256,1024]{1,0:T(8,128)(2,1)} %collective-permute-done.8.b_got_ref, bf16[256,1024]{1,0:T(8,128)(2,1)} %get-tuple-element.105.b_own_ref, bf16[256,1024]{1,0:T(8,128)(2,1)} %collective-permute-done.4.b_got_ref, ...), kind=kOutput, calls=%fused_computation.1 | convolution fusion | flops 4305453056 | bytes 10485760 | tf_op jit(solution)/shard_map/dot_general | solution.py:62
  180.0 196.8 %tail.1 = (bf16[2048,1024]{1,0:T(8,128)(2,1)}, bf16[1024,2048]{1,0:T(8,128)(2,1)}, bf16[512,1024]{1,0:T(8,128)(2,1)}, bf16[1024,512]{1,0:T(8,128)(2,1)}, bf16[10...) custom-call(bf16[2048,1024]{1,0:T(8,128)(2,1)} %convolution_convert_, ...), custom_call_target="tpu_custom_call" | custom-call | tf_op jit(solution)/shard_map/tail/pallas_call | solution.py:823
  376.8 2.3 fusion.9
  379.1 1.7 reduce_sum.279
  380.9 3.0 fusion.8
  384.0 1.6 multiply_reduce_fusion
  385.6 0.8 fusion.73
  386.6 2.4 fusion.37
  389.2 3.9 collective-permute-done.10
  393.3 4.9 %collective-permute-done.11 = f32[1,11392]{1,0:T(1,128)S(1)} collective-permute-done((f32[1,11392]{1,0:T(1,128)S(1)}, f32[1,11392]{1,0:T(1,128)S(1)}, u32[]{:S(2)}, u32[]{:S(2)}) %collective-permute-start.11) | collective-permute-done | bytes 45600 | tf_op jit(solution)/shard_map/ppermute | solution.py:853
  398.4 1.7 fusion.18
  400.2 2.8 collective-permute-done.12
  403.2 3.7 maximum_convert_fusion
  406.9 1.6 convert_element_type.123
  408.5 4.4 %convert_element_type.124 = f32[1024,2048]{1,0:T(8,128)} convert(bf16[1024,2048]{1,0:T(8,128)(2,1)S(1)} %copy-done.27) | non-fusion elementwise | flops 2097152 | bytes 12582912 | tf_op jit(solution)/shard_map/convert_element_type | solution.py:917
  412.9 4.4 %convert_element_type.125 = f32[2048,1024]{1,0:T(8,128)} convert(bf16[2048,1024]{1,0:T(8,128)(2,1)S(1)} %copy-done.26) | non-fusion elementwise | flops 2097152 | bytes 12582912 | tf_op jit(solution)/shard_map/convert_element_type | solution.py:917
  417.3 1.0 pad_maximum_fusion.3
  418.6 1.8 fusion.50
  421.0 0.6 slice.68
  421.6 0.6 fusion.72
  422.2 0.6 slice.69
  422.8 2.5 concatenate.53
  425.3 4.3 %fusion.38 = f32[128,6144]{1,0:T(8,128)} fusion(f32[16,11392]{1,0:T(8,128)S(1)} %concatenate.53), kind=kOutput, calls=%fused_computation.81 | convolution fusion | flops 150994944 | bytes 3547136 | tf_op jit(solution)/shard_map/nc,nm->cm/dot_general | solution.py:941
  (150 shorter events, 4.0 us)
Async XLA Ops:
  0.6 1.4 copy-start
  0.7 3.1 copy-start.10
  0.7 3.8 copy-start.39
  3.8 5.1 %copy-start.46 = (s32[1,4]{1,0:T(1,128)S(1)}, s32[1,4]{1,0:T(1,128)}, u32[]{:S(2)}) copy-start(s32[1,4]{1,0:T(1,128)} %param.16) | copy-start | bytes 52
  5.9 31.7 %collective-permute-start = (bf16[256,1024]{1,0:T(8,128)(2,1)}, bf16[256,1024]{1,0:T(8,128)(2,1)}, u32[]{:S(2)}, u32[]{:S(2)}) collective-permute-start(bf16[256,1024]{1,0:T(8,128)(2,1)} %get-tuple-element.103.own_ref), channel_id=1, source_target_pairs={{0,1},{1,0},{2,3},{3,2},{4,5},{5,4},{6,7},{7,6},{8,9},{9,8},{10,11... | collective-permute-start | bytes 1572872 | tf_op jit(solution)/shard_map/ppermute | solution.py:850
  8.9 23.5 %collective-permute-start.1 = (bf16[256,1024]{1,0:T(8,128)(2,1)}, bf16[256,1024]{1,0:T(8,128)(2,1)}, u32[]{:S(2)}, u32[]{:S(2)}) collective-permute-start(bf16[256,1024]{1,0:T(8,128)(2,1)} %get-tuple-element.102.own_ref), channel_id=1, source_target_pairs={{0,1},{1,0},{2,3},{3,2},{4,5},{5,4},{6,7},{7,6},{8,9},{9,8},{10,11... | collective-permute-start | bytes 1572872 | tf_op jit(solution)/shard_map/ppermute | solution.py:850
  9.0 23.3 %copy-start.1 = (bf16[3,1024,512]{2,1,0:T(8,128)(2,1)S(1)}, bf16[3,1024,512]{2,1,0:T(8,128)(2,1)}, u32[]{:S(2)}) copy-start(bf16[3,1024,512]{2,1,0:T(8,128)(2,1)} %w_qkv_hbm.1) | copy-start | bytes 9437188
  9.2 44.3 %copy-start.9 = (s32[1024]{0:T(1024)}, s32[1024]{0:T(1024)S(1)}, u32[]{:S(2)}) copy-start(s32[1024]{0:T(1024)S(1)} %get-tuple-element.90) | copy-start | bytes 12292
  12.0 25.7 %copy-start.4 = (f32[1024,128]{1,0:T(8,128)}, f32[1024,128]{1,0:T(8,128)S(1)}, u32[]{:S(2)}) copy-start(f32[1024,128]{1,0:T(8,128)S(1)} %get-tuple-element.129.cos_ref.cosine) | copy-start | bytes 1572868
  12.0 25.7 %copy-start.5 = (f32[1024,128]{1,0:T(8,128)}, f32[1024,128]{1,0:T(8,128)S(1)}, u32[]{:S(2)}) copy-start(f32[1024,128]{1,0:T(8,128)S(1)} %get-tuple-element.130.sin_ref.sine) | copy-start | bytes 1572868
  42.5 1.4 copy-start.3
  43.9 9.6 %copy-start.2 = (bf16[3,1024,512]{2,1,0:T(8,128)(2,1)}, bf16[3,1024,512]{2,1,0:T(8,128)(2,1)S(1)}, u32[]{:S(2)}) copy-start(bf16[3,1024,512]{2,1,0:T(8,128)(2,1)S(1)} %get-tuple-element.48.q_ref.k_ref.v_ref.qkv_hbm) | copy-start | bytes 9437188
  44.1 9.4 %copy-start.6 = (s32[1024,128]{1,0:T(8,128)}, s32[1024,128]{1,0:T(8,128)S(1)}, u32[]{:S(2)}) copy-start(s32[1024,128]{1,0:T(8,128)S(1)} %broadcast_in_dim.29.segc_ref.segc) | copy-start | bytes 1572868
  53.5 9.4 %copy-start.14 = (bf16[512,1024]{1,0:T(8,128)(2,1)S(1)}, bf16[512,1024]{1,0:T(8,128)(2,1)}, u32[]{:S(2)}) copy-start(bf16[512,1024]{1,0:T(8,128)(2,1)} %w_out_hbm.1) | copy-start | bytes 3145732
  62.9 26.7 %copy-start.7 = (bf16[512,512]{1,0:T(8,128)(2,1)}, bf16[512,512]{1,0:T(8,128)(2,1)S(1)}, u32[]{:S(2)}) copy-start(bf16[512,512]{1,0:T(8,128)(2,1)S(1)} %get-tuple-element.49) | copy-start | bytes 1572868
  62.9 3.1 copy-start.21
  63.4 5.7 %copy-start.11 = (bf16[512,1024]{1,0:T(8,128)(2,1)S(1)}, bf16[512,1024]{1,0:T(8,128)(2,1)}, u32[]{:S(2)}) copy-start(bf16[512,1024]{1,0:T(8,128)(2,1)} %param.14) | copy-start | bytes 3145732
  63.4 14.9 %collective-permute-start.6 = (bf16[256,1024]{1,0:T(8,128)(2,1)S(1)}, bf16[256,1024]{1,0:T(8,128)(2,1)S(1)}, u32[]{:S(2)}, u32[]{:S(2)}) collective-permute-start(bf16[256,1024]{1,0:T(8,128)(2,1)S(1)} %convolution_convert_fusion.2), channel_id=1, source_target_pairs={{0,1},{1,0},{2,3},{3,2},{4,5},{5,4},{6,7},{7,6},{8,9},{9,8},{10,11... | collective-permute-start | bytes 1572872 | tf_op jit(solution)/shard_map/ppermute | solution.py:850
  65.7 23.9 %collective-permute-start.2 = (bf16[256,1024]{1,0:T(8,128)(2,1)S(1)}, bf16[256,1024]{1,0:T(8,128)(2,1)S(1)}, u32[]{:S(2)}, u32[]{:S(2)}) collective-permute-start(bf16[256,1024]{1,0:T(8,128)(2,1)S(1)} %convolution_convert_fusion.3), channel_id=1, source_target_pairs={{0,1},{1,0},{2,3},{3,2},{4,5},{5,4},{6,7},{7,6},{8,9},{9,8},{10,11... | collective-permute-start | bytes 1572872 | tf_op jit(solution)/shard_map/ppermute | solution.py:850
  67.1 24.1 %copy-start.35 = (bf16[256,1024]{1,0:T(8,128)(2,1)}, bf16[256,1024]{1,0:T(8,128)(2,1)S(1)}, u32[]{:S(2)}) copy-start(bf16[256,1024]{1,0:T(8,128)(2,1)S(1)} %get-tuple-element.95.b_own_ref) | copy-start | bytes 1572868
  67.1 72.7 %collective-permute-start.8 = (bf16[256,1024]{1,0:T(8,128)(2,1)}, bf16[256,1024]{1,0:T(8,128)(2,1)}, u32[]{:S(2)}, u32[]{:S(2)}) collective-permute-start(bf16[256,1024]{1,0:T(8,128)(2,1)} %get-tuple-element.105.b_own_ref), channel_id=1, source_target_pairs={{0,1},{1,0},{2,3},{3,2},{4,5},{5,4},{6,7},{7,6},{8,9},{9,8},{10,11... | collective-permute-start | bytes 1572872 | tf_op jit(solution)/shard_map/ppermute | solution.py:850
  68.9 43.3 %collective-permute-start.4 = (bf16[256,1024]{1,0:T(8,128)(2,1)S(1)}, bf16[256,1024]{1,0:T(8,128)(2,1)}, u32[]{:S(2)}, u32[]{:S(2)}) collective-permute-start(bf16[256,1024]{1,0:T(8,128)(2,1)S(1)} %get-tuple-element.95.b_own_ref), channel_id=1, source_target_pairs={{0,1},{1,0},{2,3},{3,2},{4,5},{5,4},{6,7},{7,6},{8,9},{9,8},{10,11... | collective-permute-start | bytes 1572872 | tf_op jit(solution)/shard_map/ppermute | solution.py:850
  78.8 12.4 %copy-start.23 = (f32[256,1024]{1,0:T(8,128)}, f32[256,1024]{1,0:T(8,128)S(1)}, u32[]{:S(2)}) copy-start(f32[256,1024]{1,0:T(8,128)S(1)} %convert_add_fusion.2) | copy-start | bytes 3145732
  91.2 2.2 copy-start.15
  91.2 2.2 copy-start.18
  91.2 0.7 copy-start.40
  91.5 5.0 %copy-start.8 = (bf16[512,512]{1,0:T(8,128)(2,1)S(1)}, bf16[512,512]{1,0:T(8,128)(2,1)}, u32[]{:S(2)}) copy-start(bf16[512,512]{1,0:T(8,128)(2,1)} %copy-done.7) | copy-start | bytes 1572868
  93.4 30.0 %collective-permute-start.3 = (bf16[256,1024]{1,0:T(8,128)(2,1)}, bf16[256,1024]{1,0:T(8,128)(2,1)}, u32[]{:S(2)}, u32[]{:S(2)}) collective-permute-start(bf16[256,1024]{1,0:T(8,128)(2,1)} %get-tuple-element.120.own_ref), channel_id=1, source_target_pairs={{0,1},{1,0},{2,3},{3,2},{4,5},{5,4},{6,7},{7,6},{8,9},{9,8},{10,11... | collective-permute-start | bytes 1572872 | tf_op jit(solution)/shard_map/ppermute | solution.py:850
  95.8 2.0 copy-start.16
  95.8 2.0 copy-start.19
  97.5 42.3 %collective-permute-start.7 = (bf16[256,1024]{1,0:T(8,128)(2,1)}, bf16[256,1024]{1,0:T(8,128)(2,1)S(1)}, u32[]{:S(2)}, u32[]{:S(2)}) collective-permute-start(bf16[256,1024]{1,0:T(8,128)(2,1)} %get-tuple-element.121.own_ref), channel_id=1, source_target_pairs={{0,1},{1,0},{2,3},{3,2},{4,5},{5,4},{6,7},{7,6},{8,9},{9,8},{10,11... | collective-permute-start | bytes 1572872 | tf_op jit(solution)/shard_map/ppermute | solution.py:850
  139.8 0.8 copy-start.45
  157.0 229.5 %collective-permute-start.9 = (bf16[256,1024]{1,0:T(8,128)(2,1)}, bf16[256,1024]{1,0:T(8,128)(2,1)}, u32[]{:S(2)}, u32[]{:S(2)}) collective-permute-start(bf16[256,1024]{1,0:T(8,128)(2,1)} %get-tuple-element.57), channel_id=1, source_target_pairs={{0,1},{1,0},{2,3},{3,2},{4,5},{5,4},{6,7},{7,6},{8,9},{9,8},{10,11... | collective-permute-start | bytes 1572872 | tf_op jit(solution)/shard_map/ppermute | solution.py:850
  158.8 227.7 %collective-permute-start.5 = (bf16[256,1024]{1,0:T(8,128)(2,1)}, bf16[256,1024]{1,0:T(8,128)(2,1)}, u32[]{:S(2)}, u32[]{:S(2)}) collective-permute-start(bf16[256,1024]{1,0:T(8,128)(2,1)} %get-tuple-element.51), channel_id=1, source_target_pairs={{0,1},{1,0},{2,3},{3,2},{4,5},{5,4},{6,7},{7,6},{8,9},{9,8},{10,11... | collective-permute-start | bytes 1572872 | tf_op jit(solution)/shard_map/ppermute | solution.py:850
  159.1 9.6 %copy-start.33 = (f32[256,1024]{1,0:T(8,128)S(1)}, f32[256,1024]{1,0:T(8,128)}, u32[]{:S(2)}) copy-start(f32[256,1024]{1,0:T(8,128)} %get-tuple-element.62) | copy-start | bytes 3145732
  159.1 9.6 %copy-start.34 = (f32[256,1024]{1,0:T(8,128)S(1)}, f32[256,1024]{1,0:T(8,128)}, u32[]{:S(2)}) copy-start(f32[256,1024]{1,0:T(8,128)} %get-tuple-element.63) | copy-start | bytes 3145732
  168.6 1.5 copy-start.37
  168.6 1.5 copy-start.38
  168.6 3.6 copy-start.47
  170.1 2.3 copy-start.36
  180.0 196.8 %copy-start.12 = (bf16[512,1024]{1,0:T(8,128)(2,1)S(1)}, bf16[512,1024]{1,0:T(8,128)(2,1)}, u32[]{:S(2)}) copy-start(bf16[512,1024]{1,0:T(8,128)(2,1)} %param.14) | copy-start | bytes 3145732
  380.9 3.0 copy-start.24
  380.9 3.0 copy-start.25
  383.9 2.6 copy-start.17
  384.0 2.6 copy-start.20
  384.0 2.6 copy-start.22
  384.0 2.6 copy-start.32
  384.0 2.6 copy-start.43
  386.6 2.6 copy-start.44
  386.6 2.6 copy-start.41
  386.6 2.6 copy-start.42
  386.6 11.8 %copy-start.13 = (f32[2,256,1024]{2,1,0:T(8,128)S(1)}, f32[2,256,1024]{2,1,0:T(8,128)}, u32[]{:S(2)}) copy-start(f32[2,256,1024]{2,1,0:T(8,128)} %get-tuple-element.68) | copy-start | bytes 6291460
  389.1 4.0 collective-permute-start.10
  393.2 5.0 %collective-permute-start.11 = (f32[1,11392]{1,0:T(1,128)S(1)}, f32[1,11392]{1,0:T(1,128)S(1)}, u32[]{:S(2)}, u32[]{:S(2)}) collective-permute-start(f32[1,11392]{1,0:T(1,128)S(1)} %pad_maximum_fusion.11), channel_id=1, source_target_pairs={{0,16},{2,18},{4,20},{6,22},{8,24},{10,26},{12,28},{14,30},{16,0},... | collective-permute-start | bytes 136712 | tf_op jit(solution)/shard_map/ppermute | solution.py:853
  398.3 4.8 %copy-start.29 = (bf16[1024,512]{1,0:T(8,128)(2,1)S(1)}, bf16[1024,512]{1,0:T(8,128)(2,1)}, u32[]{:S(2)}) copy-start(bf16[1024,512]{1,0:T(8,128)(2,1)} %get-tuple-element.73) | copy-start | bytes 3145732
  398.3 4.8 %copy-start.30 = (bf16[1024,512]{1,0:T(8,128)(2,1)S(1)}, bf16[1024,512]{1,0:T(8,128)(2,1)}, u32[]{:S(2)}) copy-start(bf16[1024,512]{1,0:T(8,128)(2,1)} %get-tuple-element.74) | copy-start | bytes 3145732
  398.3 4.8 %copy-start.31 = (bf16[1024,512]{1,0:T(8,128)(2,1)S(1)}, bf16[1024,512]{1,0:T(8,128)(2,1)}, u32[]{:S(2)}) copy-start(bf16[1024,512]{1,0:T(8,128)(2,1)} %get-tuple-element.75) | copy-start | bytes 3145732
  398.3 4.6 %collective-permute-start.12 = (f32[2,11392]{1,0:T(2,128)S(1)}, f32[2,11392]{1,0:T(2,128)S(1)}, u32[]{:S(2)}, u32[]{:S(2)}) collective-permute-start(f32[2,11392]{1,0:T(2,128)S(1)} %pad_maximum_fusion.10), channel_id=1, source_target_pairs={{0,8},{2,10},{4,12},{6,14},{8,0},{10,2},{12,4},{14,6},{16,24},{18,... | collective-permute-start | bytes 273416 | tf_op jit(solution)/shard_map/ppermute | solution.py:853
  403.1 15.3 %collective-permute-start.13 = (f32[4,11392]{1,0:T(4,128)S(1)}, f32[4,11392]{1,0:T(4,128)S(1)}, u32[]{:S(2)}, u32[]{:S(2)}) collective-permute-start(f32[4,11392]{1,0:T(4,128)S(1)} %pad_maximum_fusion.9), channel_id=1, source_target_pairs={{0,4},{2,6},{4,0},{6,2},{8,12},{10,14},{12,8},{14,10},{16,20},{18,... | collective-permute-start | bytes 546824 | tf_op jit(solution)/shard_map/ppermute | solution.py:853
  403.2 3.7 copy-start.28
  403.2 5.3 %copy-start.27 = (bf16[1024,2048]{1,0:T(8,128)(2,1)S(1)}, bf16[1024,2048]{1,0:T(8,128)(2,1)}, u32[]{:S(2)}) copy-start(bf16[1024,2048]{1,0:T(8,128)(2,1)} %get-tuple-element.77) | copy-start | bytes 12582916
  408.5 4.5 %copy-start.26 = (bf16[2048,1024]{1,0:T(8,128)(2,1)S(1)}, bf16[2048,1024]{1,0:T(8,128)(2,1)}, u32[]{:S(2)}) copy-start(bf16[2048,1024]{1,0:T(8,128)(2,1)} %get-tuple-element.78) | copy-start | bytes 12582916
  418.6 2.3 collective-permute-start.14

commit v4 on v3

--- a/solution.py
+++ b/solution.py
@@ -498,14 +498,16 @@
 
 
 class Unit:
-    def __init__(self, part, out, row, rows, held, got, send, recv, local, place):
-        self.part, self.out, self.row, self.rows = part, out, row, rows
-        self.held, self.got, self.send, self.recv, self.local = held, got, send, recv, local
+    def __init__(self, part, out, column, got, send, recv, local, place):
+        self.part, self.out, self.got = part, out, got
+        self.send, self.recv, self.local = send, recv, local
+        self.rows, columns = 2 * got[0].shape[0], got[0].shape[1]
+        self.columns = pl.ds(column, columns)
         self.bit = [(place // (1 << b)) % 2 for b in range(EDGES)]
         self.partner = [place + (1 - 2 * self.bit[b]) * (1 << b) for b in range(EDGES)]
-        self.base = [row]
+        self.base = [0]
         for b in range(EDGES):
-            self.base.append(self.base[-1] + self.bit[b] * (rows >> (b + 1)))
+            self.base.append(self.base[-1] + self.bit[b] * (self.rows >> (b + 1)))
 
     def remote(self, src, dst, stage, b):
         return pltpu.make_async_remote_copy(
@@ -517,48 +519,30 @@
             device_id_type=MESH,
         )
 
-    def at(self, start, rows):
-        return pl.ds(pl.multiple_of(start, ADD_ROWS), rows)
-
     def halving(self, b):
         half = self.rows >> (b + 1)
-        if b == 0:
-            first = self.row if self.held is not None else 0
-            src = self.part.at[self.at(first + (1 - self.bit[0]) * half, half)]
-        else:
-            src = self.got[b - 1].at[self.at((1 - self.bit[b]) * half, half)]
-        return self.remote(src, self.got[b], b, b)
-
-    def keep(self):
-        half = self.rows // 2
-        return pltpu.make_async_copy(
-            self.part.at[self.at(self.row + self.bit[0] * half, half)], self.held, self.local.at[0]
-        )
+        source = self.part if b == 0 else self.got[b - 1]
+        away = pl.ds(pl.multiple_of((1 - self.bit[b]) * half, ADD_ROWS), half)
+        return self.remote(source.at[away], self.got[b], b, b)
+
+    def spot(self, b):
+        size = self.rows >> (b + 1)
+        return self.out.at[pl.ds(pl.multiple_of(self.base[b + 1], ADD_ROWS), size), self.columns]
 
     def own(self):
-        return pltpu.make_async_copy(
-            self.got[3], self.out.at[self.at(self.base[4], self.rows >> 4)], self.local.at[1]
-        )
+        return pltpu.make_async_copy(self.got[3], self.spot(3), self.local.at[0])
 
     def gathering(self, b):
-        size = self.rows >> (b + 1)
-        spot = self.out.at[self.at(self.base[b + 1], size)]
-        return self.remote(self.got[3] if b == 3 else spot, spot, 7 - b, b)
+        return self.remote(self.got[3] if b == 3 else self.spot(b), self.spot(b), 7 - b, b)
 
     def step(self, k):
         if k == 0:
             self.halving(0).start()
-            if self.held is not None:
-                self.keep().start()
         elif k < 5:
             b = k - 1
             self.halving(b).wait()
             half = self.rows >> (b + 1)
-            if b == 0 and self.held is not None:
-                self.keep().wait()
-                add_low(self.held, 0, self.got[0], half)
-            else:
-                add_low(self.part if b == 0 else self.got[b - 1], self.bit[b] * half, self.got[b], half)
+            add_low(self.part if b == 0 else self.got[b - 1], self.bit[b] * half, self.got[b], half)
             if b < 3:
                 self.halving(b + 1).start()
             else:
@@ -575,13 +559,12 @@
             self.gathering(0).wait()
 
 
-def unit_scratch(rows, columns, kept):
+def unit_scratch(rows, columns):
     return [
-        pltpu.VMEM((rows // 2 if kept else rows, columns), bf16),
         *[pltpu.VMEM((rows >> (b + 1), columns), bf16) for b in range(EDGES)],
         pltpu.SemaphoreType.DMA((2 * EDGES,)),
         pltpu.SemaphoreType.DMA((2 * EDGES,)),
-        pltpu.SemaphoreType.DMA((2,)),
+        pltpu.SemaphoreType.DMA((1,)),
     ]
 
 
@@ -592,31 +575,46 @@
     pl.semaphore_wait(barrier, len(targets))
 
 
+TURNS = (
+    (None, 7, 19, 26, 33, 40, 47, 62, 66),
+    (None, 11, 31, 38, 45, 52, 59, 76, 80),
+    (None, 16, 42, 49, 56, 63, 72, 92, 96),
+    (None, 23, 54, 61, 68, 75, 98, 114, 118),
+    (None, 59, 66, 71, 76, 81, 86, 104, 108),
+    (None, 84, 96, 101, 106, 111, 116, 134, 138),
+    (None, 86, 101, 106, 111, 116, 121, 140, 144),
+    (None, 88, 106, 111, 116, 121, 126, 146, 150),
+)
+WIDE = 512
+STEP_ROWS = 64
+
+
 def tail_kernel(
-    down_part, up_part, qkv_hbm, mixed_hbm, rows_hbm, w_qkv_hbm, w_out_hbm,
-    own_grad, got_grad, middle, out_grad, rows_of, lse, segr, segc, cosine, sine,
-    down_sum, up_sum, out_sum, q_sum, k_sum, v_sum, mid_grad, one_grad, col_sums,
-    qkv, mixed, rows_one, w_qkv, w_out, proj, mix_grad, d_qkv, dk, dv, kt, from_x, send_one, got_one,
-    load, x_send, x_recv, *more,
+    hidden, full_back, rows_two, grad_pre, qkv_hbm, mixed_a, mixed_b, rows_hbm, w_qkv_hbm, w_out_hbm,
+    grad_a, grad_b, got_a, got_b, mid_a, mid_b, proj_a, proj_b, tokens_hbm, cot_hbm,
+    rows_of, known, lse_a, lse_b, segr, segc, cosine, sine,
+    down_sum, up_sum, out_sum, q_sum, k_sum, v_sum, grad_x, everyone,
+    qkv, mixed, rows_one, w_qkv, w_out, proj, mix_grad, d_qkv, dk, dv, from_x, grads, middle, projected, tokens, cot,
+    part_a, part_b, part_c, part_d, part_e, col_sums, small, small_got,
+    load, x_send, x_recv, all_send, all_recv, *more,
 ):
     place, me = lax.axis_index("dp"), lax.axis_index("tensor")
-    length = rows_one.shape[0]
-    chunks, half, depth = got_grad.shape
+    length, depth = rows_one.shape
+    chunks, half, _ = from_x.shape
     chunk = 2 * half
     width = mixed.shape[1]
     pairs = width // PAIR
     across = {"tensor": 1 - me}
 
-    wide, deep = up_part.shape[0], down_part.shape[0]
     specs = [
-        (down_part, down_sum, 0, deep // 2), (down_part, down_sum, deep // 2, deep // 2),
-        (up_part, up_sum, 0, wide // 2), (up_part, up_sum, wide // 2, wide // 2),
-        (None, out_sum, 0, width), (None, v_sum, 0, depth), (None, k_sum, 0, depth), (None, q_sum, 0, depth),
+        (part_a, down_sum.at[pl.ds(0, depth)], 0), (part_b, down_sum.at[pl.ds(depth, depth)], 0),
+        (part_c, up_sum, 0), (part_d, up_sum, depth), (part_e, out_sum, 0),
+        (qkv.at[2], v_sum, 0), (qkv.at[1], k_sum, 0), (qkv.at[0], q_sum, 0),
     ]
     units = []
-    for i, (part, out, row, rows) in enumerate(specs):
-        own, *got, send, recv, local = more[8 * i : 8 * (i + 1)]
-        units.append(Unit(own if part is None else part, out, row, rows, None if part is None else own, got, send, recv, local, place))
+    for i, (part, out, column) in enumerate(specs):
+        *got, send, recv, local = more[7 * i : 7 * (i + 1)]
+        units.append(Unit(part, out, column, got, send, recv, local, place))
 
     def x_copy(src, dst, i):
         return pltpu.make_async_remote_copy(
@@ -624,22 +622,22 @@
             device_id=across, device_id_type=MESH,
         )
 
-    grads_in = [x_copy(got_grad.at[c], from_x.at[c], c) for c in range(chunks)]
-    projs = [x_copy(proj.at[c, :half], proj.at[c, half:], chunks + c) for c in range(chunks)]
-    ones = [x_copy(send_one.at[c], got_one.at[c], 2 * chunks + c) for c in range(chunks)]
-    loads = [
-        pltpu.make_async_copy(src, dst, load.at[i])
-        for i, (src, dst) in enumerate(
-            [(w_out_hbm, w_out), (mixed_hbm, mixed), (qkv_hbm, qkv), (rows_hbm, rows_one), (w_qkv_hbm, w_qkv)]
-        )
-    ]
-
-    late = [0, 5, 17, 24, 31, 38, 45, 65, 68]
-    turns = [(late[k] + (12 if k > 1 else 2) * i, k, i) for i in range(4) for k in range(STEPS)]
-    turns += [(t, k, 4) for k, t in enumerate([None, 47, 60, 66, 72, 78, 84, 104, 107]) if k]
-    for i in range(3):
-        turns += [(t + (6 if k > 1 else 3) * i, k, 5 + i) for k, t in enumerate([None, 88, 100, 106, 112, 118, 124, 134, 138]) if k]
-    turns = sorted(turns)
+    each = range(chunks)
+    grads_in = [x_copy((got_a, got_b)[c], from_x.at[c], c) for c in each]
+    projs = [x_copy(proj.at[c, :half], proj.at[c, half:], chunks + c) for c in each]
+    ones = [x_copy(proj.at[c, :half], from_x.at[c], 2 * chunks + c) for c in each]
+    smalls = x_copy(small, small_got, 3 * chunks)
+    partner = units[0].partner
+
+    loads = []
+
+    def fetch(src, dst):
+        copy = pltpu.make_async_copy(src, dst, load.at[len(loads)])
+        copy.start()
+        loads.append(copy)
+        return copy
+
+    turns = sorted((t, k, i) for i, times in enumerate(TURNS) for k, t in enumerate(times) if k)
     done = [0]
 
     def until(time):
@@ -648,72 +646,108 @@
             units[i].step(k)
             done[0] += 1
 
-    greet([*[{"dp": partner} for partner in units[0].partner], across])
-    for c in range(chunks):
-        grads_in[c].start()
-    until(4)
-    for copy in loads:
-        copy.start()
-
-    gain, scale, gate = rows_of[0:1, :], rows_of[1:2, :], rows_of[2:3, :]
-    step_rows = 64
-
-    def norm_back(c):
-        grads_in[c].wait()
-
-        @pl.loop(0, half // step_rows)
+    greet([*[{"dp": p} for p in partner], across])
+    grads_in[0].start()
+    slots = [w_qkv.at[0], w_qkv.at[1], w_qkv.at[2], d_qkv.at[2]]
+    cut = lambda t: slice(t * WIDE, (t + 1) * WIDE)
+    backs = fetch(full_back, rows_one)
+    hiddens = [fetch(hidden.at[:, cut(t)], slots[t]) for t in range(4)]
+    norms = [
+        [fetch(src, dst.at[c]) for src, dst in (
+            ((grad_a, grad_b)[c], grads), ((mid_a, mid_b)[c], middle), ((proj_a, proj_b)[c], projected),
+            (tokens_hbm.at[c * half : (c + 1) * half], tokens), (cot_hbm.at[c * half : (c + 1) * half], cot),
+        )]
+        for c in each
+    ]
+    twos = [fetch(rows_two.at[:, cut(t)], d_qkv.at[t]) for t in range(2)]
+    col_sums[...] = jnp.zeros(col_sums.shape, f32)
+
+    backs.wait()
+    pres = []
+    for t in range(4):
+        hiddens[t].wait()
+        part = (part_a, part_b)[t // 2]
+
+        @pl.loop(0, WIDE // 256)
+        def _(r):
+            at = pl.ds(pl.multiple_of(r * 256, 256), 256)
+            to = pl.ds(pl.multiple_of((t % 2) * WIDE + r * 256, 256), 256)
+            part[to, :] = mm(slots[t][:, at], rows_one[...], 0, 0).astype(bf16)
+
+        pres.append(fetch(grad_pre.at[:, cut(t)], slots[t]))
+        if t % 2:
+            units[t // 2].step(0)
+            until(4 + 4 * (t // 2))
+    main = [
+        fetch(w_out_hbm, w_out), fetch(mixed_a, mixed.at[:chunk]), fetch(mixed_b, mixed.at[chunk:]),
+        fetch(qkv_hbm, qkv), fetch(rows_hbm, rows_one),
+    ]
+
+    def up_part(t):
+        pres[t].wait()
+        part = (part_c, part_d)[t // 2]
+
+        @pl.loop(0, depth // 256)
+        def _(r):
+            to = pl.ds(pl.multiple_of(r * 256, 256), 256)
+            at = pl.ds(pl.multiple_of((r % 2) * 256, 256), 256)
+            part[to, cut(t % 2)] = mm(d_qkv[r // 2, :, at], slots[t][...], 0, 0).astype(bf16)
+
+    def fold(row, values):
+        col_sums[row : row + 1, :] += jnp.sum(values, axis=0, keepdims=True)
+
+    def norm_back(grad, values, weight):
+        center = values - jnp.mean(values, axis=1, keepdims=True)
+        root = lax.rsqrt(jnp.mean(center * center, axis=1, keepdims=True) + norm_eps)
+        normal = center * root
+        inner = grad * weight
+        back = inner - jnp.mean(inner, axis=1, keepdims=True) - normal * jnp.mean(inner * normal, axis=1, keepdims=True)
+        return root * back, normal
+
+    gain_two, scale_m, gate_a, gain_one, scale_a = [rows_of[r : r + 1, :] for r in range(5)]
+
+    def second_norm(c):
+        for copy in norms[c]:
+            copy.wait()
+
+        @pl.loop(0, half // STEP_ROWS)
         def _(i):
-            at = pl.ds(pl.multiple_of(i * step_rows, step_rows), step_rows)
-            grad = own_grad[c, at, :] + from_x[c, at, :].astype(f32)
-            values = middle[c, at, :]
-            center = values - jnp.mean(values, axis=1, keepdims=True)
-            root = lax.rsqrt(jnp.mean(center * center, axis=1, keepdims=True) + norm_eps)
-            normal = center * root
-            inner = grad * (gain * (1.0 + scale))
-            back = root * (
-                inner - jnp.mean(inner, axis=1, keepdims=True) - normal * jnp.mean(inner * normal, axis=1, keepdims=True)
-            )
-            total = back + out_grad[c, at, :].astype(f32)
-            mid_grad[c, at, :] = total
-            proj[c, at, :] = (total * gate).astype(bf16)
-            shifted = jnp.sum(grad, axis=0, keepdims=True)
-            scaled = jnp.sum(grad * normal, axis=0, keepdims=True)
-            both = jnp.concatenate([shifted, scaled, jnp.zeros((6, depth), f32)], axis=0)
-            if c == 0:
-                fresh = jnp.where(i == 0, jnp.zeros_like(both), col_sums[...])
-                col_sums[...] = fresh + both
-            else:
-                col_sums[...] += both
+            at = pl.ds(pl.multiple_of(i * STEP_ROWS, STEP_ROWS), STEP_ROWS)
+            grad = grads[c, at, :] + from_x[c, at, :].astype(f32)
+            back, normal = norm_back(grad, middle[c, at, :], gain_two * (1.0 + scale_m))
+            total = back + cot[c, at, :].astype(f32)
+            grads[c, at, :] = total
+            proj[c, at, :] = (total * gate_a).astype(bf16)
+            fold(0, grad)
+            fold(1, grad * normal)
+            fold(2, total * projected[c, at, :])
 
         projs[c].start()
 
-    norm_back(0)
-    until(20)
-    norm_back(1)
-    until(28)
-    loads[0].wait()
-    for c in range(chunks):
-        projs[c].wait()
-        mix_grad[c * chunk : (c + 1) * chunk, :] = mm(proj[c], w_out[...], 1, 1).astype(bf16)
-        until(32 + 10 * c)
-
-    loads[1].wait()
-    out_part = units[4].part
-    for r in range(0, width, 256):
-        out_part[r : r + 256, :] = (
-            mm(mixed[:chunk, r : r + 256], proj[0], 0, 0) + mm(mixed[chunk:, r : r + 256], proj[1], 0, 0)
-        ).astype(bf16)
-    units[4].step(0)
-    until(46)
-
-    loads[2].wait()
+    for copy in twos:
+        copy.wait()
+    up_part(0)
+    up_part(1)
+    units[2].step(0)
+    grads_in[0].wait()
+    grads_in[1].start()
+    second_norm(0)
+    until(16)
+    up_part(2)
+    up_part(3)
+    units[3].step(0)
+    weights = fetch(w_qkv_hbm, w_qkv)
+    until(23)
+    grads_in[1].wait()
+    second_norm(1)
+    until(32)
 
     def turn_back(u, rows):
         return (u * cosine[rows, :] - turned(u) * sine[rows, :]).astype(bf16)
 
     def attend_back(p, c):
         lanes = pl.ds(pl.multiple_of(p * PAIR, PAIR), PAIR)
-        rows = pl.ds(pl.multiple_of(c * chunk, chunk), chunk)
+        rows = slice(c * chunk, (c + 1) * chunk)
         q, g = qkv[0, rows, lanes], mix_grad[rows, lanes]
         both = (g.astype(f32) * mixed[rows, lanes].astype(f32)).T
         qh = [head_lanes(q, h) for h in range(2)]
@@ -730,116 +764,158 @@
             ps, ds = [], []
             for h in range(2):
                 s = jnp.where(same, mm(k, qh[h], 1, 1), masked_score)
-                pr = jnp.exp(s - lse[c, 2 * p + h])
+                pr = jnp.exp(s - (lse_a, lse_b)[c][2 * p + h])
                 d = (pr * (mm(v, gh[h], 1, 1) - delta[h])).astype(bf16)
                 ps.append(pr.astype(bf16))
                 ds.append(d)
                 dq[h] = dq[h] + mm(turned_k[h * HEAD : (h + 1) * HEAD, :], d, 1, 0)
             add_v = mm(jnp.concatenate(ps, axis=1), g_two, 1, 0)
             add_k = mm(jnp.concatenate(ds, axis=1), q_two, 1, 0)
-            dv[cols, :] = jnp.where(c == 0, 0.0, dv[cols, :]) + add_v
-            dk[cols, :] = jnp.where(c == 0, 0.0, dk[cols, :]) + add_k
+            if c < chunks - 1:
+                dv[cols, lanes] = add_v if c == 0 else dv[cols, lanes] + add_v
+                dk[cols, lanes] = add_k if c == 0 else dk[cols, lanes] + add_k
+            else:
+                d_qkv[1, cols, lanes] = turn_back(dk[cols, lanes] + add_k, cols)
+                d_qkv[2, cols, lanes] = (dv[cols, lanes] + add_v).astype(bf16)
         d_qkv[0, rows, lanes] = turn_back(jnp.concatenate(dq, axis=0).T * (HEAD**-0.5), rows)
 
-        @pl.when(c == chunks - 1)
-        def _():
-            @pl.loop(0, length // BLOCK)
-            def _(b):
-                at = pl.ds(pl.multiple_of(b * BLOCK, BLOCK), BLOCK)
-                d_qkv[1, at, lanes] = turn_back(dk[at, :], at)
-                d_qkv[2, at, lanes] = dv[at, :].astype(bf16)
-
-    @pl.loop(0, pairs * chunks)
-    def _(i):
-        attend_back(i // chunks, i % chunks)
-        for n in range(pairs * chunks):
-
-            @pl.when(i == n)
-            def _():
-                until(50 + 4.5 * n)
-
-    loads[4].wait()
+    for copy in main:
+        copy.wait()
+    clock = 36
+    for c in each:
+        projs[c].wait()
+        mix_grad[c * chunk : (c + 1) * chunk, :] = mm(proj[c], w_out[...], 1, 1).astype(bf16)
+        if c == chunks - 1:
+
+            @pl.loop(0, width // 256)
+            def _(r):
+                at = pl.ds(pl.multiple_of(r * 256, 256), 256)
+                part_e[at, :] = sum(
+                    mm(mixed[n * chunk : (n + 1) * chunk, at], proj[n], 0, 0) for n in each
+                ).astype(bf16)
+
+            units[4].step(0)
+            clock += 3
+        until(clock)
+
+        @pl.loop(0, pairs)
+        def _(p):
+            attend_back(p, c)
+            for n in range(pairs):
+
+                @pl.when(p == n)
+                def _():
+                    until(clock + 4.4 * (n + 1))
+
+        clock += 19
 
     def rows_back(start):
         at = slice(start, start + half)
-        return (
-            mm(d_qkv[0, at, :], w_qkv[0], 1, 1) + mm(d_qkv[1, at, :], w_qkv[1], 1, 1) + mm(d_qkv[2, at, :], w_qkv[2], 1, 1)
-        )
-
-    for c in range(chunks):
-        send_one[c] = rows_back(c * chunk + half).astype(bf16)
-        ones[c].start()
-    until(83)
-    loads[3].wait()
+        return sum(mm(d_qkv[t, at, :], w_qkv[t], 1, 1) for t in range(3))
+
+    weights.wait()
+    for c in each:
+        proj[c, :half] = rows_back(c * chunk + half).astype(bf16)
+        if c == 0:
+            ones[c].start()
+        until(clock + 2 * (c + 1))
     for i in range(3):
-        part = units[5 + i].part
 
         @pl.loop(0, depth // 256)
         def _(r):
             at = pl.ds(pl.multiple_of(r * 256, 256), 256)
-            part[at, :] = mm(rows_one[:, at], d_qkv[2 - i], 0, 0).astype(bf16)
+            qkv[2 - i, at, :] = mm(rows_one[:, at], d_qkv[2 - i], 0, 0).astype(bf16)
 
         units[5 + i].step(0)
-        until(87 + 3 * i)
-    for c in range(chunks):
-        one_grad[c] = rows_back(c * chunk)
-        until(97 + 3 * c)
-    for c in range(chunks):
+        until(clock + 6 + 2 * i)
+    for c in each:
+        middle[c] = rows_back(c * chunk)
+
+    for c in each:
         ones[c].wait()
-        one_grad[c] = one_grad[c] + got_one[c].astype(f32)
-        until(108 + 3 * c)
+        if c < chunks - 1:
+            ones[c + 1].start()
+
+        @pl.loop(0, half // STEP_ROWS)
+        def _(i):
+            at = pl.ds(pl.multiple_of(i * STEP_ROWS, STEP_ROWS), STEP_ROWS)
+            grad = middle[c, at, :] + from_x[c, at, :].astype(f32)
+            back, normal = norm_back(grad, tokens[c, at, :].astype(f32), gain_one * (1.0 + scale_a))
+            grad_x[c, at, :] = (back + grads[c, at, :]).astype(bf16)
+            fold(3, grad)
+            fold(4, grad * normal)
+
+        until(100 + 10 * c)
+
+    shift, scaled, gated, shift_one, scaled_one = [col_sums[r : r + 1, :] for r in range(5)]
+    small[...] = known[...] + jnp.concatenate(
+        [
+            shift_one, gain_one * scaled_one, gated, shift, gain_two * scaled, jnp.zeros_like(shift),
+            (1.0 + scale_a) * scaled_one, (1.0 + scale_m) * scaled, jnp.zeros((8, depth), f32),
+        ],
+        axis=0,
+    )
+    smalls.start()
+    until(112)
+    smalls.wait()
+    number = lax.broadcasted_iota(jnp.int32, small.shape, 0)
+    everyone[0] = small[...] + jnp.where(number < 9, small_got[...], 0.0)
+    for n, b in enumerate(reversed(range(EDGES))):
+        copy = pltpu.make_async_remote_copy(
+            src_ref=everyone.at[pl.ds(0, 1 << n)], dst_ref=everyone.at[pl.ds(1 << n, 1 << n)],
+            send_sem=all_send.at[n], recv_sem=all_recv.at[n],
+            device_id={"dp": partner[b]}, device_id_type=MESH,
+        )
+        copy.start()
+        until(117 + 6 * n)
+        copy.wait()
     until(1000)
 
 
-def tail(down_part, up_part, qkv, mixed, rows_one, w_qkv, w_out, own_grad, got_grad, middle, out_grad, rows_of, lse, segr, segc, cosine, sine):
+def tail(
+    hidden, full_back, rows_two, grad_pre, qkv, mixed, rows_one, w_qkv, w_out, own_grad, got_grad, middle, projected,
+    tokens, cot, rows_of, known, lse, segr, segc, cosine, sine,
+):
     _, length, width = qkv.shape
-    chunks, half, depth = got_grad.shape
+    chunks = len(mixed)
+    half, depth = got_grad[0].shape
     anywhere, near = pl.BlockSpec(memory_space=pl.ANY), pl.BlockSpec(memory_space=pltpu.VMEM)
-    shaped = jax.ShapeDtypeStruct
-    (deep, _), (_, wide) = down_part.shape, up_part.shape
+    shaped, kept = jax.ShapeDtypeStruct, pltpu.VMEM
+    in_chunks = (chunks, half, depth)
     scratch = [
-        pltpu.VMEM(qkv.shape, bf16),
-        pltpu.VMEM(mixed.shape, bf16),
-        pltpu.VMEM(rows_one.shape, bf16),
-        pltpu.VMEM(w_qkv.shape, bf16),
-        pltpu.VMEM(w_out.shape, bf16),
-        pltpu.VMEM((chunks, 2 * half, depth), bf16),
-        pltpu.VMEM((length, width), bf16),
-        pltpu.VMEM((3, length, width), bf16),
-        pltpu.VMEM((length, PAIR), f32),
-        pltpu.VMEM((length, PAIR), f32),
-        pltpu.VMEM((8, 128), f32),
-        pltpu.VMEM(got_grad.shape, bf16),
-        pltpu.VMEM(got_grad.shape, bf16),
-        pltpu.VMEM(got_grad.shape, bf16),
-        pltpu.SemaphoreType.DMA((5,)),
-        pltpu.SemaphoreType.DMA((3 * chunks,)),
-        pltpu.SemaphoreType.DMA((3 * chunks,)),
-        *unit_scratch(deep // 2, depth, True) * 2,
-        *unit_scratch(depth // 2, wide, True) * 2,
-        *unit_scratch(width, depth, False),
-        *unit_scratch(depth, width, False) * 3,
+        kept(qkv.shape, bf16), kept((length, width), bf16), kept(rows_one.shape, bf16), kept(w_qkv.shape, bf16),
+        kept(w_out.shape, bf16), kept((chunks, 2 * half, depth), bf16), kept((length, width), bf16),
+        kept((3, length, width), bf16), kept((length, width), f32), kept((length, width), f32),
+        kept(in_chunks, bf16), kept(in_chunks, f32), kept(in_chunks, f32), kept(in_chunks, f32),
+        kept(in_chunks, bf16), kept(in_chunks, bf16),
+        *[kept((depth, depth), bf16)] * 4, kept((width, depth), bf16),
+        kept((8, depth), f32), kept(known.shape, f32), kept(known.shape, f32),
+        pltpu.SemaphoreType.DMA((27,)),
+        pltpu.SemaphoreType.DMA((3 * chunks + 1,)), pltpu.SemaphoreType.DMA((3 * chunks + 1,)),
+        pltpu.SemaphoreType.DMA((EDGES,)), pltpu.SemaphoreType.DMA((EDGES,)),
+        *unit_scratch(depth, depth) * 4, *unit_scratch(width, depth), *unit_scratch(depth, width) * 3,
     ]
     return pl.pallas_call(
         tail_kernel,
-        in_specs=[anywhere] * 7 + [near] * 10,
-        out_specs=[anywhere] * 6 + [near] * 3,
+        in_specs=[anywhere] * 20 + [near] * 8,
+        out_specs=[anywhere] * 6 + [near] * 2,
         out_shape=[
-            shaped(down_part.shape, bf16), shaped(up_part.shape, bf16), shaped((width, depth), bf16),
+            shaped((hidden.shape[1], depth), bf16), shaped((depth, hidden.shape[1]), bf16), shaped((width, depth), bf16),
             *[shaped((depth, width), bf16)] * 3,
-            shaped(got_grad.shape, f32), shaped(got_grad.shape, f32), shaped((8, depth), f32),
+            shaped(in_chunks, bf16), shaped((1 << EDGES, *known.shape), f32),
         ],
         scratch_shapes=scratch,
         compiler_params=pltpu.CompilerParams(collective_id=1, has_side_effects=True, vmem_limit_bytes=61 << 20),
         name="tail",
-    )(down_part, up_part, qkv, mixed, rows_one, w_qkv, w_out, own_grad, got_grad, middle, out_grad, rows_of, lse, segr, segc, cosine, sine)
+    )(
+        hidden, full_back, rows_two, grad_pre, qkv, *mixed, rows_one, w_qkv, w_out, *own_grad, *got_grad, *middle,
+        *projected, tokens, cot, rows_of, known, *lse, segr, segc, cosine, sine,
+    )
 
 
 def body_pair(
     tokens, cond, doc_lengths, w_ada, b_ada, gain_one, w_qkv, w_out, gain_two, w_up, b_up, w_down, b_down, cotangent
 ):
-    dp_size = lax.axis_size("dp")
-    bits = dp_size.bit_length() - 1
     own, width = tokens.shape
     length = 2 * own
     chunks = 2
@@ -848,14 +924,6 @@
 
     def swap(values):
         return lax.ppermute(values, "tensor", [(0, 1), (1, 0)])
-
-    def across(values, b):
-        return lax.ppermute(values, "dp", [(d, d ^ (1 << b)) for d in range(dp_size)])
-
-    def gathered(row):
-        for b in reversed(range(bits)):
-            row = jnp.concatenate([row, across(row, b)], axis=0)
-        return row
 
     step = jnp.arange(length, dtype=jnp.int32)
     in_chunk = step % chunk
@@ -900,49 +968,36 @@
         pieces.append(rest)
     rows_two, hidden, grad_pre = state
     grad_b_up = sum(pieces[c][4] for c in each)[0]
-    grad_w_down = mm(hidden, full_back, 0, 0).astype(bf16)
-    grad_w_up = mm(rows_two, grad_pre, 0, 0).astype(bf16)
     branch = [pieces[c][2] + swap(pieces[c][3]).astype(f32) + b_down for c in each]
     output = jnp.concatenate([(middle[c] + gate_m * branch[c]).astype(bf16) for c in each], axis=0)
     grad_gate_m = sum(jnp.sum(grad_out[c] * branch[c], axis=0) for c in each)
     grad_b_down = sum(jnp.sum(back[c].astype(f32), axis=0) for c in each)
 
-    in_chunks = (chunks, half, width)
-    *sums, grad_middle, grad_act_one, columns = tail(
-        grad_w_down, grad_w_up, qkv, jnp.concatenate(mixed, axis=0), rows_one, w_qkv, w_out,
-        jnp.stack([pieces[c][0] for c in each]), jnp.stack([pieces[c][1] for c in each]),
-        jnp.stack(middle), cotangent.reshape(in_chunks), jnp.stack([gain_two, scale_m, gate_a] + [gate_a] * 5),
-        jnp.stack(lse), seg_rows, seg_cols, cosine, sine,
+    none = jnp.zeros((width,), f32)
+    known = jnp.stack(
+        [
+            none, none, none, none, none, grad_gate_m, none, none, grad_b_down,
+            grad_b_up[:width], grad_b_up[width:],
+            jnp.pad(cond[0].astype(f32), (0, width - cond.shape[1])), none, none, none, none,
+        ]
+    )
+    *sums, grad_x, everyone = tail(
+        hidden, full_back, rows_two, grad_pre, qkv, mixed, rows_one, w_qkv, w_out,
+        [pieces[c][0] for c in each], [pieces[c][1] for c in each], middle, projected, tokens, cotangent,
+        jnp.stack([gain_two, scale_m, gate_a, gain_one, scale_a, none, none, none]), known,
+        lse, seg_rows, seg_cols, cosine, sine,
     )
     grad_w_down, grad_w_up, grad_w_out, grad_q, grad_k, grad_v = [s.astype(f32) for s in sums]
     grad_w_qkv = jnp.stack([grad_q, grad_k, grad_v])
-    grad_middle, grad_act_one = grad_middle.reshape(own, width), grad_act_one.reshape(own, width)
-    grad_shift_m, grad_scale_m, grad_gain_two = columns[0], columns[1] * gain_two, columns[1] * (1.0 + scale_m)
-    grad_gate_a = jnp.sum(grad_middle * jnp.concatenate(projected, axis=0), axis=0)
-
-    x_all = tokens.astype(f32)
-    _, first_back = jax.vjp(modulate, x_all, gain_one, shift_a, scale_a)
-    grad_x, grad_gain_one, grad_shift_a, grad_scale_a = first_back(grad_act_one)
-    grad_x = (grad_x + grad_middle).astype(bf16)
-
-    small = jnp.concatenate(
-        [
-            grad_shift_a, grad_scale_a, grad_gate_a, grad_shift_m, grad_scale_m, grad_gate_m,
-            grad_gain_one, grad_gain_two, grad_b_down,
-        ]
-    )[None, :]
-    small = small + swap(small)
-    mod_size = modulation.shape[0]
-    grad_mod = small[0, :mod_size]
-    grad_cond = jnp.dot(w_ada.astype(f32), grad_mod, precision=lax.Precision.HIGHEST)[None, :]
-    everyone = gathered(jnp.concatenate([small, grad_b_up[None, :], cond.astype(f32)], axis=1))
-    conds = everyone[:, -cond.shape[1] :]
-    mods = everyone[:, :mod_size]
+    grad_x = grad_x.reshape(own, width)
+    mods = everyone[:, :6].reshape(-1, 6 * width)
+    conds = everyone[:, 11, : cond.shape[1]]
+    grad_cond = jnp.dot(w_ada.astype(f32), mods[0], precision=lax.Precision.HIGHEST)[None, :]
     grad_w_ada = jnp.einsum("nc,nm->cm", conds, mods, precision=lax.Precision.HIGHEST, preferred_element_type=f32)
-    sums = jnp.sum(everyone, axis=0)
-    grad_b_ada = sums[:mod_size]
-    grad_gain_one, grad_gain_two, grad_b_down = jnp.split(sums[mod_size : mod_size + 3 * width], 3)
-    grad_b_up = sums[mod_size + 3 * width : -cond.shape[1]]
+    total = jnp.sum(everyone, axis=0)
+    grad_b_ada = total[:6].reshape(-1)
+    grad_gain_one, grad_gain_two, grad_b_down = total[6], total[7], total[8]
+    grad_b_up = total[9:11].reshape(-1)
     return (
         output, grad_x, grad_cond, grad_w_ada, grad_b_ada, grad_gain_one, grad_w_qkv, grad_w_out, grad_gain_two,
         grad_w_up, grad_b_up, grad_w_down, grad_b_down,

time: 434 us -> 380 us (0.88)
  matrix products: 27.2 us -> 10 us
  waiting for transfers between devices: 75.8 us -> 58.8 us
  other arithmetic: 43.8 us -> 34.5 us
  Pallas kernels: 258 us -> 249 us
    dot_general x3 -> x1, matrix products: 18.9 us -> 1.84 us  [body_pair(): jnp.dot(w_ada.astype(f32), mods[0], precision=lax.Precision.HIGHEST)]
    ppermute x11 -> x10, waiting for transfers between devices: 68.1 us -> 58.8 us  [swap(): return lax.ppermute(values, 'tensor', [(0, 1), (1, 0)])]
    pallas_call x1, Pallas kernels: 197 us -> 188 us  [tail(): pl.pallas_call(tail_kernel, in_specs=[anywhere] * 20 + [near] * 8, out_sp...]
    ppermute x4 -> x0, waiting for transfers between devices: 7.7 us -> none  [across(): return lax.ppermute(values, 'dp', [(d, d ^ 1 << b) for d in range(dp_size)])]
    reduce_sum x8 -> x1, other arithmetic: 6.83 us -> 1.29 us  [body_pair(): total = jnp.sum(everyone, axis=0)]
    another operation x4 -> x1, other arithmetic: 4.63 us -> 0.01 us  [body_pair(): jnp.stack([none, none, none, none, none, grad_gate_m, none, none, grad_b_...]
    ppermute x11 -> x10, starting transfers between devices: 11.3 us -> 14.3 us  [swap(): return lax.ppermute(values, 'tensor', [(0, 1), (1, 0)])]
  transfers between devices with their start and end apart: 15 -> 10, of which waited for: 8 -> 8; matrix products, arithmetic and copies ran while one was open for 14% -> 3% of each run, Pallas kernels for 51% -> 10%
where the time goes in v4:
time: 380 us; the launch traced here: 379 us
  Pallas kernels  249 us (66%)
  waiting for transfers between devices  58.8 us (15%)
  other arithmetic  34.5 us (9%)
  starting transfers between devices  14.3 us (4%)
  local copies, waits for them, and re-layouts  10.7 us (3%)
  matrix products  10 us (3%)
    pallas_call x1, Pallas kernels, tail(): pl.pallas_call(tail_kernel, in_specs=[anywhere] * 20 + [near] * 8, out_sp...  188 us
    ppermute x10, waiting for transfers between devices, swap(): return lax.ppermute(values, 'tensor', [(0, 1), (1, 0)])  58.8 us
    pallas_call x2, Pallas kernels, mlp_pair(): pl.pallas_call(mlp_kernel, grid=(width // tile,), in_specs=[small, small,...  32.6 us
    pallas_call x2, Pallas kernels, attend_forward_pair(): pl.pallas_call(forward_chunk_kernel, grid=(pairs,), in_specs=[*pair_piece...  18.8 us
    ppermute x10, starting transfers between devices, swap(): return lax.ppermute(values, 'tensor', [(0, 1), (1, 0)])  14.3 us
    convert_element_type x3, other arithmetic, body_pair(): s.astype(f32)  12.8 us
    pallas_call x2, Pallas kernels, project_pair(): pl.pallas_call(qkv_pair_kernel, grid=(3,), in_specs=[pl.BlockSpec((half,...  10.1 us
  transfers between devices with their start and end apart: 10, of which 8 were waited for; matrix products, arithmetic and copies ran while one was open for 3% of the time, Pallas kernels for 10%

profile of v4, /device:TPU:0, one launch (start us, length us, event | category | flops | bytes accessed | tf_op | source)
XLA Modules:
  0.0 379.0 jit_solution(423409038463498542)
XLA Ops:
  0.7 1.6 convert_reduce_fusion.1
  2.3 1.6 fusion.9
  3.9 1.0 fusion.39
  4.9 1.5 fusion.13
  6.4 2.9 collective-permute-start.1
  9.4 0.1 select_reduce_fusion.2
  9.7 1.9 multiply_sine_fusion
  11.6 0.9 pad_maximum_fusion.2
  12.5 9.9 %collective-permute-done.1.got_ref = bf16[256,1024]{1,0:T(8,128)(2,1)} collective-permute-done((bf16[256,1024]{1,0:T(8,128)(2,1)}, bf16[256,1024]{1,0:T(8,128)(2,1)}, u32[]{:S(2)}, u32[]{:S(2)}) %collective-permute-start.1) | collective-permute-done | bytes 524320 | tf_op jit(solution)/shard_map/ppermute | solution.py:926
  22.4 5.3 %qkv.2 = (bf16[3,1024,512]{2,1,0:T(8,128)(2,1)S(1)}, bf16[1024,1024]{1,0:T(8,128)(2,1)S(1)}) custom-call(bf16[256,1024]{1,0:T(8,128)(2,1)} %get-tuple-element.95.own_ref, bf16[256,1024]{1,0:T(8,128)(2,1)} %collective-permute-done.1.got_ref, bf16[3,1024,512]{2,1,0:T(8,128)(2,1)S(1)} %copy-done.1, f32[1024,128]{1,0:T(8,128)S(1)} %get-tuple-element.121.cos_ref.cosine, ...), custom_call_target="tpu_custom_call" | custom-call | flops 1610612736 | bytes 4194304 | tf_op jit(solution)/shard_map/qkv/pallas_call | solution.py:309
  27.7 5.1 %collective-permute-done.got_ref = bf16[256,1024]{1,0:T(8,128)(2,1)} collective-permute-done((bf16[256,1024]{1,0:T(8,128)(2,1)}, bf16[256,1024]{1,0:T(8,128)(2,1)}, u32[]{:S(2)}, u32[]{:S(2)}) %collective-permute-start) | collective-permute-done | bytes 524320 | tf_op jit(solution)/shard_map/ppermute | solution.py:926
  32.8 4.8 %qkv.3 = (bf16[3,1024,512]{2,1,0:T(8,128)(2,1)S(1)}, bf16[1024,1024]{1,0:T(8,128)(2,1)S(1)}) custom-call(bf16[256,1024]{1,0:T(8,128)(2,1)} %get-tuple-element.96.own_ref, bf16[256,1024]{1,0:T(8,128)(2,1)} %collective-permute-done.got_ref, bf16[3,1024,512]{2,1,0:T(8,128)(2,1)S(1)} %copy-done.1, ...), custom_call_target="tpu_custom_call", output_to_operand_aliasing={{0}: (5, {}), {1}: (6, {})} | custom-call | flops 1610612736 | bytes 4194304 | tf_op jit(solution)/shard_map/qkv/pallas_call | solution.py:309
  37.7 1.4 copy-done.3
  39.1 0.2 broadcast_in_dim.25.segc_ref.segc
  39.3 9.4 %attend.3 = (bf16[512,512]{1,0:T(8,128)(2,1)S(1)}, f32[8,1,512]{2,1,0:T(1,128)S(1)}) custom-call(bf16[3,1024,512]{2,1,0:T(8,128)(2,1)S(1)} %get-tuple-element.47.q_ref.k_ref.v_ref.qkv_hbm, bf16[3,1024,512]{2,1,0:T(8,128)(2,1)S(1)} %get-tuple-element.47.q_ref.k_ref.v_ref.qkv_hbm, bf16[3,1024,512]{2,1,0:T(8,128)(2,1)S(1)} %get-tuple-element.47.q_ref.k_ref.v_ref.qkv_hbm, ...), custom_call_target="tpu_custom_call" | custom-call | flops 4294967296 | bytes 4194304 | tf_op jit(solution)/shard_map/attend/pallas_call | solution.py:371
  48.7 9.4 %attend.2 = (bf16[512,512]{1,0:T(8,128)(2,1)S(1)}, f32[8,1,512]{2,1,0:T(1,128)S(1)}) custom-call(bf16[3,1024,512]{2,1,0:T(8,128)(2,1)S(1)} %get-tuple-element.47.q_ref.k_ref.v_ref.qkv_hbm, bf16[3,1024,512]{2,1,0:T(8,128)(2,1)S(1)} %get-tuple-element.47.q_ref.k_ref.v_ref.qkv_hbm, bf16[3,1024,512]{2,1,0:T(8,128)(2,1)S(1)} %get-tuple-element.47.q_ref.k_ref.v_ref.qkv_hbm, ...), custom_call_target="tpu_custom_call" | custom-call | flops 4294967296 | bytes 4194304 | tf_op jit(solution)/shard_map/attend/pallas_call | solution.py:371
  58.2 0.4 convolution_convert_fusion
  58.6 1.8 collective-permute-start.6
  60.4 0.4 convolution_convert_fusion.1
  60.9 0.3 collective-permute-start.2
  61.2 1.3 convert_reduce_fusion.3
  62.5 1.7 collective-permute-start.4
  64.2 9.3 %collective-permute-done.6 = bf16[256,1024]{1,0:T(8,128)(2,1)S(1)} collective-permute-done((bf16[256,1024]{1,0:T(8,128)(2,1)S(1)}, bf16[256,1024]{1,0:T(8,128)(2,1)S(1)}, u32[]{:S(2)}, u32[]{:S(2)}) %collective-permute-start.6) | collective-permute-done | bytes 524320 | tf_op jit(solution)/shard_map/ppermute | solution.py:926
  73.6 0.4 convert_add_fusion.2.proj_b
  74.0 10.8 %collective-permute-done.2 = bf16[256,1024]{1,0:T(8,128)(2,1)S(1)} collective-permute-done((bf16[256,1024]{1,0:T(8,128)(2,1)S(1)}, bf16[256,1024]{1,0:T(8,128)(2,1)S(1)}, u32[]{:S(2)}, u32[]{:S(2)}) %collective-permute-start.2) | collective-permute-done | bytes 524320 | tf_op jit(solution)/shard_map/ppermute | solution.py:926
  84.8 1.6 fusion.43
  86.4 0.2 multiply_reduce_fusion
  86.7 0.3 multiply_reduce_fusion.1
  87.0 0.4 copy-done.14
  87.4 1.2 add_convert_fusion.3
  88.6 1.7 collective-permute-start.3
  90.3 0.3 collective-permute-start.8
  90.6 0.6 stack.45.rows_of
  91.3 1.7 collective-permute-start.7
  93.0 3.1 collective-permute-done.4.b_got_ref
  96.1 11.2 %collective-permute-done.3.got_ref = bf16[256,1024]{1,0:T(8,128)(2,1)} collective-permute-done((bf16[256,1024]{1,0:T(8,128)(2,1)}, bf16[256,1024]{1,0:T(8,128)(2,1)}, u32[]{:S(2)}, u32[]{:S(2)}) %collective-permute-start.3) | collective-permute-done | bytes 524320 | tf_op jit(solution)/shard_map/ppermute | solution.py:926
  107.4 16.4 %mlp.2 = (bf16[1024,1024]{1,0:T(8,128)(2,1)}, bf16[1024,2048]{1,0:T(8,128)(2,1)}, bf16[1024,2048]{1,0:T(8,128)(2,1)}, f32[256,1024]{1,0:T(8,128)}, bf16[256,1024...) custom-call(bf16[256,1024]{1,0:T(8,128)(2,1)} %get-tuple-element.112.own_ref, ...), custom_call_target="tpu_custom_call" | custom-call | flops 12884901888 | bytes 25165824 | tf_op jit(solution)/shard_map/mlp/pallas_call | solution.py:447
  123.8 1.8 collective-permute-start.5
  125.6 4.2 %collective-permute-done.7.got_ref = bf16[256,1024]{1,0:T(8,128)(2,1)S(1)} collective-permute-done((bf16[256,1024]{1,0:T(8,128)(2,1)S(1)}, bf16[256,1024]{1,0:T(8,128)(2,1)S(1)}, u32[]{:S(2)}, u32[]{:S(2)}) %collective-permute-start.7) | collective-permute-done | bytes 524320 | tf_op jit(solution)/shard_map/ppermute | solution.py:926
  129.7 0.8 copy-done.38
  130.5 16.2 %mlp.3 = (bf16[1024,1024]{1,0:T(8,128)(2,1)}, bf16[1024,2048]{1,0:T(8,128)(2,1)}, bf16[1024,2048]{1,0:T(8,128)(2,1)}, f32[256,1024]{1,0:T(8,128)}, bf16[256,1024...) custom-call(bf16[256,1024]{1,0:T(8,128)(2,1)} %copy-done.31, ...), custom_call_target="tpu_custom_call", output_to_operand_aliasing={{0}: (7, {}), {1}: (8, {}), {2}: (9, {})} | custom-call | flops 12884901888 | bytes 25165824 | tf_op jit(solution)/shard_map/mlp/pallas_call | solution.py:447
  146.8 1.8 collective-permute-start.9
  148.6 3.0 pad_maximum_fusion.full_back
  151.6 0.7 add.231
  152.4 5.2 %collective-permute-done.9 = bf16[256,1024]{1,0:T(8,128)(2,1)S(1)} collective-permute-done((bf16[256,1024]{1,0:T(8,128)(2,1)}, bf16[256,1024]{1,0:T(8,128)(2,1)S(1)}, u32[]{:S(2)}, u32[]{:S(2)}) %collective-permute-start.9) | collective-permute-done | bytes 524320 | tf_op jit(solution)/shard_map/ppermute | solution.py:926
  157.5 1.8 fusion.17
  159.3 1.3 stack.48.known
  160.6 187.6 %tail.1 = (bf16[2048,1024]{1,0:T(8,128)(2,1)}, bf16[1024,2048]{1,0:T(8,128)(2,1)}, bf16[512,1024]{1,0:T(8,128)(2,1)}, bf16[1024,512]{1,0:T(8,128)(2,1)}, bf16[10...) custom-call(bf16[1024,2048]{1,0:T(8,128)(2,1)} %get-tuple-element.57.hi, ...), custom_call_target="tpu_custom_call" | custom-call | tf_op jit(solution)/shard_map/tail/pallas_call | solution.py:898
  348.2 0.9 slice.69
  349.1 0.8 slice_bitcast_fusion
  349.9 1.3 reduce_sum.162
  351.2 1.1 slice.70
  352.3 0.6 fusion.45
  352.9 1.8 fusion.48
  354.8 0.2 copy.33
  355.0 0.6 copy.36
  355.6 0.6 reshape.185
  356.2 1.6 convert_element_type.106
  357.8 6.8 %convert_element_type.107 = f32[1024,2048]{1,0:T(8,128)} convert(bf16[1024,2048]{1,0:T(8,128)(2,1)} %get-tuple-element.75) | non-fusion elementwise | flops 2097152 | bytes 12582912 | tf_op jit(solution)/shard_map/convert_element_type | solution.py:990
  364.6 4.4 %convert_element_type.108 = f32[2048,1024]{1,0:T(8,128)} convert(bf16[2048,1024]{1,0:T(8,128)(2,1)S(1)} %copy-done.21) | non-fusion elementwise | flops 2097152 | bytes 12582912 | tf_op jit(solution)/shard_map/convert_element_type | solution.py:990
  369.0 1.0 pad_maximum_fusion.1
  370.1 4.3 %fusion.49 = f32[128,6144]{1,0:T(8,128)} fusion(f32[16,128]{1,0:T(8,128)S(1)} %bitcast.63, f32[16,6144]{1,0:T(8,128)S(1)} %bitcast.55), kind=kOutput, calls=%fused_computation.104 | convolution fusion | flops 150994944 | bytes 3547136 | tf_op jit(solution)/shard_map/nc,nm->cm/dot_general | solution.py:996
  374.4 3.2 maximum_convert_fusion
  377.6 1.0 copy.43
  (104 shorter events, 0.5 us)
Async XLA Ops:
  0.6 3.3 copy-start
  0.7 4.3 %copy-start.16 = (bf16[512,1024]{1,0:T(8,128)(2,1)S(1)}, bf16[512,1024]{1,0:T(8,128)(2,1)}, u32[]{:S(2)}) copy-start(bf16[512,1024]{1,0:T(8,128)(2,1)} %tokens_hbm.1) | copy-start | bytes 3145732
  0.7 4.2 %copy-start.32 = (f32[6144]{0:T(1024)S(1)}, f32[6144]{0:T(1024)}, u32[]{:S(2)}) copy-start(f32[6144]{0:T(1024)} %param.18) | copy-start | bytes 73732
  0.7 4.3 %copy-start.33 = (f32[1024]{0:T(1024)S(1)}, f32[1024]{0:T(1024)}, u32[]{:S(2)}) copy-start(f32[1024]{0:T(1024)} %param.19) | copy-start | bytes 12292
  0.7 8.7 %copy-start.39 = (s32[1,4]{1,0:T(1,128)S(1)}, s32[1,4]{1,0:T(1,128)}, u32[]{:S(2)}) copy-start(s32[1,4]{1,0:T(1,128)} %param.16) | copy-start | bytes 52
  6.4 16.0 %collective-permute-start.1 = (bf16[256,1024]{1,0:T(8,128)(2,1)}, bf16[256,1024]{1,0:T(8,128)(2,1)}, u32[]{:S(2)}, u32[]{:S(2)}) collective-permute-start(bf16[256,1024]{1,0:T(8,128)(2,1)} %get-tuple-element.95.own_ref), channel_id=1, source_target_pairs={{0,1},{1,0},{2,3},{3,2},{4,5},{5,4},{6,7},{7,6},{8,9},{9,8},{10,11... | collective-permute-start | bytes 1572872 | tf_op jit(solution)/shard_map/ppermute | solution.py:926
  9.4 23.5 %collective-permute-start = (bf16[256,1024]{1,0:T(8,128)(2,1)}, bf16[256,1024]{1,0:T(8,128)(2,1)}, u32[]{:S(2)}, u32[]{:S(2)}) collective-permute-start(bf16[256,1024]{1,0:T(8,128)(2,1)} %get-tuple-element.96.own_ref), channel_id=1, source_target_pairs={{0,1},{1,0},{2,3},{3,2},{4,5},{5,4},{6,7},{7,6},{8,9},{9,8},{10,11... | collective-permute-start | bytes 1572872 | tf_op jit(solution)/shard_map/ppermute | solution.py:926
  9.5 12.9 %copy-start.1 = (bf16[3,1024,512]{2,1,0:T(8,128)(2,1)S(1)}, bf16[3,1024,512]{2,1,0:T(8,128)(2,1)}, u32[]{:S(2)}) copy-start(bf16[3,1024,512]{2,1,0:T(8,128)(2,1)} %w_qkv_hbm.1) | copy-start | bytes 9437188
  9.7 39.0 %copy-start.9 = (s32[1024]{0:T(1024)}, s32[1024]{0:T(1024)S(1)}, u32[]{:S(2)}) copy-start(s32[1024]{0:T(1024)S(1)} %get-tuple-element.83) | copy-start | bytes 12292
  12.5 25.2 %copy-start.4 = (f32[1024,128]{1,0:T(8,128)}, f32[1024,128]{1,0:T(8,128)S(1)}, u32[]{:S(2)}) copy-start(f32[1024,128]{1,0:T(8,128)S(1)} %get-tuple-element.121.cos_ref.cosine) | copy-start | bytes 1572868
  12.5 25.2 %copy-start.5 = (f32[1024,128]{1,0:T(8,128)}, f32[1024,128]{1,0:T(8,128)S(1)}, u32[]{:S(2)}) copy-start(f32[1024,128]{1,0:T(8,128)S(1)} %get-tuple-element.122.sin_ref.sine) | copy-start | bytes 1572868
  37.7 1.4 copy-start.3
  39.1 9.6 %copy-start.2 = (bf16[3,1024,512]{2,1,0:T(8,128)(2,1)}, bf16[3,1024,512]{2,1,0:T(8,128)(2,1)S(1)}, u32[]{:S(2)}) copy-start(bf16[3,1024,512]{2,1,0:T(8,128)(2,1)S(1)} %get-tuple-element.47.q_ref.k_ref.v_ref.qkv_hbm) | copy-start | bytes 9437188
  39.3 9.4 %copy-start.6 = (s32[1024,128]{1,0:T(8,128)}, s32[1024,128]{1,0:T(8,128)S(1)}, u32[]{:S(2)}) copy-start(s32[1024,128]{1,0:T(8,128)S(1)} %broadcast_in_dim.25.segc_ref.segc) | copy-start | bytes 1572868
  48.7 9.4 %copy-start.10 = (f32[8,1,512]{2,1,0:T(1,128)}, f32[8,1,512]{2,1,0:T(1,128)S(1)}, u32[]{:S(2)}) copy-start(f32[8,1,512]{2,1,0:T(1,128)S(1)} %get-tuple-element.68.lse_b) | copy-start | bytes 49156
  48.7 24.8 %copy-start.7 = (bf16[512,512]{1,0:T(8,128)(2,1)}, bf16[512,512]{1,0:T(8,128)(2,1)S(1)}, u32[]{:S(2)}) copy-start(bf16[512,512]{1,0:T(8,128)(2,1)S(1)} %get-tuple-element.51.mixed_b) | copy-start | bytes 1572868
  48.7 9.4 %copy-start.12 = (bf16[512,1024]{1,0:T(8,128)(2,1)S(1)}, bf16[512,1024]{1,0:T(8,128)(2,1)}, u32[]{:S(2)}) copy-start(bf16[512,1024]{1,0:T(8,128)(2,1)} %w_out_hbm.1) | copy-start | bytes 3145732
  58.1 15.9 %copy-start.11 = (f32[8,1,512]{2,1,0:T(1,128)}, f32[8,1,512]{2,1,0:T(1,128)S(1)}, u32[]{:S(2)}) copy-start(f32[8,1,512]{2,1,0:T(1,128)S(1)} %get-tuple-element.67.lse_a) | copy-start | bytes 49156
  58.2 26.6 %copy-start.8 = (bf16[512,512]{1,0:T(8,128)(2,1)}, bf16[512,512]{1,0:T(8,128)(2,1)S(1)}, u32[]{:S(2)}) copy-start(bf16[512,512]{1,0:T(8,128)(2,1)S(1)} %get-tuple-element.48.mixed_a) | copy-start | bytes 1572868
  58.2 3.1 copy-start.18
  58.6 14.9 %collective-permute-start.6 = (bf16[256,1024]{1,0:T(8,128)(2,1)S(1)}, bf16[256,1024]{1,0:T(8,128)(2,1)S(1)}, u32[]{:S(2)}, u32[]{:S(2)}) collective-permute-start(bf16[256,1024]{1,0:T(8,128)(2,1)S(1)} %convolution_convert_fusion), channel_id=1, source_target_pairs={{0,1},{1,0},{2,3},{3,2},{4,5},{5,4},{6,7},{7,6},{8,9},{9,8},{10,11... | collective-permute-start | bytes 1572872 | tf_op jit(solution)/shard_map/ppermute | solution.py:926
  60.4 24.4 %copy-start.17 = (bf16[512,1024]{1,0:T(8,128)(2,1)S(1)}, bf16[512,1024]{1,0:T(8,128)(2,1)}, u32[]{:S(2)}) copy-start(bf16[512,1024]{1,0:T(8,128)(2,1)} %tokens_hbm.1) | copy-start | bytes 3145732
  60.9 23.9 %collective-permute-start.2 = (bf16[256,1024]{1,0:T(8,128)(2,1)S(1)}, bf16[256,1024]{1,0:T(8,128)(2,1)S(1)}, u32[]{:S(2)}, u32[]{:S(2)}) collective-permute-start(bf16[256,1024]{1,0:T(8,128)(2,1)S(1)} %convolution_convert_fusion.1), channel_id=1, source_target_pairs={{0,1},{1,0},{2,3},{3,2},{4,5},{5,4},{6,7},{7,6},{8,9},{9,8},{10,11... | collective-permute-start | bytes 1572872 | tf_op jit(solution)/shard_map/ppermute | solution.py:926
  62.5 33.6 %collective-permute-start.4 = (bf16[256,1024]{1,0:T(8,128)(2,1)}, bf16[256,1024]{1,0:T(8,128)(2,1)}, u32[]{:S(2)}, u32[]{:S(2)}) collective-permute-start(bf16[256,1024]{1,0:T(8,128)(2,1)} %get-tuple-element.88.b_own_ref), channel_id=1, source_target_pairs={{0,1},{1,0},{2,3},{3,2},{4,5},{5,4},{6,7},{7,6},{8,9},{9,8},{10,11... | collective-permute-start | bytes 1572872 | tf_op jit(solution)/shard_map/ppermute | solution.py:926
  74.0 12.4 %copy-start.20 = (f32[256,1024]{1,0:T(8,128)}, f32[256,1024]{1,0:T(8,128)S(1)}, u32[]{:S(2)}) copy-start(f32[256,1024]{1,0:T(8,128)S(1)} %convert_add_fusion.2.proj_b) | copy-start | bytes 3145732
  84.8 2.6 copy-start.34
  86.4 1.0 copy-start.14
  86.4 71.1 %copy-start.13 = (f32[256,1024]{1,0:T(8,128)}, f32[256,1024]{1,0:T(8,128)S(1)}, u32[]{:S(2)}) copy-start(f32[256,1024]{1,0:T(8,128)S(1)} %get-tuple-element.90.mid_a) | copy-start | bytes 3145732
  88.6 35.2 %copy-start.31 = (bf16[256,1024]{1,0:T(8,128)(2,1)}, bf16[256,1024]{1,0:T(8,128)(2,1)S(1)}, u32[]{:S(2)}) copy-start(bf16[256,1024]{1,0:T(8,128)(2,1)S(1)} %get-tuple-element.113.own_ref) | copy-start | bytes 1572868
  88.6 18.8 %collective-permute-start.3 = (bf16[256,1024]{1,0:T(8,128)(2,1)}, bf16[256,1024]{1,0:T(8,128)(2,1)}, u32[]{:S(2)}, u32[]{:S(2)}) collective-permute-start(bf16[256,1024]{1,0:T(8,128)(2,1)} %get-tuple-element.112.own_ref), channel_id=1, source_target_pairs={{0,1},{1,0},{2,3},{3,2},{4,5},{5,4},{6,7},{7,6},{8,9},{9,8},{10,11... | collective-permute-start | bytes 1572872 | tf_op jit(solution)/shard_map/ppermute | solution.py:926
  90.3 35.2 %collective-permute-start.8 = (bf16[256,1024]{1,0:T(8,128)(2,1)}, bf16[256,1024]{1,0:T(8,128)(2,1)}, u32[]{:S(2)}, u32[]{:S(2)}) collective-permute-start(bf16[256,1024]{1,0:T(8,128)(2,1)} %get-tuple-element.98.b_own_ref), channel_id=1, source_target_pairs={{0,1},{1,0},{2,3},{3,2},{4,5},{5,4},{6,7},{7,6},{8,9},{9,8},{10,11... | collective-permute-start | bytes 1572872 | tf_op jit(solution)/shard_map/ppermute | solution.py:926
  91.3 38.5 %collective-permute-start.7 = (bf16[256,1024]{1,0:T(8,128)(2,1)S(1)}, bf16[256,1024]{1,0:T(8,128)(2,1)S(1)}, u32[]{:S(2)}, u32[]{:S(2)}) collective-permute-start(bf16[256,1024]{1,0:T(8,128)(2,1)S(1)} %get-tuple-element.113.own_ref), channel_id=1, source_target_pairs={{0,1},{1,0},{2,3},{3,2},{4,5},{5,4},{6,7},{7,6},{8,9},{9,8},{10,11... | collective-permute-start | bytes 1572872 | tf_op jit(solution)/shard_map/ppermute | solution.py:926
  123.8 28.6 %collective-permute-start.5 = (bf16[256,1024]{1,0:T(8,128)(2,1)}, bf16[256,1024]{1,0:T(8,128)(2,1)S(1)}, u32[]{:S(2)}, u32[]{:S(2)}) collective-permute-start(bf16[256,1024]{1,0:T(8,128)(2,1)} %get-tuple-element.50), channel_id=1, source_target_pairs={{0,1},{1,0},{2,3},{3,2},{4,5},{5,4},{6,7},{7,6},{8,9},{9,8},{10,11... | collective-permute-start | bytes 1572872 | tf_op jit(solution)/shard_map/ppermute | solution.py:926
  129.7 0.8 copy-start.38
  130.5 18.1 %copy-start.37 = (bf16[1,128]{1,0:T(2,128)(2,1)S(1)}, bf16[1,128]{1,0:T(2,128)(2,1)}, u32[]{:S(2)}) copy-start(bf16[1,128]{1,0:T(2,128)(2,1)} %param.15) | copy-start | bytes 772
  146.7 4.9 %copy-start.35 = (f32[1,2048]{1,0:T(1,128)S(1)}, f32[1,2048]{1,0:T(1,128)}, u32[]{:S(2)}) copy-start(f32[1,2048]{1,0:T(1,128)} %get-tuple-element.65) | copy-start | bytes 24580
  146.7 10.8 %copy-start.15 = (f32[256,1024]{1,0:T(8,128)S(1)}, f32[256,1024]{1,0:T(8,128)}, u32[]{:S(2)}) copy-start(f32[256,1024]{1,0:T(8,128)} %copy-done.14) | copy-start | bytes 3145732
  146.7 10.8 %copy-start.19 = (bf16[512,1024]{1,0:T(8,128)(2,1)S(1)}, bf16[512,1024]{1,0:T(8,128)(2,1)}, u32[]{:S(2)}) copy-start(bf16[512,1024]{1,0:T(8,128)(2,1)} %cot_hbm.1) | copy-start | bytes 3145732
  146.8 10.8 %copy-start.27 = (f32[256,1024]{1,0:T(8,128)S(1)}, f32[256,1024]{1,0:T(8,128)}, u32[]{:S(2)}) copy-start(f32[256,1024]{1,0:T(8,128)} %get-tuple-element.49) | copy-start | bytes 3145732
  146.8 10.8 %copy-start.29 = (f32[256,1024]{1,0:T(8,128)S(1)}, f32[256,1024]{1,0:T(8,128)}, u32[]{:S(2)}) copy-start(f32[256,1024]{1,0:T(8,128)} %get-tuple-element.55) | copy-start | bytes 3145732
  146.8 10.8 %copy-start.36 = (f32[1024]{0:T(1024)S(1)}, f32[1024]{0:T(1024)}, u32[]{:S(2)}) copy-start(f32[1024]{0:T(1024)} %param.26) | copy-start | bytes 12292
  146.8 10.7 %collective-permute-start.9 = (bf16[256,1024]{1,0:T(8,128)(2,1)}, bf16[256,1024]{1,0:T(8,128)(2,1)S(1)}, u32[]{:S(2)}, u32[]{:S(2)}) collective-permute-start(bf16[256,1024]{1,0:T(8,128)(2,1)} %get-tuple-element.56), channel_id=1, source_target_pairs={{0,1},{1,0},{2,3},{3,2},{4,5},{5,4},{6,7},{7,6},{8,9},{9,8},{10,11... | collective-permute-start | bytes 1572872 | tf_op jit(solution)/shard_map/ppermute | solution.py:926
  348.2 8.0 %copy-start.28 = (bf16[512,1024]{1,0:T(8,128)(2,1)S(1)}, bf16[512,1024]{1,0:T(8,128)(2,1)}, u32[]{:S(2)}) copy-start(bf16[512,1024]{1,0:T(8,128)(2,1)} %get-tuple-element.74) | copy-start | bytes 3145732
  357.8 6.8 %copy-start.21 = (bf16[2048,1024]{1,0:T(8,128)(2,1)S(1)}, bf16[2048,1024]{1,0:T(8,128)(2,1)}, u32[]{:S(2)}) copy-start(bf16[2048,1024]{1,0:T(8,128)(2,1)} %get-tuple-element.76) | copy-start | bytes 12582916
  364.6 4.4 %copy-start.22 = (bf16[256,1024]{1,0:T(8,128)(2,1)S(1)}, bf16[256,1024]{1,0:T(8,128)(2,1)}, u32[]{:S(2)}) copy-start(bf16[256,1024]{1,0:T(8,128)(2,1)} %get-tuple-element.93) | copy-start | bytes 1572868
  364.6 4.4 %copy-start.23 = (bf16[256,1024]{1,0:T(8,128)(2,1)S(1)}, bf16[256,1024]{1,0:T(8,128)(2,1)}, u32[]{:S(2)}) copy-start(bf16[256,1024]{1,0:T(8,128)(2,1)} %get-tuple-element.94) | copy-start | bytes 1572868
  369.0 5.4 %copy-start.24 = (bf16[1024,512]{1,0:T(8,128)(2,1)S(1)}, bf16[1024,512]{1,0:T(8,128)(2,1)}, u32[]{:S(2)}) copy-start(bf16[1024,512]{1,0:T(8,128)(2,1)} %get-tuple-element.71) | copy-start | bytes 3145732
  369.0 5.4 %copy-start.25 = (bf16[1024,512]{1,0:T(8,128)(2,1)S(1)}, bf16[1024,512]{1,0:T(8,128)(2,1)}, u32[]{:S(2)}) copy-start(bf16[1024,512]{1,0:T(8,128)(2,1)} %get-tuple-element.72) | copy-start | bytes 3145732
  369.0 5.4 %copy-start.26 = (bf16[1024,512]{1,0:T(8,128)(2,1)S(1)}, bf16[1024,512]{1,0:T(8,128)(2,1)}, u32[]{:S(2)}) copy-start(bf16[1024,512]{1,0:T(8,128)(2,1)} %get-tuple-element.73) | copy-start | bytes 3145732
  374.4 3.2 copy-start.30

commit v5 on v4

--- a/solution.py
+++ b/solution.py
@@ -396,7 +396,7 @@
 
 
 def mlp_kernel(own_ref, got_ref, b_own_ref, b_got_ref, up_ref, bias_ref, down_ref, *refs):
-    rows_ref, hidden_ref, pre_ref, own_grad, got_grad, own_branch, got_branch, bias_grad, back, grads, branch = refs[-11:]
+    rows_ref, back, hidden_ref, pre_ref, own_grad, got_grad, own_branch, got_branch, bias_grad, grads, branch = refs[-11:]
     tile, tiles = pl.program_id(0), pl.num_programs(0)
     half = own_ref.shape[0]
 
@@ -455,11 +455,12 @@
             *[pl.BlockSpec(memory_space=pl.ANY) for _ in before],
         ],
         out_specs=[
-            pl.BlockSpec((chunk, depth), lambda t: (j, 0)), wide, wide,
+            pl.BlockSpec((chunk, depth), lambda t: (j, 0)), pl.BlockSpec((chunk, depth), lambda t: (j, 0)), wide, wide,
             small, small, small, small,
             pl.BlockSpec((1, tile), lambda t: (0, t)),
         ],
         out_shape=[
+            jax.ShapeDtypeStruct((length, depth), bf16),
             jax.ShapeDtypeStruct((length, depth), bf16),
             jax.ShapeDtypeStruct((length, width), bf16),
             jax.ShapeDtypeStruct((length, width), bf16),
@@ -470,7 +471,6 @@
             jax.ShapeDtypeStruct((1, width), f32),
         ],
         scratch_shapes=[
-            pltpu.VMEM((chunk, depth), bf16),
             pltpu.VMEM((chunk, depth), f32),
             pltpu.VMEM((chunk, depth), f32),
         ],
@@ -575,15 +575,15 @@
     pl.semaphore_wait(barrier, len(targets))
 
 
-TURNS = (
-    (None, 7, 19, 26, 33, 40, 47, 62, 66),
-    (None, 11, 31, 38, 45, 52, 59, 76, 80),
-    (None, 16, 42, 49, 56, 63, 72, 92, 96),
-    (None, 23, 54, 61, 68, 75, 98, 114, 118),
-    (None, 59, 66, 71, 76, 81, 86, 104, 108),
-    (None, 84, 96, 101, 106, 111, 116, 134, 138),
-    (None, 86, 101, 106, 111, 116, 121, 140, 144),
-    (None, 88, 106, 111, 116, 121, 126, 146, 150),
+ORDER = (
+    (6.5, 1, 1), (10, 3, 1), (10, 1, 2), (10, 1, 3), (10.5, 2, 1), (10.5, 3, 2), (10.5, 0, 1), (11.5, 1, 4),
+    (13.5, 1, 5), (13.5, 3, 3), (15.5, 3, 4), (16.5, 1, 6), (16.5, 2, 2), (18.5, 4, 1), (18.5, 3, 5), (19.5, 0, 2),
+    (19.5, 2, 3), (20.5, 3, 6), (21.5, 4, 2), (21.5, 2, 4), (22.5, 0, 3), (23.5, 5, 1), (24.5, 6, 1), (25.5, 4, 3),
+    (25.5, 3, 7), (25.5, 7, 1), (25.5, 2, 5), (27.5, 3, 8), (29.5, 4, 4), (30.5, 1, 7), (30.5, 0, 4), (31, 5, 2),
+    (31, 2, 6), (31, 1, 8), (31, 4, 5), (32, 0, 5), (32, 5, 3), (32, 4, 6), (32, 5, 4), (32.5, 5, 5), (33, 0, 6),
+    (34, 7, 2), (34, 2, 7), (34, 5, 6), (34, 4, 7), (35, 2, 8), (35, 4, 8), (35, 7, 3), (35, 6, 2), (36, 7, 4),
+    (36, 6, 3), (36, 7, 5), (36, 5, 7), (36, 6, 4), (36, 5, 8), (36, 7, 6), (36, 6, 5), (37, 6, 6), (37, 0, 7),
+    (99, 0, 8), (99, 7, 7), (99, 7, 8), (99, 6, 7), (99, 6, 8),
 )
 WIDE = 512
 STEP_ROWS = 64
@@ -591,12 +591,12 @@
 
 def tail_kernel(
     hidden, full_back, rows_two, grad_pre, qkv_hbm, mixed_a, mixed_b, rows_hbm, w_qkv_hbm, w_out_hbm,
-    grad_a, grad_b, got_a, got_b, mid_a, mid_b, proj_a, proj_b, tokens_hbm, cot_hbm,
+    grad_a, grad_b, got_a, got_b, mid_a, mid_b, proj_a, proj_b, branch_a, branch_b, send_a, send_b, tokens_hbm, cot_hbm,
     rows_of, known, lse_a, lse_b, segr, segc, cosine, sine,
-    down_sum, up_sum, out_sum, q_sum, k_sum, v_sum, grad_x, everyone,
+    down_sum, up_sum, out_sum, q_sum, k_sum, v_sum, output, grad_x, everyone,
     qkv, mixed, rows_one, w_qkv, w_out, proj, mix_grad, d_qkv, dk, dv, from_x, grads, middle, projected, tokens, cot,
-    part_a, part_b, part_c, part_d, part_e, col_sums, small, small_got,
-    load, x_send, x_recv, all_send, all_recv, *more,
+    part_a, part_b, part_c, part_d, part_e, branch_got, col_sums, small, small_got,
+    load, store, x_send, x_recv, all_send, all_recv, *more,
 ):
     place, me = lax.axis_index("dp"), lax.axis_index("tensor")
     length, depth = rows_one.shape
@@ -626,7 +626,11 @@
     grads_in = [x_copy((got_a, got_b)[c], from_x.at[c], c) for c in each]
     projs = [x_copy(proj.at[c, :half], proj.at[c, half:], chunks + c) for c in each]
     ones = [x_copy(proj.at[c, :half], from_x.at[c], 2 * chunks + c) for c in each]
-    smalls = x_copy(small, small_got, 3 * chunks)
+    branches = [x_copy((send_a, send_b)[c], branch_got.at[c], 3 * chunks + c) for c in each]
+    smalls = x_copy(small, small_got, 4 * chunks)
+    outputs = [
+        pltpu.make_async_copy(branch_got.at[c], output.at[c * half : (c + 1) * half], store.at[c]) for c in each
+    ]
     partner = units[0].partner
 
     loads = []
@@ -637,12 +641,11 @@
         loads.append(copy)
         return copy
 
-    turns = sorted((t, k, i) for i, times in enumerate(TURNS) for k, t in enumerate(times) if k)
     done = [0]
 
-    def until(time):
-        while done[0] < len(turns) and turns[done[0]][0] <= time:
-            _, k, i = turns[done[0]]
+    def until(place_now):
+        while done[0] < len(ORDER) and ORDER[done[0]][0] <= place_now:
+            _, i, k = ORDER[done[0]]
             units[i].step(k)
             done[0] += 1
 
@@ -665,6 +668,7 @@
     backs.wait()
     pres = []
     for t in range(4):
+        until(1 + t)
         hiddens[t].wait()
         part = (part_a, part_b)[t // 2]
 
@@ -677,7 +681,6 @@
         pres.append(fetch(grad_pre.at[:, cut(t)], slots[t]))
         if t % 2:
             units[t // 2].step(0)
-            until(4 + 4 * (t // 2))
     main = [
         fetch(w_out_hbm, w_out), fetch(mixed_a, mixed.at[:chunk]), fetch(mixed_b, mixed.at[chunk:]),
         fetch(qkv_hbm, qkv), fetch(rows_hbm, rows_one),
@@ -704,7 +707,7 @@
         back = inner - jnp.mean(inner, axis=1, keepdims=True) - normal * jnp.mean(inner * normal, axis=1, keepdims=True)
         return root * back, normal
 
-    gain_two, scale_m, gate_a, gain_one, scale_a = [rows_of[r : r + 1, :] for r in range(5)]
+    gain_two, scale_m, gate_a, gain_one, scale_a, gate_m, b_down = [rows_of[r : r + 1, :] for r in range(7)]
 
     def second_norm(c):
         for copy in norms[c]:
@@ -726,21 +729,26 @@
 
     for copy in twos:
         copy.wait()
+    until(5)
     up_part(0)
+    until(6)
     up_part(1)
     units[2].step(0)
+    until(7)
     grads_in[0].wait()
     grads_in[1].start()
     second_norm(0)
-    until(16)
+    owns = [fetch(branch_a, projected.at[0])]
+    until(8)
     up_part(2)
+    until(9)
     up_part(3)
     units[3].step(0)
     weights = fetch(w_qkv_hbm, w_qkv)
-    until(23)
+    until(10)
     grads_in[1].wait()
     second_norm(1)
-    until(32)
+    owns.append(fetch(branch_b, projected.at[1]))
 
     def turn_back(u, rows):
         return (u * cosine[rows, :] - turned(u) * sine[rows, :]).astype(bf16)
@@ -781,11 +789,17 @@
 
     for copy in main:
         copy.wait()
-    clock = 36
+    now = 11
     for c in each:
+        until(now)
         projs[c].wait()
+        if c == chunks - 1:
+            for copy in branches:
+                copy.start()
         mix_grad[c * chunk : (c + 1) * chunk, :] = mm(proj[c], w_out[...], 1, 1).astype(bf16)
+        now += 1
         if c == chunks - 1:
+            until(now)
 
             @pl.loop(0, width // 256)
             def _(r):
@@ -795,31 +809,26 @@
                 ).astype(bf16)
 
             units[4].step(0)
-            clock += 3
-        until(clock)
+            now += 1
 
         @pl.loop(0, pairs)
         def _(p):
-            attend_back(p, c)
             for n in range(pairs):
 
                 @pl.when(p == n)
                 def _():
-                    until(clock + 4.4 * (n + 1))
-
-        clock += 19
+                    until(now + n)
+
+            attend_back(p, c)
+
+        now += pairs
 
     def rows_back(start):
         at = slice(start, start + half)
         return sum(mm(d_qkv[t, at, :], w_qkv[t], 1, 1) for t in range(3))
 
-    weights.wait()
-    for c in each:
-        proj[c, :half] = rows_back(c * chunk + half).astype(bf16)
-        if c == 0:
-            ones[c].start()
-        until(clock + 2 * (c + 1))
     for i in range(3):
+        until(now + i)
 
         @pl.loop(0, depth // 256)
         def _(r):
@@ -827,11 +836,34 @@
             qkv[2 - i, at, :] = mm(rows_one[:, at], d_qkv[2 - i], 0, 0).astype(bf16)
 
         units[5 + i].step(0)
-        until(clock + 6 + 2 * i)
+    now += 3
+    weights.wait()
     for c in each:
-        middle[c] = rows_back(c * chunk)
-
+        until(now + c)
+        proj[c, :half] = rows_back(c * chunk + half).astype(bf16)
+        if c == 0:
+            ones[c].start()
+    now += chunks
     for c in each:
+        until(now + c)
+        branches[c].wait()
+        owns[c].wait()
+
+        @pl.loop(0, half // STEP_ROWS)
+        def _(i):
+            at = pl.ds(pl.multiple_of(i * STEP_ROWS, STEP_ROWS), STEP_ROWS)
+            branch = projected[c, at, :] + branch_got[c, at, :].astype(f32) + b_down
+            branch_got[c, at, :] = (middle[c, at, :] + gate_m * branch).astype(bf16)
+            fold(5, cot[c, at, :].astype(f32) * branch)
+
+        outputs[c].start()
+    now += chunks
+    for c in each:
+        until(now + c)
+        projected[c] = rows_back(c * chunk)
+    now += chunks
+    for c in each:
+        until(now + c)
         ones[c].wait()
         if c < chunks - 1:
             ones[c + 1].start()
@@ -839,24 +871,23 @@
         @pl.loop(0, half // STEP_ROWS)
         def _(i):
             at = pl.ds(pl.multiple_of(i * STEP_ROWS, STEP_ROWS), STEP_ROWS)
-            grad = middle[c, at, :] + from_x[c, at, :].astype(f32)
+            grad = projected[c, at, :] + from_x[c, at, :].astype(f32)
             back, normal = norm_back(grad, tokens[c, at, :].astype(f32), gain_one * (1.0 + scale_a))
             grad_x[c, at, :] = (back + grads[c, at, :]).astype(bf16)
             fold(3, grad)
             fold(4, grad * normal)
 
-        until(100 + 10 * c)
-
-    shift, scaled, gated, shift_one, scaled_one = [col_sums[r : r + 1, :] for r in range(5)]
+    now += chunks
+    shift, scaled, gated, shift_one, scaled_one, gated_m = [col_sums[r : r + 1, :] for r in range(6)]
     small[...] = known[...] + jnp.concatenate(
         [
-            shift_one, gain_one * scaled_one, gated, shift, gain_two * scaled, jnp.zeros_like(shift),
+            shift_one, gain_one * scaled_one, gated, shift, gain_two * scaled, gated_m,
             (1.0 + scale_a) * scaled_one, (1.0 + scale_m) * scaled, jnp.zeros((8, depth), f32),
         ],
         axis=0,
     )
     smalls.start()
-    until(112)
+    until(now)
     smalls.wait()
     number = lax.broadcasted_iota(jnp.int32, small.shape, 0)
     everyone[0] = small[...] + jnp.where(number < 9, small_got[...], 0.0)
@@ -867,14 +898,16 @@
             device_id={"dp": partner[b]}, device_id_type=MESH,
         )
         copy.start()
-        until(117 + 6 * n)
+        until(now + 1 + n)
         copy.wait()
     until(1000)
+    for copy in outputs:
+        copy.wait()
 
 
 def tail(
     hidden, full_back, rows_two, grad_pre, qkv, mixed, rows_one, w_qkv, w_out, own_grad, got_grad, middle, projected,
-    tokens, cot, rows_of, known, lse, segr, segc, cosine, sine,
+    own_branch, got_branch, tokens, cot, rows_of, known, lse, segr, segc, cosine, sine,
 ):
     _, length, width = qkv.shape
     chunks = len(mixed)
@@ -888,20 +921,20 @@
         kept((3, length, width), bf16), kept((length, width), f32), kept((length, width), f32),
         kept(in_chunks, bf16), kept(in_chunks, f32), kept(in_chunks, f32), kept(in_chunks, f32),
         kept(in_chunks, bf16), kept(in_chunks, bf16),
-        *[kept((depth, depth), bf16)] * 4, kept((width, depth), bf16),
+        *[kept((depth, depth), bf16)] * 4, kept((width, depth), bf16), kept(in_chunks, bf16),
         kept((8, depth), f32), kept(known.shape, f32), kept(known.shape, f32),
-        pltpu.SemaphoreType.DMA((27,)),
-        pltpu.SemaphoreType.DMA((3 * chunks + 1,)), pltpu.SemaphoreType.DMA((3 * chunks + 1,)),
+        pltpu.SemaphoreType.DMA((29,)), pltpu.SemaphoreType.DMA((chunks,)),
+        pltpu.SemaphoreType.DMA((4 * chunks + 1,)), pltpu.SemaphoreType.DMA((4 * chunks + 1,)),
         pltpu.SemaphoreType.DMA((EDGES,)), pltpu.SemaphoreType.DMA((EDGES,)),
         *unit_scratch(depth, depth) * 4, *unit_scratch(width, depth), *unit_scratch(depth, width) * 3,
     ]
     return pl.pallas_call(
         tail_kernel,
-        in_specs=[anywhere] * 20 + [near] * 8,
-        out_specs=[anywhere] * 6 + [near] * 2,
+        in_specs=[anywhere] * 24 + [near] * 8,
+        out_specs=[anywhere] * 7 + [near] * 2,
         out_shape=[
             shaped((hidden.shape[1], depth), bf16), shaped((depth, hidden.shape[1]), bf16), shaped((width, depth), bf16),
-            *[shaped((depth, width), bf16)] * 3,
+            *[shaped((depth, width), bf16)] * 3, shaped(tokens.shape, bf16),
             shaped(in_chunks, bf16), shaped((1 << EDGES, *known.shape), f32),
         ],
         scratch_shapes=scratch,
@@ -909,7 +942,7 @@
         name="tail",
     )(
         hidden, full_back, rows_two, grad_pre, qkv, *mixed, rows_one, w_qkv, w_out, *own_grad, *got_grad, *middle,
-        *projected, tokens, cot, rows_of, known, *lse, segr, segc, cosine, sine,
+        *projected, *own_branch, *got_branch, tokens, cot, rows_of, known, *lse, segr, segc, cosine, sine,
     )
 
 
@@ -940,51 +973,58 @@
     grad_out = [cotangent[cut].astype(f32) for cut in cuts]
     each = range(chunks)
 
+    def after(value, *others):
+        return lax.optimization_barrier((value, *others))[0]
+
     act_one = [modulate(x_rows[c], gain_one, shift_a, scale_a).astype(bf16) for c in each]
-    got_one = [swap(act_one[c]) for c in each]
     back = [(grad_out[c] * gate_m).astype(bf16) for c in each]
+    got_one = [swap(act_one[0])]
+    got_one.append(swap(after(act_one[1], got_one[0])))
+    got_back = [swap(after(back[0], got_one[1]))]
+    got_back.append(swap(after(back[1], got_back[0])))
     state = ()
     for c in each:
         state = project_pair(c, act_one[c], got_one[c], w_qkv, cosine, sine, state, length)
     qkv, rows_one = state
-    got_back = [swap(back[c]) for c in each]
-    full_back = jnp.concatenate([piece for c in each for piece in (back[c], got_back[c])], axis=0)
-
-    mixed, lse, projected, middle, act_two, got_two = [], [], [], [], [], []
+
+    mixed, lse, sums, projected, middle, act_two, got_two = [], [], [], [], [], [], []
     for c in each:
-        m, l = attend_forward_pair(c, chunk, qkv, seg_rows, seg_cols)
+        waits = () if c == 0 else (got_back[0], sums[0])
+        m, l = attend_forward_pair(c, chunk, after(qkv, *waits) if c else qkv, seg_rows, seg_cols)
+        if c:
+            m = after(m, arrived[0])
         mixed.append(m)
         lse.append(l)
-    sums = [swap(jnp.dot(mixed[c][half:], w_out, preferred_element_type=f32).astype(bf16)) for c in each]
+        sums.append(jnp.dot(m[half:], w_out, preferred_element_type=f32).astype(bf16))
+        arrived = [swap(sums[0])] if c == 0 else [arrived[0], swap(sums[1])]
     for c in each:
-        projected.append(jnp.dot(mixed[c][:half], w_out, preferred_element_type=f32) + sums[c].astype(f32))
+        projected.append(jnp.dot(mixed[c][:half], w_out, preferred_element_type=f32) + arrived[c].astype(f32))
         middle.append(x_rows[c] + gate_a * projected[c])
         act_two.append(modulate(middle[c], gain_two, shift_m, scale_m).astype(bf16))
         got_two.append(swap(act_two[c]))
+    got_two[0] = after(got_two[0], act_two[1])
     state, pieces = (), []
     for c in each:
         out = mlp_pair(c, act_two[c], got_two[c], back[c], got_back[c], w_up, b_up, w_down, state, length)
-        state, rest = out[:3], out[3:]
+        state, rest = out[:4], out[4:]
         pieces.append(rest)
-    rows_two, hidden, grad_pre = state
+    rows_two, full_back, hidden, grad_pre = state
     grad_b_up = sum(pieces[c][4] for c in each)[0]
-    branch = [pieces[c][2] + swap(pieces[c][3]).astype(f32) + b_down for c in each]
-    output = jnp.concatenate([(middle[c] + gate_m * branch[c]).astype(bf16) for c in each], axis=0)
-    grad_gate_m = sum(jnp.sum(grad_out[c] * branch[c], axis=0) for c in each)
     grad_b_down = sum(jnp.sum(back[c].astype(f32), axis=0) for c in each)
 
     none = jnp.zeros((width,), f32)
     known = jnp.stack(
         [
-            none, none, none, none, none, grad_gate_m, none, none, grad_b_down,
+            none, none, none, none, none, none, none, none, grad_b_down,
             grad_b_up[:width], grad_b_up[width:],
             jnp.pad(cond[0].astype(f32), (0, width - cond.shape[1])), none, none, none, none,
         ]
     )
-    *sums, grad_x, everyone = tail(
+    *sums, output, grad_x, everyone = tail(
         hidden, full_back, rows_two, grad_pre, qkv, mixed, rows_one, w_qkv, w_out,
-        [pieces[c][0] for c in each], [pieces[c][1] for c in each], middle, projected, tokens, cotangent,
-        jnp.stack([gain_two, scale_m, gate_a, gain_one, scale_a, none, none, none]), known,
+        *[[pieces[c][n] for c in each] for n in range(2)], middle, projected,
+        *[[pieces[c][n] for c in each] for n in range(2, 4)], tokens, cotangent,
+        jnp.stack([gain_two, scale_m, gate_a, gain_one, scale_a, gate_m, b_down, none]), known,
         lse, seg_rows, seg_cols, cosine, sine,
     )
     grad_w_down, grad_w_up, grad_w_out, grad_q, grad_k, grad_v = [s.astype(f32) for s in sums]

time: 380 us -> 332 us (0.87); the launches traced: 379 us -> 327 us
  Pallas kernels: 249 us -> 225 us
  waiting for transfers between devices: 58.8 us -> 36.4 us
  other arithmetic: 34.5 us -> 29.9 us
    pallas_call x1, Pallas kernels: 188 us -> 164 us  [tail(): pl.pallas_call(tail_kernel, in_specs=[anywhere] * 24 + [near] * 8, out_sp...]
    ppermute x10 -> x8, waiting for transfers between devices: 58.8 us -> 36.4 us  [swap(): return lax.ppermute(values, 'tensor', [(0, 1), (1, 0)])]
    concatenate x2 -> x0, other arithmetic: 4.04 us -> none  [the longest x1 3.01 us: body_pair(): jnp.concatenate([piece for c in each for piece in (back[c], got_back[c])]...]
    ppermute x10 -> x8, starting transfers between devices: 14.3 us -> 11 us  [swap(): return lax.ppermute(values, 'tensor', [(0, 1), (1, 0)])]
    unnamed x86 -> x91, local copies, waits for them, and re-layouts: 5.37 us -> 7.87 us
  transfers between devices with their start and end apart: 10 -> 8, of which waited for: 8 -> 6; matrix products, arithmetic and copies ran while one was open for 3% -> 2% of each run, Pallas kernels for 10% -> 13%
where the time goes in v5:
time: 332 us; the launch traced here: 327 us
  Pallas kernels  225 us (68%)
  waiting for transfers between devices  36.4 us (11%)
  other arithmetic  29.9 us (9%)
  local copies, waits for them, and re-layouts  13.3 us (4%)
  starting transfers between devices  11 us (3%)
  matrix products  10.1 us (3%)
    pallas_call x1, Pallas kernels, tail(): pl.pallas_call(tail_kernel, in_specs=[anywhere] * 24 + [near] * 8, out_sp...  164 us
    ppermute x8, waiting for transfers between devices, swap(): return lax.ppermute(values, 'tensor', [(0, 1), (1, 0)])  36.4 us
    pallas_call x2, Pallas kernels, mlp_pair(): pl.pallas_call(mlp_kernel, grid=(width // tile,), in_specs=[small, small,...  34 us
    pallas_call x2, Pallas kernels, attend_forward_pair(): pl.pallas_call(forward_chunk_kernel, grid=(pairs,), in_specs=[*pair_piece...  18.6 us
    convert_element_type x3, other arithmetic, body_pair(): s.astype(f32)  12.8 us
    ppermute x8, starting transfers between devices, swap(): return lax.ppermute(values, 'tensor', [(0, 1), (1, 0)])  11 us
    pallas_call x2, Pallas kernels, project_pair(): pl.pallas_call(qkv_pair_kernel, grid=(3,), in_specs=[pl.BlockSpec((half,...  8.29 us
    unnamed x91, local copies, waits for them, and re-layouts  7.87 us
  transfers between devices with their start and end apart: 8, of which 6 were waited for; matrix products, arithmetic and copies ran while one was open for 2% of the time, Pallas kernels for 13%

profile of v5, /device:TPU:0, one launch (start us, length us, event | category | flops | bytes accessed | tf_op | source)
XLA Modules:
  0.0 327.1 jit_solution(5791319138764642404)
XLA Ops:
  0.6 0.0 copy-start
  0.7 1.6 convert_reduce_fusion
  2.3 1.6 fusion.4
  3.9 1.0 fusion.32
  4.9 1.3 fusion.8
  6.2 2.9 collective-permute-start
  9.2 0.1 select_reduce_fusion.2
  9.3 0.1 select_reduce_fusion
  9.4 1.9 multiply_sine_fusion
  11.3 9.7 %collective-permute-done.got_ref = bf16[256,1024]{1,0:T(8,128)(2,1)S(1)} collective-permute-done((bf16[256,1024]{1,0:T(8,128)(2,1)S(1)}, bf16[256,1024]{1,0:T(8,128)(2,1)S(1)}, u32[]{:S(2)}, u32[]{:S(2)}) %collective-permute-start) | collective-permute-done | bytes 524320 | tf_op jit(solution)/shard_map/ppermute | solution.py:959
  21.1 0.8 copy-done.14
  21.9 1.7 collective-permute-start.1
  23.6 0.9 pad_maximum_fusion
  24.5 2.7 convert_reduce_fusion.2
  27.2 3.7 %qkv.2 = (bf16[3,1024,512]{2,1,0:T(8,128)(2,1)S(1)}, bf16[1024,1024]{1,0:T(8,128)(2,1)S(1)}) custom-call(bf16[256,1024]{1,0:T(8,128)(2,1)S(1)} %copy-done.10, bf16[256,1024]{1,0:T(8,128)(2,1)S(1)} %copy-done.15, bf16[3,1024,512]{2,1,0:T(8,128)(2,1)S(1)} %copy-done.1, f32[1024,128]{1,0:T(8,128)S(1)} %get-tuple-element.135.cos_ref.cosine, ...), custom_call_target="tpu_custom_call" | custom-call | flops 1610612736 | bytes 4194304 | tf_op jit(solution)/shard_map/qkv/pallas_call | solution.py:309
  30.9 4.2 %collective-permute-done.1.got_ref = bf16[256,1024]{1,0:T(8,128)(2,1)S(1)} collective-permute-done((bf16[256,1024]{1,0:T(8,128)(2,1)}, bf16[256,1024]{1,0:T(8,128)(2,1)S(1)}, u32[]{:S(2)}, u32[]{:S(2)}) %collective-permute-start.1) | collective-permute-done | bytes 524320 | tf_op jit(solution)/shard_map/ppermute | solution.py:959
  35.2 1.4 collective-permute-start.2
  36.6 4.6 %qkv.3 = (bf16[3,1024,512]{2,1,0:T(8,128)(2,1)S(1)}, bf16[1024,1024]{1,0:T(8,128)(2,1)S(1)}) custom-call(bf16[256,1024]{1,0:T(8,128)(2,1)} %get-tuple-element.54.own_ref, bf16[256,1024]{1,0:T(8,128)(2,1)S(1)} %collective-permute-done.1.got_ref, bf16[3,1024,512]{2,1,0:T(8,128)(2,1)S(1)} %copy-done.1, ...), custom_call_target="tpu_custom_call", output_to_operand_aliasing={{0}: (5, {}), {1}: (6, {})} | custom-call | flops 1610612736 | bytes 4194304 | tf_op jit(solution)/shard_map/qkv/pallas_call | solution.py:309
  41.2 1.4 copy-done.3
  42.6 0.2 broadcast_in_dim.27.segc_ref.segc
  42.8 9.3 %attend.2 = (bf16[512,512]{1,0:T(8,128)(2,1)S(1)}, f32[8,1,512]{2,1,0:T(1,128)S(1)}) custom-call(bf16[3,1024,512]{2,1,0:T(8,128)(2,1)S(1)} %get-tuple-element.60.q_ref.k_ref.v_ref.qkv_hbm, bf16[3,1024,512]{2,1,0:T(8,128)(2,1)S(1)} %get-tuple-element.60.q_ref.k_ref.v_ref.qkv_hbm, bf16[3,1024,512]{2,1,0:T(8,128)(2,1)S(1)} %get-tuple-element.60.q_ref.k_ref.v_ref.qkv_hbm, ...), custom_call_target="tpu_custom_call" | custom-call | flops 4294967296 | bytes 4194304 | tf_op jit(solution)/shard_map/attend/pallas_call | solution.py:371
  52.1 0.5 convolution_convert_fusion.1
  52.6 0.7 collective-permute-start.3
  53.3 0.8 copy-done.38
  54.1 9.3 %attend.3 = (bf16[512,512]{1,0:T(8,128)(2,1)S(1)}, f32[8,1,512]{2,1,0:T(1,128)S(1)}) custom-call(bf16[3,1024,512]{2,1,0:T(8,128)(2,1)S(1)} %get-tuple-element.60.q_ref.k_ref.v_ref.qkv_hbm, bf16[3,1024,512]{2,1,0:T(8,128)(2,1)S(1)} %get-tuple-element.60.q_ref.k_ref.v_ref.qkv_hbm, bf16[3,1024,512]{2,1,0:T(8,128)(2,1)S(1)} %get-tuple-element.60.q_ref.k_ref.v_ref.qkv_hbm, ...), custom_call_target="tpu_custom_call" | custom-call | flops 4294967296 | bytes 4194304 | tf_op jit(solution)/shard_map/attend/pallas_call | solution.py:371
  63.4 0.8 collective-permute-done.3
  64.3 0.4 convolution_convert_fusion
  64.7 1.0 collective-permute-start.4
  65.7 9.9 %collective-permute-done.4 = bf16[256,1024]{1,0:T(8,128)(2,1)S(1)} collective-permute-done((bf16[256,1024]{1,0:T(8,128)(2,1)S(1)}, bf16[256,1024]{1,0:T(8,128)(2,1)S(1)}, u32[]{:S(2)}, u32[]{:S(2)}) %collective-permute-start.4) | collective-permute-done | bytes 524320 | tf_op jit(solution)/shard_map/ppermute | solution.py:959
  75.6 0.4 convolution_add_fusion.proj_b
  76.1 1.6 fusion.34
  77.8 0.2 multiply_reduce_fusion.1
  78.0 0.3 multiply_reduce_fusion
  78.3 0.4 copy-done.19
  78.7 1.2 add_convert_fusion
  79.9 1.1 collective-permute-start.7
  81.0 0.7 stack.55.rows_of
  81.7 1.0 collective-permute-start.6
  82.7 1.1 collective-permute-start.5
  83.8 11.3 %collective-permute-done.7.got_ref = bf16[256,1024]{1,0:T(8,128)(2,1)} collective-permute-done((bf16[256,1024]{1,0:T(8,128)(2,1)}, bf16[256,1024]{1,0:T(8,128)(2,1)}, u32[]{:S(2)}, u32[]{:S(2)}) %collective-permute-start.7) | collective-permute-done | bytes 524320 | tf_op jit(solution)/shard_map/ppermute | solution.py:959
  95.1 16.9 %mlp.2 = (bf16[1024,1024]{1,0:T(8,128)(2,1)}, bf16[1024,1024]{1,0:T(8,128)(2,1)}, bf16[1024,2048]{1,0:T(8,128)(2,1)}, bf16[1024,2048]{1,0:T(8,128)(2,1)}, f32[25...) custom-call(bf16[256,1024]{1,0:T(8,128)(2,1)} %get-tuple-element.126, ...), custom_call_target="tpu_custom_call" | custom-call | flops 12884901888 | bytes 25165824 | tf_op jit(solution)/shard_map/mlp/pallas_call | solution.py:447
  112.0 0.5 collective-permute-done.5.got_ref
  112.5 0.3 copy-done.39
  112.8 0.5 copy-done.40
  113.3 17.1 %mlp.3 = (bf16[1024,1024]{1,0:T(8,128)(2,1)}, bf16[1024,1024]{1,0:T(8,128)(2,1)}, bf16[1024,2048]{1,0:T(8,128)(2,1)}, bf16[1024,2048]{1,0:T(8,128)(2,1)}, f32[25...) custom-call(bf16[256,1024]{1,0:T(8,128)(2,1)} %copy-done.31, ...), custom_call_target="tpu_custom_call", output_to_operand_aliasing={{0}: (7, {}), {1}: (8, {}), {2}: (9, {}), {3}: (10, {})} | custom-call | flops 12884901888 | bytes 25165824 | tf_op jit(solution)/shard_map/mlp/pallas_call | solution.py:447
  130.4 0.7 add.183
  131.1 1.3 stack.60.known
  132.4 164.1 %tail.1 = (bf16[2048,1024]{1,0:T(8,128)(2,1)}, bf16[1024,2048]{1,0:T(8,128)(2,1)}, bf16[512,1024]{1,0:T(8,128)(2,1)}, bf16[1024,512]{1,0:T(8,128)(2,1)}, bf16[10...) custom-call(bf16[1024,2048]{1,0:T(8,128)(2,1)} %get-tuple-element.69, ...), custom_call_target="tpu_custom_call" | custom-call | tf_op jit(solution)/shard_map/tail/pallas_call | solution.py:931
  296.5 0.9 slice.69
  297.5 0.8 slice_bitcast_fusion
  298.2 1.3 reduce_sum.142
  299.5 1.1 slice.70
  300.6 0.6 fusion.36
  301.3 1.8 fusion.39
  303.1 0.2 copy.34
  303.3 0.6 copy.37
  303.9 0.6 reshape.172
  304.5 1.6 convert_element_type.90
  306.1 6.8 %convert_element_type.91 = f32[1024,2048]{1,0:T(8,128)} convert(bf16[1024,2048]{1,0:T(8,128)(2,1)} %get-tuple-element.93) | non-fusion elementwise | flops 2097152 | bytes 12582912 | tf_op jit(solution)/shard_map/convert_element_type | solution.py:1030
  312.9 4.4 %convert_element_type.92 = f32[2048,1024]{1,0:T(8,128)} convert(bf16[2048,1024]{1,0:T(8,128)(2,1)S(1)} %copy-done.22) | non-fusion elementwise | flops 2097152 | bytes 12582912 | tf_op jit(solution)/shard_map/convert_element_type | solution.py:1030
  317.4 4.3 %fusion.40 = f32[128,6144]{1,0:T(8,128)} fusion(f32[16,128]{1,0:T(8,128)S(1)} %bitcast.65, f32[16,6144]{1,0:T(8,128)S(1)} %bitcast.56), kind=kOutput, calls=%fused_computation.91 | convolution fusion | flops 150994944 | bytes 3547136 | tf_op jit(solution)/shard_map/nc,nm->cm/dot_general | solution.py:1036
  321.7 3.2 maximum_convert_fusion
  324.9 1.0 copy.46
  325.9 1.0 copy.47
  (101 shorter events, 0.3 us)
Async XLA Ops:
  0.6 3.3 copy-start
  0.7 4.3 %copy-start.17 = (bf16[512,1024]{1,0:T(8,128)(2,1)S(1)}, bf16[512,1024]{1,0:T(8,128)(2,1)}, u32[]{:S(2)}) copy-start(bf16[512,1024]{1,0:T(8,128)(2,1)} %tokens_hbm.1) | copy-start | bytes 3145732
  0.7 4.2 %copy-start.32 = (f32[6144]{0:T(1024)S(1)}, f32[6144]{0:T(1024)}, u32[]{:S(2)}) copy-start(f32[6144]{0:T(1024)} %param.18) | copy-start | bytes 73732
  0.7 4.3 %copy-start.33 = (f32[1024]{0:T(1024)S(1)}, f32[1024]{0:T(1024)}, u32[]{:S(2)}) copy-start(f32[1024]{0:T(1024)} %param.19) | copy-start | bytes 12292
  0.7 8.5 %copy-start.41 = (s32[1,4]{1,0:T(1,128)S(1)}, s32[1,4]{1,0:T(1,128)}, u32[]{:S(2)}) copy-start(s32[1,4]{1,0:T(1,128)} %param.16) | copy-start | bytes 52
  6.2 17.4 %copy-start.9 = (bf16[256,1024]{1,0:T(8,128)(2,1)}, bf16[256,1024]{1,0:T(8,128)(2,1)S(1)}, u32[]{:S(2)}) copy-start(bf16[256,1024]{1,0:T(8,128)(2,1)S(1)} %get-tuple-element.109.own_ref) | copy-start | bytes 1572868
  6.2 14.9 %collective-permute-start = (bf16[256,1024]{1,0:T(8,128)(2,1)S(1)}, bf16[256,1024]{1,0:T(8,128)(2,1)S(1)}, u32[]{:S(2)}, u32[]{:S(2)}) collective-permute-start(bf16[256,1024]{1,0:T(8,128)(2,1)S(1)} %get-tuple-element.109.own_ref), channel_id=1, source_target_pairs={{0,1},{1,0},{2,3},{3,2},{4,5},{5,4},{6,7},{7,6},{8,9},{9,8},{10,11... | collective-permute-start | bytes 1572872 | tf_op jit(solution)/shard_map/ppermute | solution.py:959
  9.3 17.9 %copy-start.1 = (bf16[3,1024,512]{2,1,0:T(8,128)(2,1)S(1)}, bf16[3,1024,512]{2,1,0:T(8,128)(2,1)}, u32[]{:S(2)}) copy-start(bf16[3,1024,512]{2,1,0:T(8,128)(2,1)} %w_qkv_hbm.1) | copy-start | bytes 9437188
  9.4 43.9 %copy-start.11 = (s32[1024]{0:T(1024)}, s32[1024]{0:T(1024)S(1)}, u32[]{:S(2)}) copy-start(s32[1024]{0:T(1024)S(1)} %get-tuple-element.99) | copy-start | bytes 12292
  21.1 0.8 copy-start.14
  21.9 5.3 %copy-start.15 = (bf16[256,1024]{1,0:T(8,128)(2,1)S(1)}, bf16[256,1024]{1,0:T(8,128)(2,1)}, u32[]{:S(2)}) copy-start(bf16[256,1024]{1,0:T(8,128)(2,1)} %copy-done.14) | copy-start | bytes 1572868
  21.9 13.3 %collective-permute-start.1 = (bf16[256,1024]{1,0:T(8,128)(2,1)}, bf16[256,1024]{1,0:T(8,128)(2,1)S(1)}, u32[]{:S(2)}, u32[]{:S(2)}) collective-permute-start(bf16[256,1024]{1,0:T(8,128)(2,1)} %get-tuple-element.54.own_ref), channel_id=1, source_target_pairs={{0,1},{1,0},{2,3},{3,2},{4,5},{5,4},{6,7},{7,6},{8,9},{9,8},{10,11... | collective-permute-start | bytes 1572872 | tf_op jit(solution)/shard_map/ppermute | solution.py:959
  23.6 3.6 %copy-start.10 = (bf16[256,1024]{1,0:T(8,128)(2,1)S(1)}, bf16[256,1024]{1,0:T(8,128)(2,1)}, u32[]{:S(2)}) copy-start(bf16[256,1024]{1,0:T(8,128)(2,1)} %copy-done.9) | copy-start | bytes 1572868
  24.5 12.1 %copy-start.4 = (f32[1024,128]{1,0:T(8,128)}, f32[1024,128]{1,0:T(8,128)S(1)}, u32[]{:S(2)}) copy-start(f32[1024,128]{1,0:T(8,128)S(1)} %get-tuple-element.135.cos_ref.cosine) | copy-start | bytes 1572868
  24.5 12.1 %copy-start.5 = (f32[1024,128]{1,0:T(8,128)}, f32[1024,128]{1,0:T(8,128)S(1)}, u32[]{:S(2)}) copy-start(f32[1024,128]{1,0:T(8,128)S(1)} %get-tuple-element.136.sin_ref.sine) | copy-start | bytes 1572868
  27.2 14.0 %copy-start.30 = (bf16[256,1024]{1,0:T(8,128)(2,1)}, bf16[256,1024]{1,0:T(8,128)(2,1)S(1)}, u32[]{:S(2)}) copy-start(bf16[256,1024]{1,0:T(8,128)(2,1)S(1)} %get-tuple-element.58.b_own_ref) | copy-start | bytes 1572868
  35.2 18.1 %collective-permute-start.2 = (bf16[256,1024]{1,0:T(8,128)(2,1)S(1)}, bf16[256,1024]{1,0:T(8,128)(2,1)S(1)}, u32[]{:S(2)}, u32[]{:S(2)}) collective-permute-start(bf16[256,1024]{1,0:T(8,128)(2,1)S(1)} %get-tuple-element.58.b_own_ref), channel_id=1, source_target_pairs={{0,1},{1,0},{2,3},{3,2},{4,5},{5,4},{6,7},{7,6},{8,9},{9,8},{10,11... | collective-permute-start | bytes 1572872 | tf_op jit(solution)/shard_map/ppermute | solution.py:959
  41.2 1.4 copy-start.3
  42.6 10.7 %copy-start.2 = (bf16[3,1024,512]{2,1,0:T(8,128)(2,1)}, bf16[3,1024,512]{2,1,0:T(8,128)(2,1)S(1)}, u32[]{:S(2)}) copy-start(bf16[3,1024,512]{2,1,0:T(8,128)(2,1)S(1)} %get-tuple-element.60.q_ref.k_ref.v_ref.qkv_hbm) | copy-start | bytes 9437188
  42.8 10.5 %copy-start.6 = (s32[1024,128]{1,0:T(8,128)}, s32[1024,128]{1,0:T(8,128)S(1)}, u32[]{:S(2)}) copy-start(s32[1024,128]{1,0:T(8,128)S(1)} %broadcast_in_dim.27.segc_ref.segc) | copy-start | bytes 1572868
  42.8 9.3 %copy-start.16 = (bf16[512,1024]{1,0:T(8,128)(2,1)S(1)}, bf16[512,1024]{1,0:T(8,128)(2,1)}, u32[]{:S(2)}) copy-start(bf16[512,1024]{1,0:T(8,128)(2,1)} %w_out_hbm.1) | copy-start | bytes 3145732
  52.1 1.2 copy-start.12
  52.1 23.9 %copy-start.8 = (bf16[512,512]{1,0:T(8,128)(2,1)}, bf16[512,512]{1,0:T(8,128)(2,1)S(1)}, u32[]{:S(2)}) copy-start(bf16[512,512]{1,0:T(8,128)(2,1)S(1)} %get-tuple-element.59.mixed_a) | copy-start | bytes 1572868
  52.6 11.7 %collective-permute-start.3 = (bf16[256,1024]{1,0:T(8,128)(2,1)S(1)}, bf16[256,1024]{1,0:T(8,128)(2,1)S(1)}, u32[]{:S(2)}, u32[]{:S(2)}) collective-permute-start(bf16[256,1024]{1,0:T(8,128)(2,1)S(1)} %convolution_convert_fusion.1), channel_id=1, source_target_pairs={{0,1},{1,0},{2,3},{3,2},{4,5},{5,4},{6,7},{7,6},{8,9},{9,8},{10,11... | collective-permute-start | bytes 1572872 | tf_op jit(solution)/shard_map/ppermute | solution.py:959
  53.3 0.8 copy-start.38
  63.4 14.3 %copy-start.7 = (bf16[512,512]{1,0:T(8,128)(2,1)}, bf16[512,512]{1,0:T(8,128)(2,1)S(1)}, u32[]{:S(2)}) copy-start(bf16[512,512]{1,0:T(8,128)(2,1)S(1)} %get-tuple-element.62.mixed_b) | copy-start | bytes 1572868
  63.4 14.3 %copy-start.13 = (f32[8,1,512]{2,1,0:T(1,128)}, f32[8,1,512]{2,1,0:T(1,128)S(1)}, u32[]{:S(2)}) copy-start(f32[8,1,512]{2,1,0:T(1,128)S(1)} %get-tuple-element.85.lse_b) | copy-start | bytes 49156
  63.4 12.6 %copy-start.18 = (bf16[512,1024]{1,0:T(8,128)(2,1)S(1)}, bf16[512,1024]{1,0:T(8,128)(2,1)}, u32[]{:S(2)}) copy-start(bf16[512,1024]{1,0:T(8,128)(2,1)} %tokens_hbm.1) | copy-start | bytes 3145732
  64.7 10.9 %collective-permute-start.4 = (bf16[256,1024]{1,0:T(8,128)(2,1)S(1)}, bf16[256,1024]{1,0:T(8,128)(2,1)S(1)}, u32[]{:S(2)}, u32[]{:S(2)}) collective-permute-start(bf16[256,1024]{1,0:T(8,128)(2,1)S(1)} %convolution_convert_fusion), channel_id=1, source_target_pairs={{0,1},{1,0},{2,3},{3,2},{4,5},{5,4},{6,7},{7,6},{8,9},{9,8},{10,11... | collective-permute-start | bytes 1572872 | tf_op jit(solution)/shard_map/ppermute | solution.py:959
  76.0 1.7 copy-start.21
  76.1 2.6 copy-start.34
  77.7 1.0 copy-start.19
  77.7 2.2 copy-start.20
  77.7 3.3 %copy-start.36 = (f32[1024]{0:T(1024)S(1)}, f32[1024]{0:T(1024)}, u32[]{:S(2)}) copy-start(f32[1024]{0:T(1024)} %param.26) | copy-start | bytes 12292
  77.7 4.0 %copy-start.37 = (bf16[1,128]{1,0:T(2,128)(2,1)S(1)}, bf16[1,128]{1,0:T(2,128)(2,1)}, u32[]{:S(2)}) copy-start(bf16[1,128]{1,0:T(2,128)(2,1)} %param.15) | copy-start | bytes 772
  77.7 4.0 %copy-start.29 = (bf16[256,1024]{1,0:T(8,128)(2,1)S(1)}, bf16[256,1024]{1,0:T(8,128)(2,1)}, u32[]{:S(2)}) copy-start(bf16[256,1024]{1,0:T(8,128)(2,1)} %get-tuple-element.63.b_own_ref) | copy-start | bytes 1572868
  79.9 32.1 %copy-start.31 = (bf16[256,1024]{1,0:T(8,128)(2,1)}, bf16[256,1024]{1,0:T(8,128)(2,1)S(1)}, u32[]{:S(2)}) copy-start(bf16[256,1024]{1,0:T(8,128)(2,1)S(1)} %get-tuple-element.127.own_ref) | copy-start | bytes 1572868
  79.9 15.2 %collective-permute-start.7 = (bf16[256,1024]{1,0:T(8,128)(2,1)}, bf16[256,1024]{1,0:T(8,128)(2,1)}, u32[]{:S(2)}, u32[]{:S(2)}) collective-permute-start(bf16[256,1024]{1,0:T(8,128)(2,1)} %get-tuple-element.126.own_ref), channel_id=1, source_target_pairs={{0,1},{1,0},{2,3},{3,2},{4,5},{5,4},{6,7},{7,6},{8,9},{9,8},{10,11... | collective-permute-start | bytes 1572872 | tf_op jit(solution)/shard_map/ppermute | solution.py:959
  81.7 30.3 %collective-permute-start.6 = (bf16[256,1024]{1,0:T(8,128)(2,1)S(1)}, bf16[256,1024]{1,0:T(8,128)(2,1)S(1)}, u32[]{:S(2)}, u32[]{:S(2)}) collective-permute-start(bf16[256,1024]{1,0:T(8,128)(2,1)S(1)} %copy-done.29), channel_id=1, source_target_pairs={{0,1},{1,0},{2,3},{3,2},{4,5},{5,4},{6,7},{7,6},{8,9},{9,8},{10,11... | collective-permute-start | bytes 1572872 | tf_op jit(solution)/shard_map/ppermute | solution.py:959
  82.7 29.8 %collective-permute-start.5 = (bf16[256,1024]{1,0:T(8,128)(2,1)S(1)}, bf16[256,1024]{1,0:T(8,128)(2,1)S(1)}, u32[]{:S(2)}, u32[]{:S(2)}) collective-permute-start(bf16[256,1024]{1,0:T(8,128)(2,1)S(1)} %get-tuple-element.127.own_ref), channel_id=1, source_target_pairs={{0,1},{1,0},{2,3},{3,2},{4,5},{5,4},{6,7},{7,6},{8,9},{9,8},{10,11... | collective-permute-start | bytes 1572872 | tf_op jit(solution)/shard_map/ppermute | solution.py:959
  112.0 0.8 copy-start.39
  112.5 0.8 copy-start.40
  113.3 17.1 %copy-start.35 = (f32[1,2048]{1,0:T(1,128)S(1)}, f32[1,2048]{1,0:T(1,128)}, u32[]{:S(2)}) copy-start(f32[1,2048]{1,0:T(1,128)} %get-tuple-element.82) | copy-start | bytes 24580
  296.5 8.0 %copy-start.26 = (bf16[512,1024]{1,0:T(8,128)(2,1)S(1)}, bf16[512,1024]{1,0:T(8,128)(2,1)}, u32[]{:S(2)}) copy-start(bf16[512,1024]{1,0:T(8,128)(2,1)} %get-tuple-element.92) | copy-start | bytes 3145732
  306.1 6.8 %copy-start.22 = (bf16[2048,1024]{1,0:T(8,128)(2,1)S(1)}, bf16[2048,1024]{1,0:T(8,128)(2,1)}, u32[]{:S(2)}) copy-start(bf16[2048,1024]{1,0:T(8,128)(2,1)} %get-tuple-element.94) | copy-start | bytes 12582916
  317.4 4.3 %copy-start.23 = (bf16[1024,512]{1,0:T(8,128)(2,1)S(1)}, bf16[1024,512]{1,0:T(8,128)(2,1)}, u32[]{:S(2)}) copy-start(bf16[1024,512]{1,0:T(8,128)(2,1)} %get-tuple-element.89) | copy-start | bytes 3145732
  317.4 4.3 %copy-start.24 = (bf16[1024,512]{1,0:T(8,128)(2,1)S(1)}, bf16[1024,512]{1,0:T(8,128)(2,1)}, u32[]{:S(2)}) copy-start(bf16[1024,512]{1,0:T(8,128)(2,1)} %get-tuple-element.90) | copy-start | bytes 3145732
  317.4 4.3 %copy-start.25 = (bf16[1024,512]{1,0:T(8,128)(2,1)S(1)}, bf16[1024,512]{1,0:T(8,128)(2,1)}, u32[]{:S(2)}) copy-start(bf16[1024,512]{1,0:T(8,128)(2,1)} %get-tuple-element.91) | copy-start | bytes 3145732
  321.7 3.2 copy-start.28
  321.7 4.2 %copy-start.27 = (bf16[2,256,1024]{2,1,0:T(8,128)(2,1)S(1)}, bf16[2,256,1024]{2,1,0:T(8,128)(2,1)}, u32[]{:S(2)}) copy-start(bf16[2,256,1024]{2,1,0:T(8,128)(2,1)} %get-tuple-element.87) | copy-start | bytes 3145732

commit v6 on v5

--- a/solution.py
+++ b/solution.py
@@ -276,213 +276,6 @@
     )(flags, qkv, qkv, qkv, grad, mixed, lse, seg_rows, seg_cols, cosine, sine)
 
 
-def qkv_pair_kernel(own_ref, got_ref, w_ref, cos_ref, sin_ref, *refs):
-    o_ref, rows_ref = refs[-2:]
-    which = pl.program_id(0)
-    half = own_ref.shape[0]
-
-    @pl.when(which == 0)
-    def _():
-        rows_ref[:half, :] = own_ref[...]
-        rows_ref[half:, :] = got_ref[...]
-
-    y = mm(rows_ref[...], w_ref[...], 1, 0)
-
-    @pl.when(which < 2)
-    def _():
-        factor = jnp.where(which == 0, HEAD**-0.5, 1.0)
-        for p in range(y.shape[1] // PAIR):
-            u = y[:, p * PAIR : (p + 1) * PAIR]
-            r = u * cos_ref[...] + turned(u) * sin_ref[...]
-            o_ref[:, p * PAIR : (p + 1) * PAIR] = (r.astype(bf16) * factor.astype(bf16)).astype(bf16)
-
-    @pl.when(which == 2)
-    def _():
-        o_ref[...] = y.astype(bf16)
-
-
-def project_pair(j, own, got, w_qkv, cosine, sine, before, length):
-    half, depth = own.shape
-    width = w_qkv.shape[2]
-    chunk = 2 * half
-    table = pl.BlockSpec((chunk, PAIR), lambda t: (j, 0))
-    return pl.pallas_call(
-        qkv_pair_kernel,
-        grid=(3,),
-        in_specs=[
-            pl.BlockSpec((half, depth), lambda t: (0, 0)),
-            pl.BlockSpec((half, depth), lambda t: (0, 0)),
-            pl.BlockSpec((None, depth, width), lambda t: (t, 0, 0)),
-            table,
-            table,
-            *[pl.BlockSpec(memory_space=pl.ANY) for _ in before],
-        ],
-        out_specs=[
-            pl.BlockSpec((None, chunk, width), lambda t: (t, j, 0)),
-            pl.BlockSpec((chunk, depth), lambda t: (j, 0)),
-        ],
-        out_shape=[
-            jax.ShapeDtypeStruct((3, length, width), bf16),
-            jax.ShapeDtypeStruct((length, depth), bf16),
-        ],
-        input_output_aliases={5 + i: i for i in range(len(before))},
-        compiler_params=pltpu.CompilerParams(vmem_limit_bytes=32 << 20),
-        cost_estimate=pl.CostEstimate(
-            flops=6 * chunk * depth * width, bytes_accessed=8 * depth * width, transcendentals=0
-        ),
-        name="qkv",
-    )(own, got, w_qkv, cosine, sine, *before)
-
-
-def forward_chunk_kernel(q_ref, k_ref, v_ref, segr_ref, segc_ref, o_ref, lse_ref, vt):
-    length, count = k_ref.shape[0], q_ref.shape[0]
-    for b in range(0, length, BLOCK):
-        vt[:, b : b + BLOCK] = transposed(v_ref[b : b + BLOCK, :]).astype(bf16)
-    q = q_ref[...]
-    outs = []
-    for h in range(2):
-        qh = head_lanes(q, h)
-        scores = []
-        for b in range(0, length, BLOCK):
-            same = jnp.concatenate([segc_ref[b : b + BLOCK, :]] * (count // 128), axis=1) == segr_ref[...]
-            scores.append(jnp.where(same, mm(k_ref[b : b + BLOCK, :], qh, 1, 1), masked_score))
-        top = functools.reduce(jnp.maximum, [jnp.max(s, axis=0, keepdims=True) for s in scores])
-        total, summed = 0.0, 0.0
-        for i, s in enumerate(scores):
-            p = jnp.exp(s - top)
-            total = total + jnp.sum(p, axis=0, keepdims=True)
-            summed = summed + mm(vt[h * HEAD : (h + 1) * HEAD, i * BLOCK : (i + 1) * BLOCK], p.astype(bf16), 1, 0)
-        lse_ref[h] = top + jnp.log(total)
-        outs.append(summed / total)
-    o_ref[...] = jnp.concatenate(outs, axis=0).T.astype(bf16)
-
-
-def pair_pieces(j, length, chunk):
-    return [
-        pl.BlockSpec((None, chunk, PAIR), lambda p: (0, j, p)),
-        pl.BlockSpec((None, length, PAIR), lambda p: (1, 0, p)),
-        pl.BlockSpec((None, length, PAIR), lambda p: (2, 0, p)),
-    ]
-
-
-def attend_forward_pair(j, chunk, qkv, seg_rows, seg_cols):
-    _, length, width = qkv.shape
-    pairs = width // PAIR
-    return pl.pallas_call(
-        forward_chunk_kernel,
-        grid=(pairs,),
-        in_specs=[
-            *pair_pieces(j, length, chunk),
-            pl.BlockSpec((1, chunk), lambda p: (0, j)),
-            pl.BlockSpec((length, 128), lambda p: (0, 0)),
-        ],
-        out_specs=[
-            pl.BlockSpec((chunk, PAIR), lambda p: (0, p)),
-            pl.BlockSpec((2, 1, chunk), lambda p: (p, 0, 0)),
-        ],
-        out_shape=[
-            jax.ShapeDtypeStruct((chunk, width), bf16),
-            jax.ShapeDtypeStruct((2 * pairs, 1, chunk), f32),
-        ],
-        scratch_shapes=[pltpu.VMEM((PAIR, length), bf16)],
-        compiler_params=pltpu.CompilerParams(vmem_limit_bytes=48 << 20),
-        cost_estimate=pl.CostEstimate(
-            flops=16 * chunk * length * width,
-            bytes_accessed=8 * length * width,
-            transcendentals=chunk * length * width // HEAD,
-        ),
-        name="attend",
-    )(qkv, qkv, qkv, seg_rows, seg_cols)
-
-
-def mlp_kernel(own_ref, got_ref, b_own_ref, b_got_ref, up_ref, bias_ref, down_ref, *refs):
-    rows_ref, back, hidden_ref, pre_ref, own_grad, got_grad, own_branch, got_branch, bias_grad, grads, branch = refs[-11:]
-    tile, tiles = pl.program_id(0), pl.num_programs(0)
-    half = own_ref.shape[0]
-
-    @pl.when(tile == 0)
-    def _():
-        rows_ref[:half, :] = own_ref[...]
-        rows_ref[half:, :] = got_ref[...]
-        back[:half, :] = b_own_ref[...]
-        back[half:, :] = b_got_ref[...]
-
-    cubic, root = 0.044715, (2.0 / jnp.pi) ** 0.5
-    u = mm(rows_ref[...], up_ref[...], 1, 0) + bias_ref[...]
-    square = u * u
-    t = jnp.tanh(u * (root + (root * cubic) * square))
-    rising = 0.5 * (1.0 + t)
-    hidden = (u * rising).astype(bf16)
-    slope = rising + (0.5 * u) * (1.0 - t * t) * (root + (3.0 * cubic * root) * square)
-    grad = (mm(back[...], down_ref[...], 1, 1) * slope).astype(bf16)
-    hidden_ref[...] = hidden
-    pre_ref[...] = grad
-    bias_grad[...] = jnp.sum(grad.astype(f32), axis=0, keepdims=True)
-    more, more_branch = mm(grad, up_ref[...], 1, 1), mm(hidden, down_ref[...], 1, 0)
-
-    @pl.when(tile == 0)
-    def _():
-        grads[...] = more
-        branch[...] = more_branch
-
-    @pl.when(tile > 0)
-    def _():
-        grads[...] += more
-        branch[...] += more_branch
-
-    @pl.when(tile == tiles - 1)
-    def _():
-        own_grad[...] = grads[:half, :]
-        got_grad[...] = grads[half:, :].astype(bf16)
-        own_branch[...] = branch[:half, :]
-        got_branch[...] = branch[half:, :].astype(bf16)
-
-
-def mlp_pair(j, own, got, back_own, back_got, w_up, b_up, w_down, before, length):
-    half, depth = own.shape
-    width = w_up.shape[1]
-    chunk, tile = 2 * half, min(width, 1024)
-    small = pl.BlockSpec((half, depth), lambda t: (0, 0))
-    wide = pl.BlockSpec((chunk, tile), lambda t: (j, t))
-    return pl.pallas_call(
-        mlp_kernel,
-        grid=(width // tile,),
-        in_specs=[
-            small, small, small, small,
-            pl.BlockSpec((depth, tile), lambda t: (0, t)),
-            pl.BlockSpec((1, tile), lambda t: (0, t)),
-            pl.BlockSpec((tile, depth), lambda t: (t, 0)),
-            *[pl.BlockSpec(memory_space=pl.ANY) for _ in before],
-        ],
-        out_specs=[
-            pl.BlockSpec((chunk, depth), lambda t: (j, 0)), pl.BlockSpec((chunk, depth), lambda t: (j, 0)), wide, wide,
-            small, small, small, small,
-            pl.BlockSpec((1, tile), lambda t: (0, t)),
-        ],
-        out_shape=[
-            jax.ShapeDtypeStruct((length, depth), bf16),
-            jax.ShapeDtypeStruct((length, depth), bf16),
-            jax.ShapeDtypeStruct((length, width), bf16),
-            jax.ShapeDtypeStruct((length, width), bf16),
-            jax.ShapeDtypeStruct((half, depth), f32),
-            jax.ShapeDtypeStruct((half, depth), bf16),
-            jax.ShapeDtypeStruct((half, depth), f32),
-            jax.ShapeDtypeStruct((half, depth), bf16),
-            jax.ShapeDtypeStruct((1, width), f32),
-        ],
-        scratch_shapes=[
-            pltpu.VMEM((chunk, depth), f32),
-            pltpu.VMEM((chunk, depth), f32),
-        ],
-        input_output_aliases={7 + i: i for i in range(len(before))},
-        compiler_params=pltpu.CompilerParams(vmem_limit_bytes=56 << 20),
-        cost_estimate=pl.CostEstimate(
-            flops=12 * chunk * depth * width, bytes_accessed=12 * depth * width, transcendentals=chunk * width
-        ),
-        name="mlp",
-    )(own, got, back_own, back_got, w_up, b_up[None, :], w_down, *before)
-
-
 MESH = pl.DeviceIdType.MESH
 ADD_ROWS = 32
 STEPS = 9
@@ -498,13 +291,13 @@
 
 
 class Unit:
-    def __init__(self, part, out, column, got, send, recv, local, place):
+    def __init__(self, part, out, column, got, send, recv, local, place, bits=(0, 1, 2, 3)):
         self.part, self.out, self.got = part, out, got
         self.send, self.recv, self.local = send, recv, local
         self.rows, columns = 2 * got[0].shape[0], got[0].shape[1]
         self.columns = pl.ds(column, columns)
-        self.bit = [(place // (1 << b)) % 2 for b in range(EDGES)]
-        self.partner = [place + (1 - 2 * self.bit[b]) * (1 << b) for b in range(EDGES)]
+        self.bit = [(place // (1 << b)) % 2 for b in bits]
+        self.partner = [place + (1 - 2 * bit) * (1 << b) for bit, b in zip(self.bit, bits, strict=True)]
         self.base = [0]
         for b in range(EDGES):
             self.base.append(self.base[-1] + self.bit[b] * (self.rows >> (b + 1)))
@@ -576,26 +369,280 @@
 
 
 ORDER = (
-    (6.5, 1, 1), (10, 3, 1), (10, 1, 2), (10, 1, 3), (10.5, 2, 1), (10.5, 3, 2), (10.5, 0, 1), (11.5, 1, 4),
-    (13.5, 1, 5), (13.5, 3, 3), (15.5, 3, 4), (16.5, 1, 6), (16.5, 2, 2), (18.5, 4, 1), (18.5, 3, 5), (19.5, 0, 2),
-    (19.5, 2, 3), (20.5, 3, 6), (21.5, 4, 2), (21.5, 2, 4), (22.5, 0, 3), (23.5, 5, 1), (24.5, 6, 1), (25.5, 4, 3),
-    (25.5, 3, 7), (25.5, 7, 1), (25.5, 2, 5), (27.5, 3, 8), (29.5, 4, 4), (30.5, 1, 7), (30.5, 0, 4), (31, 5, 2),
-    (31, 2, 6), (31, 1, 8), (31, 4, 5), (32, 0, 5), (32, 5, 3), (32, 4, 6), (32, 5, 4), (32.5, 5, 5), (33, 0, 6),
-    (34, 7, 2), (34, 2, 7), (34, 5, 6), (34, 4, 7), (35, 2, 8), (35, 4, 8), (35, 7, 3), (35, 6, 2), (36, 7, 4),
-    (36, 6, 3), (36, 7, 5), (36, 5, 7), (36, 6, 4), (36, 5, 8), (36, 7, 6), (36, 6, 5), (37, 6, 6), (37, 0, 7),
-    (99, 0, 8), (99, 7, 7), (99, 7, 8), (99, 6, 7), (99, 6, 8),
+    (3.5, 0, 1), (5.5, 1, 1), (7.5, 2, 1), (7.5, 0, 2), (9.5, 1, 2), (9.5, 0, 3), (10, 3, 1), (10, 0, 4), (10, 1, 3),
+    (10, 2, 2), (10.5, 4, 1), (10.5, 1, 4), (10.5, 0, 5), (12.5, 1, 5), (12.5, 2, 3), (13.5, 3, 2), (13.5, 0, 6),
+    (14.5, 2, 4), (15.5, 1, 6), (15.5, 4, 2), (15.5, 3, 3), (15.5, 0, 7), (17.5, 0, 8), (17.5, 2, 5), (18.5, 5, 1),
+    (18.5, 1, 7), (19.5, 1, 8), (19.5, 3, 4), (20.5, 5, 2), (20.5, 4, 3), (20.5, 2, 6), (21.5, 3, 5), (23.5, 5, 3),
+    (23.5, 4, 4), (23.5, 6, 1), (26.5, 7, 1), (26.5, 5, 4), (26.5, 2, 7), (29.5, 6, 2), (29.5, 8, 1), (29.5, 5, 5),
+    (29.5, 2, 8), (30.5, 4, 5), (31, 7, 2), (31, 3, 6), (32, 6, 3), (32, 8, 2), (32, 6, 4), (32, 7, 3), (32, 5, 6),
+    (33, 4, 6), (33, 3, 7), (33, 8, 3), (33, 6, 5), (33, 7, 4), (34, 3, 8), (34, 8, 4), (34, 5, 7), (34, 7, 5),
+    (35, 5, 8), (35, 6, 6), (35, 8, 5), (36, 7, 6), (36, 4, 7), (36, 4, 8), (36, 6, 7), (36, 8, 6), (37, 6, 8),
+    (99, 7, 7), (99, 7, 8), (99, 8, 7), (99, 8, 8),
 )
 WIDE = 512
 STEP_ROWS = 64
 
 
+def fetcher(sems):
+    count = [0]
+
+    def fetch(src, dst):
+        copy = pltpu.make_async_copy(src, dst, sems.at[count[0]])
+        copy.start()
+        count[0] += 1
+        return copy
+
+    return fetch
+
+
+def head_kernel(
+    tokens_hbm, cot_hbm, w_qkv_hbm, w_out_hbm, w_up_hbm, w_down_hbm,
+    mods, gain_one, gain_two, sequence, b_up, segr, segc, cosine, sine,
+    qkv_out, mixed_out, one_out, back_out, two_out, hidden_out, pre_out, own_grad, send_grad, middle_out,
+    projected_out, own_branch, send_branch, lse, known,
+    tokens, cot, w_qkv, w_out, w_up, w_down, rows_one, full_back, rows_two, qkv, mixed, from_sum, send_sum, projected,
+    middle, hidden, pre, grads, branch, low_grads, low_branch, bias, bias_down, load, x_send, x_recv,
+):
+    me = lax.axis_index("tensor")
+    length, depth = rows_one.shape
+    chunks, half, _ = from_sum.shape
+    chunk = 2 * half
+    width = mixed.shape[1]
+    pairs = width // PAIR
+    across = {"tensor": 1 - me}
+    each = range(chunks)
+    own = [slice(c * chunk, c * chunk + half) for c in each]
+    got = [slice(c * chunk + half, (c + 1) * chunk) for c in each]
+    whole = [slice(c * chunk, (c + 1) * chunk) for c in each]
+    fetch = fetcher(load)
+
+    def x_copy(src, dst, i):
+        return pltpu.make_async_remote_copy(
+            src_ref=src, dst_ref=dst, send_sem=x_send.at[i], recv_sem=x_recv.at[i],
+            device_id=across, device_id_type=MESH,
+        )
+
+    ones = [x_copy(rows_one.at[own[c]], rows_one.at[got[c]], c) for c in each]
+    backs = [x_copy(full_back.at[own[c]], full_back.at[got[c]], chunks + c) for c in each]
+    shares = [x_copy(send_sum.at[c], from_sum.at[c], 2 * chunks + c) for c in each]
+    twos = [x_copy(rows_two.at[own[c]], rows_two.at[got[c]], 3 * chunks + c) for c in each]
+
+    shift_a, scale_a, gate_a, shift_m, scale_m, gate_m = [mods[r : r + 1, :] for r in range(6)]
+    gain_one, gain_two = gain_one[...], gain_two[...]
+    reads = [fetch(tokens_hbm, tokens), fetch(w_qkv_hbm, w_qkv), fetch(cot_hbm, cot)]
+    reads += [fetch(w_out_hbm, w_out), fetch(w_up_hbm, w_up), fetch(w_down_hbm, w_down)]
+    writes = []
+    greet([across])
+
+    def normal_of(values):
+        center = values - jnp.mean(values, axis=1, keepdims=True)
+        return center * lax.rsqrt(jnp.mean(center * center, axis=1, keepdims=True) + norm_eps)
+
+    def by_rows(work):
+        @pl.loop(0, half // STEP_ROWS)
+        def _(i):
+            work(pl.multiple_of(i * STEP_ROWS, STEP_ROWS))
+
+    reads[0].wait()
+    for c in each:
+
+        def first_norm(at, c=c):
+            values = tokens[pl.ds(c * half + at, STEP_ROWS), :].astype(f32)
+            out = normal_of(values) * gain_one * (1.0 + scale_a) + shift_a
+            rows_one[pl.ds(c * chunk + at, STEP_ROWS), :] = out.astype(bf16)
+
+        by_rows(first_norm)
+        if c == 0:
+            ones[c].start()
+    reads[2].wait()
+    bias_down[...] = jnp.zeros(bias_down.shape, f32)
+    for c in each:
+
+        def weigh(at, c=c):
+            low = (cot[pl.ds(c * half + at, STEP_ROWS), :].astype(f32) * gate_m).astype(bf16)
+            full_back[pl.ds(c * chunk + at, STEP_ROWS), :] = low
+            bias_down[...] += jnp.sum(low.astype(f32), axis=0, keepdims=True)
+
+        by_rows(weigh)
+    reads[1].wait()
+
+    def project(c):
+        rows = whole[c]
+        for t in range(3):
+            y = mm(rows_one[rows, :], w_qkv[t], 1, 0)
+            if t == 2:
+                qkv[t, rows, :] = y.astype(bf16)
+                continue
+            for p in range(pairs):
+                lanes = slice(p * PAIR, (p + 1) * PAIR)
+                u = y[:, lanes]
+                low = (u * cosine[rows, :] + turned(u) * sine[rows, :]).astype(bf16)
+                qkv[t, rows, lanes] = low * jnp.asarray(HEAD**-0.5 if t == 0 else 1.0, bf16)
+
+    ones[0].wait()
+    ones[1].start()
+    project(0)
+    ones[1].wait()
+    backs[0].start()
+    project(1)
+    writes.append(fetch(rows_one, one_out))
+    writes.append(fetch(qkv, qkv_out))
+
+    def attend(p, c):
+        lanes = pl.ds(pl.multiple_of(p * PAIR, PAIR), PAIR)
+        q = qkv[0, whole[c], lanes]
+        docs = segr[:, whole[c]]
+        outs = []
+        for h in range(2):
+            qh = head_lanes(q, h)
+            scores = []
+            for b in range(0, length, BLOCK):
+                same = jnp.concatenate([segc[b : b + BLOCK, :]] * (chunk // 128), axis=1) == docs
+                scores.append(jnp.where(same, mm(qkv[1, b : b + BLOCK, lanes], qh, 1, 1), masked_score))
+            top = functools.reduce(jnp.maximum, [jnp.max(s, axis=0, keepdims=True) for s in scores])
+            total, summed = 0.0, 0.0
+            for i, s in enumerate(scores):
+                pr = jnp.exp(s - top)
+                total = total + jnp.sum(pr, axis=0, keepdims=True)
+                v = transposed(qkv[2, i * BLOCK : (i + 1) * BLOCK, lanes]).astype(bf16)
+                summed = summed + mm(v[h * HEAD : (h + 1) * HEAD, :], pr.astype(bf16), 1, 0)
+            lse[c, 2 * p + h] = top + jnp.log(total)
+            outs.append(summed / total)
+        mixed[whole[c], lanes] = jnp.concatenate(outs, axis=0).T.astype(bf16)
+
+    for c in each:
+
+        @pl.loop(0, pairs)
+        def _(p):
+            attend(p, c)
+
+        if c == 0:
+            reads[3].wait()
+        send_sum[c] = mm(mixed[got[c], :], w_out[...], 1, 0).astype(bf16)
+        shares[c].start()
+        projected[c] = mm(mixed[own[c], :], w_out[...], 1, 0)
+    writes.append(fetch(mixed, mixed_out))
+
+    def second_norm(c):
+        shares[c].wait()
+
+        def work(at):
+            rows = pl.ds(at, STEP_ROWS)
+            share = projected[c, rows, :] + from_sum[c, rows, :].astype(f32)
+            projected[c, rows, :] = share
+            values = tokens[pl.ds(c * half + at, STEP_ROWS), :].astype(f32) + gate_a * share
+            middle[c, rows, :] = values
+            out = normal_of(values) * gain_two * (1.0 + scale_m) + shift_m
+            rows_two[pl.ds(c * chunk + at, STEP_ROWS), :] = out.astype(bf16)
+
+        by_rows(work)
+        twos[c].start()
+
+    cubic, root = 0.044715, (2.0 / jnp.pi) ** 0.5
+    tile = 2 * WIDE
+    bias[...] = jnp.zeros(bias.shape, f32)
+    held = [[], []]
+
+    def feed_forward(slot, rows):
+        for copy in held[slot]:
+            copy.wait()
+
+        @pl.loop(0, w_up.shape[1] // tile)
+        def _(t):
+            at = pl.ds(pl.multiple_of(t * tile, tile), tile)
+            u = mm(rows_two[rows, :], w_up[:, at], 1, 0) + b_up[:, at]
+            square = u * u
+            t_h = jnp.tanh(u * (root + (root * cubic) * square))
+            rising = 0.5 * (1.0 + t_h)
+            low_hidden = (u * rising).astype(bf16)
+            slope = rising + (0.5 * u) * (1.0 - t_h * t_h) * (root + (3.0 * cubic * root) * square)
+            low = (mm(full_back[rows, :], w_down[at, :], 1, 1) * slope).astype(bf16)
+            hidden[slot, :, at] = low_hidden
+            pre[slot, :, at] = low
+            bias[:, at] += jnp.sum(low.astype(f32), axis=0, keepdims=True)
+            more, more_branch = mm(low, w_up[:, at], 1, 1), mm(low_hidden, w_down[at, :], 1, 0)
+
+            @pl.when(t == 0)
+            def _():
+                grads[slot] = more
+                branch[slot] = more_branch
+
+            @pl.when(t > 0)
+            def _():
+                grads[slot] += more
+                branch[slot] += more_branch
+
+        held[slot] = [fetch(hidden.at[slot], hidden_out.at[rows]), fetch(pre.at[slot], pre_out.at[rows])]
+
+    second_norm(0)
+    for read in reads[4:]:
+        read.wait()
+    for c in each:
+        if c:
+            second_norm(c)
+        feed_forward(c, own[c])
+        held[c] += [fetch(grads.at[c], own_grad.at[c]), fetch(branch.at[c], own_branch.at[c])]
+    writes.append(fetch(middle, middle_out))
+    writes.append(fetch(projected, projected_out))
+    for c in each:
+        twos[c].wait()
+        backs[c].wait()
+        if c == 0:
+            backs[1].start()
+        feed_forward(c, got[c])
+        low_grads[c] = grads[c].astype(bf16)
+        low_branch[c] = branch[c].astype(bf16)
+        writes += [fetch(low_grads.at[c], send_grad.at[c]), fetch(low_branch.at[c], send_branch.at[c]), *held[c]]
+    writes += [fetch(full_back, back_out), fetch(rows_two, two_out)]
+    known[...] = jnp.concatenate(
+        [
+            jnp.zeros((8, depth), f32), bias_down[...], bias[:, :depth], bias[:, depth:], sequence[...],
+            jnp.zeros((4, depth), f32),
+        ],
+        axis=0,
+    )
+    for copy in writes:
+        copy.wait()
+
+
+def head(tokens, cot, w_qkv, w_out, w_up, w_down, *near_args, chunks):
+    own, depth = tokens.shape
+    length, width, wide = 2 * own, w_qkv.shape[2], w_up.shape[1]
+    half = own // chunks
+    anywhere, near = pl.BlockSpec(memory_space=pl.ANY), pl.BlockSpec(memory_space=pltpu.VMEM)
+    shaped, kept = jax.ShapeDtypeStruct, pltpu.VMEM
+    parts, rows = (chunks, half, depth), (length, depth)
+    return pl.pallas_call(
+        head_kernel,
+        in_specs=[anywhere] * 6 + [near] * len(near_args),
+        out_specs=[anywhere] * 13 + [near] * 2,
+        out_shape=[
+            shaped((3, length, width), bf16), shaped((length, width), bf16), *[shaped(rows, bf16)] * 3,
+            *[shaped((length, wide), bf16)] * 2, shaped(parts, f32), shaped(parts, bf16),
+            shaped(parts, f32), shaped(parts, f32), shaped(parts, f32), shaped(parts, bf16),
+            shaped((chunks, width // HEAD, 1, length // chunks), f32), shaped((16, depth), f32),
+        ],
+        scratch_shapes=[
+            kept(tokens.shape, bf16), kept(tokens.shape, bf16), kept(w_qkv.shape, bf16), kept(w_out.shape, bf16),
+            kept(w_up.shape, bf16), kept(w_down.shape, bf16), *[kept(rows, bf16)] * 3, kept((3, length, width), bf16),
+            kept((length, width), bf16), kept(parts, bf16), kept(parts, bf16), kept(parts, f32), kept(parts, f32),
+            *[kept((chunks, half, wide), bf16)] * 2, *[kept(parts, f32)] * 2,
+            kept(parts, bf16), kept(parts, bf16), kept((1, wide), f32), kept((1, depth), f32),
+            pltpu.SemaphoreType.DMA((32,)),
+            pltpu.SemaphoreType.DMA((4 * chunks,)), pltpu.SemaphoreType.DMA((4 * chunks,)),
+        ],
+        compiler_params=pltpu.CompilerParams(collective_id=2, has_side_effects=True, vmem_limit_bytes=61 << 20),
+        name="head",
+    )(tokens, cot, w_qkv, w_out, w_up, w_down, *near_args)
+
+
 def tail_kernel(
-    hidden, full_back, rows_two, grad_pre, qkv_hbm, mixed_a, mixed_b, rows_hbm, w_qkv_hbm, w_out_hbm,
-    grad_a, grad_b, got_a, got_b, mid_a, mid_b, proj_a, proj_b, branch_a, branch_b, send_a, send_b, tokens_hbm, cot_hbm,
-    rows_of, known, lse_a, lse_b, segr, segc, cosine, sine,
-    down_sum, up_sum, out_sum, q_sum, k_sum, v_sum, output, grad_x, everyone,
+    hidden, full_back, rows_two, grad_pre, qkv_hbm, mixed_hbm, rows_hbm, w_qkv_hbm, w_out_hbm,
+    own_grad, send_grad, mid_hbm, proj_hbm, own_branch, send_branch, tokens_hbm, cot_hbm,
+    mods, gain_one, gain_two, b_down, known, lse, segr, segc, cosine, sine,
+    down_sum, up_sum, out_sum, q_sum, k_sum, v_sum, output, ada, grad_x, mine, total,
     qkv, mixed, rows_one, w_qkv, w_out, proj, mix_grad, d_qkv, dk, dv, from_x, grads, middle, projected, tokens, cot,
-    part_a, part_b, part_c, part_d, part_e, branch_got, col_sums, small, small_got,
+    part_a, part_b, part_c, part_d, part_e, branch_got, col_sums, small, small_got, everyone,
     load, store, x_send, x_recv, all_send, all_recv, *more,
 ):
     place, me = lax.axis_index("dp"), lax.axis_index("tensor")
@@ -607,7 +654,9 @@
     across = {"tensor": 1 - me}
 
     specs = [
-        (part_a, down_sum.at[pl.ds(0, depth)], 0), (part_b, down_sum.at[pl.ds(depth, depth)], 0),
+        (part_a.at[pl.ds(0, WIDE)], down_sum.at[pl.ds(0, WIDE)], 0),
+        (part_a.at[pl.ds(WIDE, WIDE)], down_sum.at[pl.ds(WIDE, WIDE)], 0),
+        (part_b, down_sum.at[pl.ds(depth, depth)], 0),
         (part_c, up_sum, 0), (part_d, up_sum, depth), (part_e, out_sum, 0),
         (qkv.at[2], v_sum, 0), (qkv.at[1], k_sum, 0), (qkv.at[0], q_sum, 0),
     ]
@@ -623,24 +672,17 @@
         )
 
     each = range(chunks)
-    grads_in = [x_copy((got_a, got_b)[c], from_x.at[c], c) for c in each]
+    grads_in = [x_copy(send_grad.at[c], from_x.at[c], c) for c in each]
     projs = [x_copy(proj.at[c, :half], proj.at[c, half:], chunks + c) for c in each]
     ones = [x_copy(proj.at[c, :half], from_x.at[c], 2 * chunks + c) for c in each]
-    branches = [x_copy((send_a, send_b)[c], branch_got.at[c], 3 * chunks + c) for c in each]
+    branches = [x_copy(send_branch.at[c], branch_got.at[c], 3 * chunks + c) for c in each]
     smalls = x_copy(small, small_got, 4 * chunks)
     outputs = [
         pltpu.make_async_copy(branch_got.at[c], output.at[c * half : (c + 1) * half], store.at[c]) for c in each
     ]
     partner = units[0].partner
 
-    loads = []
-
-    def fetch(src, dst):
-        copy = pltpu.make_async_copy(src, dst, load.at[len(loads)])
-        copy.start()
-        loads.append(copy)
-        return copy
-
+    fetch = fetcher(load)
     done = [0]
 
     def until(place_now):
@@ -657,7 +699,7 @@
     hiddens = [fetch(hidden.at[:, cut(t)], slots[t]) for t in range(4)]
     norms = [
         [fetch(src, dst.at[c]) for src, dst in (
-            ((grad_a, grad_b)[c], grads), ((mid_a, mid_b)[c], middle), ((proj_a, proj_b)[c], projected),
+            (own_grad.at[c], grads), (mid_hbm.at[c], middle), (proj_hbm.at[c], projected),
             (tokens_hbm.at[c * half : (c + 1) * half], tokens), (cot_hbm.at[c * half : (c + 1) * half], cot),
         )]
         for c in each
@@ -679,11 +721,10 @@
             part[to, :] = mm(slots[t][:, at], rows_one[...], 0, 0).astype(bf16)
 
         pres.append(fetch(grad_pre.at[:, cut(t)], slots[t]))
-        if t % 2:
-            units[t // 2].step(0)
+        if t != 2:
+            units[min(t, 2)].step(0)
     main = [
-        fetch(w_out_hbm, w_out), fetch(mixed_a, mixed.at[:chunk]), fetch(mixed_b, mixed.at[chunk:]),
-        fetch(qkv_hbm, qkv), fetch(rows_hbm, rows_one),
+        fetch(w_out_hbm, w_out), fetch(mixed_hbm, mixed), fetch(qkv_hbm, qkv), fetch(rows_hbm, rows_one),
     ]
 
     def up_part(t):
@@ -707,7 +748,8 @@
         back = inner - jnp.mean(inner, axis=1, keepdims=True) - normal * jnp.mean(inner * normal, axis=1, keepdims=True)
         return root * back, normal
 
-    gain_two, scale_m, gate_a, gain_one, scale_a, gate_m, b_down = [rows_of[r : r + 1, :] for r in range(7)]
+    scale_a, gate_a, scale_m, gate_m = [mods[r : r + 1, :] for r in (1, 2, 4, 5)]
+    gain_one, gain_two, b_down = gain_one[...], gain_two[...], b_down[...]
 
     def second_norm(c):
         for copy in norms[c]:
@@ -733,22 +775,22 @@
     up_part(0)
     until(6)
     up_part(1)
-    units[2].step(0)
+    units[3].step(0)
     until(7)
     grads_in[0].wait()
     grads_in[1].start()
     second_norm(0)
-    owns = [fetch(branch_a, projected.at[0])]
+    owns = [fetch(own_branch.at[0], projected.at[0])]
     until(8)
     up_part(2)
     until(9)
     up_part(3)
-    units[3].step(0)
+    units[4].step(0)
     weights = fetch(w_qkv_hbm, w_qkv)
     until(10)
     grads_in[1].wait()
     second_norm(1)
-    owns.append(fetch(branch_b, projected.at[1]))
+    owns.append(fetch(own_branch.at[1], projected.at[1]))
 
     def turn_back(u, rows):
         return (u * cosine[rows, :] - turned(u) * sine[rows, :]).astype(bf16)
@@ -772,7 +814,7 @@
             ps, ds = [], []
             for h in range(2):
                 s = jnp.where(same, mm(k, qh[h], 1, 1), masked_score)
-                pr = jnp.exp(s - (lse_a, lse_b)[c][2 * p + h])
+                pr = jnp.exp(s - lse[c, 2 * p + h])
                 d = (pr * (mm(v, gh[h], 1, 1) - delta[h])).astype(bf16)
                 ps.append(pr.astype(bf16))
                 ds.append(d)
@@ -808,7 +850,7 @@
                     mm(mixed[n * chunk : (n + 1) * chunk, at], proj[n], 0, 0) for n in each
                 ).astype(bf16)
 
-            units[4].step(0)
+            units[5].step(0)
             now += 1
 
         @pl.loop(0, pairs)
@@ -835,7 +877,7 @@
             at = pl.ds(pl.multiple_of(r * 256, 256), 256)
             qkv[2 - i, at, :] = mm(rows_one[:, at], d_qkv[2 - i], 0, 0).astype(bf16)
 
-        units[5 + i].step(0)
+        units[6 + i].step(0)
     now += 3
     weights.wait()
     for c in each:
@@ -891,7 +933,7 @@
     smalls.wait()
     number = lax.broadcasted_iota(jnp.int32, small.shape, 0)
     everyone[0] = small[...] + jnp.where(number < 9, small_got[...], 0.0)
-    for n, b in enumerate(reversed(range(EDGES))):
+    for n, b in enumerate((1, 3, 2, 0)):
         copy = pltpu.make_async_remote_copy(
             src_ref=everyone.at[pl.ds(0, 1 << n)], dst_ref=everyone.at[pl.ds(1 << n, 1 << n)],
             send_sem=all_send.at[n], recv_sem=all_recv.at[n],
@@ -900,18 +942,30 @@
         copy.start()
         until(now + 1 + n)
         copy.wait()
+    mine[...] = everyone[0]
+    total[...] = sum(everyone[n] for n in range(1 << EDGES))
+    conds = jnp.concatenate([everyone[n, 11:12, : ada.shape[0]] for n in range(1 << EDGES)], axis=0)
+    spans = []
+    for j in range(ada.shape[1] // width):
+        vector, side = divmod(j * width, depth)
+        mods = jnp.concatenate([everyone[n, vector : vector + 1, side : side + width] for n in range(1 << EDGES)], axis=0)
+        rows = slice(j // 2 * ada.shape[0], (j // 2 + 1) * ada.shape[0])
+        spot = (dk, dv)[j % 2].at[rows]
+        spot[...] = lax.dot_general(
+            conds, mods, (((0,), (0,)), ((), ())), precision=lax.Precision.HIGHEST, preferred_element_type=f32
+        )
+        spans.append(pltpu.make_async_copy(spot, ada.at[:, j * width : (j + 1) * width], store.at[chunks + j]))
+        spans[-1].start()
     until(1000)
-    for copy in outputs:
+    for copy in (*outputs, *spans):
         copy.wait()
 
 
-def tail(
-    hidden, full_back, rows_two, grad_pre, qkv, mixed, rows_one, w_qkv, w_out, own_grad, got_grad, middle, projected,
-    own_branch, got_branch, tokens, cot, rows_of, known, lse, segr, segc, cosine, sine,
-):
+def tail(*args, ada_shape):
+    hidden, qkv, rows_one, w_qkv, w_out, own_grad, tokens = (args[n] for n in (0, 4, 6, 7, 8, 9, 15))
+    known = args[21]
     _, length, width = qkv.shape
-    chunks = len(mixed)
-    half, depth = got_grad[0].shape
+    chunks, half, depth = own_grad.shape
     anywhere, near = pl.BlockSpec(memory_space=pl.ANY), pl.BlockSpec(memory_space=pltpu.VMEM)
     shaped, kept = jax.ShapeDtypeStruct, pltpu.VMEM
     in_chunks = (chunks, half, depth)
@@ -922,28 +976,25 @@
         kept(in_chunks, bf16), kept(in_chunks, f32), kept(in_chunks, f32), kept(in_chunks, f32),
         kept(in_chunks, bf16), kept(in_chunks, bf16),
         *[kept((depth, depth), bf16)] * 4, kept((width, depth), bf16), kept(in_chunks, bf16),
-        kept((8, depth), f32), kept(known.shape, f32), kept(known.shape, f32),
-        pltpu.SemaphoreType.DMA((29,)), pltpu.SemaphoreType.DMA((chunks,)),
+        kept((8, depth), f32), kept(known.shape, f32), kept(known.shape, f32), kept((1 << EDGES, *known.shape), f32),
+        pltpu.SemaphoreType.DMA((30,)), pltpu.SemaphoreType.DMA((chunks + ada_shape[1] // width,)),
         pltpu.SemaphoreType.DMA((4 * chunks + 1,)), pltpu.SemaphoreType.DMA((4 * chunks + 1,)),
         pltpu.SemaphoreType.DMA((EDGES,)), pltpu.SemaphoreType.DMA((EDGES,)),
-        *unit_scratch(depth, depth) * 4, *unit_scratch(width, depth), *unit_scratch(depth, width) * 3,
+        *unit_scratch(WIDE, depth) * 2, *unit_scratch(depth, depth) * 3, *unit_scratch(width, depth), *unit_scratch(depth, width) * 3,
     ]
     return pl.pallas_call(
         tail_kernel,
-        in_specs=[anywhere] * 24 + [near] * 8,
-        out_specs=[anywhere] * 7 + [near] * 2,
+        in_specs=[anywhere] * 17 + [near] * 10,
+        out_specs=[anywhere] * 8 + [near] * 3,
         out_shape=[
             shaped((hidden.shape[1], depth), bf16), shaped((depth, hidden.shape[1]), bf16), shaped((width, depth), bf16),
             *[shaped((depth, width), bf16)] * 3, shaped(tokens.shape, bf16),
-            shaped(in_chunks, bf16), shaped((1 << EDGES, *known.shape), f32),
+            shaped(ada_shape, f32), shaped(in_chunks, bf16), shaped(known.shape, f32), shaped(known.shape, f32),
         ],
         scratch_shapes=scratch,
         compiler_params=pltpu.CompilerParams(collective_id=1, has_side_effects=True, vmem_limit_bytes=61 << 20),
         name="tail",
-    )(
-        hidden, full_back, rows_two, grad_pre, qkv, *mixed, rows_one, w_qkv, w_out, *own_grad, *got_grad, *middle,
-        *projected, *own_branch, *got_branch, tokens, cot, rows_of, known, *lse, segr, segc, cosine, sine,
-    )
+    )(*args)
 
 
 def body_pair(
@@ -955,9 +1006,6 @@
     half, chunk = own // chunks, length // chunks
     me = lax.axis_index("tensor")
 
-    def swap(values):
-        return lax.ppermute(values, "tensor", [(0, 1), (1, 0)])
-
     step = jnp.arange(length, dtype=jnp.int32)
     in_chunk = step % chunk
     places = jnp.where(in_chunk < half, me, 1 - me) * own + (step // chunk) * half + in_chunk % half
@@ -967,74 +1015,25 @@
     seg_cols = jnp.broadcast_to(segment[:, None], (length, 128))
 
     modulation = jnp.dot(cond, w_ada, preferred_element_type=f32)[0] + b_ada
-    shift_a, scale_a, gate_a, shift_m, scale_m, gate_m = jnp.split(modulation, 6)
-    cuts = [slice(c * half, (c + 1) * half) for c in range(chunks)]
-    x_rows = [tokens[cut].astype(f32) for cut in cuts]
-    grad_out = [cotangent[cut].astype(f32) for cut in cuts]
-    each = range(chunks)
-
-    def after(value, *others):
-        return lax.optimization_barrier((value, *others))[0]
-
-    act_one = [modulate(x_rows[c], gain_one, shift_a, scale_a).astype(bf16) for c in each]
-    back = [(grad_out[c] * gate_m).astype(bf16) for c in each]
-    got_one = [swap(act_one[0])]
-    got_one.append(swap(after(act_one[1], got_one[0])))
-    got_back = [swap(after(back[0], got_one[1]))]
-    got_back.append(swap(after(back[1], got_back[0])))
-    state = ()
-    for c in each:
-        state = project_pair(c, act_one[c], got_one[c], w_qkv, cosine, sine, state, length)
-    qkv, rows_one = state
-
-    mixed, lse, sums, projected, middle, act_two, got_two = [], [], [], [], [], [], []
-    for c in each:
-        waits = () if c == 0 else (got_back[0], sums[0])
-        m, l = attend_forward_pair(c, chunk, after(qkv, *waits) if c else qkv, seg_rows, seg_cols)
-        if c:
-            m = after(m, arrived[0])
-        mixed.append(m)
-        lse.append(l)
-        sums.append(jnp.dot(m[half:], w_out, preferred_element_type=f32).astype(bf16))
-        arrived = [swap(sums[0])] if c == 0 else [arrived[0], swap(sums[1])]
-    for c in each:
-        projected.append(jnp.dot(mixed[c][:half], w_out, preferred_element_type=f32) + arrived[c].astype(f32))
-        middle.append(x_rows[c] + gate_a * projected[c])
-        act_two.append(modulate(middle[c], gain_two, shift_m, scale_m).astype(bf16))
-        got_two.append(swap(act_two[c]))
-    got_two[0] = after(got_two[0], act_two[1])
-    state, pieces = (), []
-    for c in each:
-        out = mlp_pair(c, act_two[c], got_two[c], back[c], got_back[c], w_up, b_up, w_down, state, length)
-        state, rest = out[:4], out[4:]
-        pieces.append(rest)
-    rows_two, full_back, hidden, grad_pre = state
-    grad_b_up = sum(pieces[c][4] for c in each)[0]
-    grad_b_down = sum(jnp.sum(back[c].astype(f32), axis=0) for c in each)
-
-    none = jnp.zeros((width,), f32)
-    known = jnp.stack(
-        [
-            none, none, none, none, none, none, none, none, grad_b_down,
-            grad_b_up[:width], grad_b_up[width:],
-            jnp.pad(cond[0].astype(f32), (0, width - cond.shape[1])), none, none, none, none,
-        ]
+    sequence = jnp.pad(cond.astype(f32), ((0, 0), (0, width - cond.shape[1])))
+    mods = modulation.reshape(6, width)
+    (
+        qkv, mixed, rows_one, full_back, rows_two, hidden, grad_pre, own_grad, send_grad, middle, projected,
+        own_branch, send_branch, lse, known,
+    ) = head(
+        tokens, cotangent, w_qkv, w_out, w_up, w_down, mods, gain_one[None, :], gain_two[None, :], sequence,
+        b_up[None, :], seg_rows, seg_cols, cosine, sine, chunks=chunks,
     )
-    *sums, output, grad_x, everyone = tail(
-        hidden, full_back, rows_two, grad_pre, qkv, mixed, rows_one, w_qkv, w_out,
-        *[[pieces[c][n] for c in each] for n in range(2)], middle, projected,
-        *[[pieces[c][n] for c in each] for n in range(2, 4)], tokens, cotangent,
-        jnp.stack([gain_two, scale_m, gate_a, gain_one, scale_a, gate_m, b_down, none]), known,
-        lse, seg_rows, seg_cols, cosine, sine,
+    *sums, output, grad_w_ada, grad_x, mine, total = tail(
+        hidden, full_back, rows_two, grad_pre, qkv, mixed, rows_one, w_qkv, w_out, own_grad, send_grad,
+        middle, projected, own_branch, send_branch, tokens, cotangent,
+        mods, gain_one[None, :], gain_two[None, :], b_down[None, :], known,
+        lse, seg_rows, seg_cols, cosine, sine, ada_shape=w_ada.shape,
     )
     grad_w_down, grad_w_up, grad_w_out, grad_q, grad_k, grad_v = [s.astype(f32) for s in sums]
     grad_w_qkv = jnp.stack([grad_q, grad_k, grad_v])
     grad_x = grad_x.reshape(own, width)
-    mods = everyone[:, :6].reshape(-1, 6 * width)
-    conds = everyone[:, 11, : cond.shape[1]]
-    grad_cond = jnp.dot(w_ada.astype(f32), mods[0], precision=lax.Precision.HIGHEST)[None, :]
-    grad_w_ada = jnp.einsum("nc,nm->cm", conds, mods, precision=lax.Precision.HIGHEST, preferred_element_type=f32)
-    total = jnp.sum(everyone, axis=0)
+    grad_cond = jnp.dot(w_ada.astype(f32), mine[:6].reshape(-1), precision=lax.Precision.HIGHEST)[None, :]
     grad_b_ada = total[:6].reshape(-1)
     grad_gain_one, grad_gain_two, grad_b_down = total[6], total[7], total[8]
     grad_b_up = total[9:11].reshape(-1)

time: 332 us -> 314 us (0.946)
  Pallas kernels: 225 us -> 272 us
  waiting for transfers between devices: 36.4 us -> 0 us
  starting transfers between devices: 11 us -> 0 us
  other arithmetic: 29.9 us -> 22.6 us
  matrix products: 10.1 us -> 2.81 us
    pallas_call x7 -> x2, Pallas kernels: 225 us -> 272 us  [the longest x1 164 us: tail(): pl.pallas_call(tail_kernel, in_specs=[anywhere] * 17 + [near] * 10, out_s...]
    ppermute x8 -> x0, waiting for transfers between devices: 36.4 us -> none  [swap(): return lax.ppermute(values, 'tensor', [(0, 1), (1, 0)])]
    ppermute x8 -> x0, starting transfers between devices: 11 us -> none  [swap(): return lax.ppermute(values, 'tensor', [(0, 1), (1, 0)])]
    reduce_sum x7 -> x1, other arithmetic: 7.72 us -> 0.1 us  [documents(): doc_first = jnp.sum(inside * starts[None, :], axis=1)]
    dot_general x6 -> x1, matrix products: 9.11 us -> 1.84 us  [body_pair(): jnp.dot(w_ada.astype(f32), mine[:6].reshape(-1), precision=lax.Precision....]
    unnamed x91 -> x27, local copies, waits for them, and re-layouts: 7.87 us -> 7.29 us
  transfers between devices with their start and end apart: 8 -> 0, of which waited for: 6 -> 0; matrix products, arithmetic and copies ran while one was open for 2% -> 0% of each run, Pallas kernels for 13% -> 0%
where the time goes in v6:
time: 314 us; the launch traced here: 310 us
  Pallas kernels  272 us (87%)
  other arithmetic  22.6 us (7%)
  local copies, waits for them, and re-layouts  11.7 us (4%)
    pallas_call x1, Pallas kernels, tail(): pl.pallas_call(tail_kernel, in_specs=[anywhere] * 17 + [near] * 10, out_s...  164 us
    pallas_call x1, Pallas kernels, head(): pl.pallas_call(head_kernel, in_specs=[anywhere] * 6 + [near] * len(near_a...  108 us
    convert_element_type x3, other arithmetic, body_pair(): s.astype(f32)  11.7 us
    unnamed x27, local copies, waits for them, and re-layouts  7.29 us

profile of v6, /device:TPU:0, one launch (start us, length us, event | category | flops | bytes accessed | tf_op | source)
XLA Modules:
  0.0 310.3 jit_solution(12204598591483074235)
XLA Ops:
  0.6 0.0 copy-start
  0.7 0.9 select_reduce_fusion.2
  1.6 0.7 fusion.10
  2.2 1.3 pad_convert_fusion.sequence
  3.5 0.1 select_reduce_fusion
  3.6 0.0 copy-start.9
  3.6 0.0 copy-done
  3.6 1.0 fusion.11
  4.6 0.7 add.63
  5.3 0.6 reshape.99.mods
  6.0 1.0 broadcast_in_dim.50.segc
  7.0 1.9 multiply_sine_fusion
  8.8 1.8 pad_maximum_fusion
  10.7 0.0 copy-done.9
  10.7 108.4 %head.1 = (bf16[3,1024,512]{2,1,0:T(8,128)(2,1)}, bf16[1024,512]{1,0:T(8,128)(2,1)}, bf16[1024,1024]{1,0:T(8,128)(2,1)}, bf16[1024,1024]{1,0:T(8,128)(2,1)}, bf1...) custom-call(bf16[512,1024]{1,0:T(8,128)(2,1)} %tokens_hbm.3, ...), custom_call_target="tpu_custom_call" | custom-call | tf_op jit(solution)/shard_map/head/pallas_call | solution.py:615
  119.2 163.8 %tail.1 = (bf16[2048,1024]{1,0:T(8,128)(2,1)}, bf16[1024,2048]{1,0:T(8,128)(2,1)}, bf16[512,1024]{1,0:T(8,128)(2,1)}, bf16[1024,512]{1,0:T(8,128)(2,1)}, bf16[10...) custom-call(bf16[1024,2048]{1,0:T(8,128)(2,1)} %get-tuple-element.39, ...), custom_call_target="tpu_custom_call" | custom-call | tf_op jit(solution)/shard_map/tail/pallas_call | solution.py:985
  283.0 0.0 copy-start.4
  283.0 0.9 slice_bitcast_fusion.1
  283.9 0.6 copy.30
  284.5 1.4 fusion.13
  285.9 0.8 slice.19
  286.7 0.6 reshape.102
  287.3 0.0 copy-start.5
  287.3 0.0 copy-start.6
  287.3 0.9 slice_bitcast_fusion
  288.2 1.8 fusion.14
  290.1 2.8 convert_element_type.26
  292.9 0.0 copy-done.4
  292.9 0.0 copy-done.5
  292.9 0.0 copy-done.6
  292.9 0.0 copy-start.2
  292.9 3.5 %maximum_convert_fusion = f32[3,1024,512]{2,1,0:T(8,128)} fusion(bf16[1,1024,512]{2,1,0:T(8,128)(2,1)S(1)} %bitcast.40, bf16[1,1024,512]{2,1,0:T(8,128)(2,1)S(1)} %bitcast.39, bf16[1,1024,512]{2,1,0:T(8,128)(2,1)S(1)} %bitcast.38), kind=kLoop, calls=%fused_computation | loop fusion | flops 4718592 | bytes 9437184 | tf_op jit(solution)/shard_map/stack | solution.py:1034
  296.4 0.6 copy-done.2
  296.9 0.0 copy-start.1
  296.9 4.4 %convert_element_type.27 = f32[1024,2048]{1,0:T(8,128)} convert(bf16[1024,2048]{1,0:T(8,128)(2,1)S(1)} %copy-done.2) | non-fusion elementwise | flops 2097152 | bytes 12582912 | tf_op jit(solution)/shard_map/convert_element_type | solution.py:1033
  301.4 0.0 copy-done.1
  301.4 0.0 copy-start.8
  301.4 0.0 copy-start.7
  301.4 4.4 %convert_element_type.28 = f32[2048,1024]{1,0:T(8,128)} convert(bf16[2048,1024]{1,0:T(8,128)(2,1)S(1)} %copy-done.1) | non-fusion elementwise | flops 2097152 | bytes 12582912 | tf_op jit(solution)/shard_map/convert_element_type | solution.py:1033
  305.8 0.0 copy-done.8
  305.8 0.0 copy-start.3
  305.8 1.0 copy.34
  306.8 0.0 copy-done.7
  306.8 1.0 copy.35
  307.8 0.7 copy-done.3
  308.5 1.7 copy.36
  (4 shorter events, 0.1 us)
Async XLA Ops:
  0.6 3.0 copy-start
  3.6 7.1 %copy-start.9 = (s32[1024]{0:T(1024)}, s32[1024]{0:T(1024)S(1)}, u32[]{:S(2)}) copy-start(s32[1024]{0:T(1024)S(1)} %get-tuple-element.66) | copy-start | bytes 12292
  283.0 9.9 %copy-start.4 = (bf16[1024,512]{1,0:T(8,128)(2,1)S(1)}, bf16[1024,512]{1,0:T(8,128)(2,1)}, u32[]{:S(2)}) copy-start(bf16[1024,512]{1,0:T(8,128)(2,1)} %get-tuple-element.59) | copy-start | bytes 3145732
  287.3 5.6 %copy-start.5 = (bf16[1024,512]{1,0:T(8,128)(2,1)S(1)}, bf16[1024,512]{1,0:T(8,128)(2,1)}, u32[]{:S(2)}) copy-start(bf16[1024,512]{1,0:T(8,128)(2,1)} %get-tuple-element.60) | copy-start | bytes 3145732
  287.3 5.6 %copy-start.6 = (bf16[1024,512]{1,0:T(8,128)(2,1)S(1)}, bf16[1024,512]{1,0:T(8,128)(2,1)}, u32[]{:S(2)}) copy-start(bf16[1024,512]{1,0:T(8,128)(2,1)} %get-tuple-element.61) | copy-start | bytes 3145732
  292.9 4.1 %copy-start.2 = (bf16[1024,2048]{1,0:T(8,128)(2,1)S(1)}, bf16[1024,2048]{1,0:T(8,128)(2,1)}, u32[]{:S(2)}) copy-start(bf16[1024,2048]{1,0:T(8,128)(2,1)} %get-tuple-element.63) | copy-start | bytes 12582916
  296.9 4.5 %copy-start.1 = (bf16[2048,1024]{1,0:T(8,128)(2,1)S(1)}, bf16[2048,1024]{1,0:T(8,128)(2,1)}, u32[]{:S(2)}) copy-start(bf16[2048,1024]{1,0:T(8,128)(2,1)} %get-tuple-element.64) | copy-start | bytes 12582916
  301.4 4.4 %copy-start.8 = (bf16[512,1024]{1,0:T(8,128)(2,1)S(1)}, bf16[512,1024]{1,0:T(8,128)(2,1)}, u32[]{:S(2)}) copy-start(bf16[512,1024]{1,0:T(8,128)(2,1)} %get-tuple-element.87) | copy-start | bytes 3145732
  301.4 5.4 %copy-start.7 = (bf16[2,256,1024]{2,1,0:T(8,128)(2,1)S(1)}, bf16[2,256,1024]{2,1,0:T(8,128)(2,1)}, u32[]{:S(2)}) copy-start(bf16[2,256,1024]{2,1,0:T(8,128)(2,1)} %get-tuple-element.55) | copy-start | bytes 3145732
  305.8 2.6 copy-start.3
